TPU v7x, 32 devices: a whole 2x2x4 slice. The times are simulated.
32 devices in a mesh: face: 8 (over y, x, core), band: 4 (over z).
Axes of the slice: x: 2, y: 2, z: 4, core: 2. Of those that a mesh axis runs over, the one named last changes fastest.
Arguments:
- coarse: bfloat16 [48, 128, 256], P('band', 'face'), may hold values from -6 to 6
- skip: bfloat16 [96, 256, 256], P('band', 'face'), may hold values from -6 to 6
- up_weight: bfloat16 [3, 3, 256, 256], replicated, may hold values from -0.25 to 0.25
- conv_weight: bfloat16 [3, 3, 256, 256], replicated, may hold values from -0.125 to 0.125
- cotangent: bfloat16 [96, 256, 256], P('band', 'face'), may hold values from -6 to 6
Outputs:
- decoded: bfloat16 [96, 256, 256], P('band', 'face')
- grad_coarse: bfloat16 [48, 128, 256], P('band', 'face')
- grad_up_weight: float32 [2304, 256], P('face', 'band')
- grad_conv_weight: float32 [2304, 256], P('face', 'band')
All inputs are finite; a program needn't handle non-finite values.
Results may differ from a plain program's by a relative error of at most 0.0049.
Values may be sent and summed in bfloat16 or wider, within the bound.
No kernel may reach another device: no remote copies, remote signals or barrier semaphores. Data moves between devices by JAX's collectives and lax.ppermute only.
A program may use at most 128 MiB of HBM per device.

v0:
```python
import jax
import jax.numpy as jnp
from jax import lax
from jax.sharding import PartitionSpec as P

forward_taps = ((1, 1), (0, 0), (1, 0))
backward_taps = ((1, 0), (0, 1), (1, 1))


def with_halo(x, sides, width, wrap):
    for axis, dim in sides:
        count, length = (lax.axis_size(axis), x.shape[dim])
        up = [(i, (i + 1) % count) for i in range(count if wrap else count - 1)]
        down = [(j, i) for i, j in up]
        last = lax.slice_in_dim(x, length - width, length, axis=dim)
        first = lax.slice_in_dim(x, 0, width, axis=dim)
        before = lax.ppermute(last, axis, up)
        after = lax.ppermute(first, axis, down)
        x = jnp.concatenate([before, x, after], axis=dim)
    return x


def from_behind(block, axis, distance):
    devices = range(lax.axis_size(axis))
    route = [((i - distance) % len(devices), i) for i in devices]
    return lax.ppermute(block, axis, route)


def from_behind_2(block, axis, distance):
    devices = range(lax.axis_size(axis))
    route = [(i - distance, i) for i in devices if i - distance in devices]
    return lax.ppermute(block, axis, route)


def up_phases(extended, up_weight, n_rows, n_cols):
    channels = extended.shape[-1]
    totals = {}
    for row_tap in range(3):
        row_phase, row_off = forward_taps[row_tap]
        for col_tap in range(3):
            col_phase, col_off = forward_taps[col_tap]
            source = extended[row_off : row_off + n_rows, col_off : col_off + n_cols].reshape(
                -1, channels
            )
            term = jnp.dot(source, up_weight[row_tap, col_tap], preferred_element_type=jnp.float32)
            name = (row_phase, col_phase)
            totals[name] = totals[name] + term if name in totals else term
    per_row = []
    for row_phase in range(2):
        per_row.append(
            jnp.stack(
                [
                    totals[row_phase, col_phase].reshape(n_rows, n_cols, channels)
                    for col_phase in range(2)
                ],
                axis=2,
            )
        )
    return jnp.stack(per_row, axis=1)


def conv_forward(act_pad, conv_weight, n_rows, n_cols):
    channels = act_pad.shape[-1]
    total = jnp.zeros((n_rows * n_cols, channels), jnp.float32)
    for row_tap in range(3):
        for col_tap in range(3):
            source = act_pad[row_tap : row_tap + n_rows, col_tap : col_tap + n_cols].reshape(
                -1, channels
            )
            total = total + jnp.dot(
                source, conv_weight[row_tap, col_tap], preferred_element_type=jnp.float32
            )
    return total


def conv_backward(grad_pad, conv_weight, n_rows, n_cols):
    channels = grad_pad.shape[-1]
    total = jnp.zeros((n_rows * n_cols, channels), jnp.float32)
    for row_tap in range(3):
        for col_tap in range(3):
            source = grad_pad[
                2 - row_tap : 2 - row_tap + n_rows, 2 - col_tap : 2 - col_tap + n_cols
            ].reshape(-1, channels)
            total = total + jnp.dot(
                source, conv_weight[row_tap, col_tap].T, preferred_element_type=jnp.float32
            )
    return total


def conv_wgrad(act_pad, grad_flat, n_rows, n_cols):
    channels = act_pad.shape[-1]
    blocks = []
    for row_tap in range(3):
        for col_tap in range(3):
            source = act_pad[row_tap : row_tap + n_rows, col_tap : col_tap + n_cols].reshape(
                -1, channels
            )
            blocks.append(jnp.dot(source.T, grad_flat, preferred_element_type=jnp.float32))
    return jnp.concatenate(blocks, axis=0)


def down_backward(grad_ext, coarse, up_weight, n_rows, n_cols):
    channels = coarse.shape[-1]
    coarse_flat = coarse.reshape(-1, channels)
    grad_in = jnp.zeros((n_rows * n_cols, channels), jnp.float32)
    blocks = []
    for row_tap in range(3):
        row_phase, row_start = backward_taps[row_tap]
        for col_tap in range(3):
            col_phase, col_start = backward_taps[col_tap]
            source = grad_ext[
                row_start : row_start + n_rows, row_phase, col_start : col_start + n_cols, col_phase
            ].reshape(-1, channels)
            grad_in = grad_in + jnp.dot(
                source, up_weight[row_tap, col_tap].T, preferred_element_type=jnp.float32
            )
            blocks.append(jnp.dot(coarse_flat.T, source, preferred_element_type=jnp.float32))
    return (grad_in, jnp.concatenate(blocks, axis=0))


def fine_halo(field):
    beside_all = with_halo(field, (("face", 1),), 1, True)
    return with_halo(beside_all, (("band", 0),), 1, False)


def local(coarse, skip, up_weight, conv_weight, cotangent):
    n_rows, n_cols, channels = coarse.shape
    padded = jnp.pad(coarse, ((1, 1), (1, 1), (0, 0)))
    spread = up_phases(padded, up_weight, n_rows + 1, n_cols + 1)
    col_part = from_behind(spread[:, :, :1, 1:], "face", -1)
    spread = spread.at[:, :, n_cols:, 1:].add(col_part)
    spread = spread[:, :, 1:]
    row_part = from_behind_2(spread[:1, 1:], "band", -1)
    spread = spread.at[n_rows:, 1:].add(row_part)
    upsampled = spread[1:]
    preact = upsampled.reshape(2 * n_rows, 2 * n_cols, channels) + skip.astype(jnp.float32)
    act = jax.nn.silu(preact).astype(jnp.bfloat16)
    act_pad = fine_halo(act)
    decoded = conv_forward(act_pad, conv_weight, 2 * n_rows, 2 * n_cols)
    decoded = decoded.reshape(2 * n_rows, 2 * n_cols, channels).astype(jnp.bfloat16)
    grad_pad = fine_halo(cotangent)
    grad_act = conv_backward(grad_pad, conv_weight, 2 * n_rows, 2 * n_cols).reshape(
        2 * n_rows, 2 * n_cols, channels
    )
    sigma = jax.nn.sigmoid(preact)
    grad_pre = (grad_act * sigma * (1.0 + preact * (1.0 - sigma))).astype(jnp.bfloat16)
    phased = grad_pre.reshape(n_rows, 2, n_cols, 2, channels)
    col_prev = from_behind(phased[:, :, n_cols - 1 :, 1:], "face", 1)
    col_full = jnp.pad(col_prev, ((0, 0), (0, 0), (0, 0), (1, 0), (0, 0)))
    widened_grad = jnp.concatenate([col_full, phased], axis=2)
    row_prev = from_behind_2(widened_grad[n_rows - 1 :, 1:], "band", 1)
    row_full = jnp.pad(row_prev, ((0, 0), (1, 0), (0, 0), (0, 0), (0, 0)))
    grad_ext = jnp.concatenate([row_full, widened_grad], axis=0)
    grad_in, grad_up = down_backward(grad_ext, coarse, up_weight, n_rows, n_cols)
    grad_conv = conv_wgrad(act_pad, cotangent.reshape(-1, channels), 2 * n_rows, 2 * n_cols)
    grad_coarse = grad_in.reshape(n_rows, n_cols, channels).astype(jnp.bfloat16)
    face_parts = (
        lax.psum_scatter(grad_up, "face", scatter_dimension=0, tiled=True),
        lax.psum_scatter(grad_conv, "face", scatter_dimension=0, tiled=True),
    )
    owned_up, owned_conv = (
        lax.psum_scatter(face_parts[0], "band", scatter_dimension=1, tiled=True),
        lax.psum_scatter(face_parts[1], "band", scatter_dimension=1, tiled=True),
    )
    return (decoded, grad_coarse, owned_up, owned_conv)


def solution(mesh):
    return jax.shard_map(
        local,
        mesh=mesh,
        in_specs=(
            P("band", "face", None),
            P("band", "face", None),
            P(),
            P(),
            P("band", "face", None),
        ),
        out_specs=(
            P("band", "face", None),
            P("band", "face", None),
            P("face", "band"),
            P("face", "band"),
        ),
        check_vma=False,
    )
```

profile of v0, /device:TPU:0, one launch (start us, length us, event | category | flops | bytes accessed | tf_op | source)
XLA Modules:
  0.0 200.5 jit_solution(9083889292047308268)
XLA Ops:
  7.2 1.2 pad_slice_fusion.7
  10.8 3.4 %collective-permute-start = (f32[13,2,1,1,256]{4,2,0,3,1:T(1,128)S(1)}, f32[13,2,1,1,256]{4,2,0,3,1:T(1,128)S(1)}, u32[]{:S(2)}, u32[]{:S(2)}) collective-permute-start(f32[13,2,1,1,256]{4,2,0,3,1:T(1,128)S(1)} %fusion.110), channel_id=1, source_target_pairs={{4,0},{8,4},{12,8},{16,12},{20,16},{24,20},{28,24},{0,28},{5,1},{9... | collective-permute-start | bytes 79880 | tf_op jit(solution)/shard_map/ppermute | solution.py:26
  14.3 2.6 %collective-permute-start.7 = (bf16[24,1,256]{2,1,0:T(2,128)(2,1)S(1)}, bf16[24,1,256]{2,1,0:T(2,128)(2,1)S(1)}, u32[]{:S(2)}, u32[]{:S(2)}) collective-permute-start(bf16[24,1,256]{2,1,0:T(2,128)(2,1)S(1)} %get-tuple-element.76), channel_id=1, source_target_pairs={{4,0},{8,4},{12,8},{16,12},{20,16},{24,20},{28,24},{0,28},{5,1},{9... | collective-permute-start | bytes 36872 | tf_op jit(solution)/shard_map/ppermute | solution.py:18
  18.5 1.3 collective-permute-start.8
  19.8 4.5 %collective-permute-start.9 = (bf16[1,34,256]{2,1,0:T(8,128)(2,1)S(1)}, bf16[1,34,256]{2,1,0:T(8,128)(2,1)S(1)}, u32[]{:S(2)}, u32[]{:S(2)}) collective-permute-start(bf16[1,34,256]{2,1,0:T(8,128)(2,1)S(1)} %get-tuple-element.62), channel_id=1, source_target_pairs={{0,1},{1,2},{2,3},{4,5},{5,6},{6,7},{8,9},{9,10},{10,11},{12,13},{... | collective-permute-start | bytes 52232 | tf_op jit(solution)/shard_map/ppermute | solution.py:17
  25.7 1.3 collective-permute-start.1
  32.9 1.4 reshape.208
  34.3 2.5 %multiply_convert_fusion = (bf16[24,32,256]{2,1,0:T(8,128)(2,1)}, bf16[24,32,256]{2,1,0:T(8,128)(2,1)S(1)}) fusion(f32[24,32,256]{2,1,0:T(8,128)} %bitcast.281, f32[24,32,256]{2,1,0:T(8,128)} %reshape.208, bf16[24,32,256]{2,1,0:T(8,128)(2,1)S(1)} %copy-done.17), kind=kLoop, calls=%fused_computation.75 | loop fusion | flops 2555904 | bytes 2752512 | tf_op jit(solution)/shard_map/convert_element_type | solution.py:146
  36.9 2.6 %collective-permute-start.3 = (bf16[24,1,256]{2,1,0:T(2,128)(2,1)S(1)}, bf16[24,1,256]{2,1,0:T(2,128)(2,1)S(1)}, u32[]{:S(2)}, u32[]{:S(2)}) collective-permute-start(bf16[24,1,256]{2,1,0:T(2,128)(2,1)S(1)} %get-tuple-element.80), channel_id=1, source_target_pairs={{4,0},{8,4},{12,8},{16,12},{20,16},{24,20},{28,24},{0,28},{5,1},{9... | collective-permute-start | bytes 36872 | tf_op jit(solution)/shard_map/ppermute | solution.py:18
  39.5 1.6 collective-permute-done.2
  41.2 4.6 %collective-permute-start.4 = (bf16[1,34,256]{2,1,0:T(8,128)(2,1)S(1)}, bf16[1,34,256]{2,1,0:T(8,128)(2,1)S(1)}, u32[]{:S(2)}, u32[]{:S(2)}) collective-permute-start(bf16[1,34,256]{2,1,0:T(8,128)(2,1)S(1)} %get-tuple-element.65), channel_id=1, source_target_pairs={{0,1},{1,2},{2,3},{4,5},{5,6},{6,7},{8,9},{9,10},{10,11},{12,13},{... | collective-permute-start | bytes 52232 | tf_op jit(solution)/shard_map/ppermute | solution.py:17
  45.9 1.3 collective-permute-start.5
  47.5 4.0 %collective-permute-done.5 = bf16[1,34,256]{2,1,0:T(8,128)(2,1)S(1)} collective-permute-done((bf16[1,34,256]{2,1,0:T(8,128)(2,1)S(1)}, bf16[1,34,256]{2,1,0:T(8,128)(2,1)S(1)}, u32[]{:S(2)}, u32[]{:S(2)}) %collective-permute-start.5) | collective-permute-done | bytes 17440 | tf_op jit(solution)/shard_map/ppermute | solution.py:18
  62.4 4.1 %collective-permute-done.10 = bf16[12,2,1,1,256]{4,2,0,3,1:T(2,128)(2,1)S(1)} collective-permute-done((bf16[12,2,1,1,256]{4,2,0,3,1:T(2,128)(2,1)S(1)}, bf16[12,2,1,1,256]{4,2,0,3,1:T(2,128)(2,1)S(1)}, u32[]{:S(2)}, u32[]{:S(2)}) %collective-permute-start.10) | collective-permute-done | bytes 12320 | tf_op jit(solution)/shard_map/ppermute | solution.py:26
  66.6 3.5 %collective-permute-start.11 = (bf16[1,1,17,2,256]{4,2,0,3,1:T(8,128)(2,1)S(1)}, bf16[1,1,17,2,256]{4,2,0,3,1:T(8,128)(2,1)S(1)}, u32[]{:S(2)}, u32[]{:S(2)}) collective-permute-start(bf16[1,1,17,2,256]{4,2,0,3,1:T(8,128)(2,1)S(1)} %pad_maximum_fusion.9), channel_id=1, source_target_pairs={{0,1},{1,2},{2,3},{4,5},{5,6},{6,7},{8,9},{9,10},{10,11},{12,13},{... | collective-permute-start | bytes 52232 | tf_op jit(solution)/shard_map/ppermute | solution.py:32
  70.2 1.4 collective-permute-done.11
  87.4 15.1 %reduce-scatter.11.cloned.1.call-done = f32[288,256]{1,0:T(8,128)} async-done(((f32[2304,256]{1,0:T(8,128)}), f32[288,256]{1,0:T(8,128)}) %reduce-scatter.11.cloned.1.call-update) | async-done | bytes 294928 | tf_op jit(solution)/shard_map/reduce_scatter | solution.py:159
  102.6 1.9 copy.31
  104.5 1.6 fusion.3
  106.4 42.4 %reduce-scatter.9.cloned.1.call-done = f32[288,256]{1,0:T(8,128)} async-done(((f32[2304,256]{1,0:T(8,128)}), f32[288,256]{1,0:T(8,128)}) %reduce-scatter.9.cloned.1.call-update) | async-done | bytes 294928 | tf_op jit(solution)/shard_map/reduce_scatter | solution.py:158
  148.8 1.9 copy.29
  150.7 1.8 fusion.24
  154.5 17.8 %reduce-scatter.15.cloned.1.call-done = f32[64,288]{1,0:T(8,128)} async-done(((f32[256,288]{1,0:T(8,128)}), f32[64,288]{1,0:T(8,128)}) %reduce-scatter.15.cloned.1.call-update) | async-done | bytes 73744
  172.3 21.7 %reduce-scatter.13.cloned.1.call-done = f32[64,288]{1,0:T(8,128)} async-done(((f32[256,288]{1,0:T(8,128)}), f32[64,288]{1,0:T(8,128)}) %reduce-scatter.13.cloned.1.call-update) | async-done | bytes 73744
  (143 shorter events, 40.4 us)
Async XLA Ops:
  7.2 95.4 %reduce-scatter.11.cloned.1.call-start = ((), (), s32[]{:S(2)}) async-start(), calls=%async_computation.5 | async-start | bytes 2654208 | tf_op jit(solution)/shard_map/reduce_scatter | solution.py:159
  10.6 6.3 %copy-start.2 = (bf16[3,3,256,256]{3,2,1,0:T(8,128)(2,1)S(1)}, bf16[3,3,256,256]{3,2,1,0:T(8,128)(2,1)}, u32[]{:S(2)}) copy-start(bf16[3,3,256,256]{3,2,1,0:T(8,128)(2,1)} %param.12) | copy-start | bytes 3538948
  10.8 3.4 %copy-start.1 = (bf16[24,32,256]{2,1,0:T(8,128)(2,1)S(1)}, bf16[24,32,256]{2,1,0:T(8,128)(2,1)}, u32[]{:S(2)}) copy-start(bf16[24,32,256]{2,1,0:T(8,128)(2,1)} %param.13) | copy-start | bytes 1179652
  10.8 14.6 %collective-permute-start = (f32[13,2,1,1,256]{4,2,0,3,1:T(1,128)S(1)}, f32[13,2,1,1,256]{4,2,0,3,1:T(1,128)S(1)}, u32[]{:S(2)}, u32[]{:S(2)}) collective-permute-start(f32[13,2,1,1,256]{4,2,0,3,1:T(1,128)S(1)} %fusion.110), channel_id=1, source_target_pairs={{4,0},{8,4},{12,8},{16,12},{20,16},{24,20},{28,24},{0,28},{5,1},{9... | collective-permute-start | bytes 79880 | tf_op jit(solution)/shard_map/ppermute | solution.py:26
  14.2 4.2 %collective-permute-start.6 = (bf16[24,1,256]{2,1,0:T(2,128)(2,1)S(1)}, bf16[24,1,256]{2,1,0:T(2,128)(2,1)S(1)}, u32[]{:S(2)}, u32[]{:S(2)}) collective-permute-start(bf16[24,1,256]{2,1,0:T(2,128)(2,1)S(1)} %get-tuple-element.75), channel_id=1, source_target_pairs={{0,4},{4,8},{8,12},{12,16},{16,20},{20,24},{24,28},{28,0},{1,5},{5... | collective-permute-start | bytes 36872 | tf_op jit(solution)/shard_map/ppermute | solution.py:17
  14.3 4.2 %collective-permute-start.7 = (bf16[24,1,256]{2,1,0:T(2,128)(2,1)S(1)}, bf16[24,1,256]{2,1,0:T(2,128)(2,1)S(1)}, u32[]{:S(2)}, u32[]{:S(2)}) collective-permute-start(bf16[24,1,256]{2,1,0:T(2,128)(2,1)S(1)} %get-tuple-element.76), channel_id=1, source_target_pairs={{4,0},{8,4},{12,8},{16,12},{20,16},{24,20},{28,24},{0,28},{5,1},{9... | collective-permute-start | bytes 36872 | tf_op jit(solution)/shard_map/ppermute | solution.py:18
  18.5 8.5 %collective-permute-start.8 = (bf16[1,34,256]{2,1,0:T(8,128)(2,1)S(1)}, bf16[1,34,256]{2,1,0:T(8,128)(2,1)S(1)}, u32[]{:S(2)}, u32[]{:S(2)}) collective-permute-start(bf16[1,34,256]{2,1,0:T(8,128)(2,1)S(1)} %get-tuple-element.61), channel_id=1, source_target_pairs={{1,0},{2,1},{3,2},{5,4},{6,5},{7,6},{9,8},{10,9},{11,10},{13,12},{... | collective-permute-start | bytes 52232 | tf_op jit(solution)/shard_map/ppermute | solution.py:18
  19.8 7.2 %collective-permute-start.9 = (bf16[1,34,256]{2,1,0:T(8,128)(2,1)S(1)}, bf16[1,34,256]{2,1,0:T(8,128)(2,1)S(1)}, u32[]{:S(2)}, u32[]{:S(2)}) collective-permute-start(bf16[1,34,256]{2,1,0:T(8,128)(2,1)S(1)} %get-tuple-element.62), channel_id=1, source_target_pairs={{0,1},{1,2},{2,3},{4,5},{5,6},{6,7},{8,9},{9,10},{10,11},{12,13},{... | collective-permute-start | bytes 52232 | tf_op jit(solution)/shard_map/ppermute | solution.py:17
  25.7 6.5 %collective-permute-start.1 = (f32[1,1,16,2,256]{4,2,0,3,1:T(8,128)S(1)}, f32[1,1,16,2,256]{4,2,0,3,1:T(8,128)S(1)}, u32[]{:S(2)}, u32[]{:S(2)}) collective-permute-start(f32[1,1,16,2,256]{4,2,0,3,1:T(8,128)S(1)} %slice.381), channel_id=1, source_target_pairs={{1,0},{2,1},{3,2},{5,4},{6,5},{7,6},{9,8},{10,9},{11,10},{13,12},{... | collective-permute-start | bytes 98312 | tf_op jit(solution)/shard_map/ppermute | solution.py:32
  36.8 4.3 %collective-permute-start.2 = (bf16[24,1,256]{2,1,0:T(2,128)(2,1)S(1)}, bf16[24,1,256]{2,1,0:T(2,128)(2,1)S(1)}, u32[]{:S(2)}, u32[]{:S(2)}) collective-permute-start(bf16[24,1,256]{2,1,0:T(2,128)(2,1)S(1)} %get-tuple-element.79), channel_id=1, source_target_pairs={{0,4},{4,8},{8,12},{12,16},{16,20},{20,24},{24,28},{28,0},{1,5},{5... | collective-permute-start | bytes 36872 | tf_op jit(solution)/shard_map/ppermute | solution.py:17
  36.9 4.3 %collective-permute-start.3 = (bf16[24,1,256]{2,1,0:T(2,128)(2,1)S(1)}, bf16[24,1,256]{2,1,0:T(2,128)(2,1)S(1)}, u32[]{:S(2)}, u32[]{:S(2)}) collective-permute-start(bf16[24,1,256]{2,1,0:T(2,128)(2,1)S(1)} %get-tuple-element.80), channel_id=1, source_target_pairs={{4,0},{8,4},{12,8},{16,12},{20,16},{24,20},{28,24},{0,28},{5,1},{9... | collective-permute-start | bytes 36872 | tf_op jit(solution)/shard_map/ppermute | solution.py:18
  41.2 6.3 %collective-permute-start.4 = (bf16[1,34,256]{2,1,0:T(8,128)(2,1)S(1)}, bf16[1,34,256]{2,1,0:T(8,128)(2,1)S(1)}, u32[]{:S(2)}, u32[]{:S(2)}) collective-permute-start(bf16[1,34,256]{2,1,0:T(8,128)(2,1)S(1)} %get-tuple-element.65), channel_id=1, source_target_pairs={{0,1},{1,2},{2,3},{4,5},{5,6},{6,7},{8,9},{9,10},{10,11},{12,13},{... | collective-permute-start | bytes 52232 | tf_op jit(solution)/shard_map/ppermute | solution.py:17
  45.9 5.7 %collective-permute-start.5 = (bf16[1,34,256]{2,1,0:T(8,128)(2,1)S(1)}, bf16[1,34,256]{2,1,0:T(8,128)(2,1)S(1)}, u32[]{:S(2)}, u32[]{:S(2)}) collective-permute-start(bf16[1,34,256]{2,1,0:T(8,128)(2,1)S(1)} %get-tuple-element.66), channel_id=1, source_target_pairs={{1,0},{2,1},{3,2},{5,4},{6,5},{7,6},{9,8},{10,9},{11,10},{13,12},{... | collective-permute-start | bytes 52232 | tf_op jit(solution)/shard_map/ppermute | solution.py:18
  47.5 7.5 %copy-start.11 = (bf16[24,32,256]{2,1,0:T(8,128)(2,1)}, bf16[24,32,256]{2,1,0:T(8,128)(2,1)S(1)}, u32[]{:S(2)}) copy-start(bf16[24,32,256]{2,1,0:T(8,128)(2,1)S(1)} %get-tuple-element.78) | copy-start | bytes 1179652
  47.5 9.5 %copy-start.9 = (bf16[24,32,256]{2,1,0:T(8,128)(2,1)}, bf16[24,32,256]{2,1,0:T(8,128)(2,1)S(1)}, u32[]{:S(2)}) copy-start(bf16[24,32,256]{2,1,0:T(8,128)(2,1)S(1)} %get-tuple-element.77) | copy-start | bytes 1179652
  61.1 87.7 %reduce-scatter.9.cloned.1.call-start = ((), (), s32[]{:S(2)}) async-start(), calls=%async_computation.4 | async-start | bytes 2654208 | tf_op jit(solution)/shard_map/reduce_scatter | solution.py:158
  62.3 4.2 %collective-permute-start.10 = (bf16[12,2,1,1,256]{4,2,0,3,1:T(2,128)(2,1)S(1)}, bf16[12,2,1,1,256]{4,2,0,3,1:T(2,128)(2,1)S(1)}, u32[]{:S(2)}, u32[]{:S(2)}) collective-permute-start(bf16[12,2,1,1,256]{4,2,0,3,1:T(2,128)(2,1)S(1)} %slice.397), channel_id=1, source_target_pairs={{28,0},{0,4},{4,8},{8,12},{12,16},{16,20},{20,24},{24,28},{29,1},{... | collective-permute-start | bytes 36872 | tf_op jit(solution)/shard_map/ppermute | solution.py:26
  66.6 5.0 %collective-permute-start.11 = (bf16[1,1,17,2,256]{4,2,0,3,1:T(8,128)(2,1)S(1)}, bf16[1,1,17,2,256]{4,2,0,3,1:T(8,128)(2,1)S(1)}, u32[]{:S(2)}, u32[]{:S(2)}) collective-permute-start(bf16[1,1,17,2,256]{4,2,0,3,1:T(8,128)(2,1)S(1)} %pad_maximum_fusion.9), channel_id=1, source_target_pairs={{0,1},{1,2},{2,3},{4,5},{5,6},{6,7},{8,9},{9,10},{10,11},{12,13},{... | collective-permute-start | bytes 52232 | tf_op jit(solution)/shard_map/ppermute | solution.py:32
  70.2 4.6 %copy-start.15 = (bf16[12,1,16,1,256]{4,2,0,3,1:T(8,128)(2,1)}, bf16[12,1,16,1,256]{4,2,0,3,1:T(8,128)(2,1)S(1)}, u32[]{:S(2)}) copy-start(bf16[12,1,16,1,256]{4,2,0,3,1:T(8,128)(2,1)S(1)} %get-tuple-element.71) | copy-start | bytes 294916
  70.2 5.5 %copy-start.13 = (bf16[12,1,16,1,256]{4,2,0,3,1:T(8,128)(2,1)}, bf16[12,1,16,1,256]{4,2,0,3,1:T(8,128)(2,1)S(1)}, u32[]{:S(2)}) copy-start(bf16[12,1,16,1,256]{4,2,0,3,1:T(8,128)(2,1)S(1)} %get-tuple-element.70) | copy-start | bytes 294916
  80.4 91.8 %reduce-scatter.15.cloned.1.call-start = ((), (), s32[]{:S(2)}) async-start(), calls=%async_computation.7 | async-start | bytes 491520
  80.7 2.4 %copy-start.16 = (bf16[12,1,16,1,256]{4,2,0,3,1:T(8,128)(2,1)S(1)}, bf16[12,1,16,1,256]{4,2,0,3,1:T(8,128)(2,1)}, u32[]{:S(2)}) copy-start(bf16[12,1,16,1,256]{4,2,0,3,1:T(8,128)(2,1)} %copy-done.15) | copy-start | bytes 294916
  86.2 18.3 %copy-start.6 = (f32[768,256]{1,0:T(8,128)S(1)}, f32[768,256]{1,0:T(8,128)}, u32[]{:S(2)}) copy-start(f32[768,256]{1,0:T(8,128)} %fusion.39) | copy-start | bytes 2359300
  104.5 89.5 %reduce-scatter.13.cloned.1.call-start = ((), (), s32[]{:S(2)}) async-start(), calls=%async_computation.6 | async-start | bytes 491520
  (10 other events, 12.9 us)
Sparse Core Ops, SparseCore 0:
  61.2 41.3 reduce-scatter.10
  106.3 42.4 reduce-scatter.8
  151.7 20.5 reduce-scatter.14
  175.1 18.8 reduce-scatter.12
where the time goes:
time: 201 us; the launch traced here: 200 us
  waiting for transfers between devices  109 us (54%)
  matrix products  33.4 us (17%)
  starting transfers between devices  25.7 us (13%)
  between operations  14.4 us (7%)
  local copies, waits for them, and re-layouts  13.2 us (7%)
  other arithmetic  5.18 us (3%)
    reduce_scatter x1, waiting for transfers between devices, local(): lax.psum_scatter(grad_up, 'face', scatter_dimension=0, tiled=True)  42.4 us
    unnamed x6, waiting for transfers between devices  39.5 us
    reduce_scatter x1, waiting for transfers between devices, local(): lax.psum_scatter(grad_conv, 'face', scatter_dimension=0, tiled=True)  15.1 us
    ppermute x4, starting transfers between devices, with_halo(): before = lax.ppermute(last, axis, up)  9.3 us
    dot_general x9, matrix products, conv_wgrad(): jnp.dot(source.T, grad_flat, preferred_element_type=jnp.float32)  9.17 us
    dot_general x9, matrix products, down_backward(): jnp.dot(coarse_flat.T, source, preferred_element_type=jnp.float32)  8.48 us
    ppermute x4, starting transfers between devices, with_halo(): after = lax.ppermute(first, axis, down)  7.85 us
    unnamed x38, local copies, waits for them, and re-layouts  7.07 us
  transfers between devices with their start and end apart: 16, of which 9 were waited for; matrix products, arithmetic and copies ran while one was open for 15% of the time, Pallas kernels for 0%

commit v1 on v0

v1 whole, which is shorter than its diff:
```python
import functools

import jax
import jax.numpy as jnp
from jax import lax
from jax.experimental import pallas as pl
from jax.experimental.pallas import tpu as pltpu
from jax.sharding import PartitionSpec as P

f32, bf16 = jnp.float32, jnp.bfloat16
forward_taps = ((1, 1), (0, 0), (1, 0))
backward_taps = ((1, 0), (0, 1), (1, 1))
MARGIN = 8
LANES = 128


def sds(shape, dtype):
    return jax.ShapeDtypeStruct(shape, dtype)


def kernel_call(body, outs, scratch, flops, *args):
    vmem = pl.BlockSpec(memory_space=pltpu.VMEM)
    smem = pl.BlockSpec(memory_space=pltpu.SMEM)
    moved = sum(a.size * a.dtype.itemsize for a in args)
    moved += sum(a.size * a.dtype.itemsize for a in outs)
    return pl.pallas_call(
        body,
        out_shape=tuple(outs),
        in_specs=[smem if a.dtype == jnp.int32 else vmem for a in args],
        out_specs=tuple(vmem for _ in outs),
        scratch_shapes=scratch,
        compiler_params=pltpu.CompilerParams(vmem_limit_bytes=44 * 2**20),
        cost_estimate=pl.CostEstimate(flops=flops, bytes_accessed=moved, transcendentals=0),
    )(*args)


def dot(a, b):
    return jnp.dot(a, b, preferred_element_type=f32)


def dot_nt(a, b):
    return lax.dot_general(a, b, (((1,), (1,)), ((), ())), preferred_element_type=f32)


def pairs(count, wrap):
    first = [(i, i ^ 1) for i in range(count)]
    second = []
    for i in range(count):
        j = i + 1 if i % 2 else i - 1
        if wrap or 0 <= j < count:
            second.append((i, j % count))
    return first, second


def exchange(to_before, to_after, axis, wrap):
    first, second = pairs(lax.axis_size(axis), wrap)
    even = lax.axis_index(axis) % 2 == 0
    to_first = jnp.where(even, to_after, to_before)
    to_second = jnp.where(even, to_before, to_after)
    got_first = lax.ppermute(to_first, axis, first)
    got_second = lax.ppermute(to_second, axis, second)
    before = jnp.where(even, got_second, got_first)
    after = jnp.where(even, got_first, got_second)
    return before, after


def rows_of(parts, total):
    stacked = jnp.concatenate(parts, axis=0)
    return jnp.pad(stacked, ((0, total - stacked.shape[0]), (0, 0)))


def up16(n):
    return (n + 15) // 16 * 16


def halves(n_rows, channels):
    return pltpu.VMEM((channels // LANES, n_rows, LANES), f32)


def put(ref, start, value, step=1):
    for part in range(ref.shape[0]):
        rows = pl.ds(start, value.shape[0], stride=step if step > 1 else None)
        ref[part, rows, :] = value[:, part * LANES : (part + 1) * LANES]


def get(ref, start, count, step=1):
    rows = pl.ds(start, count, stride=step if step > 1 else None)
    return jnp.concatenate([ref[part, rows, :] for part in range(ref.shape[0])], axis=1)


def put_edges(padded, stride, width, n_rows, left, right, upper, lower, corner):
    last = (n_rows + 1) * stride
    put(padded, stride + MARGIN - 1, left, stride)
    put(padded, stride + MARGIN + width, right, stride)
    put(padded, MARGIN - 1, upper[corner : corner + 1])
    put(padded, MARGIN + width, upper[corner + 1 : corner + 2])
    put(padded, last + MARGIN - 1, lower[corner : corner + 1])
    put(padded, last + MARGIN + width, lower[corner + 1 : corner + 2])


def three_shifts(padded, stride, width, n_rows, shifted):
    for row in range(n_rows):
        for shift in range(3):
            start = row * stride + MARGIN - 1 + shift
            shifted[shift, row] = get(padded, start, width).astype(bf16)


def split_by_core(place, partial, keep, send, groups, block):
    core = place[0]
    for group in range(groups):
        mine = pl.multiple_of((2 * group + core) * block, 16)
        theirs = pl.multiple_of((2 * group + 1 - core) * block, 16)
        keep[group] = partial[pl.ds(mine, block), :]
        send[group] = partial[pl.ds(theirs, block), :].astype(bf16)


def act_kernel(
    place, coarse, skip, cot, left, right, upper, lower, up_w,
    shifted, near, act, slope, keep, send, padded, pre, partial,
):
    n_rows, n_cols, channels = coarse.shape
    fine_rows, fine_cols, _ = skip.shape
    stride = fine_cols + 2 * MARGIN
    left_all, right_all = left[...].astype(f32), right[...].astype(f32)
    upper_all, lower_all = upper[...].astype(f32), lower[...].astype(f32)
    corner = fine_cols + n_cols
    for row in range(n_rows):
        near[0, row] = coarse[row]
        put(padded, row * stride, coarse[row].astype(f32))
    near[0, n_rows] = lower[fine_cols : fine_cols + n_cols]
    put(padded, n_rows * stride, lower_all[fine_cols : fine_cols + n_cols])
    put(padded, n_cols, right_all[fine_rows : fine_rows + n_rows], stride)
    put(padded, n_rows * stride + n_cols, lower_all[corner + 2 : corner + 3])
    for row in range(n_rows + 1):
        near[1, row] = get(padded, row * stride + 1, n_cols).astype(bf16)
    for row in range(n_rows + 1, near.shape[1]):
        for side in range(2):
            near[side, row] = jnp.zeros((n_cols, channels), bf16)
    sums = {}
    for k in range(3):
        row_phase, row_off = forward_taps[k]
        for l in range(3):
            col_phase, col_off = forward_taps[l]
            source = near[col_off, pl.ds(row_off, n_rows)].reshape(n_rows * n_cols, channels)
            term = dot(source, up_w[k, l])
            name = (row_phase, col_phase)
            sums[name] = sums[name] + term if name in sums else term
    for (row_phase, col_phase), total in sums.items():
        for row in range(n_rows):
            start = (2 * row + row_phase) * fine_cols + col_phase
            put(pre, start, total[row * n_cols : (row + 1) * n_cols], 2)
    preact = get(pre, 0, fine_rows * fine_cols) + skip[...].reshape(fine_rows * fine_cols, channels).astype(f32)
    sigma = jax.nn.sigmoid(preact)
    value = preact * sigma
    slope[...] = sigma + value * (1.0 - sigma)
    act_flat = value.astype(bf16)
    act[...] = act_flat.reshape(act.shape)
    put(padded, MARGIN, upper_all[:fine_cols])
    put(padded, (fine_rows + 1) * stride + MARGIN, lower_all[:fine_cols])
    for row in range(fine_rows):
        put(padded, (row + 1) * stride + MARGIN, cot[row].astype(f32))
    put_edges(
        padded, stride, fine_cols, fine_rows, left_all[:fine_rows], right_all[:fine_rows],
        upper_all, lower_all, corner,
    )
    three_shifts(padded, stride, fine_cols, fine_rows + 2, shifted)
    act_t = act_flat.T
    for k in range(3):
        for l in range(3):
            source = shifted[2 - l, pl.ds(2 - k, fine_rows)].reshape(-1, channels)
            partial[pl.ds((3 * k + l) * channels, channels), :] = dot(act_t, source)
    split_by_core(place, partial, keep, send, keep.shape[0], keep.shape[1])


def grad_kernel(place, shifted, slope, near, conv_w, grad, phases, keep, send, fine, partial):
    fine_rows, fine_cols = shifted.shape[1] - 2, shifted.shape[2]
    channels = shifted.shape[3]
    n_rows, n_cols = fine_rows // 2, fine_cols // 2
    total = jnp.zeros((fine_rows * fine_cols, channels), f32)
    for k in range(3):
        for l in range(3):
            source = shifted[2 - l, pl.ds(2 - k, fine_rows)].reshape(-1, channels)
            total = total + dot_nt(source, conv_w[k, l])
    rounded = (total * slope[...]).astype(bf16)
    grad[...] = rounded.reshape(grad.shape)
    put(fine, 0, rounded.astype(f32))
    for row_phase in range(2):
        for col_phase in range(2):
            for row in range(n_rows):
                start = (2 * row + row_phase) * fine_cols + col_phase
                phases[row_phase, col_phase, row] = get(fine, start, n_cols, 2).astype(bf16)
            for row in range(n_rows, phases.shape[2]):
                phases[row_phase, col_phase, row] = jnp.zeros((n_cols, channels), bf16)
    whole = phases.shape[2]
    turned = {}
    for row_off in range(2):
        for col_off in range(2):
            if row_off:
                cells = near[col_off, pl.ds(1, whole)]
            else:
                cells = near[col_off, pl.ds(0, whole)]
            turned[row_off, col_off] = cells.reshape(whole * n_cols, channels).T
    for k in range(3):
        row_phase, row_off = forward_taps[k]
        for l in range(3):
            col_phase, col_off = forward_taps[l]
            source = phases[row_phase, col_phase].reshape(whole * n_cols, channels)
            partial[pl.ds((3 * k + l) * channels, channels), :] = dot(
                turned[row_off, col_off], source
            )
    split_by_core(place, partial, keep, send, keep.shape[0], keep.shape[1])


def out_kernel(
    act, phases, left, right, upper, lower, conv_w, up_w, decoded, coarse_out,
    padded, shifted, moved,
):
    fine_rows, fine_cols, channels = act.shape
    n_rows, n_cols = fine_rows // 2, fine_cols // 2
    stride = fine_cols + 2 * MARGIN
    left_all, right_all = left[...].astype(f32), right[...].astype(f32)
    upper_all, lower_all = upper[...].astype(f32), lower[...].astype(f32)
    corner = 2 * fine_cols
    put(padded, MARGIN, upper_all[:fine_cols])
    put(padded, (fine_rows + 1) * stride + MARGIN, lower_all[:fine_cols])
    for row in range(fine_rows):
        put(padded, (row + 1) * stride + MARGIN, act[row].astype(f32))
    put_edges(
        padded, stride, fine_cols, fine_rows, left_all[:fine_rows], right_all[:fine_rows],
        upper_all, lower_all, corner,
    )
    three_shifts(padded, stride, fine_cols, fine_rows + 2, shifted)
    total = jnp.zeros((fine_rows * fine_cols, channels), f32)
    for k in range(3):
        for l in range(3):
            source = shifted[l, pl.ds(k, fine_rows)].reshape(-1, channels)
            total = total + dot(source, conv_w[k, l])
    decoded[...] = total.astype(bf16).reshape(decoded.shape)
    put(padded, 0, upper_all[fine_cols : 2 * fine_cols])
    moved[0, 0] = get(padded, 0, n_cols, 2).astype(bf16)
    moved[1, 0] = get(padded, 1, n_cols, 2).astype(bf16)
    for phase in range(2):
        for row in range(n_rows):
            moved[phase, 1 + row] = phases[1, phase, row]
    for row_phase in range(2):
        for row in range(n_rows):
            put(padded, (row + 1) * stride + MARGIN, phases[row_phase, 1, row].astype(f32))
        spare = (n_rows + 1) * stride
        put(padded, spare, left_all[fine_rows : 2 * fine_rows])
        put(padded, stride + MARGIN - 1, get(padded, spare + row_phase, n_rows, 2), stride)
        if row_phase:
            put(padded, MARGIN, moved[1, 0].astype(f32))
            put(padded, MARGIN - 1, upper_all[corner + 2 : corner + 3])
            for row in range(n_rows + 1):
                moved[2, row] = get(padded, row * stride + MARGIN - 1, n_cols).astype(bf16)
        else:
            for row in range(n_rows):
                moved[3, row] = get(padded, (row + 1) * stride + MARGIN - 1, n_cols).astype(bf16)
    total = jnp.zeros((n_rows * n_cols, channels), f32)
    for k in range(3):
        for l in range(3):
            if k == 1:
                if l == 0:
                    source = moved[3, pl.ds(0, n_rows)]
                else:
                    source = phases[0, l - 1, pl.ds(0, n_rows)]
            else:
                source = moved[(2, 0, 1)[l], pl.ds(k // 2, n_rows)]
            total = total + dot_nt(source.reshape(n_rows * n_cols, channels), up_w[k, l])
    coarse_out[...] = total.astype(bf16).reshape(coarse_out.shape)


def sum_kernel(place, keep, got, own, *messages):
    chip = place[1]
    own[...] = keep[chip] + got[chip].astype(f32)
    for k, message in enumerate(messages):
        other = chip ^ (k + 1)
        message[...] = (keep[other] + got[other].astype(f32)).astype(bf16)


def packing(rows, cols):
    side = max(1, 128 // cols)
    return side if rows % (16 * side) == 0 else 1


def plane_kernel(place, own, *refs):
    n_bands, peers = refs[-1].shape[0], refs[: -(refs[-1].shape[0] + 1)]
    outs, cut = refs[len(peers) : -1], refs[-1]
    total = own[...]
    for peer in peers:
        total = total + peer[...].astype(f32)
    cols = total.shape[1] // n_bands
    side = packing(total.shape[0], cols)
    rows = total.shape[0] // side
    for band in range(n_bands):
        for part in range(side):
            cut[band, :, part * cols : (part + 1) * cols] = total[
                part * rows : (part + 1) * rows, band * cols : (band + 1) * cols
            ]
    band = place[2]
    outs[0][...] = cut[band]
    for k in range(1, n_bands):
        outs[k][...] = cut[band ^ k].astype(bf16)


def last_kernel(own, *refs):
    peers, out = refs[:-1], refs[-1]
    total = own[...]
    for peer in peers:
        total = total + peer[...].astype(f32)
    rows, cols = total.shape[0], out.shape[1]
    for part in range(out.shape[0] // rows):
        out[part * rows : (part + 1) * rows, :] = total[:, part * cols : (part + 1) * cols]


def xor_pairs(count, bits):
    return [(i, i ^ bits) for i in range(count)]


def reduce_partial(place, keep, send):
    faces, bands = lax.axis_size("face"), lax.axis_size("band")
    groups, block, channels = keep.shape
    got = lax.ppermute(send, "face", xor_pairs(faces, 1))
    shape = (block, channels)
    own, *messages = kernel_call(
        sum_kernel, [sds(shape, f32)] + [sds(shape, bf16)] * (groups - 1), [], 0, place, keep, got
    )
    order = sorted(range(1, groups), key=lambda k: -bin(k).count("1"))
    got = [lax.ppermute(messages[k - 1], "face", xor_pairs(faces, 2 * k)) for k in order]
    cols = channels // bands
    side = packing(block, cols)
    shape = (block // side, cols * side)
    own, *messages = kernel_call(
        plane_kernel, [sds(shape, f32)] + [sds(shape, bf16)] * (bands - 1),
        [pltpu.VMEM((bands,) + shape, f32)], 0, place, own, *got,
    )
    order = sorted(range(1, bands), key=lambda k: -k)
    got = [lax.ppermute(messages[k - 1], "band", xor_pairs(bands, k)) for k in order]
    return kernel_call(last_kernel, [sds((block, cols), f32)], [], 0, own, *got)[0]


def local(coarse, skip, up_weight, conv_weight, cotangent):
    n_rows, n_cols, channels = coarse.shape
    fine_rows, fine_cols, _ = skip.shape
    faces = lax.axis_size("face")
    face, band = lax.axis_index("face"), lax.axis_index("band")
    place = jnp.stack([face % 2, face // 2, band]).astype(jnp.int32)
    groups, block = faces // 2, 9 * channels // faces

    size = up16(fine_rows + n_rows)
    left, right = exchange(
        rows_of([cotangent[:, 0], coarse[:, 0]], size),
        rows_of([cotangent[:, -1], coarse[:, -1]], size),
        "face", True,
    )
    size = up16(fine_cols + n_cols + 3)
    upper, lower = exchange(
        rows_of([cotangent[0], coarse[0], left[:1], right[:1], right[fine_rows : fine_rows + 1]], size),
        rows_of([cotangent[-1], coarse[-1], left[fine_rows - 1 : fine_rows], right[fine_rows - 1 : fine_rows]], size),
        "band", False,
    )

    fine_flat = (fine_rows * fine_cols, channels)
    cells = n_rows * n_cols
    stride = fine_cols + 2 * MARGIN
    padded = halves((fine_rows + 2) * stride, channels)
    flat = halves(fine_rows * fine_cols, channels)
    shift_shape = (3, fine_rows + 2, fine_cols, channels)
    whole = -(-cells // 256) * 256 // n_cols
    one_tap = 2 * cells * channels * channels
    partials = [sds((groups, block, channels), f32), sds((groups, block, channels), bf16)]
    partial = pltpu.VMEM((9 * channels, channels), f32)
    shifted, near, act, slope, keep_conv, send_conv = kernel_call(
        act_kernel,
        [
            sds(shift_shape, bf16), sds((2, whole + 1, n_cols, channels), bf16),
            sds(skip.shape, bf16), sds(fine_flat, f32), *partials,
        ],
        [padded, flat, partial],
        45 * one_tap, place, coarse, skip, cotangent, left, right, upper, lower, up_weight,
    )
    grad, phases, keep_up, send_up = kernel_call(
        grad_kernel,
        [sds(skip.shape, bf16), sds((2, 2, whole, n_cols, channels), bf16), *partials],
        [flat, partial],
        45 * one_tap, place, shifted, slope, near, conv_weight,
    )

    grad_conv = reduce_partial(place, keep_conv, send_conv)
    grad_up = reduce_partial(place, keep_up, send_up)

    size = up16(2 * fine_rows)
    left, right = exchange(
        rows_of([act[:, 0]], size), rows_of([act[:, -1], grad[:, -1]], size), "face", True
    )
    size = up16(2 * fine_cols + 3)
    blank = jnp.zeros((fine_cols, channels), bf16)
    upper, lower = exchange(
        rows_of([act[0], blank, left[:1], right[:1]], size),
        rows_of([act[-1], grad[-1], left[fine_rows - 1 : fine_rows], right[fine_rows - 1 : fine_rows], left[2 * fine_rows - 1 : 2 * fine_rows]], size),
        "band", False,
    )
    decoded, grad_coarse = kernel_call(
        out_kernel,
        [sds(skip.shape, bf16), sds(coarse.shape, bf16)],
        [padded, pltpu.VMEM(shift_shape, bf16), pltpu.VMEM((4, n_rows + 1, n_cols, channels), bf16)],
        45 * one_tap, act, phases, left, right, upper, lower, conv_weight, up_weight,
    )
    return (decoded, grad_coarse, grad_up, grad_conv)


def solution(mesh):
    return jax.shard_map(
        local,
        mesh=mesh,
        in_specs=(
            P("band", "face", None),
            P("band", "face", None),
            P(),
            P(),
            P("band", "face", None),
        ),
        out_specs=(
            P("band", "face", None),
            P("band", "face", None),
            P("face", "band"),
            P("face", "band"),
        ),
        check_vma=False,
    )
```

time: 201 us -> 66.6 us (0.33)
  waiting for transfers between devices: 109 us -> 3.52 us
  matrix products: 33.4 us -> 0 us
  between operations: 14.4 us -> 0.95 us
  Pallas kernels: 0 us -> 12.1 us
  starting transfers between devices: 25.7 us -> 31.4 us
  other arithmetic: 5.18 us -> 0.98 us
  local copies, waits for them, and re-layouts: 13.2 us -> 17 us
    reduce_scatter x2 -> x0, waiting for transfers between devices: 57.5 us -> none  [the longest x1 42.4 us: local(): lax.psum_scatter(grad_up, 'face', scatter_dimension=0, tiled=True)]
    unnamed x6 -> x0, waiting for transfers between devices: 39.5 us -> none
    dot_general x54 -> x0, matrix products: 33.4 us -> none  [the longest x9 9.17 us: conv_wgrad(): jnp.dot(source.T, grad_flat, preferred_element_type=jnp.float32)]
    pallas_call x0 -> x9, Pallas kernels: none -> 12.1 us  [kernel_call(): pl.pallas_call(body, out_shape=tuple(outs), in_specs=[smem if a.dtype ==...]
    ppermute x12 -> x22, waiting for transfers between devices: 11.4 us -> 3.52 us  [the longest x4 2.22 us: exchange(): got_second = lax.ppermute(to_second, axis, second)]
    ppermute x12 -> x22, starting transfers between devices: 25.4 us -> 31.4 us  [the longest x4 9.46 us: exchange(): got_first = lax.ppermute(to_first, axis, first)]
    concatenate x0 -> x3, local copies, waits for them, and re-layouts: none -> 4.5 us  [rows_of(): stacked = jnp.concatenate(parts, axis=0)]
    squeeze x0 -> x8, local copies, waits for them, and re-layouts: none -> 2.69 us  [the longest x1 0.74 us: local(): cotangent[-1]]
  transfers between devices with their start and end apart: 16 -> 22, of which waited for: 9 -> 3; matrix products, arithmetic and copies ran while one was open for 15% -> 13% of each run, Pallas kernels for 0% -> 8%
where the time goes in v1:
time: 66.6 us; the launch traced here: 65.9 us
  starting transfers between devices  31.4 us (47%)
  local copies, waits for them, and re-layouts  17 us (26%)
  Pallas kernels  12.1 us (18%)
  waiting for transfers between devices  3.52 us (5%)
  other arithmetic  0.98 us (1%)
  between operations  0.95 us (1%)
    pallas_call x9, Pallas kernels, kernel_call(): pl.pallas_call(body, out_shape=tuple(outs), in_specs=[smem if a.dtype ==...  12.1 us
    ppermute x4, starting transfers between devices, exchange(): got_first = lax.ppermute(to_first, axis, first)  9.46 us
    ppermute x6, starting transfers between devices, reduce_partial(): lax.ppermute(messages[k - 1], 'band', xor_pairs(bands, k))  8.97 us
    ppermute x6, starting transfers between devices, reduce_partial(): lax.ppermute(messages[k - 1], 'face', xor_pairs(faces, 2 * k))  7.09 us
    unnamed x34, local copies, waits for them, and re-layouts  6.92 us
    ppermute x4, starting transfers between devices, exchange(): got_second = lax.ppermute(to_second, axis, second)  5.37 us
    concatenate x3, local copies, waits for them, and re-layouts, rows_of(): stacked = jnp.concatenate(parts, axis=0)  4.5 us
    ppermute x4, waiting for transfers between devices, exchange(): got_second = lax.ppermute(to_second, axis, second)  2.22 us
  transfers between devices with their start and end apart: 22, of which 3 were waited for; matrix products, arithmetic and copies ran while one was open for 13% of the time, Pallas kernels for 8%

profile of v1, /device:TPU:0, one launch (start us, length us, event | category | flops | bytes accessed | tf_op | source)
XLA Modules:
  0.0 65.9 jit_solution(5768290316516230768)
XLA Ops:
  0.6 1.0 %fusion.13 = (bf16[24,1,256]{2,1,0:T(2,128)(2,1)S(1)}, bf16[24,1,256]{2,1,0:T(2,128)(2,1)S(1)}) fusion(bf16[24,32,256]{2,1,0:T(8,128)(2,1)} %cot.1), kind=kLoop, calls=%fused_computation.48 | loop fusion | bytes 49152 | tf_op jit(solution)/shard_map/slice | solution.py:352
  1.6 0.8 %fusion.14 = (bf16[12,1,256]{2,1,0:T(2,128)(2,1)S(1)}, bf16[12,1,256]{2,1,0:T(2,128)(2,1)S(1)}) fusion(bf16[12,16,256]{2,1,0:T(8,128)(2,1)} %coarse.1), kind=kLoop, calls=%fused_computation.49 | loop fusion | bytes 24576 | tf_op jit(solution)/shard_map/slice | solution.py:352
  2.5 3.4 %collective-permute-start = (bf16[48,256]{1,0:T(8,128)(2,1)S(1)}, bf16[48,256]{1,0:T(8,128)(2,1)S(1)}, u32[]{:S(2)}, u32[]{:S(2)}) collective-permute-start(bf16[48,256]{1,0:T(8,128)(2,1)S(1)} %get-tuple-element.89), channel_id=1, source_target_pairs={{0,28},{4,8},{8,4},{12,16},{16,12},{20,24},{24,20},{28,0},{1,29},{... | collective-permute-start | bytes 73736 | tf_op jit(solution)/shard_map/ppermute | solution.py:61
  8.2 5.4 %collective-permute-start.3 = (bf16[64,256]{1,0:T(8,128)(2,1)S(1)}, bf16[64,256]{1,0:T(8,128)(2,1)S(1)}, u32[]{:S(2)}, u32[]{:S(2)}) collective-permute-start(bf16[64,256]{1,0:T(8,128)(2,1)S(1)} %get-tuple-element.82), channel_id=1, source_target_pairs={{0,1},{1,0},{2,3},{3,2},{4,5},{5,4},{6,7},{7,6},{8,9},{9,8},{10,11... | collective-permute-start | bytes 98312 | tf_op jit(solution)/shard_map/ppermute | solution.py:60
  14.2 1.3 %collective-permute-done.3 = bf16[64,256]{1,0:T(8,128)(2,1)S(1)} collective-permute-done((bf16[64,256]{1,0:T(8,128)(2,1)S(1)}, bf16[64,256]{1,0:T(8,128)(2,1)S(1)}, u32[]{:S(2)}, u32[]{:S(2)}) %collective-permute-start.3) | collective-permute-done | bytes 32800 | tf_op jit(solution)/shard_map/ppermute | solution.py:60
  15.5 1.0 %copy-done.6 = bf16[24,32,256]{2,1,0:T(8,128)(2,1)S(1)} copy-done((bf16[24,32,256]{2,1,0:T(8,128)(2,1)S(1)}, bf16[24,32,256]{2,1,0:T(8,128)(2,1)}, u32[]{:S(2)}) %copy-start.6) | copy-done | bytes 393240
  16.5 0.9 %copy-done.7 = bf16[12,16,256]{2,1,0:T(8,128)(2,1)S(1)} copy-done((bf16[12,16,256]{2,1,0:T(8,128)(2,1)S(1)}, bf16[12,16,256]{2,1,0:T(8,128)(2,1)}, u32[]{:S(2)}) %copy-start.7) | copy-done | bytes 98328
  17.4 1.3 %copy-done.8 = bf16[3,3,256,256]{3,2,1,0:T(8,128)(2,1)S(1)} copy-done((bf16[3,3,256,256]{3,2,1,0:T(8,128)(2,1)S(1)}, bf16[3,3,256,256]{3,2,1,0:T(8,128)(2,1)}, u32[]{:S(2)}) %copy-start.8) | copy-done | bytes 1179672
  18.7 1.0 %copy-done.12 = bf16[24,32,256]{2,1,0:T(8,128)(2,1)S(1)} copy-done((bf16[24,32,256]{2,1,0:T(8,128)(2,1)S(1)}, bf16[24,32,256]{2,1,0:T(8,128)(2,1)}, u32[]{:S(2)}) %copy-start.12) | copy-done | bytes 393240
  19.7 3.2 %shard_map.84 = (bf16[3,26,32,256]{3,2,1,0:T(8,128)(2,1)S(1)}, bf16[2,17,16,256]{3,2,1,0:T(8,128)(2,1)S(1)}, bf16[24,32,256]{2,1,0:T(8,128)(2,1)S(1)}, f32[768,2...) custom-call(s32[3]{0:T(128)S(1)} %pad_add_fusion.place, ...), custom_call_target="tpu_custom_call" | custom-call | flops 1132462080 | bytes 6684684 | tf_op jit(solution)/shard_map/pallas_call | solution.py:26
  23.8 3.7 %shard_map.85 = (bf16[24,32,256]{2,1,0:T(8,128)(2,1)S(1)}, bf16[2,2,16,16,256]{4,3,2,1,0:T(8,128)(2,1)S(1)}, f32[4,288,256]{2,1,0:T(8,128)S(1)}, bf16[4,288,256]{2,1,0:T(8,128)(2,1)}) custom-call(s32[3]{0:T(128)S(1)} %pad_add_fusion.place, bf16[3,26,32,256]{3,2,1,0:T(8,128)(2,1)S(1)} %get-tuple-element.33.shifted, f32[768,256]{1,0:T(8,128)S(1)} %get-tuple-element.34.slope, ...), custom_call_target="tpu_custom_call" | custom-call | flops 1132462080 | bytes 6209548 | tf_op jit(solution)/shard_map/pallas_call | solution.py:26
  29.8 2.2 %collective-permute-done.4 = bf16[48,256]{1,0:T(8,128)(2,1)S(1)} collective-permute-done((bf16[48,256]{1,0:T(8,128)(2,1)S(1)}, bf16[48,256]{1,0:T(8,128)(2,1)S(1)}, u32[]{:S(2)}, u32[]{:S(2)}) %collective-permute-start.4) | collective-permute-done | bytes 24608 | tf_op jit(solution)/shard_map/ppermute | solution.py:61
  33.8 3.9 %concatenate.27 = bf16[67,256]{1,0:T(8,128)(2,1)} concatenate(bf16[32,256]{1,0:T(8,128)(2,1)} %get-tuple-element.65, bf16[32,256]{1,0:T(8,128)(2,1)} %slice_bitcast_fusion, bf16[1,256]{1,0:T(2,128)(2,1)} %get-tuple-element.94, bf16[1,256]{1,0:T(2,128)(2,1)S(1)} %get-tuple-element.96, bf16[1,256]{1,0:T(2,128)(2,1)} %get-tuple-element.93), dimensions={0} | concatenate | bytes 68608 | tf_op jit(solution)/shard_map/concatenate | solution.py:68
  37.7 0.8 %pad_maximum_fusion = bf16[66,256]{1,0:T(8,128)(2,1)S(1)} fusion(bf16[1,256]{1,0:T(2,128)(2,1)S(1)} %get-tuple-element.95, bf16[1,256]{1,0:T(2,128)(2,1)S(1)} %get-tuple-element.92, bf16[32,256]{1,0:T(8,128)(2,1)} %get-tuple-element.64, bf16[66]{0:T(256)(128)(2,1)} %pad.35.clone), kind=kLoop, calls=%fused_computation.14 | loop fusion | flops 135168 | bytes 51332 | tf_op jit(solution)/shard_map/concatenate | solution.py:68
  39.2 0.8 %collective-permute-start.16 = (bf16[288,256]{1,0:T(8,128)(2,1)S(1)}, bf16[288,256]{1,0:T(8,128)(2,1)S(1)}, u32[]{:S(2)}, u32[]{:S(2)}) collective-permute-start(bf16[288,256]{1,0:T(8,128)(2,1)S(1)} %get-tuple-element.53), channel_id=1, source_target_pairs={{0,24},{4,28},{8,16},{12,20},{16,8},{20,12},{24,0},{28,4},{1,25},{... | collective-permute-start | bytes 442376 | tf_op jit(solution)/shard_map/ppermute | solution.py:329
  40.0 2.1 %collective-permute-start.17 = (bf16[288,256]{1,0:T(8,128)(2,1)S(1)}, bf16[288,256]{1,0:T(8,128)(2,1)S(1)}, u32[]{:S(2)}, u32[]{:S(2)}) collective-permute-start(bf16[288,256]{1,0:T(8,128)(2,1)S(1)} %get-tuple-element.54), channel_id=1, source_target_pairs={{0,8},{4,12},{8,0},{12,4},{16,24},{20,28},{24,16},{28,20},{1,9},{5... | collective-permute-start | bytes 442376 | tf_op jit(solution)/shard_map/ppermute | solution.py:329
  43.4 3.8 %collective-permute-start.7 = (bf16[80,256]{1,0:T(8,128)(2,1)S(1)}, bf16[80,256]{1,0:T(8,128)(2,1)S(1)}, u32[]{:S(2)}, u32[]{:S(2)}) collective-permute-start(bf16[80,256]{1,0:T(8,128)(2,1)S(1)} %get-tuple-element.78), channel_id=1, source_target_pairs={{0,1},{1,0},{2,3},{3,2},{4,5},{5,4},{6,7},{7,6},{8,9},{9,8},{10,11... | collective-permute-start | bytes 122888 | tf_op jit(solution)/shard_map/ppermute | solution.py:60
  48.0 1.4 %collective-permute-start.11 = (bf16[288,256]{1,0:T(8,128)(2,1)S(1)}, bf16[288,256]{1,0:T(8,128)(2,1)S(1)}, u32[]{:S(2)}, u32[]{:S(2)}) collective-permute-start(bf16[288,256]{1,0:T(8,128)(2,1)S(1)} %get-tuple-element.45), channel_id=1, source_target_pairs={{0,16},{4,20},{8,24},{12,28},{16,0},{20,4},{24,8},{28,12},{1,17},{... | collective-permute-start | bytes 442376 | tf_op jit(solution)/shard_map/ppermute | solution.py:329
  49.5 2.0 %collective-permute-start.9 = (bf16[288,256]{1,0:T(8,128)(2,1)S(1)}, bf16[288,256]{1,0:T(8,128)(2,1)S(1)}, u32[]{:S(2)}, u32[]{:S(2)}) collective-permute-start(bf16[288,256]{1,0:T(8,128)(2,1)S(1)} %get-tuple-element.43), channel_id=1, source_target_pairs={{0,24},{4,28},{8,16},{12,20},{16,8},{20,12},{24,0},{28,4},{1,25},{... | collective-permute-start | bytes 442376 | tf_op jit(solution)/shard_map/ppermute | solution.py:329
  52.2 2.5 %collective-permute-start.19 = (bf16[144,128]{1,0:T(8,128)(2,1)S(1)}, bf16[144,128]{1,0:T(8,128)(2,1)S(1)}, u32[]{:S(2)}, u32[]{:S(2)}) collective-permute-start(bf16[144,128]{1,0:T(8,128)(2,1)S(1)} %get-tuple-element.57), channel_id=1, source_target_pairs={{0,3},{1,2},{2,1},{3,0},{4,7},{5,6},{6,5},{7,4},{8,11},{9,10},{10,... | collective-permute-start | bytes 110600 | tf_op jit(solution)/shard_map/ppermute | solution.py:338
  55.0 1.8 %collective-permute-start.21 = (bf16[144,128]{1,0:T(8,128)(2,1)S(1)}, bf16[144,128]{1,0:T(8,128)(2,1)S(1)}, u32[]{:S(2)}, u32[]{:S(2)}) collective-permute-start(bf16[144,128]{1,0:T(8,128)(2,1)S(1)} %get-tuple-element.59), channel_id=1, source_target_pairs={{0,1},{1,0},{2,3},{3,2},{4,5},{5,4},{6,7},{7,6},{8,9},{9,8},{10,11... | collective-permute-start | bytes 110600 | tf_op jit(solution)/shard_map/ppermute | solution.py:338
  57.5 2.5 %collective-permute-start.12 = (bf16[144,128]{1,0:T(8,128)(2,1)S(1)}, bf16[144,128]{1,0:T(8,128)(2,1)S(1)}, u32[]{:S(2)}, u32[]{:S(2)}) collective-permute-start(bf16[144,128]{1,0:T(8,128)(2,1)S(1)} %get-tuple-element.47), channel_id=1, source_target_pairs={{0,3},{1,2},{2,1},{3,0},{4,7},{5,6},{6,5},{7,4},{8,11},{9,10},{10,... | collective-permute-start | bytes 110600 | tf_op jit(solution)/shard_map/ppermute | solution.py:338
  60.0 1.9 %collective-permute-start.14 = (bf16[144,128]{1,0:T(8,128)(2,1)S(1)}, bf16[144,128]{1,0:T(8,128)(2,1)S(1)}, u32[]{:S(2)}, u32[]{:S(2)}) collective-permute-start(bf16[144,128]{1,0:T(8,128)(2,1)S(1)} %get-tuple-element.49), channel_id=1, source_target_pairs={{0,1},{1,0},{2,3},{3,2},{4,5},{5,4},{6,7},{7,6},{8,9},{9,8},{10,11... | collective-permute-start | bytes 110600 | tf_op jit(solution)/shard_map/ppermute | solution.py:338
  62.0 2.2 %shard_map.86 = (bf16[24,32,256]{2,1,0:T(8,128)(2,1)}, bf16[12,16,256]{2,1,0:T(8,128)(2,1)}) custom-call(bf16[24,32,256]{2,1,0:T(8,128)(2,1)S(1)} %copy-done.1, bf16[2,2,16,16,256]{4,3,2,1,0:T(8,128)(2,1)S(1)} %copy-done.14, bf16[48,256]{1,0:T(8,128)(2,1)S(1)} %copy-done.3, bf16[48,256]{1,0:T(8,128)(2,1)S(1)} %copy-done.5, ...), custom_call_target="tpu_custom_call" | custom-call | flops 1132462080 | bytes 3899392 | tf_op jit(solution)/shard_map/pallas_call | solution.py:26
  (93 shorter events, 14.0 us)
Async XLA Ops:
  2.5 4.9 %collective-permute-start = (bf16[48,256]{1,0:T(8,128)(2,1)S(1)}, bf16[48,256]{1,0:T(8,128)(2,1)S(1)}, u32[]{:S(2)}, u32[]{:S(2)}) collective-permute-start(bf16[48,256]{1,0:T(8,128)(2,1)S(1)} %get-tuple-element.89), channel_id=1, source_target_pairs={{0,28},{4,8},{8,4},{12,16},{16,12},{20,24},{24,20},{28,0},{1,29},{... | collective-permute-start | bytes 73736 | tf_op jit(solution)/shard_map/ppermute | solution.py:61
  5.9 1.5 %collective-permute-start.1 = (bf16[48,256]{1,0:T(8,128)(2,1)S(1)}, bf16[48,256]{1,0:T(8,128)(2,1)S(1)}, u32[]{:S(2)}, u32[]{:S(2)}) collective-permute-start(bf16[48,256]{1,0:T(8,128)(2,1)S(1)} %get-tuple-element.88), channel_id=1, source_target_pairs={{0,4},{4,0},{8,12},{12,8},{16,20},{20,16},{24,28},{28,24},{1,5},{5... | collective-permute-start | bytes 73736 | tf_op jit(solution)/shard_map/ppermute | solution.py:60
  7.6 6.7 %collective-permute-start.2 = (bf16[64,256]{1,0:T(8,128)(2,1)S(1)}, bf16[64,256]{1,0:T(8,128)(2,1)S(1)}, u32[]{:S(2)}, u32[]{:S(2)}) collective-permute-start(bf16[64,256]{1,0:T(8,128)(2,1)S(1)} %get-tuple-element.83), channel_id=1, source_target_pairs={{1,2},{2,1},{5,6},{6,5},{9,10},{10,9},{13,14},{14,13},{17,18},{18,... | collective-permute-start | bytes 98312 | tf_op jit(solution)/shard_map/ppermute | solution.py:61
  8.2 7.3 %collective-permute-start.3 = (bf16[64,256]{1,0:T(8,128)(2,1)S(1)}, bf16[64,256]{1,0:T(8,128)(2,1)S(1)}, u32[]{:S(2)}, u32[]{:S(2)}) collective-permute-start(bf16[64,256]{1,0:T(8,128)(2,1)S(1)} %get-tuple-element.82), channel_id=1, source_target_pairs={{0,1},{1,0},{2,3},{3,2},{4,5},{5,4},{6,7},{7,6},{8,9},{9,8},{10,11... | collective-permute-start | bytes 98312 | tf_op jit(solution)/shard_map/ppermute | solution.py:60
  27.7 4.2 %collective-permute-start.4 = (bf16[48,256]{1,0:T(8,128)(2,1)S(1)}, bf16[48,256]{1,0:T(8,128)(2,1)S(1)}, u32[]{:S(2)}, u32[]{:S(2)}) collective-permute-start(bf16[48,256]{1,0:T(8,128)(2,1)S(1)} %get-tuple-element.91), channel_id=1, source_target_pairs={{0,28},{4,8},{8,4},{12,16},{16,12},{20,24},{24,20},{28,0},{1,29},{... | collective-permute-start | bytes 73736 | tf_op jit(solution)/shard_map/ppermute | solution.py:61
  28.4 3.6 %collective-permute-start.5 = (bf16[48,256]{1,0:T(8,128)(2,1)S(1)}, bf16[48,256]{1,0:T(8,128)(2,1)S(1)}, u32[]{:S(2)}, u32[]{:S(2)}) collective-permute-start(bf16[48,256]{1,0:T(8,128)(2,1)S(1)} %get-tuple-element.90), channel_id=1, source_target_pairs={{0,4},{4,0},{8,12},{12,8},{16,20},{20,16},{24,28},{28,24},{1,5},{5... | collective-permute-start | bytes 73736 | tf_op jit(solution)/shard_map/ppermute | solution.py:60
  29.3 9.2 %collective-permute-start.15 = (bf16[4,288,256]{2,1,0:T(8,128)(2,1)}, bf16[4,288,256]{2,1,0:T(8,128)(2,1)S(1)}, u32[]{:S(2)}, u32[]{:S(2)}) collective-permute-start(bf16[4,288,256]{2,1,0:T(8,128)(2,1)} %get-tuple-element.51), channel_id=1, source_target_pairs={{0,4},{4,0},{8,12},{12,8},{16,20},{20,16},{24,28},{28,24},{1,5},{5... | collective-permute-start | bytes 1769480 | tf_op jit(solution)/shard_map/ppermute | solution.py:323
  29.5 13.9 %collective-permute-start.8 = (bf16[4,288,256]{2,1,0:T(8,128)(2,1)}, bf16[4,288,256]{2,1,0:T(8,128)(2,1)S(1)}, u32[]{:S(2)}, u32[]{:S(2)}) collective-permute-start(bf16[4,288,256]{2,1,0:T(8,128)(2,1)} %get-tuple-element.41), channel_id=1, source_target_pairs={{0,4},{4,0},{8,12},{12,8},{16,20},{20,16},{24,28},{28,24},{1,5},{5... | collective-permute-start | bytes 1769480 | tf_op jit(solution)/shard_map/ppermute | solution.py:323
  39.2 8.8 %collective-permute-start.16 = (bf16[288,256]{1,0:T(8,128)(2,1)S(1)}, bf16[288,256]{1,0:T(8,128)(2,1)S(1)}, u32[]{:S(2)}, u32[]{:S(2)}) collective-permute-start(bf16[288,256]{1,0:T(8,128)(2,1)S(1)} %get-tuple-element.53), channel_id=1, source_target_pairs={{0,24},{4,28},{8,16},{12,20},{16,8},{20,12},{24,0},{28,4},{1,25},{... | collective-permute-start | bytes 442376 | tf_op jit(solution)/shard_map/ppermute | solution.py:329
  40.0 8.1 %collective-permute-start.17 = (bf16[288,256]{1,0:T(8,128)(2,1)S(1)}, bf16[288,256]{1,0:T(8,128)(2,1)S(1)}, u32[]{:S(2)}, u32[]{:S(2)}) collective-permute-start(bf16[288,256]{1,0:T(8,128)(2,1)S(1)} %get-tuple-element.54), channel_id=1, source_target_pairs={{0,8},{4,12},{8,0},{12,4},{16,24},{20,28},{24,16},{28,20},{1,9},{5... | collective-permute-start | bytes 442376 | tf_op jit(solution)/shard_map/ppermute | solution.py:329
  42.1 7.4 %collective-permute-start.18 = (bf16[288,256]{1,0:T(8,128)(2,1)S(1)}, bf16[288,256]{1,0:T(8,128)(2,1)S(1)}, u32[]{:S(2)}, u32[]{:S(2)}) collective-permute-start(bf16[288,256]{1,0:T(8,128)(2,1)S(1)} %get-tuple-element.55), channel_id=1, source_target_pairs={{0,16},{4,20},{8,24},{12,28},{16,0},{20,4},{24,8},{28,12},{1,17},{... | collective-permute-start | bytes 442376 | tf_op jit(solution)/shard_map/ppermute | solution.py:329
  42.8 9.5 %collective-permute-start.6 = (bf16[80,256]{1,0:T(8,128)(2,1)S(1)}, bf16[80,256]{1,0:T(8,128)(2,1)S(1)}, u32[]{:S(2)}, u32[]{:S(2)}) collective-permute-start(bf16[80,256]{1,0:T(8,128)(2,1)S(1)} %get-tuple-element.79), channel_id=1, source_target_pairs={{1,2},{2,1},{5,6},{6,5},{9,10},{10,9},{13,14},{14,13},{17,18},{18,... | collective-permute-start | bytes 122888 | tf_op jit(solution)/shard_map/ppermute | solution.py:61
  43.4 11.3 %collective-permute-start.7 = (bf16[80,256]{1,0:T(8,128)(2,1)S(1)}, bf16[80,256]{1,0:T(8,128)(2,1)S(1)}, u32[]{:S(2)}, u32[]{:S(2)}) collective-permute-start(bf16[80,256]{1,0:T(8,128)(2,1)S(1)} %get-tuple-element.78), channel_id=1, source_target_pairs={{0,1},{1,0},{2,3},{3,2},{4,5},{5,4},{6,7},{7,6},{8,9},{9,8},{10,11... | collective-permute-start | bytes 122888 | tf_op jit(solution)/shard_map/ppermute | solution.py:60
  47.2 14.7 %copy-start.11 = (bf16[3,3,256,256]{3,2,1,0:T(8,128)(2,1)S(1)}, bf16[3,3,256,256]{3,2,1,0:T(8,128)(2,1)}, u32[]{:S(2)}) copy-start(bf16[3,3,256,256]{3,2,1,0:T(8,128)(2,1)} %conv_w.3) | copy-start | bytes 3538948
  47.2 14.7 %copy-start.14 = (bf16[2,2,16,16,256]{4,3,2,1,0:T(8,128)(2,1)S(1)}, bf16[2,2,16,16,256]{4,3,2,1,0:T(8,128)(2,1)}, u32[]{:S(2)}) copy-start(bf16[2,2,16,16,256]{4,3,2,1,0:T(8,128)(2,1)} %copy-done.13) | copy-start | bytes 1572868
  47.9 7.0 %collective-permute-start.10 = (bf16[288,256]{1,0:T(8,128)(2,1)S(1)}, bf16[288,256]{1,0:T(8,128)(2,1)S(1)}, u32[]{:S(2)}, u32[]{:S(2)}) collective-permute-start(bf16[288,256]{1,0:T(8,128)(2,1)S(1)} %get-tuple-element.44), channel_id=1, source_target_pairs={{0,8},{4,12},{8,0},{12,4},{16,24},{20,28},{24,16},{28,20},{1,9},{5... | collective-permute-start | bytes 442376 | tf_op jit(solution)/shard_map/ppermute | solution.py:329
  48.0 8.7 %collective-permute-start.11 = (bf16[288,256]{1,0:T(8,128)(2,1)S(1)}, bf16[288,256]{1,0:T(8,128)(2,1)S(1)}, u32[]{:S(2)}, u32[]{:S(2)}) collective-permute-start(bf16[288,256]{1,0:T(8,128)(2,1)S(1)} %get-tuple-element.45), channel_id=1, source_target_pairs={{0,16},{4,20},{8,24},{12,28},{16,0},{20,4},{24,8},{28,12},{1,17},{... | collective-permute-start | bytes 442376 | tf_op jit(solution)/shard_map/ppermute | solution.py:329
  49.5 7.3 %collective-permute-start.9 = (bf16[288,256]{1,0:T(8,128)(2,1)S(1)}, bf16[288,256]{1,0:T(8,128)(2,1)S(1)}, u32[]{:S(2)}, u32[]{:S(2)}) collective-permute-start(bf16[288,256]{1,0:T(8,128)(2,1)S(1)} %get-tuple-element.43), channel_id=1, source_target_pairs={{0,24},{4,28},{8,16},{12,20},{16,8},{20,12},{24,0},{28,4},{1,25},{... | collective-permute-start | bytes 442376 | tf_op jit(solution)/shard_map/ppermute | solution.py:329
  52.2 7.8 %collective-permute-start.19 = (bf16[144,128]{1,0:T(8,128)(2,1)S(1)}, bf16[144,128]{1,0:T(8,128)(2,1)S(1)}, u32[]{:S(2)}, u32[]{:S(2)}) collective-permute-start(bf16[144,128]{1,0:T(8,128)(2,1)S(1)} %get-tuple-element.57), channel_id=1, source_target_pairs={{0,3},{1,2},{2,1},{3,0},{4,7},{5,6},{6,5},{7,4},{8,11},{9,10},{10,... | collective-permute-start | bytes 110600 | tf_op jit(solution)/shard_map/ppermute | solution.py:338
  54.8 9.4 %collective-permute-start.20 = (bf16[144,128]{1,0:T(8,128)(2,1)S(1)}, bf16[144,128]{1,0:T(8,128)(2,1)S(1)}, u32[]{:S(2)}, u32[]{:S(2)}) collective-permute-start(bf16[144,128]{1,0:T(8,128)(2,1)S(1)} %get-tuple-element.58), channel_id=1, source_target_pairs={{0,2},{1,3},{2,0},{3,1},{4,6},{5,7},{6,4},{7,5},{8,10},{9,11},{10,... | collective-permute-start | bytes 110600 | tf_op jit(solution)/shard_map/ppermute | solution.py:338
  55.0 9.2 %collective-permute-start.21 = (bf16[144,128]{1,0:T(8,128)(2,1)S(1)}, bf16[144,128]{1,0:T(8,128)(2,1)S(1)}, u32[]{:S(2)}, u32[]{:S(2)}) collective-permute-start(bf16[144,128]{1,0:T(8,128)(2,1)S(1)} %get-tuple-element.59), channel_id=1, source_target_pairs={{0,1},{1,0},{2,3},{3,2},{4,5},{5,4},{6,7},{7,6},{8,9},{9,8},{10,11... | collective-permute-start | bytes 110600 | tf_op jit(solution)/shard_map/ppermute | solution.py:338
  57.5 7.6 %collective-permute-start.12 = (bf16[144,128]{1,0:T(8,128)(2,1)S(1)}, bf16[144,128]{1,0:T(8,128)(2,1)S(1)}, u32[]{:S(2)}, u32[]{:S(2)}) collective-permute-start(bf16[144,128]{1,0:T(8,128)(2,1)S(1)} %get-tuple-element.47), channel_id=1, source_target_pairs={{0,3},{1,2},{2,1},{3,0},{4,7},{5,6},{6,5},{7,4},{8,11},{9,10},{10,... | collective-permute-start | bytes 110600 | tf_op jit(solution)/shard_map/ppermute | solution.py:338
  60.0 5.0 %collective-permute-start.13 = (bf16[144,128]{1,0:T(8,128)(2,1)S(1)}, bf16[144,128]{1,0:T(8,128)(2,1)S(1)}, u32[]{:S(2)}, u32[]{:S(2)}) collective-permute-start(bf16[144,128]{1,0:T(8,128)(2,1)S(1)} %get-tuple-element.48), channel_id=1, source_target_pairs={{0,2},{1,3},{2,0},{3,1},{4,6},{5,7},{6,4},{7,5},{8,10},{9,11},{10,... | collective-permute-start | bytes 110600 | tf_op jit(solution)/shard_map/ppermute | solution.py:338
  60.0 5.0 %collective-permute-start.14 = (bf16[144,128]{1,0:T(8,128)(2,1)S(1)}, bf16[144,128]{1,0:T(8,128)(2,1)S(1)}, u32[]{:S(2)}, u32[]{:S(2)}) collective-permute-start(bf16[144,128]{1,0:T(8,128)(2,1)S(1)} %get-tuple-element.49), channel_id=1, source_target_pairs={{0,1},{1,0},{2,3},{3,2},{4,5},{5,4},{6,7},{7,6},{8,9},{9,8},{10,11... | collective-permute-start | bytes 110600 | tf_op jit(solution)/shard_map/ppermute | solution.py:338
  (14 other events, 77.4 us)

commit v2 on v1

v2 whole, which is shorter than its diff:
```python
import jax
import jax.numpy as jnp
from jax import lax
from jax.experimental import pallas as pl
from jax.experimental.pallas import tpu as pltpu
from jax.sharding import PartitionSpec as P

f32, bf16 = jnp.float32, jnp.bfloat16
forward_taps = ((1, 1), (0, 0), (1, 0))
backward_taps = ((1, 0), (0, 1), (1, 1))
MARGIN = 8
LANES = 128


def sds(shape, dtype):
    return jax.ShapeDtypeStruct(shape, dtype)


def kernel_call(body, outs, scratch, flops, *args, far=()):
    vmem = pl.BlockSpec(memory_space=pltpu.VMEM)
    smem = pl.BlockSpec(memory_space=pltpu.SMEM)
    anywhere = pl.BlockSpec(memory_space=pl.ANY)
    moved = sum(a.size * a.dtype.itemsize for a in args)
    moved += sum(a.size * a.dtype.itemsize for a in outs)
    return pl.pallas_call(
        body,
        out_shape=tuple(outs),
        in_specs=[
            anywhere if i in far else smem if a.dtype == jnp.int32 else vmem
            for i, a in enumerate(args)
        ],
        out_specs=tuple(vmem for _ in outs),
        scratch_shapes=scratch,
        compiler_params=pltpu.CompilerParams(vmem_limit_bytes=28 * 2**20),
        cost_estimate=pl.CostEstimate(flops=flops, bytes_accessed=moved, transcendentals=0),
    )(*args)


def dot(a, b):
    return jnp.dot(a, b, preferred_element_type=f32)


def dot_nt(a, b):
    return lax.dot_general(a, b, (((1,), (1,)), ((), ())), preferred_element_type=f32)


def pairs(count, wrap):
    first = [(i, i ^ 1) for i in range(count)]
    second = []
    for i in range(count):
        j = i + 1 if i % 2 else i - 1
        if wrap or 0 <= j < count:
            second.append((i, j % count))
    return first, second


def up16(n):
    return (n + 15) // 16 * 16


def halves(n_rows, channels):
    return pltpu.VMEM((channels // LANES, n_rows, LANES), f32)


def put(ref, start, value, step=1):
    for part in range(ref.shape[0]):
        rows = pl.ds(start, value.shape[0], stride=step if step > 1 else None)
        ref[part, rows, :] = value[:, part * LANES : (part + 1) * LANES]


def get(ref, start, count, step=1):
    rows = pl.ds(start, count, stride=step if step > 1 else None)
    return jnp.concatenate([ref[part, rows, :] for part in range(ref.shape[0])], axis=1)


def fill(ref, start, value):
    ref[start : start + value.shape[0], :] = value


def split_by_core(place, partial, keep, send):
    groups, block, _ = keep.shape
    for group in range(groups):
        mine = pl.multiple_of((2 * group + place[0]) * block, 16)
        theirs = pl.multiple_of((2 * group + 1 - place[0]) * block, 16)
        keep[group] = partial[pl.ds(mine, block), :]
        send[group] = partial[pl.ds(theirs, block), :].astype(bf16)


class Layout:
    def __init__(self, n_rows, n_cols):
        rows, cols = 2 * n_rows, 2 * n_cols
        self.cot, self.cot_2, self.skip, self.coarse = 0, rows, 2 * rows, 3 * rows
        self.face_size = up16(3 * rows + n_rows)
        self.row_cot, self.row_cot_2, self.row_skip = 0, cols, 2 * cols
        self.row_coarse, self.corner = 3 * cols, 3 * cols + n_cols
        self.band_size = self.corner + 16
        ring = (cols + 2 + 7) // 8 * 8
        self.top, self.bottom, self.left, self.right = 0, ring, 2 * ring, 2 * ring + rows
        self.ring_size = up16(2 * ring + 2 * rows)
        self.grad_left, self.grad_size = ring, up16(ring + rows)


COT, COT_2, SKIP, COARSE = (0, 1, 2), (3, 4, 5), (6, None, 7), (8, None, 9)


def face_message(place, coarse, skip, cot, first, second, cot_v, skip_v, coarse_v, flat, before, after, sems):
    rows, cols, _ = cot.shape
    n_rows, n_cols, _ = coarse.shape
    at = Layout(n_rows, n_cols)
    copies = [
        pltpu.make_async_copy(source, target, sems.at[i])
        for i, (source, target) in enumerate(((cot, cot_v), (skip, skip_v), (coarse, coarse_v)))
    ]
    for copy in copies:
        copy.start()
    before[...] = jnp.zeros_like(before)
    after[...] = jnp.zeros_like(after)
    copies[0].wait()
    put(flat, 0, cot_v[...].reshape(rows * cols, -1).astype(f32))
    fill(before, at.cot, get(flat, 0, rows, cols))
    fill(after, at.cot, get(flat, cols - 1, rows, cols))
    fill(after, at.cot_2, get(flat, cols - 2, rows, cols))
    copies[1].wait()
    put(flat, 0, skip_v[...].reshape(rows * cols, -1).astype(f32))
    fill(before, at.skip, get(flat, 0, rows, cols))
    fill(after, at.skip, get(flat, cols - 1, rows, cols))
    copies[2].wait()
    put(flat, 0, coarse_v[...].reshape(n_rows * n_cols, -1).astype(f32))
    fill(before, at.coarse, get(flat, 0, n_rows, n_cols))
    fill(after, at.coarse, get(flat, n_cols - 1, n_rows, n_cols))
    even = place[0] == 0
    first[...] = jnp.where(even, after[...], before[...]).astype(bf16)
    second[...] = jnp.where(even, before[...], after[...]).astype(bf16)


def band_message(place, coarse, skip, cot, got_first, got_second, first, second, left, right, before, after):
    rows, cols, channels = cot.shape
    n_rows, n_cols, _ = coarse.shape
    at = Layout(n_rows, n_cols)
    even = place[0] == 0
    one, two = got_first[...].astype(f32), got_second[...].astype(f32)
    left[...] = jnp.where(even, two, one)
    right[...] = jnp.where(even, one, two)
    for message, row, row_2, cell in ((before, 0, None, 0), (after, rows - 1, rows - 2, n_rows - 1)):
        fill(message, at.row_cot, cot[row].astype(f32))
        if row_2 is None:
            fill(message, at.row_cot_2, jnp.zeros((cols, channels), f32))
        else:
            fill(message, at.row_cot_2, cot[row_2].astype(f32))
        fill(message, at.row_skip, skip[row].astype(f32))
        fill(message, at.row_coarse, coarse[cell].astype(f32))
        fill(message, at.corner, jnp.zeros((16, channels), f32))
        corners = [
            (COT[0], left, at.cot + row), (COT[1], left, at.cot_2 + row), (COT[2], right, at.cot + row),
            (SKIP[0], left, at.skip + row), (SKIP[2], right, at.skip + row),
            (COARSE[0], left, at.coarse + cell), (COARSE[2], right, at.coarse + cell),
        ]
        if row_2 is not None:
            corners += [
                (COT_2[0], left, at.cot + row_2), (COT_2[1], left, at.cot_2 + row_2),
                (COT_2[2], right, at.cot + row_2),
            ]
        for corner, side, source in corners:
            fill(message, at.corner + corner, side[source : source + 1, :])
    even = lax.rem(place[2], 2) == 0
    first[...] = jnp.where(even, after[...], before[...]).astype(bf16)
    second[...] = jnp.where(even, before[...], after[...]).astype(bf16)


def act_kernel(
    place, coarse, skip, cot, left, right, got_first, got_second, up_w, conv_w,
    shifted, near, act, slope, keep, send, upper, lower, up_v, conv_v,
    padded, pre, partial, sems,
):
    n_rows, n_cols, channels = coarse.shape
    rows, cols, _ = skip.shape
    at = Layout(n_rows, n_cols)
    stride = cols + 2 * MARGIN
    copies = [
        pltpu.make_async_copy(up_w, up_v, sems.at[0]),
        pltpu.make_async_copy(conv_w, conv_v, sems.at[1]),
    ]
    for copy in copies:
        copy.start()
    even = lax.rem(place[2], 2) == 0
    one, two = got_first[...].astype(f32), got_second[...].astype(f32)
    upper[...] = jnp.where(even, two, one)
    lower[...] = jnp.where(even, one, two)
    for row in range(n_rows):
        near[0, row] = coarse[row]
        put(padded, row * stride, coarse[row].astype(f32))
    below = lower[at.row_coarse : at.row_coarse + n_cols, :]
    near[0, n_rows] = below.astype(bf16)
    put(padded, n_rows * stride, below)
    put(padded, n_cols, right[at.coarse : at.coarse + n_rows, :], stride)
    corner = at.corner + COARSE[2]
    put(padded, n_rows * stride + n_cols, lower[corner : corner + 1, :])
    for row in range(n_rows + 1):
        near[1, row] = get(padded, row * stride + 1, n_cols).astype(bf16)
    for row in range(n_rows + 1, near.shape[1]):
        for side in range(2):
            near[side, row] = jnp.zeros((n_cols, channels), bf16)
    put(padded, MARGIN, upper[at.row_cot : at.row_cot + cols, :])
    put(padded, (rows + 1) * stride + MARGIN, lower[at.row_cot : at.row_cot + cols, :])
    for row in range(rows):
        put(padded, (row + 1) * stride + MARGIN, cot[row].astype(f32))
    put(padded, stride + MARGIN - 1, left[at.cot : at.cot + rows, :], stride)
    put(padded, stride + MARGIN + cols, right[at.cot : at.cot + rows, :], stride)
    for row, message in ((0, upper), (rows + 1, lower)):
        for col, corner in ((-1, at.corner + COT[0]), (cols, at.corner + COT[2])):
            put(padded, row * stride + MARGIN + col, message[corner : corner + 1, :])
    for row in range(rows + 2):
        for shift in (0, 2):
            start = row * stride + MARGIN - 1 + shift
            shifted[shift, row] = get(padded, start, cols).astype(bf16)
    shifted[1, 0] = upper[at.row_cot : at.row_cot + cols, :].astype(bf16)
    shifted[1, rows + 1] = lower[at.row_cot : at.row_cot + cols, :].astype(bf16)
    for row in range(rows):
        shifted[1, row + 1] = cot[row]
    copies[0].wait()
    sums = {}
    for k in range(3):
        row_phase, row_off = forward_taps[k]
        for l in range(3):
            col_phase, col_off = forward_taps[l]
            source = near[col_off, pl.ds(row_off, n_rows)].reshape(n_rows * n_cols, channels)
            term = dot(source, up_v[k, l])
            name = (row_phase, col_phase)
            sums[name] = sums[name] + term if name in sums else term
    for (row_phase, col_phase), total in sums.items():
        for row in range(n_rows):
            start = (2 * row + row_phase) * cols + col_phase
            put(pre, start, total[row * n_cols : (row + 1) * n_cols], 2)
    preact = get(pre, 0, rows * cols) + skip[...].reshape(rows * cols, channels).astype(f32)
    sigma = jax.nn.sigmoid(preact)
    value = preact * sigma
    slope[...] = sigma + value * (1.0 - sigma)
    act_flat = value.astype(bf16)
    act[...] = act_flat.reshape(act.shape)
    act_t = act_flat.T
    for k in range(3):
        for l in range(3):
            source = shifted[2 - l, pl.ds(2 - k, rows)].reshape(-1, channels)
            partial[pl.ds((3 * k + l) * channels, channels), :] = dot(act_t, source)
    split_by_core(place, partial, keep, send)
    copies[1].wait()


def grad_kernel(place, shifted, slope, near, conv_w, phases, keep, send, fine, partial):
    rows, cols = shifted.shape[1] - 2, shifted.shape[2]
    channels = shifted.shape[3]
    n_rows, n_cols = rows // 2, cols // 2
    total = jnp.zeros((rows * cols, channels), f32)
    for k in range(3):
        for l in range(3):
            source = shifted[2 - l, pl.ds(2 - k, rows)].reshape(-1, channels)
            total = total + dot_nt(source, conv_w[k, l])
    put(fine, 0, (total * slope[...]).astype(bf16).astype(f32))
    whole = phases.shape[2]
    for row_phase in range(2):
        for col_phase in range(2):
            for row in range(n_rows):
                start = (2 * row + row_phase) * cols + col_phase
                phases[row_phase, col_phase, row] = get(fine, start, n_cols, 2).astype(bf16)
            for row in range(n_rows, whole):
                phases[row_phase, col_phase, row] = jnp.zeros((n_cols, channels), bf16)
    turned = {}
    for row_off in range(2):
        for col_off in range(2):
            cells = near[col_off, pl.ds(row_off, whole)]
            turned[row_off, col_off] = cells.reshape(whole * n_cols, channels).T
    for k in range(3):
        row_phase, row_off = forward_taps[k]
        for l in range(3):
            col_phase, col_off = forward_taps[l]
            source = phases[row_phase, col_phase].reshape(whole * n_cols, channels)
            partial[pl.ds((3 * k + l) * channels, channels), :] = dot(
                turned[row_off, col_off], source
            )
    split_by_core(place, partial, keep, send)


def out_kernel(
    place, coarse, cot, act, phases, left, right, upper, lower, conv_w, up_w,
    decoded, coarse_out, padded, shifted, moved, ring, wide,
):
    rows, cols, channels = act.shape
    n_rows, n_cols = rows // 2, cols // 2
    at = Layout(n_rows, n_cols)
    stride, step = cols + 2 * MARGIN, n_cols + 2 * MARGIN
    has_upper, has_lower = place[2] > 0, place[2] < place[3] - 1

    def corner(message, which):
        return message[at.corner + which : at.corner + which + 1, :]

    def cell(i, j):
        return (i + 1) * step + MARGIN + j

    for row in range(n_rows):
        put(wide, cell(row, 0), coarse[row].astype(f32))
    for row, message in ((-1, upper), (n_rows, lower)):
        put(wide, cell(row, 0), message[at.row_coarse : at.row_coarse + n_cols, :])
        put(wide, cell(row, -1), corner(message, COARSE[0]))
        put(wide, cell(row, n_cols), corner(message, COARSE[2]))
    put(wide, cell(0, -1), left[at.coarse : at.coarse + n_rows, :], step)
    put(wide, cell(0, n_cols), right[at.coarse : at.coarse + n_rows, :], step)
    total = jnp.zeros((at.ring_size, channels), f32)
    for k in range(3):
        for l in range(3):
            put(ring, 0, jnp.zeros((at.ring_size, channels), f32))
            for base, i in ((at.bottom, n_rows),) if k == 1 else ((at.top, k // 2 * -1),):
                start = cell(i, -1 if l == 2 else 0)
                put(ring, base + (l == 1), get(wide, start, n_cols + 1), 2)
            base, j = (at.right, n_cols) if l == 1 else (at.left, -(l // 2))
            start = cell(1 if k == 0 else 0, j)
            put(ring, base + (k != 1), get(wide, start, n_rows, step), 2)
            total = total + dot(get(ring, 0, at.ring_size).astype(bf16), up_w[k, l])
    put(ring, 0, jnp.zeros((at.ring_size, channels), f32))
    for base, message in ((at.top, upper), (at.bottom, lower)):
        put(ring, base + 1, message[at.row_skip : at.row_skip + cols, :])
        put(ring, base, corner(message, SKIP[0]))
        put(ring, base + cols + 1, corner(message, SKIP[2]))
    put(ring, at.left, left[at.skip : at.skip + rows, :])
    put(ring, at.right, right[at.skip : at.skip + rows, :])
    preact = total + get(ring, 0, at.ring_size)
    sigma = jax.nn.sigmoid(preact)
    value = preact * sigma
    slope = sigma + value * (1.0 - sigma)
    value = value.astype(bf16).astype(f32)
    for row in range(rows):
        put(padded, (row + 1) * stride + MARGIN, act[row].astype(f32))
    for row, base, exists in ((0, at.top, has_upper), (rows + 1, at.bottom, has_lower)):
        strip = value[base : base + cols + 2]
        put(padded, row * stride + MARGIN - 1, jnp.where(exists, strip, 0.0))
    put(padded, stride + MARGIN - 1, value[at.left : at.left + rows], stride)
    put(padded, stride + MARGIN + cols, value[at.right : at.right + rows], stride)
    for row in range(rows + 2):
        for shift in range(3):
            start = row * stride + MARGIN - 1 + shift
            shifted[shift, row] = get(padded, start, cols).astype(bf16)
    total = jnp.zeros((rows * cols, channels), f32)
    for k in range(3):
        for l in range(3):
            source = shifted[l, pl.ds(k, rows)].reshape(-1, channels)
            total = total + dot(source, conv_w[k, l])
    decoded[...] = total.astype(bf16).reshape(decoded.shape)

    def fine(p, q):
        return (p + 2) * stride + MARGIN + q

    for row in range(rows):
        put(wide, fine(row, 0), cot[row].astype(f32))
    for row, message, start, which in (
        (-1, upper, at.row_cot, COT), (-2, upper, at.row_cot_2, COT_2), (rows, lower, at.row_cot, COT),
    ):
        put(wide, fine(row, 0), message[start : start + cols, :])
        for col, one in ((-1, which[0]), (-2, which[1]), (cols, which[2])):
            put(wide, fine(row, col), corner(message, one))
    put(wide, fine(0, -1), left[at.cot : at.cot + rows, :], stride)
    put(wide, fine(0, -2), left[at.cot_2 : at.cot_2 + rows, :], stride)
    put(wide, fine(0, cols), right[at.cot : at.cot + rows, :], stride)
    total = jnp.zeros((at.grad_size, channels), f32)
    for k in range(3):
        for l in range(3):
            put(ring, at.top, get(wide, fine(-k, -l), cols + 1))
            put(ring, at.grad_left, get(wide, fine(1 - k, -l), rows, stride))
            source = get(ring, 0, at.grad_size).astype(bf16)
            total = total + dot_nt(source, conv_w[k, l])
    strip = (total[: cols + 1] * slope[at.top : at.top + cols + 1]).astype(bf16).astype(f32)
    put(ring, at.top, jnp.where(has_upper, strip, 0.0))
    strip = total[at.grad_left : at.grad_left + rows] * slope[at.left : at.left + rows]
    put(ring, at.grad_left, strip.astype(bf16).astype(f32))
    for phase, start in ((0, 1), (1, 2), (2, 0)):
        moved[phase, 0] = get(ring, at.top + start, n_cols, 2).astype(bf16)
    for phase in range(2):
        for row in range(n_rows):
            moved[phase, 1 + row] = phases[1, phase, row]
    for row_phase in range(2):
        for row in range(n_rows):
            put(padded, row * stride + MARGIN, phases[row_phase, 1, row].astype(f32))
        put(padded, MARGIN - 1, get(ring, at.grad_left + row_phase, n_rows, 2), stride)
        for row in range(n_rows):
            cells = get(padded, row * stride + MARGIN - 1, n_cols).astype(bf16)
            if row_phase:
                moved[2, 1 + row] = cells
            else:
                moved[3, row] = cells
    total = jnp.zeros((n_rows * n_cols, channels), f32)
    for k in range(3):
        for l in range(3):
            if k == 1:
                if l == 0:
                    source = moved[3, pl.ds(0, n_rows)]
                else:
                    source = phases[0, l - 1, pl.ds(0, n_rows)]
            else:
                source = moved[(2, 0, 1)[l], pl.ds(k // 2, n_rows)]
            total = total + dot_nt(source.reshape(n_rows * n_cols, channels), up_w[k, l])
    coarse_out[...] = total.astype(bf16).reshape(coarse_out.shape)


def sum_kernel(place, keep, got, own, *messages):
    chip = place[1]
    own[...] = keep[chip] + got[chip].astype(f32)
    for k, message in enumerate(messages):
        other = chip ^ (k + 1)
        message[...] = (keep[other] + got[other].astype(f32)).astype(bf16)


def packing(rows, cols):
    side = max(1, 128 // cols)
    return side if rows % (16 * side) == 0 else 1


def plane_kernel(place, own, *refs):
    n_bands, peers = refs[-1].shape[0], refs[: -(refs[-1].shape[0] + 1)]
    outs, cut = refs[len(peers) : -1], refs[-1]
    total = own[...]
    for peer in peers:
        total = total + peer[...].astype(f32)
    cols = total.shape[1] // n_bands
    side = packing(total.shape[0], cols)
    rows = total.shape[0] // side
    for band in range(n_bands):
        for part in range(side):
            cut[band, :, part * cols : (part + 1) * cols] = total[
                part * rows : (part + 1) * rows, band * cols : (band + 1) * cols
            ]
    band = place[2]
    outs[0][...] = cut[band]
    for k in range(1, n_bands):
        outs[k][...] = cut[band ^ k].astype(bf16)


def last_kernel(own, *refs):
    peers, out = refs[:-1], refs[-1]
    total = own[...]
    for peer in peers:
        total = total + peer[...].astype(f32)
    rows, cols = total.shape[0], out.shape[0]
    turned = total.T
    for part in range(out.shape[1] // rows):
        out[:, part * rows : (part + 1) * rows] = turned[part * cols : (part + 1) * cols, :]


def xor_pairs(count, bits):
    return [(i, i ^ bits) for i in range(count)]


def reduce_partial(place, keep, send):
    faces, bands = lax.axis_size("face"), lax.axis_size("band")
    groups, block, channels = keep.shape
    got = lax.ppermute(send, "face", xor_pairs(faces, 1))
    shape = (block, channels)
    own, *messages = kernel_call(
        sum_kernel, [sds(shape, f32)] + [sds(shape, bf16)] * (groups - 1), [], 0, place, keep, got
    )
    order = sorted(range(1, groups), key=lambda k: -bin(k).count("1"))
    got = [lax.ppermute(messages[k - 1], "face", xor_pairs(faces, 2 * k)) for k in order]
    cols = channels // bands
    side = packing(block, cols)
    shape = (block // side, cols * side)
    own, *messages = kernel_call(
        plane_kernel, [sds(shape, f32)] + [sds(shape, bf16)] * (bands - 1),
        [pltpu.VMEM((bands,) + shape, f32)], 0, place, own, *got,
    )
    order = sorted(range(1, bands), key=lambda k: -k)
    got = [lax.ppermute(messages[k - 1], "band", xor_pairs(bands, k)) for k in order]
    return kernel_call(last_kernel, [sds((cols, block), f32)], [], 0, own, *got)[0].T


def swap(first, second, axis, wrap):
    one, two = pairs(lax.axis_size(axis), wrap)
    return lax.ppermute(first, axis, one), lax.ppermute(second, axis, two)


def local(coarse, skip, up_weight, conv_weight, cotangent):
    n_rows, n_cols, channels = coarse.shape
    rows, cols, _ = skip.shape
    at = Layout(n_rows, n_cols)
    faces, bands = lax.axis_size("face"), lax.axis_size("band")
    face, band = lax.axis_index("face"), lax.axis_index("band")
    place = jnp.stack([face % 2, face // 2, band, bands]).astype(jnp.int32)
    groups, block = faces // 2, 9 * channels // faces

    flat = halves(rows * cols, channels)
    message = sds((at.face_size, channels), bf16)
    edges = pltpu.VMEM(message.shape, f32)
    first, second, cotangent, skip, coarse = kernel_call(
        face_message,
        [message, message, sds(cotangent.shape, bf16), sds(skip.shape, bf16), sds(coarse.shape, bf16)],
        [flat, edges, edges, pltpu.SemaphoreType.DMA((3,))],
        0, place, coarse, skip, cotangent, far=(1, 2, 3),
    )
    first, second = swap(first, second, "face", True)
    side = sds(message.shape, f32)
    message = sds((at.band_size, channels), bf16)
    edges = pltpu.VMEM(message.shape, f32)
    first, second, left, right = kernel_call(
        band_message, [message, message, side, side], [edges, edges],
        0, place, coarse, skip, cotangent, first, second,
    )
    first, second = swap(first, second, "band", False)

    cells = n_rows * n_cols
    stride = cols + 2 * MARGIN
    padded = halves((rows + 2) * stride, channels)
    shift_shape = (3, rows + 2, cols, channels)
    whole = -(-cells // 256) * 256 // n_cols
    one_tap = 2 * cells * channels * channels
    partials = [sds((groups, block, channels), f32), sds((groups, block, channels), bf16)]
    partial = pltpu.VMEM((9 * channels, channels), f32)
    side = sds(message.shape, f32)
    shifted, near, act, slope, keep_conv, send_conv, upper, lower, up_weight, conv_weight = kernel_call(
        act_kernel,
        [
            sds(shift_shape, bf16), sds((2, whole + 1, n_cols, channels), bf16),
            sds(skip.shape, bf16), sds((rows * cols, channels), f32), *partials, side, side,
            sds(up_weight.shape, bf16), sds(conv_weight.shape, bf16),
        ],
        [padded, flat, partial, pltpu.SemaphoreType.DMA((2,))],
        45 * one_tap, place, coarse, skip, cotangent, left, right, first, second,
        up_weight, conv_weight, far=(8, 9),
    )
    phases, keep_up, send_up = kernel_call(
        grad_kernel,
        [sds((2, 2, whole, n_cols, channels), bf16), *partials],
        [flat, partial],
        45 * one_tap, place, shifted, slope, near, conv_weight,
    )
    decoded, grad_coarse = kernel_call(
        out_kernel,
        [sds(skip.shape, bf16), sds(coarse.shape, bf16)],
        [
            padded, pltpu.VMEM(shift_shape, bf16), pltpu.VMEM((4, n_rows + 1, n_cols, channels), bf16),
            halves(at.ring_size, channels), halves((rows + 3) * stride, channels),
        ],
        60 * one_tap, place, coarse, cotangent, act, phases, left, right, upper, lower,
        conv_weight, up_weight,
    )
    grad_conv = reduce_partial(place, keep_conv, send_conv)
    grad_up = reduce_partial(place, keep_up, send_up)
    return (decoded, grad_coarse, grad_up, grad_conv)


def solution(mesh):
    return jax.shard_map(
        local,
        mesh=mesh,
        in_specs=(
            P("band", "face", None),
            P("band", "face", None),
            P(),
            P(),
            P("band", "face", None),
        ),
        out_specs=(
            P("band", "face", None),
            P("band", "face", None),
            P("face", "band"),
            P("face", "band"),
        ),
        check_vma=False,
    )
```

time: 66.6 us -> 55.8 us (0.84)
  local copies, waits for them, and re-layouts: 17 us -> 4.16 us
  starting transfers between devices: 31.4 us -> 27 us
  waiting for transfers between devices: 3.52 us -> 7.7 us
  Pallas kernels: 12.1 us -> 15.9 us
  other arithmetic: 0.98 us -> 0.08 us
    ppermute x8 -> x4, starting transfers between devices: 14.8 us -> 6.53 us  [swap(): return (lax.ppermute(first, axis, one), lax.ppermute(second, axis, two))]
    concatenate x3 -> x0, local copies, waits for them, and re-layouts: 4.5 us -> none  [rows_of(): stacked = jnp.concatenate(parts, axis=0)]
    ppermute x6, waiting for transfers between devices: 0.02 us -> 4.03 us  [reduce_partial(): lax.ppermute(messages[k - 1], 'face', xor_pairs(faces, 2 * k))]
    pallas_call x9 -> x11, Pallas kernels: 12.1 us -> 15.9 us  [kernel_call(): pl.pallas_call(body, out_shape=tuple(outs), in_specs=[anywhere if i in fa...]
    unnamed x34 -> x10, local copies, waits for them, and re-layouts: 6.92 us -> 4.16 us
    squeeze x8 -> x0, local copies, waits for them, and re-layouts: 2.69 us -> none  [the longest x1 0.74 us: local(): cotangent[-1]]
    slice x6 -> x0, local copies, waits for them, and re-layouts: 2.43 us -> none  [the longest x1 0.99 us: local(): cotangent[:, 0]]
    ppermute x6, starting transfers between devices: 8.97 us -> 11.3 us  [reduce_partial(): lax.ppermute(messages[k - 1], 'band', xor_pairs(bands, k))]
  transfers between devices with their start and end apart: 22 -> 18, of which waited for: 3 -> 5; matrix products, arithmetic and copies ran while one was open for 13% -> 0% of each run, Pallas kernels for 8% -> 18%
where the time goes in v2:
time: 55.8 us; the launch traced here: 55.6 us
  starting transfers between devices  27 us (48%)
  Pallas kernels  15.9 us (28%)
  waiting for transfers between devices  7.7 us (14%)
  local copies, waits for them, and re-layouts  4.16 us (7%)
  between operations  0.76 us (1%)
    pallas_call x11, Pallas kernels, kernel_call(): pl.pallas_call(body, out_shape=tuple(outs), in_specs=[anywhere if i in fa...  15.9 us
    ppermute x6, starting transfers between devices, reduce_partial(): lax.ppermute(messages[k - 1], 'band', xor_pairs(bands, k))  11.3 us
    ppermute x6, starting transfers between devices, reduce_partial(): lax.ppermute(messages[k - 1], 'face', xor_pairs(faces, 2 * k))  8.48 us
    ppermute x4, starting transfers between devices, swap(): return (lax.ppermute(first, axis, one), lax.ppermute(second, axis, two))  6.53 us
    unnamed x10, local copies, waits for them, and re-layouts  4.16 us
    ppermute x6, waiting for transfers between devices, reduce_partial(): lax.ppermute(messages[k - 1], 'face', xor_pairs(faces, 2 * k))  4.03 us
    ppermute x4, waiting for transfers between devices, swap(): return (lax.ppermute(first, axis, one), lax.ppermute(second, axis, two))  3.64 us
  transfers between devices with their start and end apart: 18, of which 5 were waited for; matrix products, arithmetic and copies ran while one was open for 0% of the time, Pallas kernels for 18%

profile of v2, /device:TPU:0, one launch (start us, length us, event | category | flops | bytes accessed | tf_op | source)
XLA Modules:
  0.0 55.6 jit_solution(15467304462734908809)
XLA Ops:
  0.7 1.0 %copy-done = bf16[24,32,256]{2,1,0:T(8,128)(2,1)S(1)} copy-done((bf16[24,32,256]{2,1,0:T(8,128)(2,1)S(1)}, bf16[24,32,256]{2,1,0:T(8,128)(2,1)}, u32[]{:S(2)}) %copy-start) | copy-done | bytes 393240
  1.7 1.0 %copy-done.1 = bf16[24,32,256]{2,1,0:T(8,128)(2,1)S(1)} copy-done((bf16[24,32,256]{2,1,0:T(8,128)(2,1)S(1)}, bf16[24,32,256]{2,1,0:T(8,128)(2,1)}, u32[]{:S(2)}) %copy-start.1) | copy-done | bytes 393240
  2.7 0.9 %copy-done.2 = bf16[12,16,256]{2,1,0:T(8,128)(2,1)S(1)} copy-done((bf16[12,16,256]{2,1,0:T(8,128)(2,1)S(1)}, bf16[12,16,256]{2,1,0:T(8,128)(2,1)}, u32[]{:S(2)}) %copy-start.2) | copy-done | bytes 98328
  3.6 1.3 %shard_map.84 = (bf16[96,256]{1,0:T(8,128)(2,1)S(1)}, bf16[96,256]{1,0:T(8,128)(2,1)S(1)}, bf16[24,32,256]{2,1,0:T(8,128)(2,1)S(1)}, bf16[24,32,256]{2,1,0:T(8,128)(2,1)S(1)}, bf16[12,16,256]{2,1,0:T(8,128)(2,1)S(1)}) custom-call(s32[4]{0:T(128)S(1)} %pad_add_fusion.place, bf16[12,16,256]{2,1,0:T(8,128)(2,1)S(1)} %copy-done.2, ...), custom_call_target="tpu_custom_call" | custom-call | bytes 1867792 | tf_op jit(solution)/shard_map/pallas_call | solution.py:25
  5.4 3.6 %collective-permute-start.1 = (bf16[96,256]{1,0:T(8,128)(2,1)S(1)}, bf16[96,256]{1,0:T(8,128)(2,1)S(1)}, u32[]{:S(2)}, u32[]{:S(2)}) collective-permute-start(bf16[96,256]{1,0:T(8,128)(2,1)S(1)} %get-tuple-element.48), channel_id=1, source_target_pairs={{0,28},{4,8},{8,4},{12,16},{16,12},{20,24},{24,20},{28,0},{1,29},{... | collective-permute-start | bytes 147464 | tf_op jit(solution)/shard_map/ppermute | solution.py:474
  9.0 1.8 %collective-permute-done.1.got_second = bf16[96,256]{1,0:T(8,128)(2,1)S(1)} collective-permute-done((bf16[96,256]{1,0:T(8,128)(2,1)S(1)}, bf16[96,256]{1,0:T(8,128)(2,1)S(1)}, u32[]{:S(2)}, u32[]{:S(2)}) %collective-permute-start.1) | collective-permute-done | bytes 49184 | tf_op jit(solution)/shard_map/ppermute | solution.py:474
  11.3 1.8 %collective-permute-start.2 = (bf16[128,256]{1,0:T(8,128)(2,1)S(1)}, bf16[128,256]{1,0:T(8,128)(2,1)S(1)}, u32[]{:S(2)}, u32[]{:S(2)}) collective-permute-start(bf16[128,256]{1,0:T(8,128)(2,1)S(1)} %get-tuple-element.51), channel_id=1, source_target_pairs={{0,1},{1,0},{2,3},{3,2},{4,5},{5,4},{6,7},{7,6},{8,9},{9,8},{10,11... | collective-permute-start | bytes 196616 | tf_op jit(solution)/shard_map/ppermute | solution.py:474
  13.8 1.9 %collective-permute-done.2.got_first = bf16[128,256]{1,0:T(8,128)(2,1)S(1)} collective-permute-done((bf16[128,256]{1,0:T(8,128)(2,1)S(1)}, bf16[128,256]{1,0:T(8,128)(2,1)S(1)}, u32[]{:S(2)}, u32[]{:S(2)}) %collective-permute-start.2) | collective-permute-done | bytes 65568 | tf_op jit(solution)/shard_map/ppermute | solution.py:474
  15.7 1.3 %copy-done.4 = bf16[3,3,256,256]{3,2,1,0:T(8,128)(2,1)S(1)} copy-done((bf16[3,3,256,256]{3,2,1,0:T(8,128)(2,1)S(1)}, bf16[3,3,256,256]{3,2,1,0:T(8,128)(2,1)}, u32[]{:S(2)}) %copy-start.4) | copy-done | bytes 1179672
  17.0 3.1 %shard_map.86 = (bf16[3,26,32,256]{3,2,1,0:T(8,128)(2,1)S(1)}, bf16[2,17,16,256]{3,2,1,0:T(8,128)(2,1)S(1)}, bf16[24,32,256]{2,1,0:T(8,128)(2,1)S(1)}, f32[768,2...) custom-call(s32[4]{0:T(128)S(1)} %pad_add_fusion.place, ...), custom_call_target="tpu_custom_call" | custom-call | flops 1132462080 | bytes 10698768 | tf_op jit(solution)/shard_map/pallas_call | solution.py:25
  20.1 2.9 %shard_map.87 = (bf16[2,2,16,16,256]{4,3,2,1,0:T(8,128)(2,1)S(1)}, f32[4,288,256]{2,1,0:T(8,128)S(1)}, bf16[4,288,256]{2,1,0:T(8,128)(2,1)S(1)}) custom-call(s32[4]{0:T(128)S(1)} %pad_add_fusion.place, bf16[3,26,32,256]{3,2,1,0:T(8,128)(2,1)S(1)} %get-tuple-element.54.shifted, f32[768,256]{1,0:T(8,128)S(1)} %get-tuple-element.55.slope, ...), custom_call_target="tpu_custom_call" | custom-call | flops 1132462080 | bytes 5816336 | tf_op jit(solution)/shard_map/pallas_call | solution.py:25
  24.3 2.2 %collective-permute-start.12 = (bf16[288,256]{1,0:T(8,128)(2,1)S(1)}, bf16[288,256]{1,0:T(8,128)(2,1)S(1)}, u32[]{:S(2)}, u32[]{:S(2)}) collective-permute-start(bf16[288,256]{1,0:T(8,128)(2,1)S(1)} %get-tuple-element.77), channel_id=1, source_target_pairs={{0,24},{4,28},{8,16},{12,20},{16,8},{20,12},{24,0},{28,4},{1,25},{... | collective-permute-start | bytes 442376 | tf_op jit(solution)/shard_map/ppermute | solution.py:459
  26.5 1.0 %collective-permute-start.13 = (bf16[288,256]{1,0:T(8,128)(2,1)S(1)}, bf16[288,256]{1,0:T(8,128)(2,1)S(1)}, u32[]{:S(2)}, u32[]{:S(2)}) collective-permute-start(bf16[288,256]{1,0:T(8,128)(2,1)S(1)} %get-tuple-element.78), channel_id=1, source_target_pairs={{0,8},{4,12},{8,0},{12,4},{16,24},{20,28},{24,16},{28,20},{1,9},{5... | collective-permute-start | bytes 442376 | tf_op jit(solution)/shard_map/ppermute | solution.py:459
  28.5 2.2 %collective-permute-start.5 = (bf16[288,256]{1,0:T(8,128)(2,1)S(1)}, bf16[288,256]{1,0:T(8,128)(2,1)S(1)}, u32[]{:S(2)}, u32[]{:S(2)}) collective-permute-start(bf16[288,256]{1,0:T(8,128)(2,1)S(1)} %get-tuple-element.67), channel_id=1, source_target_pairs={{0,24},{4,28},{8,16},{12,20},{16,8},{20,12},{24,0},{28,4},{1,25},{... | collective-permute-start | bytes 442376 | tf_op jit(solution)/shard_map/ppermute | solution.py:459
  30.7 1.0 %collective-permute-start.6 = (bf16[288,256]{1,0:T(8,128)(2,1)S(1)}, bf16[288,256]{1,0:T(8,128)(2,1)S(1)}, u32[]{:S(2)}, u32[]{:S(2)}) collective-permute-start(bf16[288,256]{1,0:T(8,128)(2,1)S(1)} %get-tuple-element.68), channel_id=1, source_target_pairs={{0,8},{4,12},{8,0},{12,4},{16,24},{20,28},{24,16},{28,20},{1,9},{5... | collective-permute-start | bytes 442376 | tf_op jit(solution)/shard_map/ppermute | solution.py:459
  32.0 1.7 %collective-permute-start.7 = (bf16[288,256]{1,0:T(8,128)(2,1)S(1)}, bf16[288,256]{1,0:T(8,128)(2,1)S(1)}, u32[]{:S(2)}, u32[]{:S(2)}) collective-permute-start(bf16[288,256]{1,0:T(8,128)(2,1)S(1)} %get-tuple-element.69), channel_id=1, source_target_pairs={{0,16},{4,20},{8,24},{12,28},{16,0},{20,4},{24,8},{28,12},{1,17},{... | collective-permute-start | bytes 442376 | tf_op jit(solution)/shard_map/ppermute | solution.py:459
  33.7 1.7 %collective-permute-done.13.refs_1_ = bf16[288,256]{1,0:T(8,128)(2,1)S(1)} collective-permute-done((bf16[288,256]{1,0:T(8,128)(2,1)S(1)}, bf16[288,256]{1,0:T(8,128)(2,1)S(1)}, u32[]{:S(2)}, u32[]{:S(2)}) %collective-permute-start.13) | collective-permute-done | bytes 147488 | tf_op jit(solution)/shard_map/ppermute | solution.py:459
  35.4 2.1 %collective-permute-done.14.refs_2_ = bf16[288,256]{1,0:T(8,128)(2,1)S(1)} collective-permute-done((bf16[288,256]{1,0:T(8,128)(2,1)S(1)}, bf16[288,256]{1,0:T(8,128)(2,1)S(1)}, u32[]{:S(2)}, u32[]{:S(2)}) %collective-permute-start.14) | collective-permute-done | bytes 147488 | tf_op jit(solution)/shard_map/ppermute | solution.py:459
  38.2 3.9 %collective-permute-start.15 = (bf16[144,128]{1,0:T(8,128)(2,1)S(1)}, bf16[144,128]{1,0:T(8,128)(2,1)S(1)}, u32[]{:S(2)}, u32[]{:S(2)}) collective-permute-start(bf16[144,128]{1,0:T(8,128)(2,1)S(1)} %get-tuple-element.81), channel_id=1, source_target_pairs={{0,3},{1,2},{2,1},{3,0},{4,7},{5,6},{6,5},{7,4},{8,11},{9,10},{10,... | collective-permute-start | bytes 110600 | tf_op jit(solution)/shard_map/ppermute | solution.py:468
  42.0 2.5 %collective-permute-start.16 = (bf16[144,128]{1,0:T(8,128)(2,1)S(1)}, bf16[144,128]{1,0:T(8,128)(2,1)S(1)}, u32[]{:S(2)}, u32[]{:S(2)}) collective-permute-start(bf16[144,128]{1,0:T(8,128)(2,1)S(1)} %get-tuple-element.82), channel_id=1, source_target_pairs={{0,2},{1,3},{2,0},{3,1},{4,6},{5,7},{6,4},{7,5},{8,10},{9,11},{10,... | collective-permute-start | bytes 110600 | tf_op jit(solution)/shard_map/ppermute | solution.py:468
  45.8 2.4 %collective-permute-start.8 = (bf16[144,128]{1,0:T(8,128)(2,1)S(1)}, bf16[144,128]{1,0:T(8,128)(2,1)S(1)}, u32[]{:S(2)}, u32[]{:S(2)}) collective-permute-start(bf16[144,128]{1,0:T(8,128)(2,1)S(1)} %get-tuple-element.71), channel_id=1, source_target_pairs={{0,3},{1,2},{2,1},{3,0},{4,7},{5,6},{6,5},{7,4},{8,11},{9,10},{10,... | collective-permute-start | bytes 110600 | tf_op jit(solution)/shard_map/ppermute | solution.py:468
  48.8 1.4 %collective-permute-start.10 = (bf16[144,128]{1,0:T(8,128)(2,1)S(1)}, bf16[144,128]{1,0:T(8,128)(2,1)S(1)}, u32[]{:S(2)}, u32[]{:S(2)}) collective-permute-start(bf16[144,128]{1,0:T(8,128)(2,1)S(1)} %get-tuple-element.73), channel_id=1, source_target_pairs={{0,1},{1,0},{2,3},{3,2},{4,5},{5,4},{6,7},{7,6},{8,9},{9,8},{10,11... | collective-permute-start | bytes 110600 | tf_op jit(solution)/shard_map/ppermute | solution.py:468
  50.2 3.7 %shard_map.88 = (bf16[24,32,256]{2,1,0:T(8,128)(2,1)}, bf16[12,16,256]{2,1,0:T(8,128)(2,1)}) custom-call(s32[4]{0:T(128)S(1)} %pad_add_fusion.place, bf16[12,16,256]{2,1,0:T(8,128)(2,1)S(1)} %get-tuple-element.44.coarse, bf16[24,32,256]{2,1,0:T(8,128)(2,1)S(1)} %get-tuple-element.45.cot, bf16[24,32,256]{2,1,0:T(8,128)(2,1)S(1)} %get-tuple-element.53.act, ...), custom_call_target="tpu_custom_call" | custom-call | flops 1509949440 | bytes 4718608 | tf_op jit(solution)/shard_map/pallas_call | solution.py:25
  53.9 0.8 %shard_map.94 = f32[64,288]{1,0:T(8,128)} custom-call(f32[144,128]{1,0:T(8,128)S(1)} %get-tuple-element.80.own, bf16[144,128]{1,0:T(8,128)(2,1)S(1)} %collective-permute-done.15.refs_0_, bf16[144,128]{1,0:T(8,128)(2,1)S(1)} %collective-permute-done.16.refs_1_, bf16[144,128]{1,0:T(8,128)(2,1)S(1)} %collective-permute-done.17.refs_2_), custom_call_target="tpu_custom_call" | custom-call | bytes 258048 | tf_op jit(solution)/shard_map/pallas_call | solution.py:25
  (34 shorter events, 7.8 us)
Async XLA Ops:
  0.7 1.0 %copy-start = (bf16[24,32,256]{2,1,0:T(8,128)(2,1)S(1)}, bf16[24,32,256]{2,1,0:T(8,128)(2,1)}, u32[]{:S(2)}) copy-start(bf16[24,32,256]{2,1,0:T(8,128)(2,1)} %skip.1) | copy-start | bytes 1179652
  1.7 1.0 %copy-start.1 = (bf16[24,32,256]{2,1,0:T(8,128)(2,1)S(1)}, bf16[24,32,256]{2,1,0:T(8,128)(2,1)}, u32[]{:S(2)}) copy-start(bf16[24,32,256]{2,1,0:T(8,128)(2,1)} %cot.1) | copy-start | bytes 1179652
  2.7 0.9 %copy-start.2 = (bf16[12,16,256]{2,1,0:T(8,128)(2,1)S(1)}, bf16[12,16,256]{2,1,0:T(8,128)(2,1)}, u32[]{:S(2)}) copy-start(bf16[12,16,256]{2,1,0:T(8,128)(2,1)} %coarse.1) | copy-start | bytes 294916
  3.6 12.1 %copy-start.3 = (bf16[3,3,256,256]{3,2,1,0:T(8,128)(2,1)S(1)}, bf16[3,3,256,256]{3,2,1,0:T(8,128)(2,1)}, u32[]{:S(2)}) copy-start(bf16[3,3,256,256]{3,2,1,0:T(8,128)(2,1)} %up_w.1) | copy-start | bytes 3538948
  4.9 4.1 %collective-permute-start = (bf16[96,256]{1,0:T(8,128)(2,1)S(1)}, bf16[96,256]{1,0:T(8,128)(2,1)S(1)}, u32[]{:S(2)}, u32[]{:S(2)}) collective-permute-start(bf16[96,256]{1,0:T(8,128)(2,1)S(1)} %get-tuple-element.47), channel_id=1, source_target_pairs={{0,4},{4,0},{8,12},{12,8},{16,20},{20,16},{24,28},{28,24},{1,5},{5... | collective-permute-start | bytes 147464 | tf_op jit(solution)/shard_map/ppermute | solution.py:474
  5.4 5.3 %collective-permute-start.1 = (bf16[96,256]{1,0:T(8,128)(2,1)S(1)}, bf16[96,256]{1,0:T(8,128)(2,1)S(1)}, u32[]{:S(2)}, u32[]{:S(2)}) collective-permute-start(bf16[96,256]{1,0:T(8,128)(2,1)S(1)} %get-tuple-element.48), channel_id=1, source_target_pairs={{0,28},{4,8},{8,4},{12,16},{16,12},{20,24},{24,20},{28,0},{1,29},{... | collective-permute-start | bytes 147464 | tf_op jit(solution)/shard_map/ppermute | solution.py:474
  11.3 4.3 %collective-permute-start.2 = (bf16[128,256]{1,0:T(8,128)(2,1)S(1)}, bf16[128,256]{1,0:T(8,128)(2,1)S(1)}, u32[]{:S(2)}, u32[]{:S(2)}) collective-permute-start(bf16[128,256]{1,0:T(8,128)(2,1)S(1)} %get-tuple-element.51), channel_id=1, source_target_pairs={{0,1},{1,0},{2,3},{3,2},{4,5},{5,4},{6,7},{7,6},{8,9},{9,8},{10,11... | collective-permute-start | bytes 196616 | tf_op jit(solution)/shard_map/ppermute | solution.py:474
  13.1 2.5 %collective-permute-start.3 = (bf16[128,256]{1,0:T(8,128)(2,1)S(1)}, bf16[128,256]{1,0:T(8,128)(2,1)S(1)}, u32[]{:S(2)}, u32[]{:S(2)}) collective-permute-start(bf16[128,256]{1,0:T(8,128)(2,1)S(1)} %get-tuple-element.52), channel_id=1, source_target_pairs={{1,2},{2,1},{5,6},{6,5},{9,10},{10,9},{13,14},{14,13},{17,18},{18,... | collective-permute-start | bytes 196616 | tf_op jit(solution)/shard_map/ppermute | solution.py:474
  15.7 1.3 %copy-start.4 = (bf16[3,3,256,256]{3,2,1,0:T(8,128)(2,1)S(1)}, bf16[3,3,256,256]{3,2,1,0:T(8,128)(2,1)}, u32[]{:S(2)}) copy-start(bf16[3,3,256,256]{3,2,1,0:T(8,128)(2,1)} %conv_w.1) | copy-start | bytes 3538948
  20.1 3.6 %collective-permute-start.11 = (bf16[4,288,256]{2,1,0:T(8,128)(2,1)S(1)}, bf16[4,288,256]{2,1,0:T(8,128)(2,1)S(1)}, u32[]{:S(2)}, u32[]{:S(2)}) collective-permute-start(bf16[4,288,256]{2,1,0:T(8,128)(2,1)S(1)} %get-tuple-element.75), channel_id=1, source_target_pairs={{0,4},{4,0},{8,12},{12,8},{16,20},{20,16},{24,28},{28,24},{1,5},{5... | collective-permute-start | bytes 1769480 | tf_op jit(solution)/shard_map/ppermute | solution.py:453
  23.1 4.8 %collective-permute-start.4 = (bf16[4,288,256]{2,1,0:T(8,128)(2,1)S(1)}, bf16[4,288,256]{2,1,0:T(8,128)(2,1)S(1)}, u32[]{:S(2)}, u32[]{:S(2)}) collective-permute-start(bf16[4,288,256]{2,1,0:T(8,128)(2,1)S(1)} %get-tuple-element.65), channel_id=1, source_target_pairs={{0,4},{4,0},{8,12},{12,8},{16,20},{20,16},{24,28},{28,24},{1,5},{5... | collective-permute-start | bytes 1769480 | tf_op jit(solution)/shard_map/ppermute | solution.py:453
  24.3 7.7 %collective-permute-start.12 = (bf16[288,256]{1,0:T(8,128)(2,1)S(1)}, bf16[288,256]{1,0:T(8,128)(2,1)S(1)}, u32[]{:S(2)}, u32[]{:S(2)}) collective-permute-start(bf16[288,256]{1,0:T(8,128)(2,1)S(1)} %get-tuple-element.77), channel_id=1, source_target_pairs={{0,24},{4,28},{8,16},{12,20},{16,8},{20,12},{24,0},{28,4},{1,25},{... | collective-permute-start | bytes 442376 | tf_op jit(solution)/shard_map/ppermute | solution.py:459
  26.5 8.9 %collective-permute-start.13 = (bf16[288,256]{1,0:T(8,128)(2,1)S(1)}, bf16[288,256]{1,0:T(8,128)(2,1)S(1)}, u32[]{:S(2)}, u32[]{:S(2)}) collective-permute-start(bf16[288,256]{1,0:T(8,128)(2,1)S(1)} %get-tuple-element.78), channel_id=1, source_target_pairs={{0,8},{4,12},{8,0},{12,4},{16,24},{20,28},{24,16},{28,20},{1,9},{5... | collective-permute-start | bytes 442376 | tf_op jit(solution)/shard_map/ppermute | solution.py:459
  27.5 10.0 %collective-permute-start.14 = (bf16[288,256]{1,0:T(8,128)(2,1)S(1)}, bf16[288,256]{1,0:T(8,128)(2,1)S(1)}, u32[]{:S(2)}, u32[]{:S(2)}) collective-permute-start(bf16[288,256]{1,0:T(8,128)(2,1)S(1)} %get-tuple-element.79), channel_id=1, source_target_pairs={{0,16},{4,20},{8,24},{12,28},{16,0},{20,4},{24,8},{28,12},{1,17},{... | collective-permute-start | bytes 442376 | tf_op jit(solution)/shard_map/ppermute | solution.py:459
  28.5 16.1 %collective-permute-start.5 = (bf16[288,256]{1,0:T(8,128)(2,1)S(1)}, bf16[288,256]{1,0:T(8,128)(2,1)S(1)}, u32[]{:S(2)}, u32[]{:S(2)}) collective-permute-start(bf16[288,256]{1,0:T(8,128)(2,1)S(1)} %get-tuple-element.67), channel_id=1, source_target_pairs={{0,24},{4,28},{8,16},{12,20},{16,8},{20,12},{24,0},{28,4},{1,25},{... | collective-permute-start | bytes 442376 | tf_op jit(solution)/shard_map/ppermute | solution.py:459
  30.7 14.3 %collective-permute-start.6 = (bf16[288,256]{1,0:T(8,128)(2,1)S(1)}, bf16[288,256]{1,0:T(8,128)(2,1)S(1)}, u32[]{:S(2)}, u32[]{:S(2)}) collective-permute-start(bf16[288,256]{1,0:T(8,128)(2,1)S(1)} %get-tuple-element.68), channel_id=1, source_target_pairs={{0,8},{4,12},{8,0},{12,4},{16,24},{20,28},{24,16},{28,20},{1,9},{5... | collective-permute-start | bytes 442376 | tf_op jit(solution)/shard_map/ppermute | solution.py:459
  32.0 13.1 %collective-permute-start.7 = (bf16[288,256]{1,0:T(8,128)(2,1)S(1)}, bf16[288,256]{1,0:T(8,128)(2,1)S(1)}, u32[]{:S(2)}, u32[]{:S(2)}) collective-permute-start(bf16[288,256]{1,0:T(8,128)(2,1)S(1)} %get-tuple-element.69), channel_id=1, source_target_pairs={{0,16},{4,20},{8,24},{12,28},{16,0},{20,4},{24,8},{28,12},{1,17},{... | collective-permute-start | bytes 442376 | tf_op jit(solution)/shard_map/ppermute | solution.py:459
  38.2 10.7 %collective-permute-start.15 = (bf16[144,128]{1,0:T(8,128)(2,1)S(1)}, bf16[144,128]{1,0:T(8,128)(2,1)S(1)}, u32[]{:S(2)}, u32[]{:S(2)}) collective-permute-start(bf16[144,128]{1,0:T(8,128)(2,1)S(1)} %get-tuple-element.81), channel_id=1, source_target_pairs={{0,3},{1,2},{2,1},{3,0},{4,7},{5,6},{6,5},{7,4},{8,11},{9,10},{10,... | collective-permute-start | bytes 110600 | tf_op jit(solution)/shard_map/ppermute | solution.py:468
  42.0 11.9 %collective-permute-start.16 = (bf16[144,128]{1,0:T(8,128)(2,1)S(1)}, bf16[144,128]{1,0:T(8,128)(2,1)S(1)}, u32[]{:S(2)}, u32[]{:S(2)}) collective-permute-start(bf16[144,128]{1,0:T(8,128)(2,1)S(1)} %get-tuple-element.82), channel_id=1, source_target_pairs={{0,2},{1,3},{2,0},{3,1},{4,6},{5,7},{6,4},{7,5},{8,10},{9,11},{10,... | collective-permute-start | bytes 110600 | tf_op jit(solution)/shard_map/ppermute | solution.py:468
  44.6 9.3 %collective-permute-start.17 = (bf16[144,128]{1,0:T(8,128)(2,1)S(1)}, bf16[144,128]{1,0:T(8,128)(2,1)S(1)}, u32[]{:S(2)}, u32[]{:S(2)}) collective-permute-start(bf16[144,128]{1,0:T(8,128)(2,1)S(1)} %get-tuple-element.83), channel_id=1, source_target_pairs={{0,1},{1,0},{2,3},{3,2},{4,5},{5,4},{6,7},{7,6},{8,9},{9,8},{10,11... | collective-permute-start | bytes 110600 | tf_op jit(solution)/shard_map/ppermute | solution.py:468
  45.8 9.0 %collective-permute-start.8 = (bf16[144,128]{1,0:T(8,128)(2,1)S(1)}, bf16[144,128]{1,0:T(8,128)(2,1)S(1)}, u32[]{:S(2)}, u32[]{:S(2)}) collective-permute-start(bf16[144,128]{1,0:T(8,128)(2,1)S(1)} %get-tuple-element.71), channel_id=1, source_target_pairs={{0,3},{1,2},{2,1},{3,0},{4,7},{5,6},{6,5},{7,4},{8,11},{9,10},{10,... | collective-permute-start | bytes 110600 | tf_op jit(solution)/shard_map/ppermute | solution.py:468
  48.2 6.5 %collective-permute-start.9 = (bf16[144,128]{1,0:T(8,128)(2,1)S(1)}, bf16[144,128]{1,0:T(8,128)(2,1)S(1)}, u32[]{:S(2)}, u32[]{:S(2)}) collective-permute-start(bf16[144,128]{1,0:T(8,128)(2,1)S(1)} %get-tuple-element.72), channel_id=1, source_target_pairs={{0,2},{1,3},{2,0},{3,1},{4,6},{5,7},{6,4},{7,5},{8,10},{9,11},{10,... | collective-permute-start | bytes 110600 | tf_op jit(solution)/shard_map/ppermute | solution.py:468
  48.8 5.9 %collective-permute-start.10 = (bf16[144,128]{1,0:T(8,128)(2,1)S(1)}, bf16[144,128]{1,0:T(8,128)(2,1)S(1)}, u32[]{:S(2)}, u32[]{:S(2)}) collective-permute-start(bf16[144,128]{1,0:T(8,128)(2,1)S(1)} %get-tuple-element.73), channel_id=1, source_target_pairs={{0,1},{1,0},{2,3},{3,2},{4,5},{5,4},{6,7},{7,6},{8,9},{9,8},{10,11... | collective-permute-start | bytes 110600 | tf_op jit(solution)/shard_map/ppermute | solution.py:468

commit v3 on v2

--- a/solution.py
+++ b/solution.py
@@ -19,7 +19,7 @@
 def kernel_call(body, outs, scratch, flops, *args, far=()):
     vmem = pl.BlockSpec(memory_space=pltpu.VMEM)
     smem = pl.BlockSpec(memory_space=pltpu.SMEM)
-    anywhere = pl.BlockSpec(memory_space=pl.ANY)
+    anywhere = pl.BlockSpec(memory_space=pltpu.HBM)
     moved = sum(a.size * a.dtype.itemsize for a in args)
     moved += sum(a.size * a.dtype.itemsize for a in outs)
     return pl.pallas_call(
@@ -246,7 +246,7 @@
     copies[1].wait()
 
 
-def grad_kernel(place, shifted, slope, near, conv_w, phases, keep, send, fine, partial):
+def grad_kernel(shifted, slope, conv_w, phases, fine):
     rows, cols = shifted.shape[1] - 2, shifted.shape[2]
     channels = shifted.shape[3]
     n_rows, n_cols = rows // 2, cols // 2
@@ -264,6 +264,10 @@
                 phases[row_phase, col_phase, row] = get(fine, start, n_cols, 2).astype(bf16)
             for row in range(n_rows, whole):
                 phases[row_phase, col_phase, row] = jnp.zeros((n_cols, channels), bf16)
+
+
+def up_kernel(place, near, phases, keep, send, partial):
+    _, _, whole, n_cols, channels = phases.shape
     turned = {}
     for row_off in range(2):
         for col_off in range(2):
@@ -447,16 +451,24 @@
     return [(i, i ^ bits) for i in range(count)]
 
 
-def reduce_partial(place, keep, send):
-    faces, bands = lax.axis_size("face"), lax.axis_size("band")
+def core_sum(place, keep, send):
     groups, block, channels = keep.shape
-    got = lax.ppermute(send, "face", xor_pairs(faces, 1))
+    got = lax.ppermute(send, "face", xor_pairs(lax.axis_size("face"), 1))
     shape = (block, channels)
-    own, *messages = kernel_call(
-        sum_kernel, [sds(shape, f32)] + [sds(shape, bf16)] * (groups - 1), [], 0, place, keep, got
-    )
-    order = sorted(range(1, groups), key=lambda k: -bin(k).count("1"))
-    got = [lax.ppermute(messages[k - 1], "face", xor_pairs(faces, 2 * k)) for k in order]
+    outs = [sds(shape, f32)] + [sds(shape, bf16)] * (groups - 1)
+    own, *messages = kernel_call(sum_kernel, outs, [], 0, place, keep, got)
+    return own, messages
+
+
+def plane_swap(messages):
+    faces = lax.axis_size("face")
+    order = sorted(range(1, faces // 2), key=lambda k: -bin(k).count("1"))
+    return [lax.ppermute(messages[k - 1], "face", xor_pairs(faces, 2 * k)) for k in order]
+
+
+def band_sum(place, own, got):
+    bands = lax.axis_size("band")
+    block, channels = own.shape
     cols = channels // bands
     side = packing(block, cols)
     shape = (block // side, cols * side)
@@ -467,6 +479,10 @@
     order = sorted(range(1, bands), key=lambda k: -k)
     got = [lax.ppermute(messages[k - 1], "band", xor_pairs(bands, k)) for k in order]
     return kernel_call(last_kernel, [sds((cols, block), f32)], [], 0, own, *got)[0].T
+
+
+def after(value, *others):
+    return lax.optimization_barrier((value, *others))[0]
 
 
 def swap(first, second, axis, wrap):
@@ -522,12 +538,18 @@
         45 * one_tap, place, coarse, skip, cotangent, left, right, first, second,
         up_weight, conv_weight, far=(8, 9),
     )
-    phases, keep_up, send_up = kernel_call(
+    own_conv, to_plane = core_sum(place, keep_conv, send_conv)
+    from_plane = plane_swap(to_plane)
+    phases = kernel_call(
         grad_kernel,
-        [sds((2, 2, whole, n_cols, channels), bf16), *partials],
-        [flat, partial],
-        45 * one_tap, place, shifted, slope, near, conv_weight,
-    )
+        [sds((2, 2, whole, n_cols, channels), bf16)],
+        [flat],
+        36 * one_tap, shifted, slope, conv_weight,
+    )[0]
+    keep_up, send_up = kernel_call(
+        up_kernel, partials, [partial], 9 * one_tap, place, after(near, to_plane[0]), phases
+    )
+    own_up, to_plane = core_sum(place, keep_up, send_up)
     decoded, grad_coarse = kernel_call(
         out_kernel,
         [sds(skip.shape, bf16), sds(coarse.shape, bf16)],
@@ -535,11 +557,11 @@
             padded, pltpu.VMEM(shift_shape, bf16), pltpu.VMEM((4, n_rows + 1, n_cols, channels), bf16),
             halves(at.ring_size, channels), halves((rows + 3) * stride, channels),
         ],
-        60 * one_tap, place, coarse, cotangent, act, phases, left, right, upper, lower,
-        conv_weight, up_weight,
-    )
-    grad_conv = reduce_partial(place, keep_conv, send_conv)
-    grad_up = reduce_partial(place, keep_up, send_up)
+        60 * one_tap, place, coarse, cotangent, after(act, to_plane[0]), phases, left, right,
+        upper, lower, conv_weight, up_weight,
+    )
+    grad_conv = band_sum(place, after(own_conv, decoded), from_plane)
+    grad_up = band_sum(place, own_up, plane_swap(to_plane))
     return (decoded, grad_coarse, grad_up, grad_conv)
 
 

time: 55.8 us -> 55.1 us (0.987)
  Pallas kernels: 15.9 us -> 15.3 us
    pallas_call x11 -> x12, Pallas kernels: 15.9 us -> 15.3 us  [kernel_call(): pl.pallas_call(body, out_shape=tuple(outs), in_specs=[anywhere if i in fa...]
  transfers between devices with their start and end apart: 18 -> 18, of which waited for: 5 -> 6; matrix products, arithmetic and copies ran while one was open for 0% -> 0% of each run, Pallas kernels for 18% -> 14%
where the time goes in v3:
time: 55.1 us; the launch traced here: 54.8 us
  starting transfers between devices  27.3 us (50%)
  Pallas kernels  15.3 us (28%)
  waiting for transfers between devices  7.22 us (13%)
  local copies, waits for them, and re-layouts  4.16 us (8%)
  between operations  0.76 us (1%)
    pallas_call x12, Pallas kernels, kernel_call(): pl.pallas_call(body, out_shape=tuple(outs), in_specs=[anywhere if i in fa...  15.3 us
    ppermute x6, starting transfers between devices, band_sum(): lax.ppermute(messages[k - 1], 'band', xor_pairs(bands, k))  12.1 us
    ppermute x6, starting transfers between devices, plane_swap(): lax.ppermute(messages[k - 1], 'face', xor_pairs(faces, 2 * k))  8.42 us
    ppermute x4, starting transfers between devices, swap(): return (lax.ppermute(first, axis, one), lax.ppermute(second, axis, two))  6.53 us
    unnamed x10, local copies, waits for them, and re-layouts  4.16 us
    ppermute x4, waiting for transfers between devices, swap(): return (lax.ppermute(first, axis, one), lax.ppermute(second, axis, two))  3.64 us
    ppermute x6, waiting for transfers between devices, band_sum(): lax.ppermute(messages[k - 1], 'band', xor_pairs(bands, k))  2.54 us
  transfers between devices with their start and end apart: 18, of which 6 were waited for; matrix products, arithmetic and copies ran while one was open for 0% of the time, Pallas kernels for 14%

profile of v3, /device:TPU:0, one launch (start us, length us, event | category | flops | bytes accessed | tf_op | source)
XLA Modules:
  0.0 54.8 jit_solution(7095821223826390940)
XLA Ops:
  0.7 1.0 %copy-done = bf16[24,32,256]{2,1,0:T(8,128)(2,1)S(1)} copy-done((bf16[24,32,256]{2,1,0:T(8,128)(2,1)S(1)}, bf16[24,32,256]{2,1,0:T(8,128)(2,1)}, u32[]{:S(2)}) %copy-start) | copy-done | bytes 393240
  1.7 1.0 %copy-done.1 = bf16[24,32,256]{2,1,0:T(8,128)(2,1)S(1)} copy-done((bf16[24,32,256]{2,1,0:T(8,128)(2,1)S(1)}, bf16[24,32,256]{2,1,0:T(8,128)(2,1)}, u32[]{:S(2)}) %copy-start.1) | copy-done | bytes 393240
  2.7 0.9 %copy-done.2 = bf16[12,16,256]{2,1,0:T(8,128)(2,1)S(1)} copy-done((bf16[12,16,256]{2,1,0:T(8,128)(2,1)S(1)}, bf16[12,16,256]{2,1,0:T(8,128)(2,1)}, u32[]{:S(2)}) %copy-start.2) | copy-done | bytes 98328
  3.6 1.3 %shard_map.84 = (bf16[96,256]{1,0:T(8,128)(2,1)S(1)}, bf16[96,256]{1,0:T(8,128)(2,1)S(1)}, bf16[24,32,256]{2,1,0:T(8,128)(2,1)S(1)}, bf16[24,32,256]{2,1,0:T(8,128)(2,1)S(1)}, bf16[12,16,256]{2,1,0:T(8,128)(2,1)S(1)}) custom-call(s32[4]{0:T(128)S(1)} %pad_add_fusion.place, bf16[12,16,256]{2,1,0:T(8,128)(2,1)S(1)} %copy-done.2, ...), custom_call_target="tpu_custom_call" | custom-call | bytes 1867792 | tf_op jit(solution)/shard_map/pallas_call | solution.py:25
  5.4 3.6 %collective-permute-start.1 = (bf16[96,256]{1,0:T(8,128)(2,1)S(1)}, bf16[96,256]{1,0:T(8,128)(2,1)S(1)}, u32[]{:S(2)}, u32[]{:S(2)}) collective-permute-start(bf16[96,256]{1,0:T(8,128)(2,1)S(1)} %get-tuple-element.50), channel_id=1, source_target_pairs={{0,28},{4,8},{8,4},{12,16},{16,12},{20,24},{24,20},{28,0},{1,29},{... | collective-permute-start | bytes 147464 | tf_op jit(solution)/shard_map/ppermute | solution.py:490
  9.0 1.8 %collective-permute-done.1.got_second = bf16[96,256]{1,0:T(8,128)(2,1)S(1)} collective-permute-done((bf16[96,256]{1,0:T(8,128)(2,1)S(1)}, bf16[96,256]{1,0:T(8,128)(2,1)S(1)}, u32[]{:S(2)}, u32[]{:S(2)}) %collective-permute-start.1) | collective-permute-done | bytes 49184 | tf_op jit(solution)/shard_map/ppermute | solution.py:490
  11.3 1.8 %collective-permute-start.2 = (bf16[128,256]{1,0:T(8,128)(2,1)S(1)}, bf16[128,256]{1,0:T(8,128)(2,1)S(1)}, u32[]{:S(2)}, u32[]{:S(2)}) collective-permute-start(bf16[128,256]{1,0:T(8,128)(2,1)S(1)} %get-tuple-element.53), channel_id=1, source_target_pairs={{0,1},{1,0},{2,3},{3,2},{4,5},{5,4},{6,7},{7,6},{8,9},{9,8},{10,11... | collective-permute-start | bytes 196616 | tf_op jit(solution)/shard_map/ppermute | solution.py:490
  13.8 1.9 %collective-permute-done.2.got_first = bf16[128,256]{1,0:T(8,128)(2,1)S(1)} collective-permute-done((bf16[128,256]{1,0:T(8,128)(2,1)S(1)}, bf16[128,256]{1,0:T(8,128)(2,1)S(1)}, u32[]{:S(2)}, u32[]{:S(2)}) %collective-permute-start.2) | collective-permute-done | bytes 65568 | tf_op jit(solution)/shard_map/ppermute | solution.py:490
  15.7 1.3 %copy-done.4 = bf16[3,3,256,256]{3,2,1,0:T(8,128)(2,1)S(1)} copy-done((bf16[3,3,256,256]{3,2,1,0:T(8,128)(2,1)S(1)}, bf16[3,3,256,256]{3,2,1,0:T(8,128)(2,1)}, u32[]{:S(2)}) %copy-start.4) | copy-done | bytes 1179672
  17.0 3.1 %shard_map.86 = (bf16[3,26,32,256]{3,2,1,0:T(8,128)(2,1)S(1)}, bf16[2,17,16,256]{3,2,1,0:T(8,128)(2,1)S(1)}, bf16[24,32,256]{2,1,0:T(8,128)(2,1)S(1)}, f32[768,2...) custom-call(s32[4]{0:T(128)S(1)} %pad_add_fusion.place, ...), custom_call_target="tpu_custom_call" | custom-call | flops 1132462080 | bytes 10698768 | tf_op jit(solution)/shard_map/pallas_call | solution.py:25
  20.1 1.2 %shard_map.88.phases = bf16[2,2,16,16,256]{4,3,2,1,0:T(8,128)(2,1)S(1)} custom-call(bf16[3,26,32,256]{3,2,1,0:T(8,128)(2,1)S(1)} %get-tuple-element.61.shifted, f32[768,256]{1,0:T(8,128)S(1)} %get-tuple-element.62.slope, bf16[3,3,256,256]{3,2,1,0:T(8,128)(2,1)S(1)} %get-tuple-element.63.conv_w), custom_call_target="tpu_custom_call" | custom-call | flops 905969664 | bytes 3768320 | tf_op jit(solution)/shard_map/pallas_call | solution.py:25
  22.8 1.2 %shard_map.89 = (f32[4,288,256]{2,1,0:T(8,128)S(1)}, bf16[4,288,256]{2,1,0:T(8,128)(2,1)S(1)}) custom-call(s32[4]{0:T(128)S(1)} %pad_add_fusion.place, bf16[2,17,16,256]{3,2,1,0:T(8,128)(2,1)S(1)} %get-tuple-element.60.near, bf16[2,2,16,16,256]{4,3,2,1,0:T(8,128)(2,1)S(1)} %shard_map.88.phases), custom_call_target="tpu_custom_call" | custom-call | flops 226492416 | bytes 2572304 | tf_op jit(solution)/shard_map/pallas_call | solution.py:25
  24.2 2.2 %collective-permute-start.12 = (bf16[288,256]{1,0:T(8,128)(2,1)S(1)}, bf16[288,256]{1,0:T(8,128)(2,1)S(1)}, u32[]{:S(2)}, u32[]{:S(2)}) collective-permute-start(bf16[288,256]{1,0:T(8,128)(2,1)S(1)} %get-tuple-element.82), channel_id=1, source_target_pairs={{0,24},{4,28},{8,16},{12,20},{16,8},{20,12},{24,0},{28,4},{1,25},{... | collective-permute-start | bytes 442376 | tf_op jit(solution)/shard_map/ppermute | solution.py:466
  26.8 0.8 %collective-permute-start.13 = (bf16[288,256]{1,0:T(8,128)(2,1)S(1)}, bf16[288,256]{1,0:T(8,128)(2,1)S(1)}, u32[]{:S(2)}, u32[]{:S(2)}) collective-permute-start(bf16[288,256]{1,0:T(8,128)(2,1)S(1)} %get-tuple-element.59), channel_id=1, source_target_pairs={{0,8},{4,12},{8,0},{12,4},{16,24},{20,28},{24,16},{28,20},{1,9},{5... | collective-permute-start | bytes 442376 | tf_op jit(solution)/shard_map/ppermute | solution.py:466
  28.3 1.2 %collective-permute-start.7 = (bf16[288,256]{1,0:T(8,128)(2,1)S(1)}, bf16[288,256]{1,0:T(8,128)(2,1)S(1)}, u32[]{:S(2)}, u32[]{:S(2)}) collective-permute-start(bf16[288,256]{1,0:T(8,128)(2,1)S(1)} %get-tuple-element.66), channel_id=1, source_target_pairs={{0,8},{4,12},{8,0},{12,4},{16,24},{20,28},{24,16},{28,20},{1,9},{5... | collective-permute-start | bytes 442376 | tf_op jit(solution)/shard_map/ppermute | solution.py:466
  29.6 2.0 %collective-permute-start.6 = (bf16[288,256]{1,0:T(8,128)(2,1)S(1)}, bf16[288,256]{1,0:T(8,128)(2,1)S(1)}, u32[]{:S(2)}, u32[]{:S(2)}) collective-permute-start(bf16[288,256]{1,0:T(8,128)(2,1)S(1)} %get-tuple-element.74), channel_id=1, source_target_pairs={{0,24},{4,28},{8,16},{12,20},{16,8},{20,12},{24,0},{28,4},{1,25},{... | collective-permute-start | bytes 442376 | tf_op jit(solution)/shard_map/ppermute | solution.py:466
  31.8 1.7 %collective-permute-start.8 = (bf16[288,256]{1,0:T(8,128)(2,1)S(1)}, bf16[288,256]{1,0:T(8,128)(2,1)S(1)}, u32[]{:S(2)}, u32[]{:S(2)}) collective-permute-start(bf16[288,256]{1,0:T(8,128)(2,1)S(1)} %get-tuple-element.75), channel_id=1, source_target_pairs={{0,16},{4,20},{8,24},{12,28},{16,0},{20,4},{24,8},{28,12},{1,17},{... | collective-permute-start | bytes 442376 | tf_op jit(solution)/shard_map/ppermute | solution.py:466
  33.5 3.7 %shard_map.91 = (bf16[24,32,256]{2,1,0:T(8,128)(2,1)}, bf16[12,16,256]{2,1,0:T(8,128)(2,1)}) custom-call(s32[4]{0:T(128)S(1)} %pad_add_fusion.place, bf16[12,16,256]{2,1,0:T(8,128)(2,1)S(1)} %get-tuple-element.46.coarse, bf16[24,32,256]{2,1,0:T(8,128)(2,1)S(1)} %get-tuple-element.47.cot, bf16[24,32,256]{2,1,0:T(8,128)(2,1)S(1)} %get-tuple-element.67.act, ...), custom_call_target="tpu_custom_call" | custom-call | flops 1509949440 | bytes 4718608 | tf_op jit(solution)/shard_map/pallas_call | solution.py:25
  37.9 3.8 %collective-permute-start.15 = (bf16[144,128]{1,0:T(8,128)(2,1)S(1)}, bf16[144,128]{1,0:T(8,128)(2,1)S(1)}, u32[]{:S(2)}, u32[]{:S(2)}) collective-permute-start(bf16[144,128]{1,0:T(8,128)(2,1)S(1)} %get-tuple-element.85), channel_id=1, source_target_pairs={{0,3},{1,2},{2,1},{3,0},{4,7},{5,6},{6,5},{7,4},{8,11},{9,10},{10,... | collective-permute-start | bytes 110600 | tf_op jit(solution)/shard_map/ppermute | solution.py:480
  41.7 2.5 %collective-permute-start.16 = (bf16[144,128]{1,0:T(8,128)(2,1)S(1)}, bf16[144,128]{1,0:T(8,128)(2,1)S(1)}, u32[]{:S(2)}, u32[]{:S(2)}) collective-permute-start(bf16[144,128]{1,0:T(8,128)(2,1)S(1)} %get-tuple-element.86), channel_id=1, source_target_pairs={{0,2},{1,3},{2,0},{3,1},{4,6},{5,7},{6,4},{7,5},{8,10},{9,11},{10,... | collective-permute-start | bytes 110600 | tf_op jit(solution)/shard_map/ppermute | solution.py:480
  44.2 1.2 %collective-permute-start.17 = (bf16[144,128]{1,0:T(8,128)(2,1)S(1)}, bf16[144,128]{1,0:T(8,128)(2,1)S(1)}, u32[]{:S(2)}, u32[]{:S(2)}) collective-permute-start(bf16[144,128]{1,0:T(8,128)(2,1)S(1)} %get-tuple-element.87), channel_id=1, source_target_pairs={{0,1},{1,0},{2,3},{3,2},{4,5},{5,4},{6,7},{7,6},{8,9},{9,8},{10,11... | collective-permute-start | bytes 110600 | tf_op jit(solution)/shard_map/ppermute | solution.py:480
  46.2 3.0 %collective-permute-start.9 = (bf16[144,128]{1,0:T(8,128)(2,1)S(1)}, bf16[144,128]{1,0:T(8,128)(2,1)S(1)}, u32[]{:S(2)}, u32[]{:S(2)}) collective-permute-start(bf16[144,128]{1,0:T(8,128)(2,1)S(1)} %get-tuple-element.77), channel_id=1, source_target_pairs={{0,3},{1,2},{2,1},{3,0},{4,7},{5,6},{6,5},{7,4},{8,11},{9,10},{10,... | collective-permute-start | bytes 110600 | tf_op jit(solution)/shard_map/ppermute | solution.py:480
  49.2 1.5 %collective-permute-start.11 = (bf16[144,128]{1,0:T(8,128)(2,1)S(1)}, bf16[144,128]{1,0:T(8,128)(2,1)S(1)}, u32[]{:S(2)}, u32[]{:S(2)}) collective-permute-start(bf16[144,128]{1,0:T(8,128)(2,1)S(1)} %get-tuple-element.79), channel_id=1, source_target_pairs={{0,1},{1,0},{2,3},{3,2},{4,5},{5,4},{6,7},{7,6},{8,9},{9,8},{10,11... | collective-permute-start | bytes 110600 | tf_op jit(solution)/shard_map/ppermute | solution.py:480
  52.0 2.0 %collective-permute-done.10.refs_1_ = bf16[144,128]{1,0:T(8,128)(2,1)S(1)} collective-permute-done((bf16[144,128]{1,0:T(8,128)(2,1)S(1)}, bf16[144,128]{1,0:T(8,128)(2,1)S(1)}, u32[]{:S(2)}, u32[]{:S(2)}) %collective-permute-start.10) | collective-permute-done | bytes 36896 | tf_op jit(solution)/shard_map/ppermute | solution.py:480
  (35 shorter events, 8.6 us)
Async XLA Ops:
  0.7 1.0 %copy-start = (bf16[24,32,256]{2,1,0:T(8,128)(2,1)S(1)}, bf16[24,32,256]{2,1,0:T(8,128)(2,1)}, u32[]{:S(2)}) copy-start(bf16[24,32,256]{2,1,0:T(8,128)(2,1)} %skip.1) | copy-start | bytes 1179652
  1.7 1.0 %copy-start.1 = (bf16[24,32,256]{2,1,0:T(8,128)(2,1)S(1)}, bf16[24,32,256]{2,1,0:T(8,128)(2,1)}, u32[]{:S(2)}) copy-start(bf16[24,32,256]{2,1,0:T(8,128)(2,1)} %cot.1) | copy-start | bytes 1179652
  2.7 0.9 %copy-start.2 = (bf16[12,16,256]{2,1,0:T(8,128)(2,1)S(1)}, bf16[12,16,256]{2,1,0:T(8,128)(2,1)}, u32[]{:S(2)}) copy-start(bf16[12,16,256]{2,1,0:T(8,128)(2,1)} %coarse.1) | copy-start | bytes 294916
  3.6 12.1 %copy-start.3 = (bf16[3,3,256,256]{3,2,1,0:T(8,128)(2,1)S(1)}, bf16[3,3,256,256]{3,2,1,0:T(8,128)(2,1)}, u32[]{:S(2)}) copy-start(bf16[3,3,256,256]{3,2,1,0:T(8,128)(2,1)} %up_w.1) | copy-start | bytes 3538948
  4.9 4.1 %collective-permute-start = (bf16[96,256]{1,0:T(8,128)(2,1)S(1)}, bf16[96,256]{1,0:T(8,128)(2,1)S(1)}, u32[]{:S(2)}, u32[]{:S(2)}) collective-permute-start(bf16[96,256]{1,0:T(8,128)(2,1)S(1)} %get-tuple-element.49), channel_id=1, source_target_pairs={{0,4},{4,0},{8,12},{12,8},{16,20},{20,16},{24,28},{28,24},{1,5},{5... | collective-permute-start | bytes 147464 | tf_op jit(solution)/shard_map/ppermute | solution.py:490
  5.4 5.3 %collective-permute-start.1 = (bf16[96,256]{1,0:T(8,128)(2,1)S(1)}, bf16[96,256]{1,0:T(8,128)(2,1)S(1)}, u32[]{:S(2)}, u32[]{:S(2)}) collective-permute-start(bf16[96,256]{1,0:T(8,128)(2,1)S(1)} %get-tuple-element.50), channel_id=1, source_target_pairs={{0,28},{4,8},{8,4},{12,16},{16,12},{20,24},{24,20},{28,0},{1,29},{... | collective-permute-start | bytes 147464 | tf_op jit(solution)/shard_map/ppermute | solution.py:490
  11.3 4.3 %collective-permute-start.2 = (bf16[128,256]{1,0:T(8,128)(2,1)S(1)}, bf16[128,256]{1,0:T(8,128)(2,1)S(1)}, u32[]{:S(2)}, u32[]{:S(2)}) collective-permute-start(bf16[128,256]{1,0:T(8,128)(2,1)S(1)} %get-tuple-element.53), channel_id=1, source_target_pairs={{0,1},{1,0},{2,3},{3,2},{4,5},{5,4},{6,7},{7,6},{8,9},{9,8},{10,11... | collective-permute-start | bytes 196616 | tf_op jit(solution)/shard_map/ppermute | solution.py:490
  13.1 2.5 %collective-permute-start.3 = (bf16[128,256]{1,0:T(8,128)(2,1)S(1)}, bf16[128,256]{1,0:T(8,128)(2,1)S(1)}, u32[]{:S(2)}, u32[]{:S(2)}) collective-permute-start(bf16[128,256]{1,0:T(8,128)(2,1)S(1)} %get-tuple-element.54), channel_id=1, source_target_pairs={{1,2},{2,1},{5,6},{6,5},{9,10},{10,9},{13,14},{14,13},{17,18},{18,... | collective-permute-start | bytes 196616 | tf_op jit(solution)/shard_map/ppermute | solution.py:490
  15.7 1.3 %copy-start.4 = (bf16[3,3,256,256]{3,2,1,0:T(8,128)(2,1)S(1)}, bf16[3,3,256,256]{3,2,1,0:T(8,128)(2,1)}, u32[]{:S(2)}) copy-start(bf16[3,3,256,256]{3,2,1,0:T(8,128)(2,1)} %conv_w.1) | copy-start | bytes 3538948
  20.1 2.1 %collective-permute-start.4 = (bf16[4,288,256]{2,1,0:T(8,128)(2,1)S(1)}, bf16[4,288,256]{2,1,0:T(8,128)(2,1)S(1)}, u32[]{:S(2)}, u32[]{:S(2)}) collective-permute-start(bf16[4,288,256]{2,1,0:T(8,128)(2,1)S(1)} %get-tuple-element.58), channel_id=1, source_target_pairs={{0,4},{4,0},{8,12},{12,8},{16,20},{20,16},{24,28},{28,24},{1,5},{5... | collective-permute-start | bytes 1769480 | tf_op jit(solution)/shard_map/ppermute | solution.py:456
  24.0 3.7 %collective-permute-start.5 = (bf16[4,288,256]{2,1,0:T(8,128)(2,1)S(1)}, bf16[4,288,256]{2,1,0:T(8,128)(2,1)S(1)}, u32[]{:S(2)}, u32[]{:S(2)}) collective-permute-start(bf16[4,288,256]{2,1,0:T(8,128)(2,1)S(1)} %get-tuple-element.65), channel_id=1, source_target_pairs={{0,4},{4,0},{8,12},{12,8},{16,20},{20,16},{24,28},{28,24},{1,5},{5... | collective-permute-start | bytes 1769480 | tf_op jit(solution)/shard_map/ppermute | solution.py:456
  24.2 7.6 %collective-permute-start.12 = (bf16[288,256]{1,0:T(8,128)(2,1)S(1)}, bf16[288,256]{1,0:T(8,128)(2,1)S(1)}, u32[]{:S(2)}, u32[]{:S(2)}) collective-permute-start(bf16[288,256]{1,0:T(8,128)(2,1)S(1)} %get-tuple-element.82), channel_id=1, source_target_pairs={{0,24},{4,28},{8,16},{12,20},{16,8},{20,12},{24,0},{28,4},{1,25},{... | collective-permute-start | bytes 442376 | tf_op jit(solution)/shard_map/ppermute | solution.py:466
  26.3 10.8 %collective-permute-start.14 = (bf16[288,256]{1,0:T(8,128)(2,1)S(1)}, bf16[288,256]{1,0:T(8,128)(2,1)S(1)}, u32[]{:S(2)}, u32[]{:S(2)}) collective-permute-start(bf16[288,256]{1,0:T(8,128)(2,1)S(1)} %get-tuple-element.83), channel_id=1, source_target_pairs={{0,16},{4,20},{8,24},{12,28},{16,0},{20,4},{24,8},{28,12},{1,17},{... | collective-permute-start | bytes 442376 | tf_op jit(solution)/shard_map/ppermute | solution.py:466
  26.8 10.3 %collective-permute-start.13 = (bf16[288,256]{1,0:T(8,128)(2,1)S(1)}, bf16[288,256]{1,0:T(8,128)(2,1)S(1)}, u32[]{:S(2)}, u32[]{:S(2)}) collective-permute-start(bf16[288,256]{1,0:T(8,128)(2,1)S(1)} %get-tuple-element.59), channel_id=1, source_target_pairs={{0,8},{4,12},{8,0},{12,4},{16,24},{20,28},{24,16},{28,20},{1,9},{5... | collective-permute-start | bytes 442376 | tf_op jit(solution)/shard_map/ppermute | solution.py:466
  28.3 17.1 %collective-permute-start.7 = (bf16[288,256]{1,0:T(8,128)(2,1)S(1)}, bf16[288,256]{1,0:T(8,128)(2,1)S(1)}, u32[]{:S(2)}, u32[]{:S(2)}) collective-permute-start(bf16[288,256]{1,0:T(8,128)(2,1)S(1)} %get-tuple-element.66), channel_id=1, source_target_pairs={{0,8},{4,12},{8,0},{12,4},{16,24},{20,28},{24,16},{28,20},{1,9},{5... | collective-permute-start | bytes 442376 | tf_op jit(solution)/shard_map/ppermute | solution.py:466
  29.6 14.6 %collective-permute-start.6 = (bf16[288,256]{1,0:T(8,128)(2,1)S(1)}, bf16[288,256]{1,0:T(8,128)(2,1)S(1)}, u32[]{:S(2)}, u32[]{:S(2)}) collective-permute-start(bf16[288,256]{1,0:T(8,128)(2,1)S(1)} %get-tuple-element.74), channel_id=1, source_target_pairs={{0,24},{4,28},{8,16},{12,20},{16,8},{20,12},{24,0},{28,4},{1,25},{... | collective-permute-start | bytes 442376 | tf_op jit(solution)/shard_map/ppermute | solution.py:466
  31.8 13.7 %collective-permute-start.8 = (bf16[288,256]{1,0:T(8,128)(2,1)S(1)}, bf16[288,256]{1,0:T(8,128)(2,1)S(1)}, u32[]{:S(2)}, u32[]{:S(2)}) collective-permute-start(bf16[288,256]{1,0:T(8,128)(2,1)S(1)} %get-tuple-element.75), channel_id=1, source_target_pairs={{0,16},{4,20},{8,24},{12,28},{16,0},{20,4},{24,8},{28,12},{1,17},{... | collective-permute-start | bytes 442376 | tf_op jit(solution)/shard_map/ppermute | solution.py:466
  37.9 11.3 %collective-permute-start.15 = (bf16[144,128]{1,0:T(8,128)(2,1)S(1)}, bf16[144,128]{1,0:T(8,128)(2,1)S(1)}, u32[]{:S(2)}, u32[]{:S(2)}) collective-permute-start(bf16[144,128]{1,0:T(8,128)(2,1)S(1)} %get-tuple-element.85), channel_id=1, source_target_pairs={{0,3},{1,2},{2,1},{3,0},{4,7},{5,6},{6,5},{7,4},{8,11},{9,10},{10,... | collective-permute-start | bytes 110600 | tf_op jit(solution)/shard_map/ppermute | solution.py:480
  41.7 8.9 %collective-permute-start.16 = (bf16[144,128]{1,0:T(8,128)(2,1)S(1)}, bf16[144,128]{1,0:T(8,128)(2,1)S(1)}, u32[]{:S(2)}, u32[]{:S(2)}) collective-permute-start(bf16[144,128]{1,0:T(8,128)(2,1)S(1)} %get-tuple-element.86), channel_id=1, source_target_pairs={{0,2},{1,3},{2,0},{3,1},{4,6},{5,7},{6,4},{7,5},{8,10},{9,11},{10,... | collective-permute-start | bytes 110600 | tf_op jit(solution)/shard_map/ppermute | solution.py:480
  44.2 6.4 %collective-permute-start.17 = (bf16[144,128]{1,0:T(8,128)(2,1)S(1)}, bf16[144,128]{1,0:T(8,128)(2,1)S(1)}, u32[]{:S(2)}, u32[]{:S(2)}) collective-permute-start(bf16[144,128]{1,0:T(8,128)(2,1)S(1)} %get-tuple-element.87), channel_id=1, source_target_pairs={{0,1},{1,0},{2,3},{3,2},{4,5},{5,4},{6,7},{7,6},{8,9},{9,8},{10,11... | collective-permute-start | bytes 110600 | tf_op jit(solution)/shard_map/ppermute | solution.py:480
  46.2 5.9 %collective-permute-start.9 = (bf16[144,128]{1,0:T(8,128)(2,1)S(1)}, bf16[144,128]{1,0:T(8,128)(2,1)S(1)}, u32[]{:S(2)}, u32[]{:S(2)}) collective-permute-start(bf16[144,128]{1,0:T(8,128)(2,1)S(1)} %get-tuple-element.77), channel_id=1, source_target_pairs={{0,3},{1,2},{2,1},{3,0},{4,7},{5,6},{6,5},{7,4},{8,11},{9,10},{10,... | collective-permute-start | bytes 110600 | tf_op jit(solution)/shard_map/ppermute | solution.py:480
  49.1 4.9 %collective-permute-start.10 = (bf16[144,128]{1,0:T(8,128)(2,1)S(1)}, bf16[144,128]{1,0:T(8,128)(2,1)S(1)}, u32[]{:S(2)}, u32[]{:S(2)}) collective-permute-start(bf16[144,128]{1,0:T(8,128)(2,1)S(1)} %get-tuple-element.78), channel_id=1, source_target_pairs={{0,2},{1,3},{2,0},{3,1},{4,6},{5,7},{6,4},{7,5},{8,10},{9,11},{10,... | collective-permute-start | bytes 110600 | tf_op jit(solution)/shard_map/ppermute | solution.py:480
  49.2 4.9 %collective-permute-start.11 = (bf16[144,128]{1,0:T(8,128)(2,1)S(1)}, bf16[144,128]{1,0:T(8,128)(2,1)S(1)}, u32[]{:S(2)}, u32[]{:S(2)}) collective-permute-start(bf16[144,128]{1,0:T(8,128)(2,1)S(1)} %get-tuple-element.79), channel_id=1, source_target_pairs={{0,1},{1,0},{2,3},{3,2},{4,5},{5,4},{6,7},{7,6},{8,9},{9,8},{10,11... | collective-permute-start | bytes 110600 | tf_op jit(solution)/shard_map/ppermute | solution.py:480

commit v4 on v3

--- a/solution.py
+++ b/solution.py
@@ -19,14 +19,18 @@
 def kernel_call(body, outs, scratch, flops, *args, far=()):
     vmem = pl.BlockSpec(memory_space=pltpu.VMEM)
     smem = pl.BlockSpec(memory_space=pltpu.SMEM)
-    anywhere = pl.BlockSpec(memory_space=pltpu.HBM)
+    hbm = pl.BlockSpec(memory_space=pltpu.HBM)
     moved = sum(a.size * a.dtype.itemsize for a in args)
     moved += sum(a.size * a.dtype.itemsize for a in outs)
+    args = [
+        pltpu.with_memory_space_constraint(a, pltpu.HBM) if i in far else a
+        for i, a in enumerate(args)
+    ]
     return pl.pallas_call(
         body,
         out_shape=tuple(outs),
         in_specs=[
-            anywhere if i in far else smem if a.dtype == jnp.int32 else vmem
+            hbm if i in far else smem if a.dtype == jnp.int32 else vmem
             for i, a in enumerate(args)
         ],
         out_specs=tuple(vmem for _ in outs),

time: 55.1 us -> 51.9 us (0.942)
  local copies, waits for them, and re-layouts: 4.16 us -> 0 us
  Pallas kernels: 15.3 us -> 16.4 us
    unnamed x10 -> x0, local copies, waits for them, and re-layouts: 4.16 us -> none
    pallas_call x12, Pallas kernels: 15.3 us -> 16.4 us  [kernel_call(): pl.pallas_call(body, out_shape=tuple(outs), in_specs=[hbm if i in far els...]
  transfers between devices with their start and end apart: 18 -> 18, of which waited for: 6 -> 6; matrix products, arithmetic and copies ran while one was open for 0% -> 0% of each run, Pallas kernels for 14% -> 15%
where the time goes in v4:
time: 51.9 us; the launch traced here: 51.7 us
  starting transfers between devices  27.3 us (53%)
  Pallas kernels  16.4 us (32%)
  waiting for transfers between devices  7.22 us (14%)
  between operations  0.75 us (1%)
    pallas_call x12, Pallas kernels, kernel_call(): pl.pallas_call(body, out_shape=tuple(outs), in_specs=[hbm if i in far els...  16.4 us
    ppermute x6, starting transfers between devices, band_sum(): lax.ppermute(messages[k - 1], 'band', xor_pairs(bands, k))  12.1 us
    ppermute x6, starting transfers between devices, plane_swap(): lax.ppermute(messages[k - 1], 'face', xor_pairs(faces, 2 * k))  8.42 us
    ppermute x4, starting transfers between devices, swap(): return (lax.ppermute(first, axis, one), lax.ppermute(second, axis, two))  6.53 us
    ppermute x4, waiting for transfers between devices, swap(): return (lax.ppermute(first, axis, one), lax.ppermute(second, axis, two))  3.64 us
    ppermute x6, waiting for transfers between devices, band_sum(): lax.ppermute(messages[k - 1], 'band', xor_pairs(bands, k))  2.54 us
  transfers between devices with their start and end apart: 18, of which 6 were waited for; matrix products, arithmetic and copies ran while one was open for 0% of the time, Pallas kernels for 15%

profile of v4, /device:TPU:0, one launch (start us, length us, event | category | flops | bytes accessed | tf_op | source)
XLA Modules:
  0.0 51.7 jit_solution(16766308510069334186)
XLA Ops:
  0.7 1.8 %shard_map.84 = (bf16[96,256]{1,0:T(8,128)(2,1)S(1)}, bf16[96,256]{1,0:T(8,128)(2,1)S(1)}, bf16[24,32,256]{2,1,0:T(8,128)(2,1)S(1)}, bf16[24,32,256]{2,1,0:T(8,128)(2,1)S(1)}, bf16[12,16,256]{2,1,0:T(8,128)(2,1)S(1)}) custom-call(s32[4]{0:T(128)S(1)} %pad_add_fusion.place, bf16[12,16,256]{2,1,0:T(8,128)(2,1)} %coarse.1, bf16[24,32,256]{2,1,0:T(8,128)(2,1)} %skip.1, ...), custom_call_target="tpu_custom_call" | custom-call | bytes 1867792 | tf_op jit(solution)/shard_map/pallas_call | solution.py:29
  3.0 3.6 %collective-permute-start.1 = (bf16[96,256]{1,0:T(8,128)(2,1)S(1)}, bf16[96,256]{1,0:T(8,128)(2,1)S(1)}, u32[]{:S(2)}, u32[]{:S(2)}) collective-permute-start(bf16[96,256]{1,0:T(8,128)(2,1)S(1)} %get-tuple-element.50), channel_id=1, source_target_pairs={{0,28},{4,8},{8,4},{12,16},{16,12},{20,24},{24,20},{28,0},{1,29},{... | collective-permute-start | bytes 147464 | tf_op jit(solution)/shard_map/ppermute | solution.py:494
  6.6 1.8 %collective-permute-done.1.got_second = bf16[96,256]{1,0:T(8,128)(2,1)S(1)} collective-permute-done((bf16[96,256]{1,0:T(8,128)(2,1)S(1)}, bf16[96,256]{1,0:T(8,128)(2,1)S(1)}, u32[]{:S(2)}, u32[]{:S(2)}) %collective-permute-start.1) | collective-permute-done | bytes 49184 | tf_op jit(solution)/shard_map/ppermute | solution.py:494
  9.0 1.8 %collective-permute-start.2 = (bf16[128,256]{1,0:T(8,128)(2,1)S(1)}, bf16[128,256]{1,0:T(8,128)(2,1)S(1)}, u32[]{:S(2)}, u32[]{:S(2)}) collective-permute-start(bf16[128,256]{1,0:T(8,128)(2,1)S(1)} %get-tuple-element.53), channel_id=1, source_target_pairs={{0,1},{1,0},{2,3},{3,2},{4,5},{5,4},{6,7},{7,6},{8,9},{9,8},{10,11... | collective-permute-start | bytes 196616 | tf_op jit(solution)/shard_map/ppermute | solution.py:494
  11.4 1.9 %collective-permute-done.2.got_first = bf16[128,256]{1,0:T(8,128)(2,1)S(1)} collective-permute-done((bf16[128,256]{1,0:T(8,128)(2,1)S(1)}, bf16[128,256]{1,0:T(8,128)(2,1)S(1)}, u32[]{:S(2)}, u32[]{:S(2)}) %collective-permute-start.2) | collective-permute-done | bytes 65568 | tf_op jit(solution)/shard_map/ppermute | solution.py:494
  13.3 3.6 %shard_map.86 = (bf16[3,26,32,256]{3,2,1,0:T(8,128)(2,1)S(1)}, bf16[2,17,16,256]{3,2,1,0:T(8,128)(2,1)S(1)}, bf16[24,32,256]{2,1,0:T(8,128)(2,1)S(1)}, f32[768,2...) custom-call(s32[4]{0:T(128)S(1)} %pad_add_fusion.place, ...), custom_call_target="tpu_custom_call" | custom-call | flops 1132462080 | bytes 10698768 | tf_op jit(solution)/shard_map/pallas_call | solution.py:29
  17.0 1.2 %shard_map.88.phases = bf16[2,2,16,16,256]{4,3,2,1,0:T(8,128)(2,1)S(1)} custom-call(bf16[3,26,32,256]{3,2,1,0:T(8,128)(2,1)S(1)} %get-tuple-element.61.shifted, f32[768,256]{1,0:T(8,128)S(1)} %get-tuple-element.62.slope, bf16[3,3,256,256]{3,2,1,0:T(8,128)(2,1)S(1)} %get-tuple-element.63.conv_w), custom_call_target="tpu_custom_call" | custom-call | flops 905969664 | bytes 3768320 | tf_op jit(solution)/shard_map/pallas_call | solution.py:29
  18.2 0.8 %collective-permute-done.4.got = bf16[4,288,256]{2,1,0:T(8,128)(2,1)S(1)} collective-permute-done((bf16[4,288,256]{2,1,0:T(8,128)(2,1)S(1)}, bf16[4,288,256]{2,1,0:T(8,128)(2,1)S(1)}, u32[]{:S(2)}, u32[]{:S(2)}) %collective-permute-start.4) | collective-permute-done | bytes 589856 | tf_op jit(solution)/shard_map/ppermute | solution.py:460
  19.7 1.2 %shard_map.89 = (f32[4,288,256]{2,1,0:T(8,128)S(1)}, bf16[4,288,256]{2,1,0:T(8,128)(2,1)S(1)}) custom-call(s32[4]{0:T(128)S(1)} %pad_add_fusion.place, bf16[2,17,16,256]{3,2,1,0:T(8,128)(2,1)S(1)} %get-tuple-element.60.near, bf16[2,2,16,16,256]{4,3,2,1,0:T(8,128)(2,1)S(1)} %shard_map.88.phases), custom_call_target="tpu_custom_call" | custom-call | flops 226492416 | bytes 2572304 | tf_op jit(solution)/shard_map/pallas_call | solution.py:29
  21.1 2.2 %collective-permute-start.12 = (bf16[288,256]{1,0:T(8,128)(2,1)S(1)}, bf16[288,256]{1,0:T(8,128)(2,1)S(1)}, u32[]{:S(2)}, u32[]{:S(2)}) collective-permute-start(bf16[288,256]{1,0:T(8,128)(2,1)S(1)} %get-tuple-element.82), channel_id=1, source_target_pairs={{0,24},{4,28},{8,16},{12,20},{16,8},{20,12},{24,0},{28,4},{1,25},{... | collective-permute-start | bytes 442376 | tf_op jit(solution)/shard_map/ppermute | solution.py:470
  23.7 0.8 %collective-permute-start.13 = (bf16[288,256]{1,0:T(8,128)(2,1)S(1)}, bf16[288,256]{1,0:T(8,128)(2,1)S(1)}, u32[]{:S(2)}, u32[]{:S(2)}) collective-permute-start(bf16[288,256]{1,0:T(8,128)(2,1)S(1)} %get-tuple-element.59), channel_id=1, source_target_pairs={{0,8},{4,12},{8,0},{12,4},{16,24},{20,28},{24,16},{28,20},{1,9},{5... | collective-permute-start | bytes 442376 | tf_op jit(solution)/shard_map/ppermute | solution.py:470
  25.2 1.2 %collective-permute-start.7 = (bf16[288,256]{1,0:T(8,128)(2,1)S(1)}, bf16[288,256]{1,0:T(8,128)(2,1)S(1)}, u32[]{:S(2)}, u32[]{:S(2)}) collective-permute-start(bf16[288,256]{1,0:T(8,128)(2,1)S(1)} %get-tuple-element.66), channel_id=1, source_target_pairs={{0,8},{4,12},{8,0},{12,4},{16,24},{20,28},{24,16},{28,20},{1,9},{5... | collective-permute-start | bytes 442376 | tf_op jit(solution)/shard_map/ppermute | solution.py:470
  26.5 2.0 %collective-permute-start.6 = (bf16[288,256]{1,0:T(8,128)(2,1)S(1)}, bf16[288,256]{1,0:T(8,128)(2,1)S(1)}, u32[]{:S(2)}, u32[]{:S(2)}) collective-permute-start(bf16[288,256]{1,0:T(8,128)(2,1)S(1)} %get-tuple-element.74), channel_id=1, source_target_pairs={{0,24},{4,28},{8,16},{12,20},{16,8},{20,12},{24,0},{28,4},{1,25},{... | collective-permute-start | bytes 442376 | tf_op jit(solution)/shard_map/ppermute | solution.py:470
  28.7 1.7 %collective-permute-start.8 = (bf16[288,256]{1,0:T(8,128)(2,1)S(1)}, bf16[288,256]{1,0:T(8,128)(2,1)S(1)}, u32[]{:S(2)}, u32[]{:S(2)}) collective-permute-start(bf16[288,256]{1,0:T(8,128)(2,1)S(1)} %get-tuple-element.75), channel_id=1, source_target_pairs={{0,16},{4,20},{8,24},{12,28},{16,0},{20,4},{24,8},{28,12},{1,17},{... | collective-permute-start | bytes 442376 | tf_op jit(solution)/shard_map/ppermute | solution.py:470
  30.4 3.6 %shard_map.91 = (bf16[24,32,256]{2,1,0:T(8,128)(2,1)}, bf16[12,16,256]{2,1,0:T(8,128)(2,1)}) custom-call(s32[4]{0:T(128)S(1)} %pad_add_fusion.place, bf16[12,16,256]{2,1,0:T(8,128)(2,1)S(1)} %get-tuple-element.46.coarse, bf16[24,32,256]{2,1,0:T(8,128)(2,1)S(1)} %get-tuple-element.47.cot, bf16[24,32,256]{2,1,0:T(8,128)(2,1)S(1)} %get-tuple-element.67.act, ...), custom_call_target="tpu_custom_call" | custom-call | flops 1509949440 | bytes 4718608 | tf_op jit(solution)/shard_map/pallas_call | solution.py:29
  34.0 0.7 %shard_map.94 = (f32[144,128]{1,0:T(8,128)S(1)}, bf16[144,128]{1,0:T(8,128)(2,1)S(1)}, bf16[144,128]{1,0:T(8,128)(2,1)S(1)}, bf16[144,128]{1,0:T(8,128)(2,1)S(1)}) custom-call(s32[4]{0:T(128)S(1)} %pad_add_fusion.place, f32[288,256]{1,0:T(8,128)S(1)} %get-tuple-element.81.own, bf16[288,256]{1,0:T(8,128)(2,1)S(1)} %collective-permute-done.12.refs_0_, ...), custom_call_target="tpu_custom_call" | custom-call | bytes 921616 | tf_op jit(solution)/shard_map/pallas_call | solution.py:29
  34.7 3.8 %collective-permute-start.15 = (bf16[144,128]{1,0:T(8,128)(2,1)S(1)}, bf16[144,128]{1,0:T(8,128)(2,1)S(1)}, u32[]{:S(2)}, u32[]{:S(2)}) collective-permute-start(bf16[144,128]{1,0:T(8,128)(2,1)S(1)} %get-tuple-element.85), channel_id=1, source_target_pairs={{0,3},{1,2},{2,1},{3,0},{4,7},{5,6},{6,5},{7,4},{8,11},{9,10},{10,... | collective-permute-start | bytes 110600 | tf_op jit(solution)/shard_map/ppermute | solution.py:484
  38.6 2.5 %collective-permute-start.16 = (bf16[144,128]{1,0:T(8,128)(2,1)S(1)}, bf16[144,128]{1,0:T(8,128)(2,1)S(1)}, u32[]{:S(2)}, u32[]{:S(2)}) collective-permute-start(bf16[144,128]{1,0:T(8,128)(2,1)S(1)} %get-tuple-element.86), channel_id=1, source_target_pairs={{0,2},{1,3},{2,0},{3,1},{4,6},{5,7},{6,4},{7,5},{8,10},{9,11},{10,... | collective-permute-start | bytes 110600 | tf_op jit(solution)/shard_map/ppermute | solution.py:484
  41.1 1.2 %collective-permute-start.17 = (bf16[144,128]{1,0:T(8,128)(2,1)S(1)}, bf16[144,128]{1,0:T(8,128)(2,1)S(1)}, u32[]{:S(2)}, u32[]{:S(2)}) collective-permute-start(bf16[144,128]{1,0:T(8,128)(2,1)S(1)} %get-tuple-element.87), channel_id=1, source_target_pairs={{0,1},{1,0},{2,3},{3,2},{4,5},{5,4},{6,7},{7,6},{8,9},{9,8},{10,11... | collective-permute-start | bytes 110600 | tf_op jit(solution)/shard_map/ppermute | solution.py:484
  43.1 3.0 %collective-permute-start.9 = (bf16[144,128]{1,0:T(8,128)(2,1)S(1)}, bf16[144,128]{1,0:T(8,128)(2,1)S(1)}, u32[]{:S(2)}, u32[]{:S(2)}) collective-permute-start(bf16[144,128]{1,0:T(8,128)(2,1)S(1)} %get-tuple-element.77), channel_id=1, source_target_pairs={{0,3},{1,2},{2,1},{3,0},{4,7},{5,6},{6,5},{7,4},{8,11},{9,10},{10,... | collective-permute-start | bytes 110600 | tf_op jit(solution)/shard_map/ppermute | solution.py:484
  46.0 1.5 %collective-permute-start.11 = (bf16[144,128]{1,0:T(8,128)(2,1)S(1)}, bf16[144,128]{1,0:T(8,128)(2,1)S(1)}, u32[]{:S(2)}, u32[]{:S(2)}) collective-permute-start(bf16[144,128]{1,0:T(8,128)(2,1)S(1)} %get-tuple-element.79), channel_id=1, source_target_pairs={{0,1},{1,0},{2,3},{3,2},{4,5},{5,4},{6,7},{7,6},{8,9},{9,8},{10,11... | collective-permute-start | bytes 110600 | tf_op jit(solution)/shard_map/ppermute | solution.py:484
  47.5 0.8 %shard_map.95 = f32[64,288]{1,0:T(8,128)} custom-call(f32[144,128]{1,0:T(8,128)S(1)} %get-tuple-element.84.own, bf16[144,128]{1,0:T(8,128)(2,1)S(1)} %collective-permute-done.15.refs_0_, bf16[144,128]{1,0:T(8,128)(2,1)S(1)} %collective-permute-done.16.refs_1_, bf16[144,128]{1,0:T(8,128)(2,1)S(1)} %collective-permute-done.17.refs_2_), custom_call_target="tpu_custom_call" | custom-call | bytes 258048 | tf_op jit(solution)/shard_map/pallas_call | solution.py:29
  48.9 2.0 %collective-permute-done.10.refs_1_ = bf16[144,128]{1,0:T(8,128)(2,1)S(1)} collective-permute-done((bf16[144,128]{1,0:T(8,128)(2,1)S(1)}, bf16[144,128]{1,0:T(8,128)(2,1)S(1)}, u32[]{:S(2)}, u32[]{:S(2)}) %collective-permute-start.10) | collective-permute-done | bytes 36896 | tf_op jit(solution)/shard_map/ppermute | solution.py:484
  50.9 0.8 %shard_map.93 = f32[64,288]{1,0:T(8,128)} custom-call(f32[144,128]{1,0:T(8,128)S(1)} %get-tuple-element.76.own, bf16[144,128]{1,0:T(8,128)(2,1)S(1)} %collective-permute-done.9.refs_0_, bf16[144,128]{1,0:T(8,128)(2,1)S(1)} %collective-permute-done.10.refs_1_, bf16[144,128]{1,0:T(8,128)(2,1)S(1)} %collective-permute-done.11.refs_2_), custom_call_target="tpu_custom_call" | custom-call | bytes 258048 | tf_op jit(solution)/shard_map/pallas_call | solution.py:29
  (25 shorter events, 5.4 us)
Async XLA Ops:
  2.5 4.1 %collective-permute-start = (bf16[96,256]{1,0:T(8,128)(2,1)S(1)}, bf16[96,256]{1,0:T(8,128)(2,1)S(1)}, u32[]{:S(2)}, u32[]{:S(2)}) collective-permute-start(bf16[96,256]{1,0:T(8,128)(2,1)S(1)} %get-tuple-element.49), channel_id=1, source_target_pairs={{0,4},{4,0},{8,12},{12,8},{16,20},{20,16},{24,28},{28,24},{1,5},{5... | collective-permute-start | bytes 147464 | tf_op jit(solution)/shard_map/ppermute | solution.py:494
  3.0 5.3 %collective-permute-start.1 = (bf16[96,256]{1,0:T(8,128)(2,1)S(1)}, bf16[96,256]{1,0:T(8,128)(2,1)S(1)}, u32[]{:S(2)}, u32[]{:S(2)}) collective-permute-start(bf16[96,256]{1,0:T(8,128)(2,1)S(1)} %get-tuple-element.50), channel_id=1, source_target_pairs={{0,28},{4,8},{8,4},{12,16},{16,12},{20,24},{24,20},{28,0},{1,29},{... | collective-permute-start | bytes 147464 | tf_op jit(solution)/shard_map/ppermute | solution.py:494
  9.0 4.3 %collective-permute-start.2 = (bf16[128,256]{1,0:T(8,128)(2,1)S(1)}, bf16[128,256]{1,0:T(8,128)(2,1)S(1)}, u32[]{:S(2)}, u32[]{:S(2)}) collective-permute-start(bf16[128,256]{1,0:T(8,128)(2,1)S(1)} %get-tuple-element.53), channel_id=1, source_target_pairs={{0,1},{1,0},{2,3},{3,2},{4,5},{5,4},{6,7},{7,6},{8,9},{9,8},{10,11... | collective-permute-start | bytes 196616 | tf_op jit(solution)/shard_map/ppermute | solution.py:494
  10.8 2.5 %collective-permute-start.3 = (bf16[128,256]{1,0:T(8,128)(2,1)S(1)}, bf16[128,256]{1,0:T(8,128)(2,1)S(1)}, u32[]{:S(2)}, u32[]{:S(2)}) collective-permute-start(bf16[128,256]{1,0:T(8,128)(2,1)S(1)} %get-tuple-element.54), channel_id=1, source_target_pairs={{1,2},{2,1},{5,6},{6,5},{9,10},{10,9},{13,14},{14,13},{17,18},{18,... | collective-permute-start | bytes 196616 | tf_op jit(solution)/shard_map/ppermute | solution.py:494
  16.9 2.1 %collective-permute-start.4 = (bf16[4,288,256]{2,1,0:T(8,128)(2,1)S(1)}, bf16[4,288,256]{2,1,0:T(8,128)(2,1)S(1)}, u32[]{:S(2)}, u32[]{:S(2)}) collective-permute-start(bf16[4,288,256]{2,1,0:T(8,128)(2,1)S(1)} %get-tuple-element.58), channel_id=1, source_target_pairs={{0,4},{4,0},{8,12},{12,8},{16,20},{20,16},{24,28},{28,24},{1,5},{5... | collective-permute-start | bytes 1769480 | tf_op jit(solution)/shard_map/ppermute | solution.py:460
  20.9 3.7 %collective-permute-start.5 = (bf16[4,288,256]{2,1,0:T(8,128)(2,1)S(1)}, bf16[4,288,256]{2,1,0:T(8,128)(2,1)S(1)}, u32[]{:S(2)}, u32[]{:S(2)}) collective-permute-start(bf16[4,288,256]{2,1,0:T(8,128)(2,1)S(1)} %get-tuple-element.65), channel_id=1, source_target_pairs={{0,4},{4,0},{8,12},{12,8},{16,20},{20,16},{24,28},{28,24},{1,5},{5... | collective-permute-start | bytes 1769480 | tf_op jit(solution)/shard_map/ppermute | solution.py:460
  21.1 7.6 %collective-permute-start.12 = (bf16[288,256]{1,0:T(8,128)(2,1)S(1)}, bf16[288,256]{1,0:T(8,128)(2,1)S(1)}, u32[]{:S(2)}, u32[]{:S(2)}) collective-permute-start(bf16[288,256]{1,0:T(8,128)(2,1)S(1)} %get-tuple-element.82), channel_id=1, source_target_pairs={{0,24},{4,28},{8,16},{12,20},{16,8},{20,12},{24,0},{28,4},{1,25},{... | collective-permute-start | bytes 442376 | tf_op jit(solution)/shard_map/ppermute | solution.py:470
  23.2 10.8 %collective-permute-start.14 = (bf16[288,256]{1,0:T(8,128)(2,1)S(1)}, bf16[288,256]{1,0:T(8,128)(2,1)S(1)}, u32[]{:S(2)}, u32[]{:S(2)}) collective-permute-start(bf16[288,256]{1,0:T(8,128)(2,1)S(1)} %get-tuple-element.83), channel_id=1, source_target_pairs={{0,16},{4,20},{8,24},{12,28},{16,0},{20,4},{24,8},{28,12},{1,17},{... | collective-permute-start | bytes 442376 | tf_op jit(solution)/shard_map/ppermute | solution.py:470
  23.7 10.3 %collective-permute-start.13 = (bf16[288,256]{1,0:T(8,128)(2,1)S(1)}, bf16[288,256]{1,0:T(8,128)(2,1)S(1)}, u32[]{:S(2)}, u32[]{:S(2)}) collective-permute-start(bf16[288,256]{1,0:T(8,128)(2,1)S(1)} %get-tuple-element.59), channel_id=1, source_target_pairs={{0,8},{4,12},{8,0},{12,4},{16,24},{20,28},{24,16},{28,20},{1,9},{5... | collective-permute-start | bytes 442376 | tf_op jit(solution)/shard_map/ppermute | solution.py:470
  25.2 17.1 %collective-permute-start.7 = (bf16[288,256]{1,0:T(8,128)(2,1)S(1)}, bf16[288,256]{1,0:T(8,128)(2,1)S(1)}, u32[]{:S(2)}, u32[]{:S(2)}) collective-permute-start(bf16[288,256]{1,0:T(8,128)(2,1)S(1)} %get-tuple-element.66), channel_id=1, source_target_pairs={{0,8},{4,12},{8,0},{12,4},{16,24},{20,28},{24,16},{28,20},{1,9},{5... | collective-permute-start | bytes 442376 | tf_op jit(solution)/shard_map/ppermute | solution.py:470
  26.5 14.6 %collective-permute-start.6 = (bf16[288,256]{1,0:T(8,128)(2,1)S(1)}, bf16[288,256]{1,0:T(8,128)(2,1)S(1)}, u32[]{:S(2)}, u32[]{:S(2)}) collective-permute-start(bf16[288,256]{1,0:T(8,128)(2,1)S(1)} %get-tuple-element.74), channel_id=1, source_target_pairs={{0,24},{4,28},{8,16},{12,20},{16,8},{20,12},{24,0},{28,4},{1,25},{... | collective-permute-start | bytes 442376 | tf_op jit(solution)/shard_map/ppermute | solution.py:470
  28.7 13.7 %collective-permute-start.8 = (bf16[288,256]{1,0:T(8,128)(2,1)S(1)}, bf16[288,256]{1,0:T(8,128)(2,1)S(1)}, u32[]{:S(2)}, u32[]{:S(2)}) collective-permute-start(bf16[288,256]{1,0:T(8,128)(2,1)S(1)} %get-tuple-element.75), channel_id=1, source_target_pairs={{0,16},{4,20},{8,24},{12,28},{16,0},{20,4},{24,8},{28,12},{1,17},{... | collective-permute-start | bytes 442376 | tf_op jit(solution)/shard_map/ppermute | solution.py:470
  34.7 11.3 %collective-permute-start.15 = (bf16[144,128]{1,0:T(8,128)(2,1)S(1)}, bf16[144,128]{1,0:T(8,128)(2,1)S(1)}, u32[]{:S(2)}, u32[]{:S(2)}) collective-permute-start(bf16[144,128]{1,0:T(8,128)(2,1)S(1)} %get-tuple-element.85), channel_id=1, source_target_pairs={{0,3},{1,2},{2,1},{3,0},{4,7},{5,6},{6,5},{7,4},{8,11},{9,10},{10,... | collective-permute-start | bytes 110600 | tf_op jit(solution)/shard_map/ppermute | solution.py:484
  38.6 8.9 %collective-permute-start.16 = (bf16[144,128]{1,0:T(8,128)(2,1)S(1)}, bf16[144,128]{1,0:T(8,128)(2,1)S(1)}, u32[]{:S(2)}, u32[]{:S(2)}) collective-permute-start(bf16[144,128]{1,0:T(8,128)(2,1)S(1)} %get-tuple-element.86), channel_id=1, source_target_pairs={{0,2},{1,3},{2,0},{3,1},{4,6},{5,7},{6,4},{7,5},{8,10},{9,11},{10,... | collective-permute-start | bytes 110600 | tf_op jit(solution)/shard_map/ppermute | solution.py:484
  41.1 6.4 %collective-permute-start.17 = (bf16[144,128]{1,0:T(8,128)(2,1)S(1)}, bf16[144,128]{1,0:T(8,128)(2,1)S(1)}, u32[]{:S(2)}, u32[]{:S(2)}) collective-permute-start(bf16[144,128]{1,0:T(8,128)(2,1)S(1)} %get-tuple-element.87), channel_id=1, source_target_pairs={{0,1},{1,0},{2,3},{3,2},{4,5},{5,4},{6,7},{7,6},{8,9},{9,8},{10,11... | collective-permute-start | bytes 110600 | tf_op jit(solution)/shard_map/ppermute | solution.py:484
  43.1 5.9 %collective-permute-start.9 = (bf16[144,128]{1,0:T(8,128)(2,1)S(1)}, bf16[144,128]{1,0:T(8,128)(2,1)S(1)}, u32[]{:S(2)}, u32[]{:S(2)}) collective-permute-start(bf16[144,128]{1,0:T(8,128)(2,1)S(1)} %get-tuple-element.77), channel_id=1, source_target_pairs={{0,3},{1,2},{2,1},{3,0},{4,7},{5,6},{6,5},{7,4},{8,11},{9,10},{10,... | collective-permute-start | bytes 110600 | tf_op jit(solution)/shard_map/ppermute | solution.py:484
  46.0 4.9 %collective-permute-start.10 = (bf16[144,128]{1,0:T(8,128)(2,1)S(1)}, bf16[144,128]{1,0:T(8,128)(2,1)S(1)}, u32[]{:S(2)}, u32[]{:S(2)}) collective-permute-start(bf16[144,128]{1,0:T(8,128)(2,1)S(1)} %get-tuple-element.78), channel_id=1, source_target_pairs={{0,2},{1,3},{2,0},{3,1},{4,6},{5,7},{6,4},{7,5},{8,10},{9,11},{10,... | collective-permute-start | bytes 110600 | tf_op jit(solution)/shard_map/ppermute | solution.py:484
  46.0 4.9 %collective-permute-start.11 = (bf16[144,128]{1,0:T(8,128)(2,1)S(1)}, bf16[144,128]{1,0:T(8,128)(2,1)S(1)}, u32[]{:S(2)}, u32[]{:S(2)}) collective-permute-start(bf16[144,128]{1,0:T(8,128)(2,1)S(1)} %get-tuple-element.79), channel_id=1, source_target_pairs={{0,1},{1,0},{2,3},{3,2},{4,5},{5,4},{6,7},{7,6},{8,9},{9,8},{10,11... | collective-permute-start | bytes 110600 | tf_op jit(solution)/shard_map/ppermute | solution.py:484

commit v5 on v4

--- a/solution.py
+++ b/solution.py
@@ -173,19 +173,14 @@
 
 def act_kernel(
     place, coarse, skip, cot, left, right, got_first, got_second, up_w, conv_w,
-    shifted, near, act, slope, keep, send, upper, lower, up_v, conv_v,
-    padded, pre, partial, sems,
+    shifted, near, act, slope, keep, send, upper, lower, conv_v, padded, pre, partial, sem,
 ):
     n_rows, n_cols, channels = coarse.shape
     rows, cols, _ = skip.shape
     at = Layout(n_rows, n_cols)
     stride = cols + 2 * MARGIN
-    copies = [
-        pltpu.make_async_copy(up_w, up_v, sems.at[0]),
-        pltpu.make_async_copy(conv_w, conv_v, sems.at[1]),
-    ]
-    for copy in copies:
-        copy.start()
+    copy = pltpu.make_async_copy(conv_w, conv_v, sem)
+    copy.start()
     even = lax.rem(place[2], 2) == 0
     one, two = got_first[...].astype(f32), got_second[...].astype(f32)
     upper[...] = jnp.where(even, two, one)
@@ -221,14 +216,13 @@
     shifted[1, rows + 1] = lower[at.row_cot : at.row_cot + cols, :].astype(bf16)
     for row in range(rows):
         shifted[1, row + 1] = cot[row]
-    copies[0].wait()
     sums = {}
     for k in range(3):
         row_phase, row_off = forward_taps[k]
         for l in range(3):
             col_phase, col_off = forward_taps[l]
             source = near[col_off, pl.ds(row_off, n_rows)].reshape(n_rows * n_cols, channels)
-            term = dot(source, up_v[k, l])
+            term = dot(source, up_w[k, l])
             name = (row_phase, col_phase)
             sums[name] = sums[name] + term if name in sums else term
     for (row_phase, col_phase), total in sums.items():
@@ -247,7 +241,7 @@
             source = shifted[2 - l, pl.ds(2 - k, rows)].reshape(-1, channels)
             partial[pl.ds((3 * k + l) * channels, channels), :] = dot(act_t, source)
     split_by_core(place, partial, keep, send)
-    copies[1].wait()
+    copy.wait()
 
 
 def grad_kernel(shifted, slope, conv_w, phases, fine):
@@ -407,48 +401,59 @@
     coarse_out[...] = total.astype(bf16).reshape(coarse_out.shape)
 
 
-def sum_kernel(place, keep, got, own, *messages):
-    chip = place[1]
-    own[...] = keep[chip] + got[chip].astype(f32)
+def halving(count):
+    bits = (count // 2).bit_length() - 1
+    return [[(step + core) % bits for step in range(bits)] for core in range(2)]
+
+
+def mask_of(slot, order):
+    last = len(order) - 1
+    return sum(1 << bit for step, bit in enumerate(order) if slot >> (last - step) & 1)
+
+
+def core_kernel(place, keep, got, own, message):
+    slots, half = keep.shape[0], own.shape[0]
+    even, odd = halving(2 * slots)
+    for slot in range(slots):
+        chip = place[1] ^ jnp.where(place[0] == 0, mask_of(slot, even), mask_of(slot, odd))
+        total = keep[chip] + got[chip].astype(f32)
+        if slot < half:
+            own[slot] = total
+        else:
+            message[slot - half] = total.astype(bf16)
+
+
+def plane_kernel(before, got, own, message):
+    half = own.shape[0]
+    for slot in range(2 * half):
+        total = before[slot] + got[slot].astype(f32)
+        if slot < half:
+            own[slot] = total
+        else:
+            message[slot - half] = total.astype(bf16)
+
+
+def band_kernel(place, conv, got_conv, up, got_up, own, *refs):
+    n_bands, messages, cut = len(refs), refs[:-1], refs[-1]
+    conv_total = conv[0] + got_conv[0].astype(f32)
+    up_total = up[0] + got_up[0].astype(f32)
+    cols = conv_total.shape[1] // n_bands
+    for band in range(n_bands):
+        cut[band, :, :cols] = conv_total[:, band * cols : (band + 1) * cols]
+        cut[band, :, cols:] = up_total[:, band * cols : (band + 1) * cols]
+    own[...] = cut[place[2]]
     for k, message in enumerate(messages):
-        other = chip ^ (k + 1)
-        message[...] = (keep[other] + got[other].astype(f32)).astype(bf16)
-
-
-def packing(rows, cols):
-    side = max(1, 128 // cols)
-    return side if rows % (16 * side) == 0 else 1
-
-
-def plane_kernel(place, own, *refs):
-    n_bands, peers = refs[-1].shape[0], refs[: -(refs[-1].shape[0] + 1)]
-    outs, cut = refs[len(peers) : -1], refs[-1]
+        message[...] = cut[place[2] ^ (k + 1)].astype(bf16)
+
+
+def last_kernel(own, *refs):
+    peers, (conv, up) = refs[:-2], refs[-2:]
     total = own[...]
     for peer in peers:
         total = total + peer[...].astype(f32)
-    cols = total.shape[1] // n_bands
-    side = packing(total.shape[0], cols)
-    rows = total.shape[0] // side
-    for band in range(n_bands):
-        for part in range(side):
-            cut[band, :, part * cols : (part + 1) * cols] = total[
-                part * rows : (part + 1) * rows, band * cols : (band + 1) * cols
-            ]
-    band = place[2]
-    outs[0][...] = cut[band]
-    for k in range(1, n_bands):
-        outs[k][...] = cut[band ^ k].astype(bf16)
-
-
-def last_kernel(own, *refs):
-    peers, out = refs[:-1], refs[-1]
-    total = own[...]
-    for peer in peers:
-        total = total + peer[...].astype(f32)
-    rows, cols = total.shape[0], out.shape[0]
     turned = total.T
-    for part in range(out.shape[1] // rows):
-        out[:, part * rows : (part + 1) * rows] = turned[part * cols : (part + 1) * cols, :]
+    conv[...] = turned[: conv.shape[0]]
+    up[...] = turned[conv.shape[0] :]
 
 
 def xor_pairs(count, bits):
@@ -458,31 +463,33 @@
 def core_sum(place, keep, send):
     groups, block, channels = keep.shape
     got = lax.ppermute(send, "face", xor_pairs(lax.axis_size("face"), 1))
-    shape = (block, channels)
-    outs = [sds(shape, f32)] + [sds(shape, bf16)] * (groups - 1)
-    own, *messages = kernel_call(sum_kernel, outs, [], 0, place, keep, got)
-    return own, messages
-
-
-def plane_swap(messages):
+    shape = (groups // 2, block, channels)
+    return kernel_call(core_kernel, [sds(shape, f32), sds(shape, bf16)], [], 0, place, keep, got)
+
+
+def plane_swap(message, step):
     faces = lax.axis_size("face")
-    order = sorted(range(1, faces // 2), key=lambda k: -bin(k).count("1"))
-    return [lax.ppermute(messages[k - 1], "face", xor_pairs(faces, 2 * k)) for k in order]
-
-
-def band_sum(place, own, got):
+    orders = halving(faces)
+    return lax.ppermute(message, "face", [(i, i ^ 2 << orders[i % 2][step]) for i in range(faces)])
+
+
+def plane_sum(own, got):
+    half, block, channels = own.shape
+    shape = (half // 2, block, channels)
+    return kernel_call(plane_kernel, [sds(shape, f32), sds(shape, bf16)], [], 0, own, got)
+
+
+def band_sum(place, conv, got_conv, up, got_up):
     bands = lax.axis_size("band")
-    block, channels = own.shape
+    _, block, channels = conv.shape
     cols = channels // bands
-    side = packing(block, cols)
-    shape = (block // side, cols * side)
+    shape = (block, 2 * cols)
     own, *messages = kernel_call(
-        plane_kernel, [sds(shape, f32)] + [sds(shape, bf16)] * (bands - 1),
-        [pltpu.VMEM((bands,) + shape, f32)], 0, place, own, *got,
+        band_kernel, [sds(shape, f32)] + [sds(shape, bf16)] * (bands - 1),
+        [pltpu.VMEM((bands,) + shape, f32)], 0, place, conv, got_conv, up, got_up,
     )
-    order = sorted(range(1, bands), key=lambda k: -k)
-    got = [lax.ppermute(messages[k - 1], "band", xor_pairs(bands, k)) for k in order]
-    return kernel_call(last_kernel, [sds((cols, block), f32)], [], 0, own, *got)[0].T
+    got = [lax.ppermute(messages[k - 1], "band", xor_pairs(bands, k)) for k in range(bands - 1, 0, -1)]
+    return [a.T for a in kernel_call(last_kernel, [sds((cols, block), f32)] * 2, [], 0, own, *got)]
 
 
 def after(value, *others):
@@ -531,41 +538,50 @@
     partials = [sds((groups, block, channels), f32), sds((groups, block, channels), bf16)]
     partial = pltpu.VMEM((9 * channels, channels), f32)
     side = sds(message.shape, f32)
-    shifted, near, act, slope, keep_conv, send_conv, upper, lower, up_weight, conv_weight = kernel_call(
+    shifted, near, act, slope, keep_conv, send_conv, upper, lower, conv_weight = kernel_call(
         act_kernel,
         [
             sds(shift_shape, bf16), sds((2, whole + 1, n_cols, channels), bf16),
             sds(skip.shape, bf16), sds((rows * cols, channels), f32), *partials, side, side,
-            sds(up_weight.shape, bf16), sds(conv_weight.shape, bf16),
+            sds(conv_weight.shape, bf16),
         ],
-        [padded, flat, partial, pltpu.SemaphoreType.DMA((2,))],
+        [padded, flat, partial, pltpu.SemaphoreType.DMA],
         45 * one_tap, place, coarse, skip, cotangent, left, right, first, second,
-        up_weight, conv_weight, far=(8, 9),
+        up_weight, conv_weight, far=(9,),
     )
-    own_conv, to_plane = core_sum(place, keep_conv, send_conv)
-    from_plane = plane_swap(to_plane)
+    own_conv, to_conv = core_sum(place, keep_conv, send_conv)
+    got_conv = plane_swap(to_conv, 0)
     phases = kernel_call(
         grad_kernel,
         [sds((2, 2, whole, n_cols, channels), bf16)],
         [flat],
-        36 * one_tap, shifted, slope, conv_weight,
+        0, shifted, slope, conv_weight,
     )[0]
     keep_up, send_up = kernel_call(
-        up_kernel, partials, [partial], 9 * one_tap, place, after(near, to_plane[0]), phases
+        up_kernel, partials, [partial], 0, place, after(near, to_conv), phases
     )
-    own_up, to_plane = core_sum(place, keep_up, send_up)
-    decoded, grad_coarse = kernel_call(
-        out_kernel,
-        [sds(skip.shape, bf16), sds(coarse.shape, bf16)],
-        [
-            padded, pltpu.VMEM(shift_shape, bf16), pltpu.VMEM((4, n_rows + 1, n_cols, channels), bf16),
-            halves(at.ring_size, channels), halves((rows + 3) * stride, channels),
-        ],
-        60 * one_tap, place, coarse, cotangent, after(act, to_plane[0]), phases, left, right,
-        upper, lower, conv_weight, up_weight,
-    )
-    grad_conv = band_sum(place, after(own_conv, decoded), from_plane)
-    grad_up = band_sum(place, own_up, plane_swap(to_plane))
+    own_up, to_up = core_sum(place, keep_up, send_up)
+    got_up = plane_swap(to_up, 0)
+    steps = (faces // 2).bit_length() - 1
+    for step in range(1, steps):
+        own_conv, to_conv = plane_sum(after(own_conv, to_up), got_conv)
+        got_conv = plane_swap(to_conv, step)
+        if step == 1:
+            decoded, grad_coarse = kernel_call(
+                out_kernel,
+                [sds(skip.shape, bf16), sds(coarse.shape, bf16)],
+                [
+                    padded, pltpu.VMEM(shift_shape, bf16),
+                    pltpu.VMEM((4, n_rows + 1, n_cols, channels), bf16),
+                    halves(at.ring_size, channels), halves((rows + 3) * stride, channels),
+                ],
+                0, place, coarse, cotangent, after(act, to_conv), phases, left, right,
+                upper, lower, conv_weight, up_weight,
+            )
+            own_up = after(own_up, decoded)
+        own_up, to_up = plane_sum(own_up, got_up)
+        got_up = plane_swap(to_up, step)
+    grad_conv, grad_up = band_sum(place, own_conv, got_conv, own_up, got_up)
     return (decoded, grad_coarse, grad_up, grad_conv)
 
 

time: 51.9 us -> 50.8 us (0.979)
  waiting for transfers between devices: 7.22 us -> 16.7 us
  starting transfers between devices: 27.3 us -> 18.3 us
  Pallas kernels: 16.4 us -> 14.8 us
    ppermute x6 -> x4, waiting for transfers between devices: 0.24 us -> 7.75 us  [plane_swap(): lax.ppermute(message, 'face', [(i, i ^ 2 << orders[i % 2][step]) for i in...]
    ppermute x6 -> x3, starting transfers between devices: 12.1 us -> 6.86 us  [band_sum(): lax.ppermute(messages[k - 1], 'band', xor_pairs(bands, k))]
    ppermute x6 -> x4, starting transfers between devices: 8.42 us -> 4.59 us  [plane_swap(): lax.ppermute(message, 'face', [(i, i ^ 2 << orders[i % 2][step]) for i in...]
    pallas_call x12, Pallas kernels: 16.4 us -> 14.8 us  [kernel_call(): pl.pallas_call(body, out_shape=tuple(outs), in_specs=[hbm if i in far els...]
    ppermute x6 -> x3, waiting for transfers between devices: 2.54 us -> 3.86 us  [band_sum(): lax.ppermute(messages[k - 1], 'band', xor_pairs(bands, k))]
    ppermute x2, waiting for transfers between devices: 0.79 us -> 1.47 us  [core_sum(): got = lax.ppermute(send, 'face', xor_pairs(lax.axis_size('face'), 1))]
  transfers between devices with their start and end apart: 18 -> 13, of which waited for: 6 -> 8; matrix products, arithmetic and copies ran while one was open for 0% -> 0% of each run, Pallas kernels for 15% -> 11%
where the time goes in v5:
time: 50.8 us; the launch traced here: 50.6 us
  starting transfers between devices  18.3 us (36%)
  waiting for transfers between devices  16.7 us (33%)
  Pallas kernels  14.8 us (29%)
  between operations  0.75 us (1%)
    pallas_call x12, Pallas kernels, kernel_call(): pl.pallas_call(body, out_shape=tuple(outs), in_specs=[hbm if i in far els...  14.8 us
    ppermute x4, waiting for transfers between devices, plane_swap(): lax.ppermute(message, 'face', [(i, i ^ 2 << orders[i % 2][step]) for i in...  7.75 us
    ppermute x3, starting transfers between devices, band_sum(): lax.ppermute(messages[k - 1], 'band', xor_pairs(bands, k))  6.86 us
    ppermute x4, starting transfers between devices, swap(): return (lax.ppermute(first, axis, one), lax.ppermute(second, axis, two))  6.53 us
    ppermute x4, starting transfers between devices, plane_swap(): lax.ppermute(message, 'face', [(i, i ^ 2 << orders[i % 2][step]) for i in...  4.59 us
    ppermute x3, waiting for transfers between devices, band_sum(): lax.ppermute(messages[k - 1], 'band', xor_pairs(bands, k))  3.86 us
    ppermute x4, waiting for transfers between devices, swap(): return (lax.ppermute(first, axis, one), lax.ppermute(second, axis, two))  3.64 us
    ppermute x2, waiting for transfers between devices, core_sum(): got = lax.ppermute(send, 'face', xor_pairs(lax.axis_size('face'), 1))  1.47 us
  transfers between devices with their start and end apart: 13, of which 8 were waited for; matrix products, arithmetic and copies ran while one was open for 0% of the time, Pallas kernels for 11%

profile of v5, /device:TPU:0, one launch (start us, length us, event | category | flops | bytes accessed | tf_op | source)
XLA Modules:
  0.0 50.6 jit_solution(14398349777243885330)
XLA Ops:
  0.7 1.8 %shard_map.84 = (bf16[96,256]{1,0:T(8,128)(2,1)S(1)}, bf16[96,256]{1,0:T(8,128)(2,1)S(1)}, bf16[24,32,256]{2,1,0:T(8,128)(2,1)S(1)}, bf16[24,32,256]{2,1,0:T(8,128)(2,1)S(1)}, bf16[12,16,256]{2,1,0:T(8,128)(2,1)S(1)}) custom-call(s32[4]{0:T(128)S(1)} %pad_add_fusion.place, bf16[12,16,256]{2,1,0:T(8,128)(2,1)} %coarse.1, bf16[24,32,256]{2,1,0:T(8,128)(2,1)} %skip.1, ...), custom_call_target="tpu_custom_call" | custom-call | bytes 1867792 | tf_op jit(solution)/shard_map/pallas_call | solution.py:29
  3.1 3.6 %collective-permute-start.1 = (bf16[96,256]{1,0:T(8,128)(2,1)S(1)}, bf16[96,256]{1,0:T(8,128)(2,1)S(1)}, u32[]{:S(2)}, u32[]{:S(2)}) collective-permute-start(bf16[96,256]{1,0:T(8,128)(2,1)S(1)} %get-tuple-element.48), channel_id=1, source_target_pairs={{0,28},{4,8},{8,4},{12,16},{16,12},{20,24},{24,20},{28,0},{1,29},{... | collective-permute-start | bytes 147464 | tf_op jit(solution)/shard_map/ppermute | solution.py:501
  6.6 1.8 %collective-permute-done.1.got_second = bf16[96,256]{1,0:T(8,128)(2,1)S(1)} collective-permute-done((bf16[96,256]{1,0:T(8,128)(2,1)S(1)}, bf16[96,256]{1,0:T(8,128)(2,1)S(1)}, u32[]{:S(2)}, u32[]{:S(2)}) %collective-permute-start.1) | collective-permute-done | bytes 49184 | tf_op jit(solution)/shard_map/ppermute | solution.py:501
  9.0 1.8 %collective-permute-start.2 = (bf16[128,256]{1,0:T(8,128)(2,1)S(1)}, bf16[128,256]{1,0:T(8,128)(2,1)S(1)}, u32[]{:S(2)}, u32[]{:S(2)}) collective-permute-start(bf16[128,256]{1,0:T(8,128)(2,1)S(1)} %get-tuple-element.51), channel_id=1, source_target_pairs={{0,1},{1,0},{2,3},{3,2},{4,5},{5,4},{6,7},{7,6},{8,9},{9,8},{10,11... | collective-permute-start | bytes 196616 | tf_op jit(solution)/shard_map/ppermute | solution.py:501
  10.8 0.7 %collective-permute-start.3 = (bf16[128,256]{1,0:T(8,128)(2,1)S(1)}, bf16[128,256]{1,0:T(8,128)(2,1)S(1)}, u32[]{:S(2)}, u32[]{:S(2)}) collective-permute-start(bf16[128,256]{1,0:T(8,128)(2,1)S(1)} %get-tuple-element.52), channel_id=1, source_target_pairs={{1,2},{2,1},{5,6},{6,5},{9,10},{10,9},{13,14},{14,13},{17,18},{18,... | collective-permute-start | bytes 196616 | tf_op jit(solution)/shard_map/ppermute | solution.py:501
  11.4 1.9 %collective-permute-done.2.got_first = bf16[128,256]{1,0:T(8,128)(2,1)S(1)} collective-permute-done((bf16[128,256]{1,0:T(8,128)(2,1)S(1)}, bf16[128,256]{1,0:T(8,128)(2,1)S(1)}, u32[]{:S(2)}, u32[]{:S(2)}) %collective-permute-start.2) | collective-permute-done | bytes 65568 | tf_op jit(solution)/shard_map/ppermute | solution.py:501
  13.3 3.4 %shard_map.86 = (bf16[3,26,32,256]{3,2,1,0:T(8,128)(2,1)S(1)}, bf16[2,17,16,256]{3,2,1,0:T(8,128)(2,1)S(1)}, bf16[24,32,256]{2,1,0:T(8,128)(2,1)S(1)}, f32[768,2...) custom-call(s32[4]{0:T(128)S(1)} %pad_add_fusion.place, ...), custom_call_target="tpu_custom_call" | custom-call | flops 1132462080 | bytes 9519120 | tf_op jit(solution)/shard_map/pallas_call | solution.py:29
  16.8 1.2 %shard_map.88.phases = bf16[2,2,16,16,256]{4,3,2,1,0:T(8,128)(2,1)S(1)} custom-call(bf16[3,26,32,256]{3,2,1,0:T(8,128)(2,1)S(1)} %get-tuple-element.60.shifted, f32[768,256]{1,0:T(8,128)S(1)} %get-tuple-element.61.slope, bf16[3,3,256,256]{3,2,1,0:T(8,128)(2,1)S(1)} %get-tuple-element.62.conv_w), custom_call_target="tpu_custom_call" | custom-call | bytes 3768320 | tf_op jit(solution)/shard_map/pallas_call | solution.py:29
  18.0 0.8 %collective-permute-done.4.got = bf16[4,288,256]{2,1,0:T(8,128)(2,1)S(1)} collective-permute-done((bf16[4,288,256]{2,1,0:T(8,128)(2,1)S(1)}, bf16[4,288,256]{2,1,0:T(8,128)(2,1)S(1)}, u32[]{:S(2)}, u32[]{:S(2)}) %collective-permute-start.4) | collective-permute-done | bytes 589856 | tf_op jit(solution)/shard_map/ppermute | solution.py:465
  19.4 1.2 %shard_map.89 = (f32[4,288,256]{2,1,0:T(8,128)S(1)}, bf16[4,288,256]{2,1,0:T(8,128)(2,1)S(1)}) custom-call(s32[4]{0:T(128)S(1)} %pad_add_fusion.place, bf16[2,17,16,256]{3,2,1,0:T(8,128)(2,1)S(1)} %get-tuple-element.59.near, bf16[2,2,16,16,256]{4,3,2,1,0:T(8,128)(2,1)S(1)} %shard_map.88.phases), custom_call_target="tpu_custom_call" | custom-call | bytes 2572304 | tf_op jit(solution)/shard_map/pallas_call | solution.py:29
  20.8 1.2 %collective-permute-start.6 = (bf16[2,288,256]{2,1,0:T(8,128)(2,1)S(1)}, bf16[2,288,256]{2,1,0:T(8,128)(2,1)S(1)}, u32[]{:S(2)}, u32[]{:S(2)}) collective-permute-start(bf16[2,288,256]{2,1,0:T(8,128)(2,1)S(1)} %get-tuple-element.58), channel_id=1, source_target_pairs={{0,8},{4,20},{8,0},{12,28},{16,24},{20,4},{24,16},{28,12},{1,9},{5... | collective-permute-start | bytes 884744 | tf_op jit(solution)/shard_map/ppermute | solution.py:473
  22.0 0.7 %collective-permute-done.5.got = bf16[4,288,256]{2,1,0:T(8,128)(2,1)S(1)} collective-permute-done((bf16[4,288,256]{2,1,0:T(8,128)(2,1)S(1)}, bf16[4,288,256]{2,1,0:T(8,128)(2,1)S(1)}, u32[]{:S(2)}, u32[]{:S(2)}) %collective-permute-start.5) | collective-permute-done | bytes 589856 | tf_op jit(solution)/shard_map/ppermute | solution.py:465
  22.7 0.6 %shard_map.90 = (f32[2,288,256]{2,1,0:T(8,128)S(1)}, bf16[2,288,256]{2,1,0:T(8,128)(2,1)S(1)}) custom-call(s32[4]{0:T(128)S(1)} %pad_add_fusion.place, f32[4,288,256]{2,1,0:T(8,128)S(1)} %get-tuple-element.63.keep, bf16[4,288,256]{2,1,0:T(8,128)(2,1)S(1)} %collective-permute-done.5.got), custom_call_target="tpu_custom_call" | custom-call | bytes 2654224 | tf_op jit(solution)/shard_map/pallas_call | solution.py:29
  23.3 1.3 %collective-permute-start.8 = (bf16[2,288,256]{2,1,0:T(8,128)(2,1)S(1)}, bf16[2,288,256]{2,1,0:T(8,128)(2,1)S(1)}, u32[]{:S(2)}, u32[]{:S(2)}) collective-permute-start(bf16[2,288,256]{2,1,0:T(8,128)(2,1)S(1)} %get-tuple-element.65), channel_id=1, source_target_pairs={{0,8},{4,20},{8,0},{12,28},{16,24},{20,4},{24,16},{28,12},{1,9},{5... | collective-permute-start | bytes 884744 | tf_op jit(solution)/shard_map/ppermute | solution.py:473
  24.6 3.0 %collective-permute-done.6.got = bf16[2,288,256]{2,1,0:T(8,128)(2,1)S(1)} collective-permute-done((bf16[2,288,256]{2,1,0:T(8,128)(2,1)S(1)}, bf16[2,288,256]{2,1,0:T(8,128)(2,1)S(1)}, u32[]{:S(2)}, u32[]{:S(2)}) %collective-permute-start.6) | collective-permute-done | bytes 294944 | tf_op jit(solution)/shard_map/ppermute | solution.py:473
  27.6 1.7 %collective-permute-start.7 = (bf16[1,288,256]{2,1,0:T(8,128)(2,1)S(1)}, bf16[1,288,256]{2,1,0:T(8,128)(2,1)S(1)}, u32[]{:S(2)}, u32[]{:S(2)}) collective-permute-start(bf16[1,288,256]{2,1,0:T(8,128)(2,1)S(1)} %get-tuple-element.67), channel_id=1, source_target_pairs={{0,16},{4,12},{8,24},{12,4},{16,0},{20,28},{24,8},{28,20},{1,17},{... | collective-permute-start | bytes 442376 | tf_op jit(solution)/shard_map/ppermute | solution.py:473
  29.4 3.6 %shard_map.92 = (bf16[24,32,256]{2,1,0:T(8,128)(2,1)}, bf16[12,16,256]{2,1,0:T(8,128)(2,1)}) custom-call(s32[4]{0:T(128)S(1)} %pad_add_fusion.place, bf16[12,16,256]{2,1,0:T(8,128)(2,1)S(1)} %get-tuple-element.44.coarse, bf16[24,32,256]{2,1,0:T(8,128)(2,1)S(1)} %get-tuple-element.45.cot, bf16[24,32,256]{2,1,0:T(8,128)(2,1)S(1)} %get-tuple-element.68.act, ...), custom_call_target="tpu_custom_call" | custom-call | bytes 4718608 | tf_op jit(solution)/shard_map/pallas_call | solution.py:29
  33.5 4.8 %collective-permute-done.9.got_up = bf16[1,288,256]{2,1,0:T(8,128)(2,1)S(1)} collective-permute-done((bf16[1,288,256]{2,1,0:T(8,128)(2,1)S(1)}, bf16[1,288,256]{2,1,0:T(8,128)(2,1)S(1)}, u32[]{:S(2)}, u32[]{:S(2)}) %collective-permute-start.9) | collective-permute-done | bytes 147488 | tf_op jit(solution)/shard_map/ppermute | solution.py:473
  38.3 0.8 %shard_map.94 = (f32[288,128]{1,0:T(8,128)S(1)}, bf16[288,128]{1,0:T(8,128)(2,1)S(1)}, bf16[288,128]{1,0:T(8,128)(2,1)S(1)}, bf16[288,128]{1,0:T(8,128)(2,1)S(1)}) custom-call(s32[4]{0:T(128)S(1)} %pad_add_fusion.place, f32[1,288,256]{2,1,0:T(8,128)S(1)} %get-tuple-element.73.conv, bf16[1,288,256]{2,1,0:T(8,128)(2,1)S(1)} %collective-permute-done.7.got_conv, ...), custom_call_target="tpu_custom_call" | custom-call | bytes 1253392 | tf_op jit(solution)/shard_map/pallas_call | solution.py:29
  39.1 3.9 %collective-permute-start.10 = (bf16[288,128]{1,0:T(8,128)(2,1)S(1)}, bf16[288,128]{1,0:T(8,128)(2,1)S(1)}, u32[]{:S(2)}, u32[]{:S(2)}) collective-permute-start(bf16[288,128]{1,0:T(8,128)(2,1)S(1)} %get-tuple-element.79), channel_id=1, source_target_pairs={{0,3},{1,2},{2,1},{3,0},{4,7},{5,6},{6,5},{7,4},{8,11},{9,10},{10,... | collective-permute-start | bytes 221192 | tf_op jit(solution)/shard_map/ppermute | solution.py:491
  42.9 2.5 %collective-permute-start.11 = (bf16[288,128]{1,0:T(8,128)(2,1)S(1)}, bf16[288,128]{1,0:T(8,128)(2,1)S(1)}, u32[]{:S(2)}, u32[]{:S(2)}) collective-permute-start(bf16[288,128]{1,0:T(8,128)(2,1)S(1)} %get-tuple-element.80), channel_id=1, source_target_pairs={{0,2},{1,3},{2,0},{3,1},{4,6},{5,7},{6,4},{7,5},{8,10},{9,11},{10,... | collective-permute-start | bytes 221192 | tf_op jit(solution)/shard_map/ppermute | solution.py:491
  46.0 2.6 %collective-permute-done.11.refs_1_ = bf16[288,128]{1,0:T(8,128)(2,1)S(1)} collective-permute-done((bf16[288,128]{1,0:T(8,128)(2,1)S(1)}, bf16[288,128]{1,0:T(8,128)(2,1)S(1)}, u32[]{:S(2)}, u32[]{:S(2)}) %collective-permute-start.11) | collective-permute-done | bytes 73760 | tf_op jit(solution)/shard_map/ppermute | solution.py:491
  48.6 1.2 %collective-permute-done.12.refs_2_ = bf16[288,128]{1,0:T(8,128)(2,1)S(1)} collective-permute-done((bf16[288,128]{1,0:T(8,128)(2,1)S(1)}, bf16[288,128]{1,0:T(8,128)(2,1)S(1)}, u32[]{:S(2)}, u32[]{:S(2)}) %collective-permute-start.12) | collective-permute-done | bytes 73760 | tf_op jit(solution)/shard_map/ppermute | solution.py:491
  49.8 0.8 %shard_map.95 = (f32[64,288]{1,0:T(8,128)}, f32[64,288]{1,0:T(8,128)}) custom-call(f32[288,128]{1,0:T(8,128)S(1)} %get-tuple-element.78.own, bf16[288,128]{1,0:T(8,128)(2,1)S(1)} %collective-permute-done.10.refs_0_, bf16[288,128]{1,0:T(8,128)(2,1)S(1)} %collective-permute-done.11.refs_1_, bf16[288,128]{1,0:T(8,128)(2,1)S(1)} %collective-permute-done.12.refs_2_), custom_call_target="tpu_custom_call" | custom-call | bytes 516096 | tf_op jit(solution)/shard_map/pallas_call | solution.py:29
  (17 shorter events, 3.2 us)
Async XLA Ops:
  0.6 12.7 %copy-start = (bf16[3,3,256,256]{3,2,1,0:T(8,128)(2,1)S(1)}, bf16[3,3,256,256]{3,2,1,0:T(8,128)(2,1)}, u32[]{:S(2)}) copy-start(bf16[3,3,256,256]{3,2,1,0:T(8,128)(2,1)} %up_w.3) | copy-start | bytes 3538948
  2.5 4.1 %collective-permute-start = (bf16[96,256]{1,0:T(8,128)(2,1)S(1)}, bf16[96,256]{1,0:T(8,128)(2,1)S(1)}, u32[]{:S(2)}, u32[]{:S(2)}) collective-permute-start(bf16[96,256]{1,0:T(8,128)(2,1)S(1)} %get-tuple-element.47), channel_id=1, source_target_pairs={{0,4},{4,0},{8,12},{12,8},{16,20},{20,16},{24,28},{28,24},{1,5},{5... | collective-permute-start | bytes 147464 | tf_op jit(solution)/shard_map/ppermute | solution.py:501
  3.1 5.3 %collective-permute-start.1 = (bf16[96,256]{1,0:T(8,128)(2,1)S(1)}, bf16[96,256]{1,0:T(8,128)(2,1)S(1)}, u32[]{:S(2)}, u32[]{:S(2)}) collective-permute-start(bf16[96,256]{1,0:T(8,128)(2,1)S(1)} %get-tuple-element.48), channel_id=1, source_target_pairs={{0,28},{4,8},{8,4},{12,16},{16,12},{20,24},{24,20},{28,0},{1,29},{... | collective-permute-start | bytes 147464 | tf_op jit(solution)/shard_map/ppermute | solution.py:501
  9.0 4.3 %collective-permute-start.2 = (bf16[128,256]{1,0:T(8,128)(2,1)S(1)}, bf16[128,256]{1,0:T(8,128)(2,1)S(1)}, u32[]{:S(2)}, u32[]{:S(2)}) collective-permute-start(bf16[128,256]{1,0:T(8,128)(2,1)S(1)} %get-tuple-element.51), channel_id=1, source_target_pairs={{0,1},{1,0},{2,3},{3,2},{4,5},{5,4},{6,7},{7,6},{8,9},{9,8},{10,11... | collective-permute-start | bytes 196616 | tf_op jit(solution)/shard_map/ppermute | solution.py:501
  10.8 2.5 %collective-permute-start.3 = (bf16[128,256]{1,0:T(8,128)(2,1)S(1)}, bf16[128,256]{1,0:T(8,128)(2,1)S(1)}, u32[]{:S(2)}, u32[]{:S(2)}) collective-permute-start(bf16[128,256]{1,0:T(8,128)(2,1)S(1)} %get-tuple-element.52), channel_id=1, source_target_pairs={{1,2},{2,1},{5,6},{6,5},{9,10},{10,9},{13,14},{14,13},{17,18},{18,... | collective-permute-start | bytes 196616 | tf_op jit(solution)/shard_map/ppermute | solution.py:501
  16.7 2.1 %collective-permute-start.4 = (bf16[4,288,256]{2,1,0:T(8,128)(2,1)S(1)}, bf16[4,288,256]{2,1,0:T(8,128)(2,1)S(1)}, u32[]{:S(2)}, u32[]{:S(2)}) collective-permute-start(bf16[4,288,256]{2,1,0:T(8,128)(2,1)S(1)} %get-tuple-element.55), channel_id=1, source_target_pairs={{0,4},{4,0},{8,12},{12,8},{16,20},{20,16},{24,28},{28,24},{1,5},{5... | collective-permute-start | bytes 1769480 | tf_op jit(solution)/shard_map/ppermute | solution.py:465
  20.6 2.1 %collective-permute-start.5 = (bf16[4,288,256]{2,1,0:T(8,128)(2,1)S(1)}, bf16[4,288,256]{2,1,0:T(8,128)(2,1)S(1)}, u32[]{:S(2)}, u32[]{:S(2)}) collective-permute-start(bf16[4,288,256]{2,1,0:T(8,128)(2,1)S(1)} %get-tuple-element.64), channel_id=1, source_target_pairs={{0,4},{4,0},{8,12},{12,8},{16,20},{20,16},{24,28},{28,24},{1,5},{5... | collective-permute-start | bytes 1769480 | tf_op jit(solution)/shard_map/ppermute | solution.py:465
  20.8 6.7 %collective-permute-start.6 = (bf16[2,288,256]{2,1,0:T(8,128)(2,1)S(1)}, bf16[2,288,256]{2,1,0:T(8,128)(2,1)S(1)}, u32[]{:S(2)}, u32[]{:S(2)}) collective-permute-start(bf16[2,288,256]{2,1,0:T(8,128)(2,1)S(1)} %get-tuple-element.58), channel_id=1, source_target_pairs={{0,8},{4,20},{8,0},{12,28},{16,24},{20,4},{24,16},{28,12},{1,9},{5... | collective-permute-start | bytes 884744 | tf_op jit(solution)/shard_map/ppermute | solution.py:473
  23.3 9.7 %collective-permute-start.8 = (bf16[2,288,256]{2,1,0:T(8,128)(2,1)S(1)}, bf16[2,288,256]{2,1,0:T(8,128)(2,1)S(1)}, u32[]{:S(2)}, u32[]{:S(2)}) collective-permute-start(bf16[2,288,256]{2,1,0:T(8,128)(2,1)S(1)} %get-tuple-element.65), channel_id=1, source_target_pairs={{0,8},{4,20},{8,0},{12,28},{16,24},{20,4},{24,16},{28,12},{1,9},{5... | collective-permute-start | bytes 884744 | tf_op jit(solution)/shard_map/ppermute | solution.py:473
  27.6 5.9 %collective-permute-start.7 = (bf16[1,288,256]{2,1,0:T(8,128)(2,1)S(1)}, bf16[1,288,256]{2,1,0:T(8,128)(2,1)S(1)}, u32[]{:S(2)}, u32[]{:S(2)}) collective-permute-start(bf16[1,288,256]{2,1,0:T(8,128)(2,1)S(1)} %get-tuple-element.67), channel_id=1, source_target_pairs={{0,16},{4,12},{8,24},{12,4},{16,0},{20,28},{24,8},{28,20},{1,17},{... | collective-permute-start | bytes 442376 | tf_op jit(solution)/shard_map/ppermute | solution.py:473
  33.1 5.2 %collective-permute-start.9 = (bf16[1,288,256]{2,1,0:T(8,128)(2,1)S(1)}, bf16[1,288,256]{2,1,0:T(8,128)(2,1)S(1)}, u32[]{:S(2)}, u32[]{:S(2)}) collective-permute-start(bf16[1,288,256]{2,1,0:T(8,128)(2,1)S(1)} %get-tuple-element.77), channel_id=1, source_target_pairs={{0,16},{4,12},{8,24},{12,4},{16,0},{20,28},{24,8},{28,20},{1,17},{... | collective-permute-start | bytes 442376 | tf_op jit(solution)/shard_map/ppermute | solution.py:473
  39.1 6.9 %collective-permute-start.10 = (bf16[288,128]{1,0:T(8,128)(2,1)S(1)}, bf16[288,128]{1,0:T(8,128)(2,1)S(1)}, u32[]{:S(2)}, u32[]{:S(2)}) collective-permute-start(bf16[288,128]{1,0:T(8,128)(2,1)S(1)} %get-tuple-element.79), channel_id=1, source_target_pairs={{0,3},{1,2},{2,1},{3,0},{4,7},{5,6},{6,5},{7,4},{8,11},{9,10},{10,... | collective-permute-start | bytes 221192 | tf_op jit(solution)/shard_map/ppermute | solution.py:491
  42.9 5.6 %collective-permute-start.11 = (bf16[288,128]{1,0:T(8,128)(2,1)S(1)}, bf16[288,128]{1,0:T(8,128)(2,1)S(1)}, u32[]{:S(2)}, u32[]{:S(2)}) collective-permute-start(bf16[288,128]{1,0:T(8,128)(2,1)S(1)} %get-tuple-element.80), channel_id=1, source_target_pairs={{0,2},{1,3},{2,0},{3,1},{4,6},{5,7},{6,4},{7,5},{8,10},{9,11},{10,... | collective-permute-start | bytes 221192 | tf_op jit(solution)/shard_map/ppermute | solution.py:491
  45.5 4.4 %collective-permute-start.12 = (bf16[288,128]{1,0:T(8,128)(2,1)S(1)}, bf16[288,128]{1,0:T(8,128)(2,1)S(1)}, u32[]{:S(2)}, u32[]{:S(2)}) collective-permute-start(bf16[288,128]{1,0:T(8,128)(2,1)S(1)} %get-tuple-element.81), channel_id=1, source_target_pairs={{0,1},{1,0},{2,3},{3,2},{4,5},{5,4},{6,7},{7,6},{8,9},{9,8},{10,11... | collective-permute-start | bytes 221192 | tf_op jit(solution)/shard_map/ppermute | solution.py:491

commit v6 on v5

--- a/solution.py
+++ b/solution.py
@@ -81,12 +81,10 @@
     ref[start : start + value.shape[0], :] = value
 
 
-def split_by_core(place, partial, keep, send):
-    groups, block, _ = keep.shape
+def other_core(place, partial, send):
+    groups, block, _ = send.shape
     for group in range(groups):
-        mine = pl.multiple_of((2 * group + place[0]) * block, 16)
         theirs = pl.multiple_of((2 * group + 1 - place[0]) * block, 16)
-        keep[group] = partial[pl.ds(mine, block), :]
         send[group] = partial[pl.ds(theirs, block), :].astype(bf16)
 
 
@@ -119,19 +117,17 @@
         copy.start()
     before[...] = jnp.zeros_like(before)
     after[...] = jnp.zeros_like(after)
-    copies[0].wait()
-    put(flat, 0, cot_v[...].reshape(rows * cols, -1).astype(f32))
-    fill(before, at.cot, get(flat, 0, rows, cols))
-    fill(after, at.cot, get(flat, cols - 1, rows, cols))
-    fill(after, at.cot_2, get(flat, cols - 2, rows, cols))
-    copies[1].wait()
-    put(flat, 0, skip_v[...].reshape(rows * cols, -1).astype(f32))
-    fill(before, at.skip, get(flat, 0, rows, cols))
-    fill(after, at.skip, get(flat, cols - 1, rows, cols))
-    copies[2].wait()
-    put(flat, 0, coarse_v[...].reshape(n_rows * n_cols, -1).astype(f32))
-    fill(before, at.coarse, get(flat, 0, n_rows, n_cols))
-    fill(after, at.coarse, get(flat, n_cols - 1, n_rows, n_cols))
+    for copy, array, start, start_2 in (
+        (copies[0], cot_v, at.cot, at.cot_2), (copies[1], skip_v, at.skip, None), (copies[2], coarse_v, at.coarse, None),
+    ):
+        copy.wait()
+        n, width, channels = array.shape
+        put(flat, 0, array[:, :16, :].astype(f32)[:, :8, :].reshape(n * 8, channels))
+        put(flat, n * 8, array[:, width - 16 :, :].astype(f32)[:, 8:, :].reshape(n * 8, channels))
+        fill(before, start, get(flat, 0, n, 8))
+        fill(after, start, get(flat, n * 8 + 7, n, 8))
+        if start_2 is not None:
+            fill(after, start_2, get(flat, n * 8 + 6, n, 8))
     even = place[0] == 0
     first[...] = jnp.where(even, after[...], before[...]).astype(bf16)
     second[...] = jnp.where(even, before[...], after[...]).astype(bf16)
@@ -173,7 +169,7 @@
 
 def act_kernel(
     place, coarse, skip, cot, left, right, got_first, got_second, up_w, conv_w,
-    shifted, near, act, slope, keep, send, upper, lower, conv_v, padded, pre, partial, sem,
+    shifted, near, act, slope, partial, send, upper, lower, conv_v, padded, pre, sem,
 ):
     n_rows, n_cols, channels = coarse.shape
     rows, cols, _ = skip.shape
@@ -240,7 +236,7 @@
         for l in range(3):
             source = shifted[2 - l, pl.ds(2 - k, rows)].reshape(-1, channels)
             partial[pl.ds((3 * k + l) * channels, channels), :] = dot(act_t, source)
-    split_by_core(place, partial, keep, send)
+    other_core(place, partial, send)
     copy.wait()
 
 
@@ -264,7 +260,7 @@
                 phases[row_phase, col_phase, row] = jnp.zeros((n_cols, channels), bf16)
 
 
-def up_kernel(place, near, phases, keep, send, partial):
+def up_kernel(place, near, phases, partial, send):
     _, _, whole, n_cols, channels = phases.shape
     turned = {}
     for row_off in range(2):
@@ -279,14 +275,13 @@
             partial[pl.ds((3 * k + l) * channels, channels), :] = dot(
                 turned[row_off, col_off], source
             )
-    split_by_core(place, partial, keep, send)
-
-
-def out_kernel(
-    place, coarse, cot, act, phases, left, right, upper, lower, conv_w, up_w,
-    decoded, coarse_out, padded, shifted, moved, ring, wide,
+    other_core(place, partial, send)
+
+
+def ring_kernel(
+    place, coarse, cot, left, right, upper, lower, conv_w, up_w, ring_act, ring_grad, ring, wide,
 ):
-    rows, cols, channels = act.shape
+    rows, cols, channels = cot.shape
     n_rows, n_cols = rows // 2, cols // 2
     at = Layout(n_rows, n_cols)
     stride, step = cols + 2 * MARGIN, n_cols + 2 * MARGIN
@@ -329,23 +324,10 @@
     value = preact * sigma
     slope = sigma + value * (1.0 - sigma)
     value = value.astype(bf16).astype(f32)
-    for row in range(rows):
-        put(padded, (row + 1) * stride + MARGIN, act[row].astype(f32))
-    for row, base, exists in ((0, at.top, has_upper), (rows + 1, at.bottom, has_lower)):
+    ring_act[...] = value
+    for base, exists in ((at.top, has_upper), (at.bottom, has_lower)):
         strip = value[base : base + cols + 2]
-        put(padded, row * stride + MARGIN - 1, jnp.where(exists, strip, 0.0))
-    put(padded, stride + MARGIN - 1, value[at.left : at.left + rows], stride)
-    put(padded, stride + MARGIN + cols, value[at.right : at.right + rows], stride)
-    for row in range(rows + 2):
-        for shift in range(3):
-            start = row * stride + MARGIN - 1 + shift
-            shifted[shift, row] = get(padded, start, cols).astype(bf16)
-    total = jnp.zeros((rows * cols, channels), f32)
-    for k in range(3):
-        for l in range(3):
-            source = shifted[l, pl.ds(k, rows)].reshape(-1, channels)
-            total = total + dot(source, conv_w[k, l])
-    decoded[...] = total.astype(bf16).reshape(decoded.shape)
+        ring_act[base : base + cols + 2, :] = jnp.where(exists, strip, 0.0)
 
     def fine(p, q):
         return (p + 2) * stride + MARGIN + q
@@ -369,18 +351,45 @@
             source = get(ring, 0, at.grad_size).astype(bf16)
             total = total + dot_nt(source, conv_w[k, l])
     strip = (total[: cols + 1] * slope[at.top : at.top + cols + 1]).astype(bf16).astype(f32)
-    put(ring, at.top, jnp.where(has_upper, strip, 0.0))
+    put(ring_grad, at.top, jnp.where(has_upper, strip, 0.0))
     strip = total[at.grad_left : at.grad_left + rows] * slope[at.left : at.left + rows]
-    put(ring, at.grad_left, strip.astype(bf16).astype(f32))
+    put(ring_grad, at.grad_left, strip.astype(bf16).astype(f32))
+
+
+def decoded_kernel(act, ring_act, conv_w, decoded, padded, shifted):
+    rows, cols, channels = act.shape
+    at = Layout(rows // 2, cols // 2)
+    stride = cols + 2 * MARGIN
+    for row in range(rows):
+        put(padded, (row + 1) * stride + MARGIN, act[row].astype(f32))
+    for row, base in ((0, at.top), (rows + 1, at.bottom)):
+        put(padded, row * stride + MARGIN - 1, ring_act[base : base + cols + 2, :])
+    put(padded, stride + MARGIN - 1, ring_act[at.left : at.left + rows, :], stride)
+    put(padded, stride + MARGIN + cols, ring_act[at.right : at.right + rows, :], stride)
+    for row in range(rows + 2):
+        for shift in range(3):
+            start = row * stride + MARGIN - 1 + shift
+            shifted[shift, row] = get(padded, start, cols).astype(bf16)
+    total = jnp.zeros((rows * cols, channels), f32)
+    for k in range(3):
+        for l in range(3):
+            source = shifted[l, pl.ds(k, rows)].reshape(-1, channels)
+            total = total + dot(source, conv_w[k, l])
+    decoded[...] = total.astype(bf16).reshape(decoded.shape)
+
+def coarse_kernel(phases, ring_grad, up_w, coarse_out, padded, moved):
+    n_rows, n_cols, channels = coarse_out.shape
+    at = Layout(n_rows, n_cols)
+    stride = n_cols + 2 * MARGIN
     for phase, start in ((0, 1), (1, 2), (2, 0)):
-        moved[phase, 0] = get(ring, at.top + start, n_cols, 2).astype(bf16)
+        moved[phase, 0] = get(ring_grad, at.top + start, n_cols, 2).astype(bf16)
     for phase in range(2):
         for row in range(n_rows):
             moved[phase, 1 + row] = phases[1, phase, row]
     for row_phase in range(2):
         for row in range(n_rows):
             put(padded, row * stride + MARGIN, phases[row_phase, 1, row].astype(f32))
-        put(padded, MARGIN - 1, get(ring, at.grad_left + row_phase, n_rows, 2), stride)
+        put(padded, MARGIN - 1, get(ring_grad, at.grad_left + row_phase, n_rows, 2), stride)
         for row in range(n_rows):
             cells = get(padded, row * stride + MARGIN - 1, n_cols).astype(bf16)
             if row_phase:
@@ -411,12 +420,13 @@
     return sum(1 << bit for step, bit in enumerate(order) if slot >> (last - step) & 1)
 
 
-def core_kernel(place, keep, got, own, message):
-    slots, half = keep.shape[0], own.shape[0]
+def core_kernel(place, partial, got, own, message):
+    slots, half, block = got.shape[0], own.shape[0], got.shape[1]
     even, odd = halving(2 * slots)
     for slot in range(slots):
         chip = place[1] ^ jnp.where(place[0] == 0, mask_of(slot, even), mask_of(slot, odd))
-        total = keep[chip] + got[chip].astype(f32)
+        mine = pl.multiple_of((2 * chip + place[0]) * block, 16)
+        total = partial[pl.ds(mine, block), :] + got[chip].astype(f32)
         if slot < half:
             own[slot] = total
         else:
@@ -460,11 +470,11 @@
     return [(i, i ^ bits) for i in range(count)]
 
 
-def core_sum(place, keep, send):
-    groups, block, channels = keep.shape
+def core_sum(place, partial, send):
+    groups, block, channels = send.shape
     got = lax.ppermute(send, "face", xor_pairs(lax.axis_size("face"), 1))
     shape = (groups // 2, block, channels)
-    return kernel_call(core_kernel, [sds(shape, f32), sds(shape, bf16)], [], 0, place, keep, got)
+    return kernel_call(core_kernel, [sds(shape, f32), sds(shape, bf16)], [], 0, place, partial, got)
 
 
 def plane_swap(message, step):
@@ -535,21 +545,20 @@
     shift_shape = (3, rows + 2, cols, channels)
     whole = -(-cells // 256) * 256 // n_cols
     one_tap = 2 * cells * channels * channels
-    partials = [sds((groups, block, channels), f32), sds((groups, block, channels), bf16)]
-    partial = pltpu.VMEM((9 * channels, channels), f32)
+    partials = [sds((9 * channels, channels), f32), sds((groups, block, channels), bf16)]
     side = sds(message.shape, f32)
-    shifted, near, act, slope, keep_conv, send_conv, upper, lower, conv_weight = kernel_call(
+    shifted, near, act, slope, part_conv, send_conv, upper, lower, conv_weight = kernel_call(
         act_kernel,
         [
             sds(shift_shape, bf16), sds((2, whole + 1, n_cols, channels), bf16),
             sds(skip.shape, bf16), sds((rows * cols, channels), f32), *partials, side, side,
             sds(conv_weight.shape, bf16),
         ],
-        [padded, flat, partial, pltpu.SemaphoreType.DMA],
+        [padded, flat, pltpu.SemaphoreType.DMA],
         45 * one_tap, place, coarse, skip, cotangent, left, right, first, second,
         up_weight, conv_weight, far=(9,),
     )
-    own_conv, to_conv = core_sum(place, keep_conv, send_conv)
+    own_conv, to_conv = core_sum(place, part_conv, send_conv)
     got_conv = plane_swap(to_conv, 0)
     phases = kernel_call(
         grad_kernel,
@@ -557,30 +566,43 @@
         [flat],
         0, shifted, slope, conv_weight,
     )[0]
-    keep_up, send_up = kernel_call(
-        up_kernel, partials, [partial], 0, place, after(near, to_conv), phases
+    part_up, send_up = kernel_call(
+        up_kernel, partials, [], 0, place, after(near, to_conv), phases
     )
-    own_up, to_up = core_sum(place, keep_up, send_up)
+    own_up, to_up = core_sum(place, part_up, send_up)
     got_up = plane_swap(to_up, 0)
+    ring_act, ring_grad = kernel_call(
+        ring_kernel,
+        [
+            sds((at.ring_size, channels), f32),
+            sds((channels // LANES, at.grad_size, LANES), f32),
+        ],
+        [halves(at.ring_size, channels), halves((rows + 3) * stride, channels)],
+        0, place, coarse, cotangent, after(left, to_up), right, upper, lower, conv_weight, up_weight,
+    )
+    own_conv = after(own_conv, ring_act)
     steps = (faces // 2).bit_length() - 1
     for step in range(1, steps):
-        own_conv, to_conv = plane_sum(after(own_conv, to_up), got_conv)
+        own_conv, to_conv = plane_sum(own_conv, got_conv)
         got_conv = plane_swap(to_conv, step)
         if step == 1:
-            decoded, grad_coarse = kernel_call(
-                out_kernel,
-                [sds(skip.shape, bf16), sds(coarse.shape, bf16)],
-                [
-                    padded, pltpu.VMEM(shift_shape, bf16),
-                    pltpu.VMEM((4, n_rows + 1, n_cols, channels), bf16),
-                    halves(at.ring_size, channels), halves((rows + 3) * stride, channels),
-                ],
-                0, place, coarse, cotangent, after(act, to_conv), phases, left, right,
-                upper, lower, conv_weight, up_weight,
-            )
+            decoded = kernel_call(
+                decoded_kernel, [sds(skip.shape, bf16)], [padded, pltpu.VMEM(shift_shape, bf16)],
+                0, act, after(ring_act, to_conv), conv_weight,
+            )[0]
             own_up = after(own_up, decoded)
         own_up, to_up = plane_sum(own_up, got_up)
         got_up = plane_swap(to_up, step)
+        if step == 1:
+            grad_coarse = kernel_call(
+                coarse_kernel, [sds(coarse.shape, bf16)],
+                [
+                    halves(n_rows * (n_cols + 2 * MARGIN), channels),
+                    pltpu.VMEM((4, n_rows + 1, n_cols, channels), bf16),
+                ],
+                0, phases, after(ring_grad, to_up), up_weight,
+            )[0]
+            own_up = after(own_up, grad_coarse)
     grad_conv, grad_up = band_sum(place, own_conv, got_conv, own_up, got_up)
     return (decoded, grad_coarse, grad_up, grad_conv)
 

time: 50.8 us -> 48.2 us (0.949)
  waiting for transfers between devices: 16.7 us -> 13.2 us
  starting transfers between devices: 18.3 us -> 19.5 us
    ppermute x4, waiting for transfers between devices: 7.75 us -> 4.2 us  [plane_swap(): lax.ppermute(message, 'face', [(i, i ^ 2 << orders[i % 2][step]) for i in...]
    ppermute x4, starting transfers between devices: 4.59 us -> 5.9 us  [plane_swap(): lax.ppermute(message, 'face', [(i, i ^ 2 << orders[i % 2][step]) for i in...]
    pallas_call x12 -> x14, Pallas kernels: 14.8 us -> 14.5 us  [kernel_call(): pl.pallas_call(body, out_shape=tuple(outs), in_specs=[hbm if i in far els...]
  transfers between devices with their start and end apart: 13 -> 13, of which waited for: 8 -> 9; matrix products, arithmetic and copies ran while one was open for 0% -> 0% of each run, Pallas kernels for 11% -> 13%
where the time goes in v6:
time: 48.2 us; the launch traced here: 48 us
  starting transfers between devices  19.5 us (40%)
  Pallas kernels  14.5 us (30%)
  waiting for transfers between devices  13.2 us (27%)
  between operations  0.76 us (2%)
    pallas_call x14, Pallas kernels, kernel_call(): pl.pallas_call(body, out_shape=tuple(outs), in_specs=[hbm if i in far els...  14.5 us
    ppermute x3, starting transfers between devices, band_sum(): lax.ppermute(messages[k - 1], 'band', xor_pairs(bands, k))  6.82 us
    ppermute x4, starting transfers between devices, swap(): return (lax.ppermute(first, axis, one), lax.ppermute(second, axis, two))  6.53 us
    ppermute x4, starting transfers between devices, plane_swap(): lax.ppermute(message, 'face', [(i, i ^ 2 << orders[i % 2][step]) for i in...  5.9 us
    ppermute x4, waiting for transfers between devices, plane_swap(): lax.ppermute(message, 'face', [(i, i ^ 2 << orders[i % 2][step]) for i in...  4.2 us
    ppermute x3, waiting for transfers between devices, band_sum(): lax.ppermute(messages[k - 1], 'band', xor_pairs(bands, k))  3.86 us
    ppermute x4, waiting for transfers between devices, swap(): return (lax.ppermute(first, axis, one), lax.ppermute(second, axis, two))  3.64 us
    ppermute x2, waiting for transfers between devices, core_sum(): got = lax.ppermute(send, 'face', xor_pairs(lax.axis_size('face'), 1))  1.48 us
  transfers between devices with their start and end apart: 13, of which 9 were waited for; matrix products, arithmetic and copies ran while one was open for 0% of the time, Pallas kernels for 13%

profile of v6, /device:TPU:0, one launch (start us, length us, event | category | flops | bytes accessed | tf_op | source)
XLA Modules:
  0.0 48.0 jit_solution(14064173774063216480)
XLA Ops:
  0.7 1.8 %shard_map.84 = (bf16[96,256]{1,0:T(8,128)(2,1)S(1)}, bf16[96,256]{1,0:T(8,128)(2,1)S(1)}, bf16[24,32,256]{2,1,0:T(8,128)(2,1)S(1)}, bf16[24,32,256]{2,1,0:T(8,128)(2,1)S(1)}, bf16[12,16,256]{2,1,0:T(8,128)(2,1)S(1)}) custom-call(s32[4]{0:T(128)S(1)} %pad_add_fusion.place, bf16[12,16,256]{2,1,0:T(8,128)(2,1)} %coarse.1, bf16[24,32,256]{2,1,0:T(8,128)(2,1)} %skip.1, ...), custom_call_target="tpu_custom_call" | custom-call | bytes 1867792 | tf_op jit(solution)/shard_map/pallas_call | solution.py:29
  3.0 3.6 %collective-permute-start.1 = (bf16[96,256]{1,0:T(8,128)(2,1)S(1)}, bf16[96,256]{1,0:T(8,128)(2,1)S(1)}, u32[]{:S(2)}, u32[]{:S(2)}) collective-permute-start(bf16[96,256]{1,0:T(8,128)(2,1)S(1)} %get-tuple-element.51), channel_id=1, source_target_pairs={{0,28},{4,8},{8,4},{12,16},{16,12},{20,24},{24,20},{28,0},{1,29},{... | collective-permute-start | bytes 147464 | tf_op jit(solution)/shard_map/ppermute | solution.py:511
  6.6 1.8 %collective-permute-done.1.got_second = bf16[96,256]{1,0:T(8,128)(2,1)S(1)} collective-permute-done((bf16[96,256]{1,0:T(8,128)(2,1)S(1)}, bf16[96,256]{1,0:T(8,128)(2,1)S(1)}, u32[]{:S(2)}, u32[]{:S(2)}) %collective-permute-start.1) | collective-permute-done | bytes 49184 | tf_op jit(solution)/shard_map/ppermute | solution.py:511
  8.9 1.8 %collective-permute-start.2 = (bf16[128,256]{1,0:T(8,128)(2,1)S(1)}, bf16[128,256]{1,0:T(8,128)(2,1)S(1)}, u32[]{:S(2)}, u32[]{:S(2)}) collective-permute-start(bf16[128,256]{1,0:T(8,128)(2,1)S(1)} %get-tuple-element.54), channel_id=1, source_target_pairs={{0,1},{1,0},{2,3},{3,2},{4,5},{5,4},{6,7},{7,6},{8,9},{9,8},{10,11... | collective-permute-start | bytes 196616 | tf_op jit(solution)/shard_map/ppermute | solution.py:511
  11.4 1.9 %collective-permute-done.2.got_first = bf16[128,256]{1,0:T(8,128)(2,1)S(1)} collective-permute-done((bf16[128,256]{1,0:T(8,128)(2,1)S(1)}, bf16[128,256]{1,0:T(8,128)(2,1)S(1)}, u32[]{:S(2)}, u32[]{:S(2)}) %collective-permute-start.2) | collective-permute-done | bytes 65568 | tf_op jit(solution)/shard_map/ppermute | solution.py:511
  13.3 2.4 %shard_map.86 = (bf16[3,26,32,256]{3,2,1,0:T(8,128)(2,1)S(1)}, bf16[2,17,16,256]{3,2,1,0:T(8,128)(2,1)S(1)}, bf16[24,32,256]{2,1,0:T(8,128)(2,1)S(1)}, f32[768,2...) custom-call(s32[4]{0:T(128)S(1)} %pad_add_fusion.place, ...), custom_call_target="tpu_custom_call" | custom-call | flops 1132462080 | bytes 10698768 | tf_op jit(solution)/shard_map/pallas_call | solution.py:29
  15.7 1.2 %shard_map.88.phases = bf16[2,2,16,16,256]{4,3,2,1,0:T(8,128)(2,1)S(1)} custom-call(bf16[3,26,32,256]{3,2,1,0:T(8,128)(2,1)S(1)} %get-tuple-element.62.shifted, f32[768,256]{1,0:T(8,128)S(1)} %get-tuple-element.63.slope, bf16[3,3,256,256]{3,2,1,0:T(8,128)(2,1)S(1)} %get-tuple-element.64.conv_w), custom_call_target="tpu_custom_call" | custom-call | bytes 3768320 | tf_op jit(solution)/shard_map/pallas_call | solution.py:29
  17.0 0.8 %collective-permute-done.4.got = bf16[4,288,256]{2,1,0:T(8,128)(2,1)S(1)} collective-permute-done((bf16[4,288,256]{2,1,0:T(8,128)(2,1)S(1)}, bf16[4,288,256]{2,1,0:T(8,128)(2,1)S(1)}, u32[]{:S(2)}, u32[]{:S(2)}) %collective-permute-start.4) | collective-permute-done | bytes 589856 | tf_op jit(solution)/shard_map/ppermute | solution.py:475
  18.4 1.1 %shard_map.89 = (f32[2304,256]{1,0:T(8,128)S(1)}, bf16[4,288,256]{2,1,0:T(8,128)(2,1)S(1)}) custom-call(s32[4]{0:T(128)S(1)} %pad_add_fusion.place, bf16[2,17,16,256]{3,2,1,0:T(8,128)(2,1)S(1)} %get-tuple-element.61.near, bf16[2,2,16,16,256]{4,3,2,1,0:T(8,128)(2,1)S(1)} %shard_map.88.phases), custom_call_target="tpu_custom_call" | custom-call | bytes 3751952 | tf_op jit(solution)/shard_map/pallas_call | solution.py:29
  19.7 1.2 %collective-permute-start.6 = (bf16[2,288,256]{2,1,0:T(8,128)(2,1)S(1)}, bf16[2,288,256]{2,1,0:T(8,128)(2,1)S(1)}, u32[]{:S(2)}, u32[]{:S(2)}) collective-permute-start(bf16[2,288,256]{2,1,0:T(8,128)(2,1)S(1)} %get-tuple-element.60), channel_id=1, source_target_pairs={{0,8},{4,20},{8,0},{12,28},{16,24},{20,4},{24,16},{28,12},{1,9},{5... | collective-permute-start | bytes 884744 | tf_op jit(solution)/shard_map/ppermute | solution.py:483
  22.2 1.2 %collective-permute-start.7 = (bf16[2,288,256]{2,1,0:T(8,128)(2,1)S(1)}, bf16[2,288,256]{2,1,0:T(8,128)(2,1)S(1)}, u32[]{:S(2)}, u32[]{:S(2)}) collective-permute-start(bf16[2,288,256]{2,1,0:T(8,128)(2,1)S(1)} %get-tuple-element.67), channel_id=1, source_target_pairs={{0,8},{4,20},{8,0},{12,28},{16,24},{20,4},{24,16},{28,12},{1,9},{5... | collective-permute-start | bytes 884744 | tf_op jit(solution)/shard_map/ppermute | solution.py:483
  23.5 1.3 %shard_map.91 = (f32[128,256]{1,0:T(8,128)S(1)}, f32[2,64,128]{2,1,0:T(8,128)S(1)}) custom-call(s32[4]{0:T(128)S(1)} %pad_add_fusion.place, bf16[12,16,256]{2,1,0:T(8,128)(2,1)S(1)} %get-tuple-element.47.coarse, bf16[24,32,256]{2,1,0:T(8,128)(2,1)S(1)} %get-tuple-element.49.cot, f32[96,256]{1,0:T(8,128)S(1)} %get-tuple-element.68.left, ...), custom_call_target="tpu_custom_call" | custom-call | bytes 3506192 | tf_op jit(solution)/shard_map/pallas_call | solution.py:29
  24.8 1.6 %collective-permute-done.6.got = bf16[2,288,256]{2,1,0:T(8,128)(2,1)S(1)} collective-permute-done((bf16[2,288,256]{2,1,0:T(8,128)(2,1)S(1)}, bf16[2,288,256]{2,1,0:T(8,128)(2,1)S(1)}, u32[]{:S(2)}, u32[]{:S(2)}) %collective-permute-start.6) | collective-permute-done | bytes 294944 | tf_op jit(solution)/shard_map/ppermute | solution.py:483
  26.5 1.7 %collective-permute-start.8 = (bf16[1,288,256]{2,1,0:T(8,128)(2,1)S(1)}, bf16[1,288,256]{2,1,0:T(8,128)(2,1)S(1)}, u32[]{:S(2)}, u32[]{:S(2)}) collective-permute-start(bf16[1,288,256]{2,1,0:T(8,128)(2,1)S(1)} %get-tuple-element.74), channel_id=1, source_target_pairs={{0,16},{4,12},{8,24},{12,4},{16,0},{20,28},{24,8},{28,20},{1,17},{... | collective-permute-start | bytes 442376 | tf_op jit(solution)/shard_map/ppermute | solution.py:483
  28.3 1.9 %shard_map.93 = bf16[24,32,256]{2,1,0:T(8,128)(2,1)} custom-call(bf16[24,32,256]{2,1,0:T(8,128)(2,1)S(1)} %get-tuple-element.56.act, f32[128,256]{1,0:T(8,128)S(1)} %get-tuple-element.75.ring_act, bf16[3,3,256,256]{3,2,1,0:T(8,128)(2,1)S(1)} %get-tuple-element.64.conv_w), custom_call_target="tpu_custom_call" | custom-call | bytes 2097152 | tf_op jit(solution)/shard_map/pallas_call | solution.py:29
  30.5 1.7 %collective-permute-start.9 = (bf16[1,288,256]{2,1,0:T(8,128)(2,1)S(1)}, bf16[1,288,256]{2,1,0:T(8,128)(2,1)S(1)}, u32[]{:S(2)}, u32[]{:S(2)}) collective-permute-start(bf16[1,288,256]{2,1,0:T(8,128)(2,1)S(1)} %get-tuple-element.79), channel_id=1, source_target_pairs={{0,16},{4,12},{8,24},{12,4},{16,0},{20,28},{24,8},{28,20},{1,17},{... | collective-permute-start | bytes 442376 | tf_op jit(solution)/shard_map/ppermute | solution.py:483
  32.2 1.2 %shard_map.95 = bf16[12,16,256]{2,1,0:T(8,128)(2,1)} custom-call(bf16[2,2,16,16,256]{4,3,2,1,0:T(8,128)(2,1)S(1)} %shard_map.88.phases, f32[2,64,128]{2,1,0:T(8,128)S(1)} %get-tuple-element.80.ring_grad, bf16[3,3,256,256]{3,2,1,0:T(8,128)(2,1)S(1)} %copy-done), custom_call_target="tpu_custom_call" | custom-call | bytes 1867776 | tf_op jit(solution)/shard_map/pallas_call | solution.py:29
  33.5 2.2 %collective-permute-done.9.got_up = bf16[1,288,256]{2,1,0:T(8,128)(2,1)S(1)} collective-permute-done((bf16[1,288,256]{2,1,0:T(8,128)(2,1)S(1)}, bf16[1,288,256]{2,1,0:T(8,128)(2,1)S(1)}, u32[]{:S(2)}, u32[]{:S(2)}) %collective-permute-start.9) | collective-permute-done | bytes 147488 | tf_op jit(solution)/shard_map/ppermute | solution.py:483
  35.7 0.8 %shard_map.96 = (f32[288,128]{1,0:T(8,128)S(1)}, bf16[288,128]{1,0:T(8,128)(2,1)S(1)}, bf16[288,128]{1,0:T(8,128)(2,1)S(1)}, bf16[288,128]{1,0:T(8,128)(2,1)S(1)}) custom-call(s32[4]{0:T(128)S(1)} %pad_add_fusion.place, f32[1,288,256]{2,1,0:T(8,128)S(1)} %get-tuple-element.81.conv, bf16[1,288,256]{2,1,0:T(8,128)(2,1)S(1)} %collective-permute-done.8.got_conv, ...), custom_call_target="tpu_custom_call" | custom-call | bytes 1253392 | tf_op jit(solution)/shard_map/pallas_call | solution.py:29
  36.5 3.8 %collective-permute-start.10 = (bf16[288,128]{1,0:T(8,128)(2,1)S(1)}, bf16[288,128]{1,0:T(8,128)(2,1)S(1)}, u32[]{:S(2)}, u32[]{:S(2)}) collective-permute-start(bf16[288,128]{1,0:T(8,128)(2,1)S(1)} %get-tuple-element.85), channel_id=1, source_target_pairs={{0,3},{1,2},{2,1},{3,0},{4,7},{5,6},{6,5},{7,4},{8,11},{9,10},{10,... | collective-permute-start | bytes 221192 | tf_op jit(solution)/shard_map/ppermute | solution.py:501
  40.3 2.5 %collective-permute-start.11 = (bf16[288,128]{1,0:T(8,128)(2,1)S(1)}, bf16[288,128]{1,0:T(8,128)(2,1)S(1)}, u32[]{:S(2)}, u32[]{:S(2)}) collective-permute-start(bf16[288,128]{1,0:T(8,128)(2,1)S(1)} %get-tuple-element.86), channel_id=1, source_target_pairs={{0,2},{1,3},{2,0},{3,1},{4,6},{5,7},{6,4},{7,5},{8,10},{9,11},{10,... | collective-permute-start | bytes 221192 | tf_op jit(solution)/shard_map/ppermute | solution.py:501
  43.3 2.6 %collective-permute-done.11.refs_1_ = bf16[288,128]{1,0:T(8,128)(2,1)S(1)} collective-permute-done((bf16[288,128]{1,0:T(8,128)(2,1)S(1)}, bf16[288,128]{1,0:T(8,128)(2,1)S(1)}, u32[]{:S(2)}, u32[]{:S(2)}) %collective-permute-start.11) | collective-permute-done | bytes 73760 | tf_op jit(solution)/shard_map/ppermute | solution.py:501
  45.9 1.3 %collective-permute-done.12.refs_2_ = bf16[288,128]{1,0:T(8,128)(2,1)S(1)} collective-permute-done((bf16[288,128]{1,0:T(8,128)(2,1)S(1)}, bf16[288,128]{1,0:T(8,128)(2,1)S(1)}, u32[]{:S(2)}, u32[]{:S(2)}) %collective-permute-start.12) | collective-permute-done | bytes 73760 | tf_op jit(solution)/shard_map/ppermute | solution.py:501
  47.2 0.8 %shard_map.97 = (f32[64,288]{1,0:T(8,128)}, f32[64,288]{1,0:T(8,128)}) custom-call(f32[288,128]{1,0:T(8,128)S(1)} %get-tuple-element.84.own, bf16[288,128]{1,0:T(8,128)(2,1)S(1)} %collective-permute-done.10.refs_0_, bf16[288,128]{1,0:T(8,128)(2,1)S(1)} %collective-permute-done.11.refs_1_, bf16[288,128]{1,0:T(8,128)(2,1)S(1)} %collective-permute-done.12.refs_2_), custom_call_target="tpu_custom_call" | custom-call | bytes 516096 | tf_op jit(solution)/shard_map/pallas_call | solution.py:29
  (19 shorter events, 5.0 us)
Async XLA Ops:
  0.6 12.7 %copy-start = (bf16[3,3,256,256]{3,2,1,0:T(8,128)(2,1)S(1)}, bf16[3,3,256,256]{3,2,1,0:T(8,128)(2,1)}, u32[]{:S(2)}) copy-start(bf16[3,3,256,256]{3,2,1,0:T(8,128)(2,1)} %up_w.5) | copy-start | bytes 3538948
  2.5 4.1 %collective-permute-start = (bf16[96,256]{1,0:T(8,128)(2,1)S(1)}, bf16[96,256]{1,0:T(8,128)(2,1)S(1)}, u32[]{:S(2)}, u32[]{:S(2)}) collective-permute-start(bf16[96,256]{1,0:T(8,128)(2,1)S(1)} %get-tuple-element.50), channel_id=1, source_target_pairs={{0,4},{4,0},{8,12},{12,8},{16,20},{20,16},{24,28},{28,24},{1,5},{5... | collective-permute-start | bytes 147464 | tf_op jit(solution)/shard_map/ppermute | solution.py:511
  3.0 5.3 %collective-permute-start.1 = (bf16[96,256]{1,0:T(8,128)(2,1)S(1)}, bf16[96,256]{1,0:T(8,128)(2,1)S(1)}, u32[]{:S(2)}, u32[]{:S(2)}) collective-permute-start(bf16[96,256]{1,0:T(8,128)(2,1)S(1)} %get-tuple-element.51), channel_id=1, source_target_pairs={{0,28},{4,8},{8,4},{12,16},{16,12},{20,24},{24,20},{28,0},{1,29},{... | collective-permute-start | bytes 147464 | tf_op jit(solution)/shard_map/ppermute | solution.py:511
  8.9 4.3 %collective-permute-start.2 = (bf16[128,256]{1,0:T(8,128)(2,1)S(1)}, bf16[128,256]{1,0:T(8,128)(2,1)S(1)}, u32[]{:S(2)}, u32[]{:S(2)}) collective-permute-start(bf16[128,256]{1,0:T(8,128)(2,1)S(1)} %get-tuple-element.54), channel_id=1, source_target_pairs={{0,1},{1,0},{2,3},{3,2},{4,5},{5,4},{6,7},{7,6},{8,9},{9,8},{10,11... | collective-permute-start | bytes 196616 | tf_op jit(solution)/shard_map/ppermute | solution.py:511
  10.7 2.5 %collective-permute-start.3 = (bf16[128,256]{1,0:T(8,128)(2,1)S(1)}, bf16[128,256]{1,0:T(8,128)(2,1)S(1)}, u32[]{:S(2)}, u32[]{:S(2)}) collective-permute-start(bf16[128,256]{1,0:T(8,128)(2,1)S(1)} %get-tuple-element.55), channel_id=1, source_target_pairs={{1,2},{2,1},{5,6},{6,5},{9,10},{10,9},{13,14},{14,13},{17,18},{18,... | collective-permute-start | bytes 196616 | tf_op jit(solution)/shard_map/ppermute | solution.py:511
  15.7 2.1 %collective-permute-start.4 = (bf16[4,288,256]{2,1,0:T(8,128)(2,1)S(1)}, bf16[4,288,256]{2,1,0:T(8,128)(2,1)S(1)}, u32[]{:S(2)}, u32[]{:S(2)}) collective-permute-start(bf16[4,288,256]{2,1,0:T(8,128)(2,1)S(1)} %get-tuple-element.59), channel_id=1, source_target_pairs={{0,4},{4,0},{8,12},{12,8},{16,20},{20,16},{24,28},{28,24},{1,5},{5... | collective-permute-start | bytes 1769480 | tf_op jit(solution)/shard_map/ppermute | solution.py:475
  19.5 2.1 %collective-permute-start.5 = (bf16[4,288,256]{2,1,0:T(8,128)(2,1)S(1)}, bf16[4,288,256]{2,1,0:T(8,128)(2,1)S(1)}, u32[]{:S(2)}, u32[]{:S(2)}) collective-permute-start(bf16[4,288,256]{2,1,0:T(8,128)(2,1)S(1)} %get-tuple-element.66), channel_id=1, source_target_pairs={{0,4},{4,0},{8,12},{12,8},{16,20},{20,16},{24,28},{28,24},{1,5},{5... | collective-permute-start | bytes 1769480 | tf_op jit(solution)/shard_map/ppermute | solution.py:475
  19.7 6.7 %collective-permute-start.6 = (bf16[2,288,256]{2,1,0:T(8,128)(2,1)S(1)}, bf16[2,288,256]{2,1,0:T(8,128)(2,1)S(1)}, u32[]{:S(2)}, u32[]{:S(2)}) collective-permute-start(bf16[2,288,256]{2,1,0:T(8,128)(2,1)S(1)} %get-tuple-element.60), channel_id=1, source_target_pairs={{0,8},{4,20},{8,0},{12,28},{16,24},{20,4},{24,16},{28,12},{1,9},{5... | collective-permute-start | bytes 884744 | tf_op jit(solution)/shard_map/ppermute | solution.py:483
  22.2 8.2 %collective-permute-start.7 = (bf16[2,288,256]{2,1,0:T(8,128)(2,1)S(1)}, bf16[2,288,256]{2,1,0:T(8,128)(2,1)S(1)}, u32[]{:S(2)}, u32[]{:S(2)}) collective-permute-start(bf16[2,288,256]{2,1,0:T(8,128)(2,1)S(1)} %get-tuple-element.67), channel_id=1, source_target_pairs={{0,8},{4,20},{8,0},{12,28},{16,24},{20,4},{24,16},{28,12},{1,9},{5... | collective-permute-start | bytes 884744 | tf_op jit(solution)/shard_map/ppermute | solution.py:483
  26.5 6.9 %collective-permute-start.8 = (bf16[1,288,256]{2,1,0:T(8,128)(2,1)S(1)}, bf16[1,288,256]{2,1,0:T(8,128)(2,1)S(1)}, u32[]{:S(2)}, u32[]{:S(2)}) collective-permute-start(bf16[1,288,256]{2,1,0:T(8,128)(2,1)S(1)} %get-tuple-element.74), channel_id=1, source_target_pairs={{0,16},{4,12},{8,24},{12,4},{16,0},{20,28},{24,8},{28,20},{1,17},{... | collective-permute-start | bytes 442376 | tf_op jit(solution)/shard_map/ppermute | solution.py:483
  30.5 5.2 %collective-permute-start.9 = (bf16[1,288,256]{2,1,0:T(8,128)(2,1)S(1)}, bf16[1,288,256]{2,1,0:T(8,128)(2,1)S(1)}, u32[]{:S(2)}, u32[]{:S(2)}) collective-permute-start(bf16[1,288,256]{2,1,0:T(8,128)(2,1)S(1)} %get-tuple-element.79), channel_id=1, source_target_pairs={{0,16},{4,12},{8,24},{12,4},{16,0},{20,28},{24,8},{28,20},{1,17},{... | collective-permute-start | bytes 442376 | tf_op jit(solution)/shard_map/ppermute | solution.py:483
  36.5 6.8 %collective-permute-start.10 = (bf16[288,128]{1,0:T(8,128)(2,1)S(1)}, bf16[288,128]{1,0:T(8,128)(2,1)S(1)}, u32[]{:S(2)}, u32[]{:S(2)}) collective-permute-start(bf16[288,128]{1,0:T(8,128)(2,1)S(1)} %get-tuple-element.85), channel_id=1, source_target_pairs={{0,3},{1,2},{2,1},{3,0},{4,7},{5,6},{6,5},{7,4},{8,11},{9,10},{10,... | collective-permute-start | bytes 221192 | tf_op jit(solution)/shard_map/ppermute | solution.py:501
  40.3 5.6 %collective-permute-start.11 = (bf16[288,128]{1,0:T(8,128)(2,1)S(1)}, bf16[288,128]{1,0:T(8,128)(2,1)S(1)}, u32[]{:S(2)}, u32[]{:S(2)}) collective-permute-start(bf16[288,128]{1,0:T(8,128)(2,1)S(1)} %get-tuple-element.86), channel_id=1, source_target_pairs={{0,2},{1,3},{2,0},{3,1},{4,6},{5,7},{6,4},{7,5},{8,10},{9,11},{10,... | collective-permute-start | bytes 221192 | tf_op jit(solution)/shard_map/ppermute | solution.py:501
  42.8 4.4 %collective-permute-start.12 = (bf16[288,128]{1,0:T(8,128)(2,1)S(1)}, bf16[288,128]{1,0:T(8,128)(2,1)S(1)}, u32[]{:S(2)}, u32[]{:S(2)}) collective-permute-start(bf16[288,128]{1,0:T(8,128)(2,1)S(1)} %get-tuple-element.87), channel_id=1, source_target_pairs={{0,1},{1,0},{2,3},{3,2},{4,5},{5,4},{6,7},{7,6},{8,9},{9,8},{10,11... | collective-permute-start | bytes 221192 | tf_op jit(solution)/shard_map/ppermute | solution.py:501

commit v7 on v6

--- a/solution.py
+++ b/solution.py
@@ -18,7 +18,6 @@
 
 def kernel_call(body, outs, scratch, flops, *args, far=()):
     vmem = pl.BlockSpec(memory_space=pltpu.VMEM)
-    smem = pl.BlockSpec(memory_space=pltpu.SMEM)
     hbm = pl.BlockSpec(memory_space=pltpu.HBM)
     moved = sum(a.size * a.dtype.itemsize for a in args)
     moved += sum(a.size * a.dtype.itemsize for a in outs)
@@ -29,15 +28,17 @@
     return pl.pallas_call(
         body,
         out_shape=tuple(outs),
-        in_specs=[
-            hbm if i in far else smem if a.dtype == jnp.int32 else vmem
-            for i, a in enumerate(args)
-        ],
+        in_specs=[hbm if i in far else vmem for i in range(len(args))],
         out_specs=tuple(vmem for _ in outs),
         scratch_shapes=scratch,
         compiler_params=pltpu.CompilerParams(vmem_limit_bytes=28 * 2**20),
         cost_estimate=pl.CostEstimate(flops=flops, bytes_accessed=moved, transcendentals=0),
     )(*args)
+
+
+def place_of():
+    face = lax.axis_index("face")
+    return lax.rem(face, 2), lax.div(face, 2), lax.axis_index("band"), lax.axis_size("band")
 
 
 def dot(a, b):
@@ -81,10 +82,11 @@
     ref[start : start + value.shape[0], :] = value
 
 
-def other_core(place, partial, send):
+def other_core(partial, send):
+    core = place_of()[0]
     groups, block, _ = send.shape
     for group in range(groups):
-        theirs = pl.multiple_of((2 * group + 1 - place[0]) * block, 16)
+        theirs = pl.multiple_of((2 * group + 1 - core) * block, 16)
         send[group] = partial[pl.ds(theirs, block), :].astype(bf16)
 
 
@@ -105,7 +107,7 @@
 COT, COT_2, SKIP, COARSE = (0, 1, 2), (3, 4, 5), (6, None, 7), (8, None, 9)
 
 
-def face_message(place, coarse, skip, cot, first, second, cot_v, skip_v, coarse_v, flat, before, after, sems):
+def face_message(coarse, skip, cot, first, second, cot_v, skip_v, coarse_v, flat, before, after, sems):
     rows, cols, _ = cot.shape
     n_rows, n_cols, _ = coarse.shape
     at = Layout(n_rows, n_cols)
@@ -128,16 +130,16 @@
         fill(after, start, get(flat, n * 8 + 7, n, 8))
         if start_2 is not None:
             fill(after, start_2, get(flat, n * 8 + 6, n, 8))
-    even = place[0] == 0
+    even = place_of()[0] == 0
     first[...] = jnp.where(even, after[...], before[...]).astype(bf16)
     second[...] = jnp.where(even, before[...], after[...]).astype(bf16)
 
 
-def band_message(place, coarse, skip, cot, got_first, got_second, first, second, left, right, before, after):
+def band_message(coarse, skip, cot, got_first, got_second, first, second, left, right, before, after):
     rows, cols, channels = cot.shape
     n_rows, n_cols, _ = coarse.shape
     at = Layout(n_rows, n_cols)
-    even = place[0] == 0
+    even = place_of()[0] == 0
     one, two = got_first[...].astype(f32), got_second[...].astype(f32)
     left[...] = jnp.where(even, two, one)
     right[...] = jnp.where(even, one, two)
@@ -162,13 +164,13 @@
             ]
         for corner, side, source in corners:
             fill(message, at.corner + corner, side[source : source + 1, :])
-    even = lax.rem(place[2], 2) == 0
+    even = lax.rem(place_of()[2], 2) == 0
     first[...] = jnp.where(even, after[...], before[...]).astype(bf16)
     second[...] = jnp.where(even, before[...], after[...]).astype(bf16)
 
 
 def act_kernel(
-    place, coarse, skip, cot, left, right, got_first, got_second, up_w, conv_w,
+    coarse, skip, cot, left, right, got_first, got_second, up_w, conv_w,
     shifted, near, act, slope, partial, send, upper, lower, conv_v, padded, pre, sem,
 ):
     n_rows, n_cols, channels = coarse.shape
@@ -177,7 +179,7 @@
     stride = cols + 2 * MARGIN
     copy = pltpu.make_async_copy(conv_w, conv_v, sem)
     copy.start()
-    even = lax.rem(place[2], 2) == 0
+    even = lax.rem(place_of()[2], 2) == 0
     one, two = got_first[...].astype(f32), got_second[...].astype(f32)
     upper[...] = jnp.where(even, two, one)
     lower[...] = jnp.where(even, one, two)
@@ -236,7 +238,7 @@
         for l in range(3):
             source = shifted[2 - l, pl.ds(2 - k, rows)].reshape(-1, channels)
             partial[pl.ds((3 * k + l) * channels, channels), :] = dot(act_t, source)
-    other_core(place, partial, send)
+    other_core(partial, send)
     copy.wait()
 
 
@@ -260,7 +262,7 @@
                 phases[row_phase, col_phase, row] = jnp.zeros((n_cols, channels), bf16)
 
 
-def up_kernel(place, near, phases, partial, send):
+def up_kernel(near, phases, partial, send):
     _, _, whole, n_cols, channels = phases.shape
     turned = {}
     for row_off in range(2):
@@ -275,17 +277,18 @@
             partial[pl.ds((3 * k + l) * channels, channels), :] = dot(
                 turned[row_off, col_off], source
             )
-    other_core(place, partial, send)
+    other_core(partial, send)
 
 
 def ring_kernel(
-    place, coarse, cot, left, right, upper, lower, conv_w, up_w, ring_act, ring_grad, ring, wide,
+    coarse, cot, left, right, upper, lower, conv_w, up_w, ring_act, ring_grad, ring, wide,
 ):
     rows, cols, channels = cot.shape
     n_rows, n_cols = rows // 2, cols // 2
     at = Layout(n_rows, n_cols)
     stride, step = cols + 2 * MARGIN, n_cols + 2 * MARGIN
-    has_upper, has_lower = place[2] > 0, place[2] < place[3] - 1
+    _, _, band, n_bands = place_of()
+    has_upper, has_lower = band > 0, band < n_bands - 1
 
     def corner(message, which):
         return message[at.corner + which : at.corner + which + 1, :]
@@ -420,13 +423,14 @@
     return sum(1 << bit for step, bit in enumerate(order) if slot >> (last - step) & 1)
 
 
-def core_kernel(place, partial, got, own, message):
+def core_kernel(partial, got, own, message):
     slots, half, block = got.shape[0], own.shape[0], got.shape[1]
+    core, chip, _, _ = place_of()
     even, odd = halving(2 * slots)
     for slot in range(slots):
-        chip = place[1] ^ jnp.where(place[0] == 0, mask_of(slot, even), mask_of(slot, odd))
-        mine = pl.multiple_of((2 * chip + place[0]) * block, 16)
-        total = partial[pl.ds(mine, block), :] + got[chip].astype(f32)
+        target = chip ^ jnp.where(core == 0, mask_of(slot, even), mask_of(slot, odd))
+        mine = pl.multiple_of((2 * target + core) * block, 16)
+        total = partial[pl.ds(mine, block), :] + got[target].astype(f32)
         if slot < half:
             own[slot] = total
         else:
@@ -443,7 +447,7 @@
             message[slot - half] = total.astype(bf16)
 
 
-def band_kernel(place, conv, got_conv, up, got_up, own, *refs):
+def band_kernel(conv, got_conv, up, got_up, own, *refs):
     n_bands, messages, cut = len(refs), refs[:-1], refs[-1]
     conv_total = conv[0] + got_conv[0].astype(f32)
     up_total = up[0] + got_up[0].astype(f32)
@@ -451,9 +455,10 @@
     for band in range(n_bands):
         cut[band, :, :cols] = conv_total[:, band * cols : (band + 1) * cols]
         cut[band, :, cols:] = up_total[:, band * cols : (band + 1) * cols]
-    own[...] = cut[place[2]]
+    band = place_of()[2]
+    own[...] = cut[band]
     for k, message in enumerate(messages):
-        message[...] = cut[place[2] ^ (k + 1)].astype(bf16)
+        message[...] = cut[lax.rem(band + k + 1, n_bands)].astype(bf16)
 
 
 def last_kernel(own, *refs):
@@ -470,11 +475,11 @@
     return [(i, i ^ bits) for i in range(count)]
 
 
-def core_sum(place, partial, send):
+def core_sum(partial, send):
     groups, block, channels = send.shape
     got = lax.ppermute(send, "face", xor_pairs(lax.axis_size("face"), 1))
     shape = (groups // 2, block, channels)
-    return kernel_call(core_kernel, [sds(shape, f32), sds(shape, bf16)], [], 0, place, partial, got)
+    return kernel_call(core_kernel, [sds(shape, f32), sds(shape, bf16)], [], 0, partial, got)
 
 
 def plane_swap(message, step):
@@ -489,16 +494,19 @@
     return kernel_call(plane_kernel, [sds(shape, f32), sds(shape, bf16)], [], 0, own, got)
 
 
-def band_sum(place, conv, got_conv, up, got_up):
+def band_sum(conv, got_conv, up, got_up):
     bands = lax.axis_size("band")
     _, block, channels = conv.shape
     cols = channels // bands
     shape = (block, 2 * cols)
     own, *messages = kernel_call(
         band_kernel, [sds(shape, f32)] + [sds(shape, bf16)] * (bands - 1),
-        [pltpu.VMEM((bands,) + shape, f32)], 0, place, conv, got_conv, up, got_up,
+        [pltpu.VMEM((bands,) + shape, f32)], 0, conv, got_conv, up, got_up,
     )
-    got = [lax.ppermute(messages[k - 1], "band", xor_pairs(bands, k)) for k in range(bands - 1, 0, -1)]
+    got = [
+        lax.ppermute(messages[k - 1], "band", [(i, (i + k) % bands) for i in range(bands)])
+        for k in range(1, bands)
+    ]
     return [a.T for a in kernel_call(last_kernel, [sds((cols, block), f32)] * 2, [], 0, own, *got)]
 
 
@@ -515,9 +523,7 @@
     n_rows, n_cols, channels = coarse.shape
     rows, cols, _ = skip.shape
     at = Layout(n_rows, n_cols)
-    faces, bands = lax.axis_size("face"), lax.axis_size("band")
-    face, band = lax.axis_index("face"), lax.axis_index("band")
-    place = jnp.stack([face % 2, face // 2, band, bands]).astype(jnp.int32)
+    faces = lax.axis_size("face")
     groups, block = faces // 2, 9 * channels // faces
 
     flat = halves(rows * cols, channels)
@@ -527,7 +533,7 @@
         face_message,
         [message, message, sds(cotangent.shape, bf16), sds(skip.shape, bf16), sds(coarse.shape, bf16)],
         [flat, edges, edges, pltpu.SemaphoreType.DMA((3,))],
-        0, place, coarse, skip, cotangent, far=(1, 2, 3),
+        0, coarse, skip, cotangent, far=(0, 1, 2),
     )
     first, second = swap(first, second, "face", True)
     side = sds(message.shape, f32)
@@ -535,7 +541,7 @@
     edges = pltpu.VMEM(message.shape, f32)
     first, second, left, right = kernel_call(
         band_message, [message, message, side, side], [edges, edges],
-        0, place, coarse, skip, cotangent, first, second,
+        0, coarse, skip, cotangent, first, second,
     )
     first, second = swap(first, second, "band", False)
 
@@ -544,7 +550,6 @@
     padded = halves((rows + 2) * stride, channels)
     shift_shape = (3, rows + 2, cols, channels)
     whole = -(-cells // 256) * 256 // n_cols
-    one_tap = 2 * cells * channels * channels
     partials = [sds((9 * channels, channels), f32), sds((groups, block, channels), bf16)]
     side = sds(message.shape, f32)
     shifted, near, act, slope, part_conv, send_conv, upper, lower, conv_weight = kernel_call(
@@ -555,21 +560,16 @@
             sds(conv_weight.shape, bf16),
         ],
         [padded, flat, pltpu.SemaphoreType.DMA],
-        45 * one_tap, place, coarse, skip, cotangent, left, right, first, second,
-        up_weight, conv_weight, far=(9,),
+        0, coarse, skip, cotangent, left, right, first, second, up_weight, conv_weight, far=(8,),
     )
-    own_conv, to_conv = core_sum(place, part_conv, send_conv)
-    got_conv = plane_swap(to_conv, 0)
     phases = kernel_call(
-        grad_kernel,
-        [sds((2, 2, whole, n_cols, channels), bf16)],
-        [flat],
+        grad_kernel, [sds((2, 2, whole, n_cols, channels), bf16)], [flat],
         0, shifted, slope, conv_weight,
     )[0]
-    part_up, send_up = kernel_call(
-        up_kernel, partials, [], 0, place, after(near, to_conv), phases
-    )
-    own_up, to_up = core_sum(place, part_up, send_up)
+    part_up, send_up = kernel_call(up_kernel, partials, [], 0, near, phases)
+    own_conv, to_conv = core_sum(after(part_conv, send_up), send_conv)
+    got_conv = plane_swap(to_conv, 0)
+    own_up, to_up = core_sum(after(part_up, to_conv), send_up)
     got_up = plane_swap(to_up, 0)
     ring_act, ring_grad = kernel_call(
         ring_kernel,
@@ -578,7 +578,7 @@
             sds((channels // LANES, at.grad_size, LANES), f32),
         ],
         [halves(at.ring_size, channels), halves((rows + 3) * stride, channels)],
-        0, place, coarse, cotangent, after(left, to_up), right, upper, lower, conv_weight, up_weight,
+        0, coarse, cotangent, after(left, to_up), right, upper, lower, conv_weight, up_weight,
     )
     own_conv = after(own_conv, ring_act)
     steps = (faces // 2).bit_length() - 1
@@ -603,7 +603,7 @@
                 0, phases, after(ring_grad, to_up), up_weight,
             )[0]
             own_up = after(own_up, grad_coarse)
-    grad_conv, grad_up = band_sum(place, own_conv, got_conv, own_up, got_up)
+    grad_conv, grad_up = band_sum(own_conv, got_conv, own_up, got_up)
     return (decoded, grad_coarse, grad_up, grad_conv)
 
 

time: 48.2 us -> 46 us (0.954)
  Pallas kernels: 14.5 us -> 10.7 us
  starting transfers between devices: 19.5 us -> 22.3 us
  waiting for transfers between devices: 13.2 us -> 12 us
    pallas_call x14, Pallas kernels: 14.5 us -> 10.7 us  [kernel_call(): pl.pallas_call(body, out_shape=tuple(outs), in_specs=[hbm if i in far els...]
    ppermute x3, starting transfers between devices: 6.82 us -> 9.18 us  [band_sum(): lax.ppermute(messages[k - 1], 'band', [(i, (i + k) % bands) for i in rang...]
    ppermute x4, waiting for transfers between devices: 4.2 us -> 6.11 us  [plane_swap(): lax.ppermute(message, 'face', [(i, i ^ 2 << orders[i % 2][step]) for i in...]
    ppermute x3, waiting for transfers between devices: 3.86 us -> 1.98 us  [band_sum(): lax.ppermute(messages[k - 1], 'band', [(i, (i + k) % bands) for i in rang...]
    ppermute x2, waiting for transfers between devices: 1.48 us -> 0.28 us  [core_sum(): got = lax.ppermute(send, 'face', xor_pairs(lax.axis_size('face'), 1))]
  transfers between devices with their start and end apart: 13 -> 13, of which waited for: 9 -> 8; matrix products, arithmetic and copies ran while one was open for 0% -> 0% of each run, Pallas kernels for 13% -> 13%
where the time goes in v7:
time: 46 us; the launch traced here: 45.8 us
  starting transfers between devices  22.3 us (48%)
  waiting for transfers between devices  12 us (26%)
  Pallas kernels  10.7 us (23%)
  between operations  0.72 us (2%)
    pallas_call x14, Pallas kernels, kernel_call(): pl.pallas_call(body, out_shape=tuple(outs), in_specs=[hbm if i in far els...  10.7 us
    ppermute x3, starting transfers between devices, band_sum(): lax.ppermute(messages[k - 1], 'band', [(i, (i + k) % bands) for i in rang...  9.18 us
    ppermute x4, starting transfers between devices, swap(): return (lax.ppermute(first, axis, one), lax.ppermute(second, axis, two))  6.53 us
    ppermute x4, waiting for transfers between devices, plane_swap(): lax.ppermute(message, 'face', [(i, i ^ 2 << orders[i % 2][step]) for i in...  6.11 us
    ppermute x4, starting transfers between devices, plane_swap(): lax.ppermute(message, 'face', [(i, i ^ 2 << orders[i % 2][step]) for i in...  5.99 us
    ppermute x4, waiting for transfers between devices, swap(): return (lax.ppermute(first, axis, one), lax.ppermute(second, axis, two))  3.64 us
    ppermute x3, waiting for transfers between devices, band_sum(): lax.ppermute(messages[k - 1], 'band', [(i, (i + k) % bands) for i in rang...  1.98 us
  transfers between devices with their start and end apart: 13, of which 8 were waited for; matrix products, arithmetic and copies ran while one was open for 0% of the time, Pallas kernels for 13%

profile of v7, /device:TPU:0, one launch (start us, length us, event | category | flops | bytes accessed | tf_op | source)
XLA Modules:
  0.0 45.8 jit_solution(18108987618900538529)
XLA Ops:
  0.6 1.3 %shard_map.84 = (bf16[96,256]{1,0:T(8,128)(2,1)S(1)}, bf16[96,256]{1,0:T(8,128)(2,1)S(1)}, bf16[24,32,256]{2,1,0:T(8,128)(2,1)S(1)}, bf16[24,32,256]{2,1,0:T(8,128)(2,1)S(1)}, bf16[12,16,256]{2,1,0:T(8,128)(2,1)S(1)}) custom-call(bf16[12,16,256]{2,1,0:T(8,128)(2,1)} %coarse.1, bf16[24,32,256]{2,1,0:T(8,128)(2,1)} %skip.1, bf16[24,32,256]{2,1,0:T(8,128)(2,1)} %cot.1), custom_call_target="tpu_custom_call" | custom-call | bytes 1867776 | tf_op jit(solution)/shard_map/pallas_call | solution.py:28
  2.5 3.6 %collective-permute-start.1 = (bf16[96,256]{1,0:T(8,128)(2,1)S(1)}, bf16[96,256]{1,0:T(8,128)(2,1)S(1)}, u32[]{:S(2)}, u32[]{:S(2)}) collective-permute-start(bf16[96,256]{1,0:T(8,128)(2,1)S(1)} %get-tuple-element.52), channel_id=1, source_target_pairs={{0,28},{4,8},{8,4},{12,16},{16,12},{20,24},{24,20},{28,0},{1,29},{... | collective-permute-start | bytes 147464 | tf_op jit(solution)/shard_map/ppermute | solution.py:519
  6.0 1.8 %collective-permute-done.1.got_second = bf16[96,256]{1,0:T(8,128)(2,1)S(1)} collective-permute-done((bf16[96,256]{1,0:T(8,128)(2,1)S(1)}, bf16[96,256]{1,0:T(8,128)(2,1)S(1)}, u32[]{:S(2)}, u32[]{:S(2)}) %collective-permute-start.1) | collective-permute-done | bytes 49184 | tf_op jit(solution)/shard_map/ppermute | solution.py:519
  7.9 1.8 %collective-permute-start.2 = (bf16[128,256]{1,0:T(8,128)(2,1)S(1)}, bf16[128,256]{1,0:T(8,128)(2,1)S(1)}, u32[]{:S(2)}, u32[]{:S(2)}) collective-permute-start(bf16[128,256]{1,0:T(8,128)(2,1)S(1)} %get-tuple-element.55), channel_id=1, source_target_pairs={{0,1},{1,0},{2,3},{3,2},{4,5},{5,4},{6,7},{7,6},{8,9},{9,8},{10,11... | collective-permute-start | bytes 196616 | tf_op jit(solution)/shard_map/ppermute | solution.py:519
  10.3 1.9 %collective-permute-done.2.got_first = bf16[128,256]{1,0:T(8,128)(2,1)S(1)} collective-permute-done((bf16[128,256]{1,0:T(8,128)(2,1)S(1)}, bf16[128,256]{1,0:T(8,128)(2,1)S(1)}, u32[]{:S(2)}, u32[]{:S(2)}) %collective-permute-start.2) | collective-permute-done | bytes 65568 | tf_op jit(solution)/shard_map/ppermute | solution.py:519
  12.2 2.2 %shard_map.86 = (bf16[3,26,32,256]{3,2,1,0:T(8,128)(2,1)S(1)}, bf16[2,17,16,256]{3,2,1,0:T(8,128)(2,1)S(1)}, bf16[24,32,256]{2,1,0:T(8,128)(2,1)S(1)}, f32[768,2...) custom-call(bf16[12,16,256]{2,1,0:T(8,128)(2,1)S(1)} %get-tuple-elem, ...), custom_call_target="tpu_custom_call" | custom-call | bytes 10698752 | tf_op jit(solution)/shard_map/pallas_call | solution.py:28
  14.5 1.2 %shard_map.87.phases = bf16[2,2,16,16,256]{4,3,2,1,0:T(8,128)(2,1)S(1)} custom-call(bf16[3,26,32,256]{3,2,1,0:T(8,128)(2,1)S(1)} %get-tuple-element.59.shifted, f32[768,256]{1,0:T(8,128)S(1)} %get-tuple-element.60.slope, bf16[3,3,256,256]{3,2,1,0:T(8,128)(2,1)S(1)} %get-tuple-element.61.conv_w), custom_call_target="tpu_custom_call" | custom-call | bytes 3768320 | tf_op jit(solution)/shard_map/pallas_call | solution.py:28
  15.7 0.8 %shard_map.88 = (f32[2304,256]{1,0:T(8,128)S(1)}, bf16[4,288,256]{2,1,0:T(8,128)(2,1)S(1)}) custom-call(bf16[2,17,16,256]{3,2,1,0:T(8,128)(2,1)S(1)} %get-tuple-element.58.near, bf16[2,2,16,16,256]{4,3,2,1,0:T(8,128)(2,1)S(1)} %shard_map.87.phases), custom_call_target="tpu_custom_call" | custom-call | bytes 3751936 | tf_op jit(solution)/shard_map/pallas_call | solution.py:28
  17.1 1.3 %collective-permute-start.6 = (bf16[2,288,256]{2,1,0:T(8,128)(2,1)S(1)}, bf16[2,288,256]{2,1,0:T(8,128)(2,1)S(1)}, u32[]{:S(2)}, u32[]{:S(2)}) collective-permute-start(bf16[2,288,256]{2,1,0:T(8,128)(2,1)S(1)} %get-tuple-element.67), channel_id=1, source_target_pairs={{0,8},{4,20},{8,0},{12,28},{16,24},{20,4},{24,16},{28,12},{1,9},{5... | collective-permute-start | bytes 884744 | tf_op jit(solution)/shard_map/ppermute | solution.py:488
  18.7 1.3 %collective-permute-start.7 = (bf16[2,288,256]{2,1,0:T(8,128)(2,1)S(1)}, bf16[2,288,256]{2,1,0:T(8,128)(2,1)S(1)}, u32[]{:S(2)}, u32[]{:S(2)}) collective-permute-start(bf16[2,288,256]{2,1,0:T(8,128)(2,1)S(1)} %get-tuple-element.69), channel_id=1, source_target_pairs={{0,8},{4,20},{8,0},{12,28},{16,24},{20,4},{24,16},{28,12},{1,9},{5... | collective-permute-start | bytes 884744 | tf_op jit(solution)/shard_map/ppermute | solution.py:488
  20.0 0.8 %shard_map.91 = (f32[128,256]{1,0:T(8,128)S(1)}, f32[2,64,128]{2,1,0:T(8,128)S(1)}) custom-call(bf16[12,16,256]{2,1,0:T(8,128)(2,1)S(1)} %get-tuple-element.48.coarse, bf16[24,32,256]{2,1,0:T(8,128)(2,1)S(1)} %get-tuple-element.50.cot, f32[96,256]{1,0:T(8,128)S(1)} %get-tuple-element.70.left, f32[96,256]{1,0:T(8,128)S(1)} %get-tuple-element.54.right, ...), custom_call_target="tpu_custom_call" | custom-call | bytes 3506176 | tf_op jit(solution)/shard_map/pallas_call | solution.py:28
  20.7 3.1 %collective-permute-done.6.got = bf16[2,288,256]{2,1,0:T(8,128)(2,1)S(1)} collective-permute-done((bf16[2,288,256]{2,1,0:T(8,128)(2,1)S(1)}, bf16[2,288,256]{2,1,0:T(8,128)(2,1)S(1)}, u32[]{:S(2)}, u32[]{:S(2)}) %collective-permute-start.6) | collective-permute-done | bytes 294944 | tf_op jit(solution)/shard_map/ppermute | solution.py:488
  23.9 1.7 %collective-permute-start.8 = (bf16[1,288,256]{2,1,0:T(8,128)(2,1)S(1)}, bf16[1,288,256]{2,1,0:T(8,128)(2,1)S(1)}, u32[]{:S(2)}, u32[]{:S(2)}) collective-permute-start(bf16[1,288,256]{2,1,0:T(8,128)(2,1)S(1)} %get-tuple-element.76), channel_id=1, source_target_pairs={{0,16},{4,12},{8,24},{12,4},{16,0},{20,28},{24,8},{28,20},{1,17},{... | collective-permute-start | bytes 442376 | tf_op jit(solution)/shard_map/ppermute | solution.py:488
  25.7 1.8 %shard_map.93 = bf16[24,32,256]{2,1,0:T(8,128)(2,1)} custom-call(bf16[24,32,256]{2,1,0:T(8,128)(2,1)S(1)} %get-tuple-element.57.act, f32[128,256]{1,0:T(8,128)S(1)} %get-tuple-element.77.ring_act, bf16[3,3,256,256]{3,2,1,0:T(8,128)(2,1)S(1)} %get-tuple-element.61.conv_w), custom_call_target="tpu_custom_call" | custom-call | bytes 2097152 | tf_op jit(solution)/shard_map/pallas_call | solution.py:28
  27.5 0.7 %collective-permute-done.7.got = bf16[2,288,256]{2,1,0:T(8,128)(2,1)S(1)} collective-permute-done((bf16[2,288,256]{2,1,0:T(8,128)(2,1)S(1)}, bf16[2,288,256]{2,1,0:T(8,128)(2,1)S(1)}, u32[]{:S(2)}, u32[]{:S(2)}) %collective-permute-start.7) | collective-permute-done | bytes 294944 | tf_op jit(solution)/shard_map/ppermute | solution.py:488
  28.3 1.7 %collective-permute-start.9 = (bf16[1,288,256]{2,1,0:T(8,128)(2,1)S(1)}, bf16[1,288,256]{2,1,0:T(8,128)(2,1)S(1)}, u32[]{:S(2)}, u32[]{:S(2)}) collective-permute-start(bf16[1,288,256]{2,1,0:T(8,128)(2,1)S(1)} %get-tuple-element.81), channel_id=1, source_target_pairs={{0,16},{4,12},{8,24},{12,4},{16,0},{20,28},{24,8},{28,20},{1,17},{... | collective-permute-start | bytes 442376 | tf_op jit(solution)/shard_map/ppermute | solution.py:488
  30.0 1.2 %shard_map.95 = bf16[12,16,256]{2,1,0:T(8,128)(2,1)} custom-call(bf16[2,2,16,16,256]{4,3,2,1,0:T(8,128)(2,1)S(1)} %shard_map.87.phases, f32[2,64,128]{2,1,0:T(8,128)S(1)} %get-tuple-element.82.ring_grad, bf16[3,3,256,256]{3,2,1,0:T(8,128)(2,1)S(1)} %copy-done), custom_call_target="tpu_custom_call" | custom-call | bytes 1867776 | tf_op jit(solution)/shard_map/pallas_call | solution.py:28
  31.3 2.2 %collective-permute-done.9.got_up = bf16[1,288,256]{2,1,0:T(8,128)(2,1)S(1)} collective-permute-done((bf16[1,288,256]{2,1,0:T(8,128)(2,1)S(1)}, bf16[1,288,256]{2,1,0:T(8,128)(2,1)S(1)}, u32[]{:S(2)}, u32[]{:S(2)}) %collective-permute-start.9) | collective-permute-done | bytes 147488 | tf_op jit(solution)/shard_map/ppermute | solution.py:488
  33.8 4.8 %collective-permute-start.10 = (bf16[288,128]{1,0:T(8,128)(2,1)S(1)}, bf16[288,128]{1,0:T(8,128)(2,1)S(1)}, u32[]{:S(2)}, u32[]{:S(2)}) collective-permute-start(bf16[288,128]{1,0:T(8,128)(2,1)S(1)} %get-tuple-element.87), channel_id=1, source_target_pairs={{0,1},{1,2},{2,3},{3,0},{4,5},{5,6},{6,7},{7,4},{8,9},{9,10},{10,1... | collective-permute-start | bytes 221192 | tf_op jit(solution)/shard_map/ppermute | solution.py:507
  38.6 1.5 %collective-permute-start.11 = (bf16[288,128]{1,0:T(8,128)(2,1)S(1)}, bf16[288,128]{1,0:T(8,128)(2,1)S(1)}, u32[]{:S(2)}, u32[]{:S(2)}) collective-permute-start(bf16[288,128]{1,0:T(8,128)(2,1)S(1)} %get-tuple-element.88), channel_id=1, source_target_pairs={{0,2},{1,3},{2,0},{3,1},{4,6},{5,7},{6,4},{7,5},{8,10},{9,11},{10,... | collective-permute-start | bytes 221192 | tf_op jit(solution)/shard_map/ppermute | solution.py:507
  40.2 2.8 %collective-permute-start.12 = (bf16[288,128]{1,0:T(8,128)(2,1)S(1)}, bf16[288,128]{1,0:T(8,128)(2,1)S(1)}, u32[]{:S(2)}, u32[]{:S(2)}) collective-permute-start(bf16[288,128]{1,0:T(8,128)(2,1)S(1)} %get-tuple-element.89), channel_id=1, source_target_pairs={{0,3},{1,0},{2,1},{3,2},{4,7},{5,4},{6,5},{7,6},{8,11},{9,8},{10,9... | collective-permute-start | bytes 221192 | tf_op jit(solution)/shard_map/ppermute | solution.py:507
  43.0 0.9 %collective-permute-done.11.refs_1_ = bf16[288,128]{1,0:T(8,128)(2,1)S(1)} collective-permute-done((bf16[288,128]{1,0:T(8,128)(2,1)S(1)}, bf16[288,128]{1,0:T(8,128)(2,1)S(1)}, u32[]{:S(2)}, u32[]{:S(2)}) %collective-permute-start.11) | collective-permute-done | bytes 73760 | tf_op jit(solution)/shard_map/ppermute | solution.py:507
  43.9 1.1 %collective-permute-done.12.refs_2_ = bf16[288,128]{1,0:T(8,128)(2,1)S(1)} collective-permute-done((bf16[288,128]{1,0:T(8,128)(2,1)S(1)}, bf16[288,128]{1,0:T(8,128)(2,1)S(1)}, u32[]{:S(2)}, u32[]{:S(2)}) %collective-permute-start.12) | collective-permute-done | bytes 73760 | tf_op jit(solution)/shard_map/ppermute | solution.py:507
  45.0 0.8 %shard_map.97 = (f32[64,288]{1,0:T(8,128)}, f32[64,288]{1,0:T(8,128)}) custom-call(f32[288,128]{1,0:T(8,128)S(1)} %get-tuple-element.86.own, bf16[288,128]{1,0:T(8,128)(2,1)S(1)} %collective-permute-done.10.refs_0_, bf16[288,128]{1,0:T(8,128)(2,1)S(1)} %collective-permute-done.11.refs_1_, bf16[288,128]{1,0:T(8,128)(2,1)S(1)} %collective-permute-done.12.refs_2_), custom_call_target="tpu_custom_call" | custom-call | bytes 516096 | tf_op jit(solution)/shard_map/pallas_call | solution.py:28
  (18 shorter events, 2.8 us)
Async XLA Ops:
  0.6 11.6 %copy-start = (bf16[3,3,256,256]{3,2,1,0:T(8,128)(2,1)S(1)}, bf16[3,3,256,256]{3,2,1,0:T(8,128)(2,1)}, u32[]{:S(2)}) copy-start(bf16[3,3,256,256]{3,2,1,0:T(8,128)(2,1)} %up_w.5) | copy-start | bytes 3538948
  2.0 4.1 %collective-permute-start = (bf16[96,256]{1,0:T(8,128)(2,1)S(1)}, bf16[96,256]{1,0:T(8,128)(2,1)S(1)}, u32[]{:S(2)}, u32[]{:S(2)}) collective-permute-start(bf16[96,256]{1,0:T(8,128)(2,1)S(1)} %get-tuple-element.51), channel_id=1, source_target_pairs={{0,4},{4,0},{8,12},{12,8},{16,20},{20,16},{24,28},{28,24},{1,5},{5... | collective-permute-start | bytes 147464 | tf_op jit(solution)/shard_map/ppermute | solution.py:519
  2.5 5.3 %collective-permute-start.1 = (bf16[96,256]{1,0:T(8,128)(2,1)S(1)}, bf16[96,256]{1,0:T(8,128)(2,1)S(1)}, u32[]{:S(2)}, u32[]{:S(2)}) collective-permute-start(bf16[96,256]{1,0:T(8,128)(2,1)S(1)} %get-tuple-element.52), channel_id=1, source_target_pairs={{0,28},{4,8},{8,4},{12,16},{16,12},{20,24},{24,20},{28,0},{1,29},{... | collective-permute-start | bytes 147464 | tf_op jit(solution)/shard_map/ppermute | solution.py:519
  7.9 4.3 %collective-permute-start.2 = (bf16[128,256]{1,0:T(8,128)(2,1)S(1)}, bf16[128,256]{1,0:T(8,128)(2,1)S(1)}, u32[]{:S(2)}, u32[]{:S(2)}) collective-permute-start(bf16[128,256]{1,0:T(8,128)(2,1)S(1)} %get-tuple-element.55), channel_id=1, source_target_pairs={{0,1},{1,0},{2,3},{3,2},{4,5},{5,4},{6,7},{7,6},{8,9},{9,8},{10,11... | collective-permute-start | bytes 196616 | tf_op jit(solution)/shard_map/ppermute | solution.py:519
  9.7 2.5 %collective-permute-start.3 = (bf16[128,256]{1,0:T(8,128)(2,1)S(1)}, bf16[128,256]{1,0:T(8,128)(2,1)S(1)}, u32[]{:S(2)}, u32[]{:S(2)}) collective-permute-start(bf16[128,256]{1,0:T(8,128)(2,1)S(1)} %get-tuple-element.56), channel_id=1, source_target_pairs={{1,2},{2,1},{5,6},{6,5},{9,10},{10,9},{13,14},{14,13},{17,18},{18,... | collective-permute-start | bytes 196616 | tf_op jit(solution)/shard_map/ppermute | solution.py:519
  14.4 2.6 %collective-permute-start.4 = (bf16[4,288,256]{2,1,0:T(8,128)(2,1)S(1)}, bf16[4,288,256]{2,1,0:T(8,128)(2,1)S(1)}, u32[]{:S(2)}, u32[]{:S(2)}) collective-permute-start(bf16[4,288,256]{2,1,0:T(8,128)(2,1)S(1)} %get-tuple-element.66), channel_id=1, source_target_pairs={{0,4},{4,0},{8,12},{12,8},{16,20},{20,16},{24,28},{28,24},{1,5},{5... | collective-permute-start | bytes 1769480 | tf_op jit(solution)/shard_map/ppermute | solution.py:480
  16.4 2.2 %collective-permute-start.5 = (bf16[4,288,256]{2,1,0:T(8,128)(2,1)S(1)}, bf16[4,288,256]{2,1,0:T(8,128)(2,1)S(1)}, u32[]{:S(2)}, u32[]{:S(2)}) collective-permute-start(bf16[4,288,256]{2,1,0:T(8,128)(2,1)S(1)} %get-tuple-element.64), channel_id=1, source_target_pairs={{0,4},{4,0},{8,12},{12,8},{16,20},{20,16},{24,28},{28,24},{1,5},{5... | collective-permute-start | bytes 1769480 | tf_op jit(solution)/shard_map/ppermute | solution.py:480
  17.1 6.8 %collective-permute-start.6 = (bf16[2,288,256]{2,1,0:T(8,128)(2,1)S(1)}, bf16[2,288,256]{2,1,0:T(8,128)(2,1)S(1)}, u32[]{:S(2)}, u32[]{:S(2)}) collective-permute-start(bf16[2,288,256]{2,1,0:T(8,128)(2,1)S(1)} %get-tuple-element.67), channel_id=1, source_target_pairs={{0,8},{4,20},{8,0},{12,28},{16,24},{20,4},{24,16},{28,12},{1,9},{5... | collective-permute-start | bytes 884744 | tf_op jit(solution)/shard_map/ppermute | solution.py:488
  18.7 9.5 %collective-permute-start.7 = (bf16[2,288,256]{2,1,0:T(8,128)(2,1)S(1)}, bf16[2,288,256]{2,1,0:T(8,128)(2,1)S(1)}, u32[]{:S(2)}, u32[]{:S(2)}) collective-permute-start(bf16[2,288,256]{2,1,0:T(8,128)(2,1)S(1)} %get-tuple-element.69), channel_id=1, source_target_pairs={{0,8},{4,20},{8,0},{12,28},{16,24},{20,4},{24,16},{28,12},{1,9},{5... | collective-permute-start | bytes 884744 | tf_op jit(solution)/shard_map/ppermute | solution.py:488
  23.9 7.3 %collective-permute-start.8 = (bf16[1,288,256]{2,1,0:T(8,128)(2,1)S(1)}, bf16[1,288,256]{2,1,0:T(8,128)(2,1)S(1)}, u32[]{:S(2)}, u32[]{:S(2)}) collective-permute-start(bf16[1,288,256]{2,1,0:T(8,128)(2,1)S(1)} %get-tuple-element.76), channel_id=1, source_target_pairs={{0,16},{4,12},{8,24},{12,4},{16,0},{20,28},{24,8},{28,20},{1,17},{... | collective-permute-start | bytes 442376 | tf_op jit(solution)/shard_map/ppermute | solution.py:488
  28.3 5.2 %collective-permute-start.9 = (bf16[1,288,256]{2,1,0:T(8,128)(2,1)S(1)}, bf16[1,288,256]{2,1,0:T(8,128)(2,1)S(1)}, u32[]{:S(2)}, u32[]{:S(2)}) collective-permute-start(bf16[1,288,256]{2,1,0:T(8,128)(2,1)S(1)} %get-tuple-element.81), channel_id=1, source_target_pairs={{0,16},{4,12},{8,24},{12,4},{16,0},{20,28},{24,8},{28,20},{1,17},{... | collective-permute-start | bytes 442376 | tf_op jit(solution)/shard_map/ppermute | solution.py:488
  33.8 9.2 %collective-permute-start.10 = (bf16[288,128]{1,0:T(8,128)(2,1)S(1)}, bf16[288,128]{1,0:T(8,128)(2,1)S(1)}, u32[]{:S(2)}, u32[]{:S(2)}) collective-permute-start(bf16[288,128]{1,0:T(8,128)(2,1)S(1)} %get-tuple-element.87), channel_id=1, source_target_pairs={{0,1},{1,2},{2,3},{3,0},{4,5},{5,6},{6,7},{7,4},{8,9},{9,10},{10,1... | collective-permute-start | bytes 221192 | tf_op jit(solution)/shard_map/ppermute | solution.py:507
  38.6 5.3 %collective-permute-start.11 = (bf16[288,128]{1,0:T(8,128)(2,1)S(1)}, bf16[288,128]{1,0:T(8,128)(2,1)S(1)}, u32[]{:S(2)}, u32[]{:S(2)}) collective-permute-start(bf16[288,128]{1,0:T(8,128)(2,1)S(1)} %get-tuple-element.88), channel_id=1, source_target_pairs={{0,2},{1,3},{2,0},{3,1},{4,6},{5,7},{6,4},{7,5},{8,10},{9,11},{10,... | collective-permute-start | bytes 221192 | tf_op jit(solution)/shard_map/ppermute | solution.py:507
  40.2 4.8 %collective-permute-start.12 = (bf16[288,128]{1,0:T(8,128)(2,1)S(1)}, bf16[288,128]{1,0:T(8,128)(2,1)S(1)}, u32[]{:S(2)}, u32[]{:S(2)}) collective-permute-start(bf16[288,128]{1,0:T(8,128)(2,1)S(1)} %get-tuple-element.89), channel_id=1, source_target_pairs={{0,3},{1,0},{2,1},{3,2},{4,7},{5,4},{6,5},{7,6},{8,11},{9,8},{10,9... | collective-permute-start | bytes 221192 | tf_op jit(solution)/shard_map/ppermute | solution.py:507

commit v8 on v7

--- a/solution.py
+++ b/solution.py
@@ -170,7 +170,7 @@
 
 
 def act_kernel(
-    coarse, skip, cot, left, right, got_first, got_second, up_w, conv_w,
+    coarse, skip, cot, left, right, got_second, got_first, up_w, conv_w,
     shifted, near, act, slope, partial, send, upper, lower, conv_v, padded, pre, sem,
 ):
     n_rows, n_cols, channels = coarse.shape
@@ -560,7 +560,7 @@
             sds(conv_weight.shape, bf16),
         ],
         [padded, flat, pltpu.SemaphoreType.DMA],
-        0, coarse, skip, cotangent, left, right, first, second, up_weight, conv_weight, far=(8,),
+        0, coarse, skip, cotangent, left, right, second, first, up_weight, conv_weight, far=(8,),
     )
     phases = kernel_call(
         grad_kernel, [sds((2, 2, whole, n_cols, channels), bf16)], [flat],

time: 46 us -> 46 us (level)
  waiting for transfers between devices: 12 us -> 13.8 us
  starting transfers between devices: 22.3 us -> 20.6 us
    ppermute x3, starting transfers between devices: 9.18 us -> 4.89 us  [band_sum(): lax.ppermute(messages[k - 1], 'band', [(i, (i + k) % bands) for i in rang...]
    ppermute x4, starting transfers between devices: 6.53 us -> 9.36 us  [swap(): return (lax.ppermute(first, axis, one), lax.ppermute(second, axis, two))]
    ppermute x3, waiting for transfers between devices: 1.98 us -> 3.12 us  [band_sum(): lax.ppermute(messages[k - 1], 'band', [(i, (i + k) % bands) for i in rang...]
where the time goes in v8:
time: 46 us; the launch traced here: 45.8 us
  starting transfers between devices  20.6 us (45%)
  waiting for transfers between devices  13.8 us (30%)
  Pallas kernels  10.7 us (23%)
  between operations  0.72 us (2%)
    pallas_call x14, Pallas kernels, kernel_call(): pl.pallas_call(body, out_shape=tuple(outs), in_specs=[hbm if i in far els...  10.7 us
    ppermute x4, starting transfers between devices, swap(): return (lax.ppermute(first, axis, one), lax.ppermute(second, axis, two))  9.36 us
    ppermute x4, waiting for transfers between devices, plane_swap(): lax.ppermute(message, 'face', [(i, i ^ 2 << orders[i % 2][step]) for i in...  6.22 us
    ppermute x4, starting transfers between devices, plane_swap(): lax.ppermute(message, 'face', [(i, i ^ 2 << orders[i % 2][step]) for i in...  5.72 us
    ppermute x3, starting transfers between devices, band_sum(): lax.ppermute(messages[k - 1], 'band', [(i, (i + k) % bands) for i in rang...  4.89 us
    ppermute x4, waiting for transfers between devices, swap(): return (lax.ppermute(first, axis, one), lax.ppermute(second, axis, two))  4.02 us
    ppermute x3, waiting for transfers between devices, band_sum(): lax.ppermute(messages[k - 1], 'band', [(i, (i + k) % bands) for i in rang...  3.12 us
  transfers between devices with their start and end apart: 13, of which 8 were waited for; matrix products, arithmetic and copies ran while one was open for 0% of the time, Pallas kernels for 13%

profile of v8, /device:TPU:0, one launch (start us, length us, event | category | flops | bytes accessed | tf_op | source)
XLA Modules:
  0.0 45.8 jit_solution(12943764392270284308)
XLA Ops:
  0.6 1.3 %shard_map.84 = (bf16[96,256]{1,0:T(8,128)(2,1)S(1)}, bf16[96,256]{1,0:T(8,128)(2,1)S(1)}, bf16[24,32,256]{2,1,0:T(8,128)(2,1)S(1)}, bf16[24,32,256]{2,1,0:T(8,128)(2,1)S(1)}, bf16[12,16,256]{2,1,0:T(8,128)(2,1)S(1)}) custom-call(bf16[12,16,256]{2,1,0:T(8,128)(2,1)} %coarse.1, bf16[24,32,256]{2,1,0:T(8,128)(2,1)} %skip.1, bf16[24,32,256]{2,1,0:T(8,128)(2,1)} %cot.1), custom_call_target="tpu_custom_call" | custom-call | bytes 1867776 | tf_op jit(solution)/shard_map/pallas_call | solution.py:28
  2.5 3.6 %collective-permute-start.1 = (bf16[96,256]{1,0:T(8,128)(2,1)S(1)}, bf16[96,256]{1,0:T(8,128)(2,1)S(1)}, u32[]{:S(2)}, u32[]{:S(2)}) collective-permute-start(bf16[96,256]{1,0:T(8,128)(2,1)S(1)} %get-tuple-element.52), channel_id=1, source_target_pairs={{0,28},{4,8},{8,4},{12,16},{16,12},{20,24},{24,20},{28,0},{1,29},{... | collective-permute-start | bytes 147464 | tf_op jit(solution)/shard_map/ppermute | solution.py:519
  6.0 1.8 %collective-permute-done.1.got_second = bf16[96,256]{1,0:T(8,128)(2,1)S(1)} collective-permute-done((bf16[96,256]{1,0:T(8,128)(2,1)S(1)}, bf16[96,256]{1,0:T(8,128)(2,1)S(1)}, u32[]{:S(2)}, u32[]{:S(2)}) %collective-permute-start.1) | collective-permute-done | bytes 49184 | tf_op jit(solution)/shard_map/ppermute | solution.py:519
  7.9 0.7 %collective-permute-start.2 = (bf16[128,256]{1,0:T(8,128)(2,1)S(1)}, bf16[128,256]{1,0:T(8,128)(2,1)S(1)}, u32[]{:S(2)}, u32[]{:S(2)}) collective-permute-start(bf16[128,256]{1,0:T(8,128)(2,1)S(1)} %get-tuple-element.55), channel_id=1, source_target_pairs={{1,2},{2,1},{5,6},{6,5},{9,10},{10,9},{13,14},{14,13},{17,18},{18,... | collective-permute-start | bytes 196616 | tf_op jit(solution)/shard_map/ppermute | solution.py:519
  8.5 4.6 %collective-permute-start.3 = (bf16[128,256]{1,0:T(8,128)(2,1)S(1)}, bf16[128,256]{1,0:T(8,128)(2,1)S(1)}, u32[]{:S(2)}, u32[]{:S(2)}) collective-permute-start(bf16[128,256]{1,0:T(8,128)(2,1)S(1)} %get-tuple-element.56), channel_id=1, source_target_pairs={{0,1},{1,0},{2,3},{3,2},{4,5},{5,4},{6,7},{7,6},{8,9},{9,8},{10,11... | collective-permute-start | bytes 196616 | tf_op jit(solution)/shard_map/ppermute | solution.py:519
  13.2 2.2 %collective-permute-done.3.got_first = bf16[128,256]{1,0:T(8,128)(2,1)S(1)} collective-permute-done((bf16[128,256]{1,0:T(8,128)(2,1)S(1)}, bf16[128,256]{1,0:T(8,128)(2,1)S(1)}, u32[]{:S(2)}, u32[]{:S(2)}) %collective-permute-start.3) | collective-permute-done | bytes 65568 | tf_op jit(solution)/shard_map/ppermute | solution.py:519
  15.4 2.2 %shard_map.86 = (bf16[3,26,32,256]{3,2,1,0:T(8,128)(2,1)S(1)}, bf16[2,17,16,256]{3,2,1,0:T(8,128)(2,1)S(1)}, bf16[24,32,256]{2,1,0:T(8,128)(2,1)S(1)}, f32[768,2...) custom-call(bf16[12,16,256]{2,1,0:T(8,128)(2,1)S(1)} %get-tuple-elem, ...), custom_call_target="tpu_custom_call" | custom-call | bytes 10698752 | tf_op jit(solution)/shard_map/pallas_call | solution.py:28
  17.7 1.2 %shard_map.87.phases = bf16[2,2,16,16,256]{4,3,2,1,0:T(8,128)(2,1)S(1)} custom-call(bf16[3,26,32,256]{3,2,1,0:T(8,128)(2,1)S(1)} %get-tuple-element.59.shifted, f32[768,256]{1,0:T(8,128)S(1)} %get-tuple-element.60.slope, bf16[3,3,256,256]{3,2,1,0:T(8,128)(2,1)S(1)} %get-tuple-element.61.conv_w), custom_call_target="tpu_custom_call" | custom-call | bytes 3768320 | tf_op jit(solution)/shard_map/pallas_call | solution.py:28
  18.9 0.8 %shard_map.88 = (f32[2304,256]{1,0:T(8,128)S(1)}, bf16[4,288,256]{2,1,0:T(8,128)(2,1)S(1)}) custom-call(bf16[2,17,16,256]{3,2,1,0:T(8,128)(2,1)S(1)} %get-tuple-element.58.near, bf16[2,2,16,16,256]{4,3,2,1,0:T(8,128)(2,1)S(1)} %shard_map.87.phases), custom_call_target="tpu_custom_call" | custom-call | bytes 3751936 | tf_op jit(solution)/shard_map/pallas_call | solution.py:28
  20.3 1.1 %collective-permute-start.6 = (bf16[2,288,256]{2,1,0:T(8,128)(2,1)S(1)}, bf16[2,288,256]{2,1,0:T(8,128)(2,1)S(1)}, u32[]{:S(2)}, u32[]{:S(2)}) collective-permute-start(bf16[2,288,256]{2,1,0:T(8,128)(2,1)S(1)} %get-tuple-element.67), channel_id=1, source_target_pairs={{0,8},{4,20},{8,0},{12,28},{16,24},{20,4},{24,16},{28,12},{1,9},{5... | collective-permute-start | bytes 884744 | tf_op jit(solution)/shard_map/ppermute | solution.py:488
  21.9 1.1 %collective-permute-start.7 = (bf16[2,288,256]{2,1,0:T(8,128)(2,1)S(1)}, bf16[2,288,256]{2,1,0:T(8,128)(2,1)S(1)}, u32[]{:S(2)}, u32[]{:S(2)}) collective-permute-start(bf16[2,288,256]{2,1,0:T(8,128)(2,1)S(1)} %get-tuple-element.69), channel_id=1, source_target_pairs={{0,8},{4,20},{8,0},{12,28},{16,24},{20,4},{24,16},{28,12},{1,9},{5... | collective-permute-start | bytes 884744 | tf_op jit(solution)/shard_map/ppermute | solution.py:488
  23.0 0.8 %shard_map.91 = (f32[128,256]{1,0:T(8,128)S(1)}, f32[2,64,128]{2,1,0:T(8,128)S(1)}) custom-call(bf16[12,16,256]{2,1,0:T(8,128)(2,1)S(1)} %get-tuple-element.48.coarse, bf16[24,32,256]{2,1,0:T(8,128)(2,1)S(1)} %get-tuple-element.50.cot, f32[96,256]{1,0:T(8,128)S(1)} %get-tuple-element.70.left, f32[96,256]{1,0:T(8,128)S(1)} %get-tuple-element.54.right, ...), custom_call_target="tpu_custom_call" | custom-call | bytes 3506176 | tf_op jit(solution)/shard_map/pallas_call | solution.py:28
  23.8 3.3 %collective-permute-done.6.got = bf16[2,288,256]{2,1,0:T(8,128)(2,1)S(1)} collective-permute-done((bf16[2,288,256]{2,1,0:T(8,128)(2,1)S(1)}, bf16[2,288,256]{2,1,0:T(8,128)(2,1)S(1)}, u32[]{:S(2)}, u32[]{:S(2)}) %collective-permute-start.6) | collective-permute-done | bytes 294944 | tf_op jit(solution)/shard_map/ppermute | solution.py:488
  27.1 1.8 %collective-permute-start.8 = (bf16[1,288,256]{2,1,0:T(8,128)(2,1)S(1)}, bf16[1,288,256]{2,1,0:T(8,128)(2,1)S(1)}, u32[]{:S(2)}, u32[]{:S(2)}) collective-permute-start(bf16[1,288,256]{2,1,0:T(8,128)(2,1)S(1)} %get-tuple-element.76), channel_id=1, source_target_pairs={{0,16},{4,12},{8,24},{12,4},{16,0},{20,28},{24,8},{28,20},{1,17},{... | collective-permute-start | bytes 442376 | tf_op jit(solution)/shard_map/ppermute | solution.py:488
  28.9 1.8 %shard_map.93 = bf16[24,32,256]{2,1,0:T(8,128)(2,1)} custom-call(bf16[24,32,256]{2,1,0:T(8,128)(2,1)S(1)} %get-tuple-element.57.act, f32[128,256]{1,0:T(8,128)S(1)} %get-tuple-element.77.ring_act, bf16[3,3,256,256]{3,2,1,0:T(8,128)(2,1)S(1)} %get-tuple-element.61.conv_w), custom_call_target="tpu_custom_call" | custom-call | bytes 2097152 | tf_op jit(solution)/shard_map/pallas_call | solution.py:28
  30.8 0.7 %collective-permute-done.7.got = bf16[2,288,256]{2,1,0:T(8,128)(2,1)S(1)} collective-permute-done((bf16[2,288,256]{2,1,0:T(8,128)(2,1)S(1)}, bf16[2,288,256]{2,1,0:T(8,128)(2,1)S(1)}, u32[]{:S(2)}, u32[]{:S(2)}) %collective-permute-start.7) | collective-permute-done | bytes 294944 | tf_op jit(solution)/shard_map/ppermute | solution.py:488
  31.5 1.8 %collective-permute-start.9 = (bf16[1,288,256]{2,1,0:T(8,128)(2,1)S(1)}, bf16[1,288,256]{2,1,0:T(8,128)(2,1)S(1)}, u32[]{:S(2)}, u32[]{:S(2)}) collective-permute-start(bf16[1,288,256]{2,1,0:T(8,128)(2,1)S(1)} %get-tuple-element.81), channel_id=1, source_target_pairs={{0,16},{4,12},{8,24},{12,4},{16,0},{20,28},{24,8},{28,20},{1,17},{... | collective-permute-start | bytes 442376 | tf_op jit(solution)/shard_map/ppermute | solution.py:488
  33.3 1.2 %shard_map.95 = bf16[12,16,256]{2,1,0:T(8,128)(2,1)} custom-call(bf16[2,2,16,16,256]{4,3,2,1,0:T(8,128)(2,1)S(1)} %shard_map.87.phases, f32[2,64,128]{2,1,0:T(8,128)S(1)} %get-tuple-element.82.ring_grad, bf16[3,3,256,256]{3,2,1,0:T(8,128)(2,1)S(1)} %copy-done), custom_call_target="tpu_custom_call" | custom-call | bytes 1867776 | tf_op jit(solution)/shard_map/pallas_call | solution.py:28
  34.5 2.2 %collective-permute-done.9.got_up = bf16[1,288,256]{2,1,0:T(8,128)(2,1)S(1)} collective-permute-done((bf16[1,288,256]{2,1,0:T(8,128)(2,1)S(1)}, bf16[1,288,256]{2,1,0:T(8,128)(2,1)S(1)}, u32[]{:S(2)}, u32[]{:S(2)}) %collective-permute-start.9) | collective-permute-done | bytes 147488 | tf_op jit(solution)/shard_map/ppermute | solution.py:488
  37.0 2.1 %collective-permute-start.10 = (bf16[288,128]{1,0:T(8,128)(2,1)S(1)}, bf16[288,128]{1,0:T(8,128)(2,1)S(1)}, u32[]{:S(2)}, u32[]{:S(2)}) collective-permute-start(bf16[288,128]{1,0:T(8,128)(2,1)S(1)} %get-tuple-element.87), channel_id=1, source_target_pairs={{0,1},{1,2},{2,3},{3,0},{4,5},{5,6},{6,7},{7,4},{8,9},{9,10},{10,1... | collective-permute-start | bytes 221192 | tf_op jit(solution)/shard_map/ppermute | solution.py:507
  39.1 2.8 %collective-permute-start.12 = (bf16[288,128]{1,0:T(8,128)(2,1)S(1)}, bf16[288,128]{1,0:T(8,128)(2,1)S(1)}, u32[]{:S(2)}, u32[]{:S(2)}) collective-permute-start(bf16[288,128]{1,0:T(8,128)(2,1)S(1)} %get-tuple-element.89), channel_id=1, source_target_pairs={{0,3},{1,0},{2,1},{3,2},{4,7},{5,4},{6,5},{7,6},{8,11},{9,8},{10,9... | collective-permute-start | bytes 221192 | tf_op jit(solution)/shard_map/ppermute | solution.py:507
  41.9 1.3 %collective-permute-done.10.refs_0_ = bf16[288,128]{1,0:T(8,128)(2,1)S(1)} collective-permute-done((bf16[288,128]{1,0:T(8,128)(2,1)S(1)}, bf16[288,128]{1,0:T(8,128)(2,1)S(1)}, u32[]{:S(2)}, u32[]{:S(2)}) %collective-permute-start.10) | collective-permute-done | bytes 73760 | tf_op jit(solution)/shard_map/ppermute | solution.py:507
  43.3 1.8 %collective-permute-done.11.refs_1_ = bf16[288,128]{1,0:T(8,128)(2,1)S(1)} collective-permute-done((bf16[288,128]{1,0:T(8,128)(2,1)S(1)}, bf16[288,128]{1,0:T(8,128)(2,1)S(1)}, u32[]{:S(2)}, u32[]{:S(2)}) %collective-permute-start.11) | collective-permute-done | bytes 73760 | tf_op jit(solution)/shard_map/ppermute | solution.py:507
  45.0 0.8 %shard_map.97 = (f32[64,288]{1,0:T(8,128)}, f32[64,288]{1,0:T(8,128)}) custom-call(f32[288,128]{1,0:T(8,128)S(1)} %get-tuple-element.86.own, bf16[288,128]{1,0:T(8,128)(2,1)S(1)} %collective-permute-done.10.refs_0_, bf16[288,128]{1,0:T(8,128)(2,1)S(1)} %collective-permute-done.11.refs_1_, bf16[288,128]{1,0:T(8,128)(2,1)S(1)} %collective-permute-done.12.refs_2_), custom_call_target="tpu_custom_call" | custom-call | bytes 516096 | tf_op jit(solution)/shard_map/pallas_call | solution.py:28
  (18 shorter events, 2.3 us)
Async XLA Ops:
  0.6 14.8 %copy-start = (bf16[3,3,256,256]{3,2,1,0:T(8,128)(2,1)S(1)}, bf16[3,3,256,256]{3,2,1,0:T(8,128)(2,1)}, u32[]{:S(2)}) copy-start(bf16[3,3,256,256]{3,2,1,0:T(8,128)(2,1)} %up_w.5) | copy-start | bytes 3538948
  2.0 4.1 %collective-permute-start = (bf16[96,256]{1,0:T(8,128)(2,1)S(1)}, bf16[96,256]{1,0:T(8,128)(2,1)S(1)}, u32[]{:S(2)}, u32[]{:S(2)}) collective-permute-start(bf16[96,256]{1,0:T(8,128)(2,1)S(1)} %get-tuple-element.51), channel_id=1, source_target_pairs={{0,4},{4,0},{8,12},{12,8},{16,20},{20,16},{24,28},{28,24},{1,5},{5... | collective-permute-start | bytes 147464 | tf_op jit(solution)/shard_map/ppermute | solution.py:519
  2.5 5.3 %collective-permute-start.1 = (bf16[96,256]{1,0:T(8,128)(2,1)S(1)}, bf16[96,256]{1,0:T(8,128)(2,1)S(1)}, u32[]{:S(2)}, u32[]{:S(2)}) collective-permute-start(bf16[96,256]{1,0:T(8,128)(2,1)S(1)} %get-tuple-element.52), channel_id=1, source_target_pairs={{0,28},{4,8},{8,4},{12,16},{16,12},{20,24},{24,20},{28,0},{1,29},{... | collective-permute-start | bytes 147464 | tf_op jit(solution)/shard_map/ppermute | solution.py:519
  7.9 5.3 %collective-permute-start.2 = (bf16[128,256]{1,0:T(8,128)(2,1)S(1)}, bf16[128,256]{1,0:T(8,128)(2,1)S(1)}, u32[]{:S(2)}, u32[]{:S(2)}) collective-permute-start(bf16[128,256]{1,0:T(8,128)(2,1)S(1)} %get-tuple-element.55), channel_id=1, source_target_pairs={{1,2},{2,1},{5,6},{6,5},{9,10},{10,9},{13,14},{14,13},{17,18},{18,... | collective-permute-start | bytes 196616 | tf_op jit(solution)/shard_map/ppermute | solution.py:519
  8.5 6.9 %collective-permute-start.3 = (bf16[128,256]{1,0:T(8,128)(2,1)S(1)}, bf16[128,256]{1,0:T(8,128)(2,1)S(1)}, u32[]{:S(2)}, u32[]{:S(2)}) collective-permute-start(bf16[128,256]{1,0:T(8,128)(2,1)S(1)} %get-tuple-element.56), channel_id=1, source_target_pairs={{0,1},{1,0},{2,3},{3,2},{4,5},{5,4},{6,7},{7,6},{8,9},{9,8},{10,11... | collective-permute-start | bytes 196616 | tf_op jit(solution)/shard_map/ppermute | solution.py:519
  17.6 2.6 %collective-permute-start.4 = (bf16[4,288,256]{2,1,0:T(8,128)(2,1)S(1)}, bf16[4,288,256]{2,1,0:T(8,128)(2,1)S(1)}, u32[]{:S(2)}, u32[]{:S(2)}) collective-permute-start(bf16[4,288,256]{2,1,0:T(8,128)(2,1)S(1)} %get-tuple-element.66), channel_id=1, source_target_pairs={{0,4},{4,0},{8,12},{12,8},{16,20},{20,16},{24,28},{28,24},{1,5},{5... | collective-permute-start | bytes 1769480 | tf_op jit(solution)/shard_map/ppermute | solution.py:480
  19.6 2.2 %collective-permute-start.5 = (bf16[4,288,256]{2,1,0:T(8,128)(2,1)S(1)}, bf16[4,288,256]{2,1,0:T(8,128)(2,1)S(1)}, u32[]{:S(2)}, u32[]{:S(2)}) collective-permute-start(bf16[4,288,256]{2,1,0:T(8,128)(2,1)S(1)} %get-tuple-element.64), channel_id=1, source_target_pairs={{0,4},{4,0},{8,12},{12,8},{16,20},{20,16},{24,28},{28,24},{1,5},{5... | collective-permute-start | bytes 1769480 | tf_op jit(solution)/shard_map/ppermute | solution.py:480
  20.3 6.8 %collective-permute-start.6 = (bf16[2,288,256]{2,1,0:T(8,128)(2,1)S(1)}, bf16[2,288,256]{2,1,0:T(8,128)(2,1)S(1)}, u32[]{:S(2)}, u32[]{:S(2)}) collective-permute-start(bf16[2,288,256]{2,1,0:T(8,128)(2,1)S(1)} %get-tuple-element.67), channel_id=1, source_target_pairs={{0,8},{4,20},{8,0},{12,28},{16,24},{20,4},{24,16},{28,12},{1,9},{5... | collective-permute-start | bytes 884744 | tf_op jit(solution)/shard_map/ppermute | solution.py:488
  21.9 9.5 %collective-permute-start.7 = (bf16[2,288,256]{2,1,0:T(8,128)(2,1)S(1)}, bf16[2,288,256]{2,1,0:T(8,128)(2,1)S(1)}, u32[]{:S(2)}, u32[]{:S(2)}) collective-permute-start(bf16[2,288,256]{2,1,0:T(8,128)(2,1)S(1)} %get-tuple-element.69), channel_id=1, source_target_pairs={{0,8},{4,20},{8,0},{12,28},{16,24},{20,4},{24,16},{28,12},{1,9},{5... | collective-permute-start | bytes 884744 | tf_op jit(solution)/shard_map/ppermute | solution.py:488
  27.1 7.3 %collective-permute-start.8 = (bf16[1,288,256]{2,1,0:T(8,128)(2,1)S(1)}, bf16[1,288,256]{2,1,0:T(8,128)(2,1)S(1)}, u32[]{:S(2)}, u32[]{:S(2)}) collective-permute-start(bf16[1,288,256]{2,1,0:T(8,128)(2,1)S(1)} %get-tuple-element.76), channel_id=1, source_target_pairs={{0,16},{4,12},{8,24},{12,4},{16,0},{20,28},{24,8},{28,20},{1,17},{... | collective-permute-start | bytes 442376 | tf_op jit(solution)/shard_map/ppermute | solution.py:488
  31.5 5.2 %collective-permute-start.9 = (bf16[1,288,256]{2,1,0:T(8,128)(2,1)S(1)}, bf16[1,288,256]{2,1,0:T(8,128)(2,1)S(1)}, u32[]{:S(2)}, u32[]{:S(2)}) collective-permute-start(bf16[1,288,256]{2,1,0:T(8,128)(2,1)S(1)} %get-tuple-element.81), channel_id=1, source_target_pairs={{0,16},{4,12},{8,24},{12,4},{16,0},{20,28},{24,8},{28,20},{1,17},{... | collective-permute-start | bytes 442376 | tf_op jit(solution)/shard_map/ppermute | solution.py:488
  37.0 6.2 %collective-permute-start.10 = (bf16[288,128]{1,0:T(8,128)(2,1)S(1)}, bf16[288,128]{1,0:T(8,128)(2,1)S(1)}, u32[]{:S(2)}, u32[]{:S(2)}) collective-permute-start(bf16[288,128]{1,0:T(8,128)(2,1)S(1)} %get-tuple-element.87), channel_id=1, source_target_pairs={{0,1},{1,2},{2,3},{3,0},{4,5},{5,6},{6,7},{7,4},{8,9},{9,10},{10,1... | collective-permute-start | bytes 221192 | tf_op jit(solution)/shard_map/ppermute | solution.py:507
  39.1 5.9 %collective-permute-start.11 = (bf16[288,128]{1,0:T(8,128)(2,1)S(1)}, bf16[288,128]{1,0:T(8,128)(2,1)S(1)}, u32[]{:S(2)}, u32[]{:S(2)}) collective-permute-start(bf16[288,128]{1,0:T(8,128)(2,1)S(1)} %get-tuple-element.88), channel_id=1, source_target_pairs={{0,2},{1,3},{2,0},{3,1},{4,6},{5,7},{6,4},{7,5},{8,10},{9,11},{10,... | collective-permute-start | bytes 221192 | tf_op jit(solution)/shard_map/ppermute | solution.py:507
  39.1 5.9 %collective-permute-start.12 = (bf16[288,128]{1,0:T(8,128)(2,1)S(1)}, bf16[288,128]{1,0:T(8,128)(2,1)S(1)}, u32[]{:S(2)}, u32[]{:S(2)}) collective-permute-start(bf16[288,128]{1,0:T(8,128)(2,1)S(1)} %get-tuple-element.89), channel_id=1, source_target_pairs={{0,3},{1,0},{2,1},{3,2},{4,7},{5,4},{6,5},{7,6},{8,11},{9,8},{10,9... | collective-permute-start | bytes 221192 | tf_op jit(solution)/shard_map/ppermute | solution.py:507

commit v9 on v8

--- a/solution.py
+++ b/solution.py
@@ -16,7 +16,7 @@
     return jax.ShapeDtypeStruct(shape, dtype)
 
 
-def kernel_call(body, outs, scratch, flops, *args, far=()):
+def kernel_call(body, outs, scratch, flops, *args, far=(), changed=None):
     vmem = pl.BlockSpec(memory_space=pltpu.VMEM)
     hbm = pl.BlockSpec(memory_space=pltpu.HBM)
     moved = sum(a.size * a.dtype.itemsize for a in args)
@@ -31,6 +31,7 @@
         in_specs=[hbm if i in far else vmem for i in range(len(args))],
         out_specs=tuple(vmem for _ in outs),
         scratch_shapes=scratch,
+        input_output_aliases=changed or {},
         compiler_params=pltpu.CompilerParams(vmem_limit_bytes=28 * 2**20),
         cost_estimate=pl.CostEstimate(flops=flops, bytes_accessed=moved, transcendentals=0),
     )(*args)
@@ -169,9 +170,9 @@
     second[...] = jnp.where(even, before[...], after[...]).astype(bf16)
 
 
-def act_kernel(
-    coarse, skip, cot, left, right, got_second, got_first, up_w, conv_w,
-    shifted, near, act, slope, partial, send, upper, lower, conv_v, padded, pre, sem,
+def inner_kernel(
+    coarse, skip, cot, left, right, up_w, conv_w,
+    shifted, near, act, slope, partial, last_pre, conv_v, padded, pre, sem,
 ):
     n_rows, n_cols, channels = coarse.shape
     rows, cols, _ = skip.shape
@@ -179,41 +180,15 @@
     stride = cols + 2 * MARGIN
     copy = pltpu.make_async_copy(conv_w, conv_v, sem)
     copy.start()
-    even = lax.rem(place_of()[2], 2) == 0
-    one, two = got_first[...].astype(f32), got_second[...].astype(f32)
-    upper[...] = jnp.where(even, two, one)
-    lower[...] = jnp.where(even, one, two)
     for row in range(n_rows):
         near[0, row] = coarse[row]
         put(padded, row * stride, coarse[row].astype(f32))
-    below = lower[at.row_coarse : at.row_coarse + n_cols, :]
-    near[0, n_rows] = below.astype(bf16)
-    put(padded, n_rows * stride, below)
     put(padded, n_cols, right[at.coarse : at.coarse + n_rows, :], stride)
-    corner = at.corner + COARSE[2]
-    put(padded, n_rows * stride + n_cols, lower[corner : corner + 1, :])
-    for row in range(n_rows + 1):
+    for row in range(n_rows):
         near[1, row] = get(padded, row * stride + 1, n_cols).astype(bf16)
-    for row in range(n_rows + 1, near.shape[1]):
+    for row in range(n_rows, near.shape[1]):
         for side in range(2):
             near[side, row] = jnp.zeros((n_cols, channels), bf16)
-    put(padded, MARGIN, upper[at.row_cot : at.row_cot + cols, :])
-    put(padded, (rows + 1) * stride + MARGIN, lower[at.row_cot : at.row_cot + cols, :])
-    for row in range(rows):
-        put(padded, (row + 1) * stride + MARGIN, cot[row].astype(f32))
-    put(padded, stride + MARGIN - 1, left[at.cot : at.cot + rows, :], stride)
-    put(padded, stride + MARGIN + cols, right[at.cot : at.cot + rows, :], stride)
-    for row, message in ((0, upper), (rows + 1, lower)):
-        for col, corner in ((-1, at.corner + COT[0]), (cols, at.corner + COT[2])):
-            put(padded, row * stride + MARGIN + col, message[corner : corner + 1, :])
-    for row in range(rows + 2):
-        for shift in (0, 2):
-            start = row * stride + MARGIN - 1 + shift
-            shifted[shift, row] = get(padded, start, cols).astype(bf16)
-    shifted[1, 0] = upper[at.row_cot : at.row_cot + cols, :].astype(bf16)
-    shifted[1, rows + 1] = lower[at.row_cot : at.row_cot + cols, :].astype(bf16)
-    for row in range(rows):
-        shifted[1, row + 1] = cot[row]
     sums = {}
     for k in range(3):
         row_phase, row_off = forward_taps[k]
@@ -227,19 +202,80 @@
         for row in range(n_rows):
             start = (2 * row + row_phase) * cols + col_phase
             put(pre, start, total[row * n_cols : (row + 1) * n_cols], 2)
+    for row in range(rows):
+        put(padded, row * stride + MARGIN, cot[row].astype(f32))
+    put(padded, MARGIN - 1, left[at.cot : at.cot + rows, :], stride)
+    put(padded, MARGIN + cols, right[at.cot : at.cot + rows, :], stride)
+    for row in range(rows):
+        for shift in (0, 2):
+            start = row * stride + MARGIN - 1 + shift
+            shifted[shift, row + 1] = get(padded, start, cols).astype(bf16)
+        shifted[1, row + 1] = cot[row]
+    for shift in range(3):
+        shifted[shift, 0] = jnp.zeros((cols, channels), bf16)
+        shifted[shift, rows + 1] = jnp.zeros((cols, channels), bf16)
     preact = get(pre, 0, rows * cols) + skip[...].reshape(rows * cols, channels).astype(f32)
+    last_pre[...] = preact[(rows - 1) * cols :]
     sigma = jax.nn.sigmoid(preact)
     value = preact * sigma
     slope[...] = sigma + value * (1.0 - sigma)
-    act_flat = value.astype(bf16)
+    row_of = lax.broadcasted_iota(jnp.int32, value.shape, 0)
+    act_flat = jnp.where(row_of < (rows - 1) * cols, value, 0.0).astype(bf16)
     act[...] = act_flat.reshape(act.shape)
     act_t = act_flat.T
     for k in range(3):
         for l in range(3):
             source = shifted[2 - l, pl.ds(2 - k, rows)].reshape(-1, channels)
             partial[pl.ds((3 * k + l) * channels, channels), :] = dot(act_t, source)
+    copy.wait()
+
+
+def act_kernel(
+    got_second, got_first, right, up_w, last_pre, shifted_in, near_in, act_in, slope_in, partial_in,
+    shifted, near, act, slope, partial, send, upper, lower, padded, pre,
+):
+    rows, cols, channels = act.shape
+    n_rows, n_cols = rows // 2, cols // 2
+    at = Layout(n_rows, n_cols)
+    even = lax.rem(place_of()[2], 2) == 0
+    one, two = got_first[...].astype(f32), got_second[...].astype(f32)
+    upper[...] = jnp.where(even, two, one)
+    lower[...] = jnp.where(even, one, two)
+    below = lower[at.row_coarse : at.row_coarse + n_cols, :]
+    corner = at.corner + COARSE[2]
+    put(padded, 0, below)
+    put(padded, n_cols, lower[corner : corner + 1, :])
+    cells = [below.astype(bf16), get(padded, 1, n_cols).astype(bf16)]
+    near[0, n_rows] = cells[0]
+    near[1, n_rows] = cells[1]
+    put(pre, 0, dot(cells[0], up_w[0, 1]), 2)
+    put(pre, 1, dot(cells[1], up_w[0, 0]) + dot(cells[0], up_w[0, 2]), 2)
+    preact = last_pre[...] + get(pre, 0, cols)
+    sigma = jax.nn.sigmoid(preact)
+    value = preact * sigma
+    slope[(rows - 1) * cols :, :] = sigma + value * (1.0 - sigma)
+    last = value.astype(bf16)
+    act[rows - 1] = last
+    for row, message in ((0, upper), (rows + 1, lower)):
+        centre = message[at.row_cot : at.row_cot + cols, :]
+        put(padded, MARGIN, centre)
+        for col, one in ((-1, COT[0]), (cols, COT[2])):
+            put(padded, MARGIN + col, message[at.corner + one : at.corner + one + 1, :])
+        shifted[0, row] = get(padded, MARGIN - 1, cols).astype(bf16)
+        shifted[1, row] = centre.astype(bf16)
+        shifted[2, row] = get(padded, MARGIN + 1, cols).astype(bf16)
+    last_t = last.T
+    both_t = jnp.concatenate([last, act_in[0]], axis=0).T
+    for k in range(3):
+        for l in range(3):
+            beside = shifted[2 - l, rows + 1 - k]
+            if k == 2:
+                term = dot(both_t, jnp.concatenate([beside, shifted[2 - l, 0]], axis=0))
+            else:
+                term = dot(last_t, beside)
+            tap = pl.ds((3 * k + l) * channels, channels)
+            partial[tap, :] = partial_in[tap, :] + term
     other_core(partial, send)
-    copy.wait()
 
 
 def grad_kernel(shifted, slope, conv_w, phases, fine):
@@ -550,23 +586,29 @@
     padded = halves((rows + 2) * stride, channels)
     shift_shape = (3, rows + 2, cols, channels)
     whole = -(-cells // 256) * 256 // n_cols
-    partials = [sds((9 * channels, channels), f32), sds((groups, block, channels), bf16)]
+    part = sds((9 * channels, channels), f32)
+    blocks = [
+        sds(shift_shape, bf16), sds((2, whole + 1, n_cols, channels), bf16),
+        sds(skip.shape, bf16), sds((rows * cols, channels), f32), part,
+    ]
+    *inner, last_pre, conv_weight = kernel_call(
+        inner_kernel,
+        [*blocks, sds((cols, channels), f32), sds(conv_weight.shape, bf16)],
+        [halves(rows * stride, channels), flat, pltpu.SemaphoreType.DMA],
+        0, coarse, skip, cotangent, left, right, up_weight, conv_weight, far=(6,),
+    )
+    send = sds((groups, block, channels), bf16)
     side = sds(message.shape, f32)
-    shifted, near, act, slope, part_conv, send_conv, upper, lower, conv_weight = kernel_call(
-        act_kernel,
-        [
-            sds(shift_shape, bf16), sds((2, whole + 1, n_cols, channels), bf16),
-            sds(skip.shape, bf16), sds((rows * cols, channels), f32), *partials, side, side,
-            sds(conv_weight.shape, bf16),
-        ],
-        [padded, flat, pltpu.SemaphoreType.DMA],
-        0, coarse, skip, cotangent, left, right, second, first, up_weight, conv_weight, far=(8,),
+    shifted, near, act, slope, part_conv, send_conv, upper, lower = kernel_call(
+        act_kernel, [*blocks, send, side, side],
+        [halves(stride, channels), halves(cols, channels)],
+        0, second, first, right, up_weight, last_pre, *inner, changed={5 + i: i for i in range(5)},
     )
     phases = kernel_call(
         grad_kernel, [sds((2, 2, whole, n_cols, channels), bf16)], [flat],
         0, shifted, slope, conv_weight,
     )[0]
-    part_up, send_up = kernel_call(up_kernel, partials, [], 0, near, phases)
+    part_up, send_up = kernel_call(up_kernel, [part, send], [], 0, near, phases)
     own_conv, to_conv = core_sum(after(part_conv, send_up), send_conv)
     got_conv = plane_swap(to_conv, 0)
     own_up, to_up = core_sum(after(part_up, to_conv), send_up)

time: 46 us -> 45.1 us (0.980)
  waiting for transfers between devices: 13.8 us -> 12.1 us
  Pallas kernels: 10.7 us -> 11.6 us
    ppermute x4, waiting for transfers between devices: 4.02 us -> 2.26 us  [swap(): return (lax.ppermute(first, axis, one), lax.ppermute(second, axis, two))]
    pallas_call x14 -> x15, Pallas kernels: 10.7 us -> 11.6 us  [kernel_call(): pl.pallas_call(body, out_shape=tuple(outs), in_specs=[hbm if i in far els...]
  transfers between devices with their start and end apart: 13 -> 13, of which waited for: 8 -> 8; matrix products, arithmetic and copies ran while one was open for 0% -> 0% of each run, Pallas kernels for 13% -> 17%
where the time goes in v9:
time: 45.1 us; the launch traced here: 45 us
  starting transfers between devices  20.5 us (45%)
  waiting for transfers between devices  12.1 us (27%)
  Pallas kernels  11.6 us (26%)
  between operations  0.73 us (2%)
    pallas_call x15, Pallas kernels, kernel_call(): pl.pallas_call(body, out_shape=tuple(outs), in_specs=[hbm if i in far els...  11.6 us
    ppermute x4, starting transfers between devices, swap(): return (lax.ppermute(first, axis, one), lax.ppermute(second, axis, two))  9.36 us
    ppermute x4, waiting for transfers between devices, plane_swap(): lax.ppermute(message, 'face', [(i, i ^ 2 << orders[i % 2][step]) for i in...  6.26 us
    ppermute x4, starting transfers between devices, plane_swap(): lax.ppermute(message, 'face', [(i, i ^ 2 << orders[i % 2][step]) for i in...  5.67 us
    ppermute x3, starting transfers between devices, band_sum(): lax.ppermute(messages[k - 1], 'band', [(i, (i + k) % bands) for i in rang...  4.88 us
    ppermute x3, waiting for transfers between devices, band_sum(): lax.ppermute(messages[k - 1], 'band', [(i, (i + k) % bands) for i in rang...  3.12 us
    ppermute x4, waiting for transfers between devices, swap(): return (lax.ppermute(first, axis, one), lax.ppermute(second, axis, two))  2.26 us
  transfers between devices with their start and end apart: 13, of which 8 were waited for; matrix products, arithmetic and copies ran while one was open for 0% of the time, Pallas kernels for 17%

profile of v9, /device:TPU:0, one launch (start us, length us, event | category | flops | bytes accessed | tf_op | source)
XLA Modules:
  0.0 45.0 jit_solution(1130335434473952824)
XLA Ops:
  0.6 1.3 %shard_map.84 = (bf16[96,256]{1,0:T(8,128)(2,1)S(1)}, bf16[96,256]{1,0:T(8,128)(2,1)S(1)}, bf16[24,32,256]{2,1,0:T(8,128)(2,1)S(1)}, bf16[24,32,256]{2,1,0:T(8,128)(2,1)S(1)}, bf16[12,16,256]{2,1,0:T(8,128)(2,1)S(1)}) custom-call(bf16[12,16,256]{2,1,0:T(8,128)(2,1)} %coarse.1, bf16[24,32,256]{2,1,0:T(8,128)(2,1)} %skip.1, bf16[24,32,256]{2,1,0:T(8,128)(2,1)} %cot.1), custom_call_target="tpu_custom_call" | custom-call | bytes 1867776 | tf_op jit(solution)/shard_map/pallas_call | solution.py:28
  2.5 3.6 %collective-permute-start.1 = (bf16[96,256]{1,0:T(8,128)(2,1)S(1)}, bf16[96,256]{1,0:T(8,128)(2,1)S(1)}, u32[]{:S(2)}, u32[]{:S(2)}) collective-permute-start(bf16[96,256]{1,0:T(8,128)(2,1)S(1)} %get-tuple-element.58), channel_id=1, source_target_pairs={{0,28},{4,8},{8,4},{12,16},{16,12},{20,24},{24,20},{28,0},{1,29},{... | collective-permute-start | bytes 147464 | tf_op jit(solution)/shard_map/ppermute | solution.py:555
  6.0 1.8 %collective-permute-done.1.got_second = bf16[96,256]{1,0:T(8,128)(2,1)S(1)} collective-permute-done((bf16[96,256]{1,0:T(8,128)(2,1)S(1)}, bf16[96,256]{1,0:T(8,128)(2,1)S(1)}, u32[]{:S(2)}, u32[]{:S(2)}) %collective-permute-start.1) | collective-permute-done | bytes 49184 | tf_op jit(solution)/shard_map/ppermute | solution.py:555
  7.9 0.7 %collective-permute-start.2 = (bf16[128,256]{1,0:T(8,128)(2,1)S(1)}, bf16[128,256]{1,0:T(8,128)(2,1)S(1)}, u32[]{:S(2)}, u32[]{:S(2)}) collective-permute-start(bf16[128,256]{1,0:T(8,128)(2,1)S(1)} %get-tuple-element.59), channel_id=1, source_target_pairs={{1,2},{2,1},{5,6},{6,5},{9,10},{10,9},{13,14},{14,13},{17,18},{18,... | collective-permute-start | bytes 196616 | tf_op jit(solution)/shard_map/ppermute | solution.py:555
  8.5 4.6 %collective-permute-start.3 = (bf16[128,256]{1,0:T(8,128)(2,1)S(1)}, bf16[128,256]{1,0:T(8,128)(2,1)S(1)}, u32[]{:S(2)}, u32[]{:S(2)}) collective-permute-start(bf16[128,256]{1,0:T(8,128)(2,1)S(1)} %get-tuple-element.60), channel_id=1, source_target_pairs={{0,1},{1,0},{2,3},{3,2},{4,5},{5,4},{6,7},{7,6},{8,9},{9,8},{10,11... | collective-permute-start | bytes 196616 | tf_op jit(solution)/shard_map/ppermute | solution.py:555
  13.2 1.7 %shard_map.86 = (bf16[3,26,32,256]{3,2,1,0:T(8,128)(2,1)S(1)}, bf16[2,17,16,256]{3,2,1,0:T(8,128)(2,1)S(1)}, bf16[24,32,256]{2,1,0:T(8,128)(2,1)S(1)}, f32[768,2...) custom-call(bf16[12,16,256]{2,1,0:T(8,128)(2,1)S(1)} %get-tuple-element.5, ...), custom_call_target="tpu_custom_call" | custom-call | bytes 9748480 | tf_op jit(solution)/shard_map/pallas_call | solution.py:28
  15.4 1.3 %shard_map.87 = (bf16[3,26,32,256]{3,2,1,0:T(8,128)(2,1)S(1)}, bf16[2,17,16,256]{3,2,1,0:T(8,128)(2,1)S(1)}, bf16[24,32,256]{2,1,0:T(8,128)(2,1)S(1)}, f32[768,2...) custom-call(bf16[128,256]{1,0:T(8,128)(2,1)S(1)} %collective-permute, ...), custom_call_target="tpu_custom_call", output_to_operand_aliasing={{0}: (5, {}), {1}: (6, {}), {2}: (7, {}), {3}: (8, {}), {4}... | custom-call | bytes 12484608 | tf_op jit(solution)/shard_map/pallas_call | solution.py:28
  16.8 1.2 %shard_map.88.phases = bf16[2,2,16,16,256]{4,3,2,1,0:T(8,128)(2,1)S(1)} custom-call(bf16[3,26,32,256]{3,2,1,0:T(8,128)(2,1)S(1)} %get-tuple-element.71.shifted, f32[768,256]{1,0:T(8,128)S(1)} %get-tuple-element.72.slope, bf16[3,3,256,256]{3,2,1,0:T(8,128)(2,1)S(1)} %get-tuple-element.73.conv_w), custom_call_target="tpu_custom_call" | custom-call | bytes 3768320 | tf_op jit(solution)/shard_map/pallas_call | solution.py:28
  18.0 0.8 %shard_map.89 = (f32[2304,256]{1,0:T(8,128)S(1)}, bf16[4,288,256]{2,1,0:T(8,128)(2,1)S(1)}) custom-call(bf16[2,17,16,256]{3,2,1,0:T(8,128)(2,1)S(1)} %get-tuple-element.70.near, bf16[2,2,16,16,256]{4,3,2,1,0:T(8,128)(2,1)S(1)} %shard_map.88.phases), custom_call_target="tpu_custom_call" | custom-call | bytes 3751936 | tf_op jit(solution)/shard_map/pallas_call | solution.py:28
  19.4 1.1 %collective-permute-start.6 = (bf16[2,288,256]{2,1,0:T(8,128)(2,1)S(1)}, bf16[2,288,256]{2,1,0:T(8,128)(2,1)S(1)}, u32[]{:S(2)}, u32[]{:S(2)}) collective-permute-start(bf16[2,288,256]{2,1,0:T(8,128)(2,1)S(1)} %get-tuple-element.79), channel_id=1, source_target_pairs={{0,8},{4,20},{8,0},{12,28},{16,24},{20,4},{24,16},{28,12},{1,9},{5... | collective-permute-start | bytes 884744 | tf_op jit(solution)/shard_map/ppermute | solution.py:524
  21.1 1.1 %collective-permute-start.7 = (bf16[2,288,256]{2,1,0:T(8,128)(2,1)S(1)}, bf16[2,288,256]{2,1,0:T(8,128)(2,1)S(1)}, u32[]{:S(2)}, u32[]{:S(2)}) collective-permute-start(bf16[2,288,256]{2,1,0:T(8,128)(2,1)S(1)} %get-tuple-element.81), channel_id=1, source_target_pairs={{0,8},{4,20},{8,0},{12,28},{16,24},{20,4},{24,16},{28,12},{1,9},{5... | collective-permute-start | bytes 884744 | tf_op jit(solution)/shard_map/ppermute | solution.py:524
  22.1 0.8 %shard_map.92 = (f32[128,256]{1,0:T(8,128)S(1)}, f32[2,64,128]{2,1,0:T(8,128)S(1)}) custom-call(bf16[12,16,256]{2,1,0:T(8,128)(2,1)S(1)} %get-tuple-element.54.coarse, bf16[24,32,256]{2,1,0:T(8,128)(2,1)S(1)} %get-tuple-element.56.cot, f32[96,256]{1,0:T(8,128)S(1)} %get-tuple-element.82.left, f32[96,256]{1,0:T(8,128)S(1)} %get-tuple-element.61.right, ...), custom_call_target="tpu_custom_call" | custom-call | bytes 3506176 | tf_op jit(solution)/shard_map/pallas_call | solution.py:28
  22.9 3.3 %collective-permute-done.6.got = bf16[2,288,256]{2,1,0:T(8,128)(2,1)S(1)} collective-permute-done((bf16[2,288,256]{2,1,0:T(8,128)(2,1)S(1)}, bf16[2,288,256]{2,1,0:T(8,128)(2,1)S(1)}, u32[]{:S(2)}, u32[]{:S(2)}) %collective-permute-start.6) | collective-permute-done | bytes 294944 | tf_op jit(solution)/shard_map/ppermute | solution.py:524
  26.3 1.8 %collective-permute-start.8 = (bf16[1,288,256]{2,1,0:T(8,128)(2,1)S(1)}, bf16[1,288,256]{2,1,0:T(8,128)(2,1)S(1)}, u32[]{:S(2)}, u32[]{:S(2)}) collective-permute-start(bf16[1,288,256]{2,1,0:T(8,128)(2,1)S(1)} %get-tuple-element.88), channel_id=1, source_target_pairs={{0,16},{4,12},{8,24},{12,4},{16,0},{20,28},{24,8},{28,20},{1,17},{... | collective-permute-start | bytes 442376 | tf_op jit(solution)/shard_map/ppermute | solution.py:524
  28.0 1.8 %shard_map.94 = bf16[24,32,256]{2,1,0:T(8,128)(2,1)} custom-call(bf16[24,32,256]{2,1,0:T(8,128)(2,1)S(1)} %get-tuple-element.69.act, f32[128,256]{1,0:T(8,128)S(1)} %get-tuple-element.89.ring_act, bf16[3,3,256,256]{3,2,1,0:T(8,128)(2,1)S(1)} %get-tuple-element.73.conv_w), custom_call_target="tpu_custom_call" | custom-call | bytes 2097152 | tf_op jit(solution)/shard_map/pallas_call | solution.py:28
  29.9 0.7 %collective-permute-done.7.got = bf16[2,288,256]{2,1,0:T(8,128)(2,1)S(1)} collective-permute-done((bf16[2,288,256]{2,1,0:T(8,128)(2,1)S(1)}, bf16[2,288,256]{2,1,0:T(8,128)(2,1)S(1)}, u32[]{:S(2)}, u32[]{:S(2)}) %collective-permute-start.7) | collective-permute-done | bytes 294944 | tf_op jit(solution)/shard_map/ppermute | solution.py:524
  30.6 1.8 %collective-permute-start.9 = (bf16[1,288,256]{2,1,0:T(8,128)(2,1)S(1)}, bf16[1,288,256]{2,1,0:T(8,128)(2,1)S(1)}, u32[]{:S(2)}, u32[]{:S(2)}) collective-permute-start(bf16[1,288,256]{2,1,0:T(8,128)(2,1)S(1)} %get-tuple-element.93), channel_id=1, source_target_pairs={{0,16},{4,12},{8,24},{12,4},{16,0},{20,28},{24,8},{28,20},{1,17},{... | collective-permute-start | bytes 442376 | tf_op jit(solution)/shard_map/ppermute | solution.py:524
  32.4 1.2 %shard_map.96 = bf16[12,16,256]{2,1,0:T(8,128)(2,1)} custom-call(bf16[2,2,16,16,256]{4,3,2,1,0:T(8,128)(2,1)S(1)} %shard_map.88.phases, f32[2,64,128]{2,1,0:T(8,128)S(1)} %get-tuple-element.94.ring_grad, bf16[3,3,256,256]{3,2,1,0:T(8,128)(2,1)S(1)} %copy-done), custom_call_target="tpu_custom_call" | custom-call | bytes 1867776 | tf_op jit(solution)/shard_map/pallas_call | solution.py:28
  33.6 2.2 %collective-permute-done.9.got_up = bf16[1,288,256]{2,1,0:T(8,128)(2,1)S(1)} collective-permute-done((bf16[1,288,256]{2,1,0:T(8,128)(2,1)S(1)}, bf16[1,288,256]{2,1,0:T(8,128)(2,1)S(1)}, u32[]{:S(2)}, u32[]{:S(2)}) %collective-permute-start.9) | collective-permute-done | bytes 147488 | tf_op jit(solution)/shard_map/ppermute | solution.py:524
  36.2 2.1 %collective-permute-start.10 = (bf16[288,128]{1,0:T(8,128)(2,1)S(1)}, bf16[288,128]{1,0:T(8,128)(2,1)S(1)}, u32[]{:S(2)}, u32[]{:S(2)}) collective-permute-start(bf16[288,128]{1,0:T(8,128)(2,1)S(1)} %get-tuple-element.99), channel_id=1, source_target_pairs={{0,1},{1,2},{2,3},{3,0},{4,5},{5,6},{6,7},{7,4},{8,9},{9,10},{10,1... | collective-permute-start | bytes 221192 | tf_op jit(solution)/shard_map/ppermute | solution.py:543
  38.2 2.8 %collective-permute-start.12 = (bf16[288,128]{1,0:T(8,128)(2,1)S(1)}, bf16[288,128]{1,0:T(8,128)(2,1)S(1)}, u32[]{:S(2)}, u32[]{:S(2)}) collective-permute-start(bf16[288,128]{1,0:T(8,128)(2,1)S(1)} %get-tuple-element.101), channel_id=1, source_target_pairs={{0,3},{1,0},{2,1},{3,2},{4,7},{5,4},{6,5},{7,6},{8,11},{9,8},{10,9... | collective-permute-start | bytes 221192 | tf_op jit(solution)/shard_map/ppermute | solution.py:543
  41.0 1.3 %collective-permute-done.10.refs_0_ = bf16[288,128]{1,0:T(8,128)(2,1)S(1)} collective-permute-done((bf16[288,128]{1,0:T(8,128)(2,1)S(1)}, bf16[288,128]{1,0:T(8,128)(2,1)S(1)}, u32[]{:S(2)}, u32[]{:S(2)}) %collective-permute-start.10) | collective-permute-done | bytes 73760 | tf_op jit(solution)/shard_map/ppermute | solution.py:543
  42.4 1.8 %collective-permute-done.11.refs_1_ = bf16[288,128]{1,0:T(8,128)(2,1)S(1)} collective-permute-done((bf16[288,128]{1,0:T(8,128)(2,1)S(1)}, bf16[288,128]{1,0:T(8,128)(2,1)S(1)}, u32[]{:S(2)}, u32[]{:S(2)}) %collective-permute-start.11) | collective-permute-done | bytes 73760 | tf_op jit(solution)/shard_map/ppermute | solution.py:543
  44.2 0.8 %shard_map.98 = (f32[64,288]{1,0:T(8,128)}, f32[64,288]{1,0:T(8,128)}) custom-call(f32[288,128]{1,0:T(8,128)S(1)} %get-tuple-element.98.own, bf16[288,128]{1,0:T(8,128)(2,1)S(1)} %collective-permute-done.10.refs_0_, bf16[288,128]{1,0:T(8,128)(2,1)S(1)} %collective-permute-done.11.refs_1_, bf16[288,128]{1,0:T(8,128)(2,1)S(1)} %collective-permute-done.12.refs_2_), custom_call_target="tpu_custom_call" | custom-call | bytes 516096 | tf_op jit(solution)/shard_map/pallas_call | solution.py:28
  (19 shorter events, 2.8 us)
Async XLA Ops:
  0.6 12.5 %copy-start = (bf16[3,3,256,256]{3,2,1,0:T(8,128)(2,1)S(1)}, bf16[3,3,256,256]{3,2,1,0:T(8,128)(2,1)}, u32[]{:S(2)}) copy-start(bf16[3,3,256,256]{3,2,1,0:T(8,128)(2,1)} %up_w.7) | copy-start | bytes 3538948
  2.0 4.1 %collective-permute-start = (bf16[96,256]{1,0:T(8,128)(2,1)S(1)}, bf16[96,256]{1,0:T(8,128)(2,1)S(1)}, u32[]{:S(2)}, u32[]{:S(2)}) collective-permute-start(bf16[96,256]{1,0:T(8,128)(2,1)S(1)} %get-tuple-element.57), channel_id=1, source_target_pairs={{0,4},{4,0},{8,12},{12,8},{16,20},{20,16},{24,28},{28,24},{1,5},{5... | collective-permute-start | bytes 147464 | tf_op jit(solution)/shard_map/ppermute | solution.py:555
  2.5 5.3 %collective-permute-start.1 = (bf16[96,256]{1,0:T(8,128)(2,1)S(1)}, bf16[96,256]{1,0:T(8,128)(2,1)S(1)}, u32[]{:S(2)}, u32[]{:S(2)}) collective-permute-start(bf16[96,256]{1,0:T(8,128)(2,1)S(1)} %get-tuple-element.58), channel_id=1, source_target_pairs={{0,28},{4,8},{8,4},{12,16},{16,12},{20,24},{24,20},{28,0},{1,29},{... | collective-permute-start | bytes 147464 | tf_op jit(solution)/shard_map/ppermute | solution.py:555
  7.9 7.0 %collective-permute-start.2 = (bf16[128,256]{1,0:T(8,128)(2,1)S(1)}, bf16[128,256]{1,0:T(8,128)(2,1)S(1)}, u32[]{:S(2)}, u32[]{:S(2)}) collective-permute-start(bf16[128,256]{1,0:T(8,128)(2,1)S(1)} %get-tuple-element.59), channel_id=1, source_target_pairs={{1,2},{2,1},{5,6},{6,5},{9,10},{10,9},{13,14},{14,13},{17,18},{18,... | collective-permute-start | bytes 196616 | tf_op jit(solution)/shard_map/ppermute | solution.py:555
  8.5 6.9 %collective-permute-start.3 = (bf16[128,256]{1,0:T(8,128)(2,1)S(1)}, bf16[128,256]{1,0:T(8,128)(2,1)S(1)}, u32[]{:S(2)}, u32[]{:S(2)}) collective-permute-start(bf16[128,256]{1,0:T(8,128)(2,1)S(1)} %get-tuple-element.60), channel_id=1, source_target_pairs={{0,1},{1,0},{2,3},{3,2},{4,5},{5,4},{6,7},{7,6},{8,9},{9,8},{10,11... | collective-permute-start | bytes 196616 | tf_op jit(solution)/shard_map/ppermute | solution.py:555
  16.7 2.6 %collective-permute-start.4 = (bf16[4,288,256]{2,1,0:T(8,128)(2,1)S(1)}, bf16[4,288,256]{2,1,0:T(8,128)(2,1)S(1)}, u32[]{:S(2)}, u32[]{:S(2)}) collective-permute-start(bf16[4,288,256]{2,1,0:T(8,128)(2,1)S(1)} %get-tuple-element.78), channel_id=1, source_target_pairs={{0,4},{4,0},{8,12},{12,8},{16,20},{20,16},{24,28},{28,24},{1,5},{5... | collective-permute-start | bytes 1769480 | tf_op jit(solution)/shard_map/ppermute | solution.py:516
  18.8 2.2 %collective-permute-start.5 = (bf16[4,288,256]{2,1,0:T(8,128)(2,1)S(1)}, bf16[4,288,256]{2,1,0:T(8,128)(2,1)S(1)}, u32[]{:S(2)}, u32[]{:S(2)}) collective-permute-start(bf16[4,288,256]{2,1,0:T(8,128)(2,1)S(1)} %get-tuple-element.76), channel_id=1, source_target_pairs={{0,4},{4,0},{8,12},{12,8},{16,20},{20,16},{24,28},{28,24},{1,5},{5... | collective-permute-start | bytes 1769480 | tf_op jit(solution)/shard_map/ppermute | solution.py:516
  19.4 6.8 %collective-permute-start.6 = (bf16[2,288,256]{2,1,0:T(8,128)(2,1)S(1)}, bf16[2,288,256]{2,1,0:T(8,128)(2,1)S(1)}, u32[]{:S(2)}, u32[]{:S(2)}) collective-permute-start(bf16[2,288,256]{2,1,0:T(8,128)(2,1)S(1)} %get-tuple-element.79), channel_id=1, source_target_pairs={{0,8},{4,20},{8,0},{12,28},{16,24},{20,4},{24,16},{28,12},{1,9},{5... | collective-permute-start | bytes 884744 | tf_op jit(solution)/shard_map/ppermute | solution.py:524
  21.1 9.5 %collective-permute-start.7 = (bf16[2,288,256]{2,1,0:T(8,128)(2,1)S(1)}, bf16[2,288,256]{2,1,0:T(8,128)(2,1)S(1)}, u32[]{:S(2)}, u32[]{:S(2)}) collective-permute-start(bf16[2,288,256]{2,1,0:T(8,128)(2,1)S(1)} %get-tuple-element.81), channel_id=1, source_target_pairs={{0,8},{4,20},{8,0},{12,28},{16,24},{20,4},{24,16},{28,12},{1,9},{5... | collective-permute-start | bytes 884744 | tf_op jit(solution)/shard_map/ppermute | solution.py:524
  26.3 7.3 %collective-permute-start.8 = (bf16[1,288,256]{2,1,0:T(8,128)(2,1)S(1)}, bf16[1,288,256]{2,1,0:T(8,128)(2,1)S(1)}, u32[]{:S(2)}, u32[]{:S(2)}) collective-permute-start(bf16[1,288,256]{2,1,0:T(8,128)(2,1)S(1)} %get-tuple-element.88), channel_id=1, source_target_pairs={{0,16},{4,12},{8,24},{12,4},{16,0},{20,28},{24,8},{28,20},{1,17},{... | collective-permute-start | bytes 442376 | tf_op jit(solution)/shard_map/ppermute | solution.py:524
  30.6 5.2 %collective-permute-start.9 = (bf16[1,288,256]{2,1,0:T(8,128)(2,1)S(1)}, bf16[1,288,256]{2,1,0:T(8,128)(2,1)S(1)}, u32[]{:S(2)}, u32[]{:S(2)}) collective-permute-start(bf16[1,288,256]{2,1,0:T(8,128)(2,1)S(1)} %get-tuple-element.93), channel_id=1, source_target_pairs={{0,16},{4,12},{8,24},{12,4},{16,0},{20,28},{24,8},{28,20},{1,17},{... | collective-permute-start | bytes 442376 | tf_op jit(solution)/shard_map/ppermute | solution.py:524
  36.2 6.2 %collective-permute-start.10 = (bf16[288,128]{1,0:T(8,128)(2,1)S(1)}, bf16[288,128]{1,0:T(8,128)(2,1)S(1)}, u32[]{:S(2)}, u32[]{:S(2)}) collective-permute-start(bf16[288,128]{1,0:T(8,128)(2,1)S(1)} %get-tuple-element.99), channel_id=1, source_target_pairs={{0,1},{1,2},{2,3},{3,0},{4,5},{5,6},{6,7},{7,4},{8,9},{9,10},{10,1... | collective-permute-start | bytes 221192 | tf_op jit(solution)/shard_map/ppermute | solution.py:543
  38.2 5.9 %collective-permute-start.11 = (bf16[288,128]{1,0:T(8,128)(2,1)S(1)}, bf16[288,128]{1,0:T(8,128)(2,1)S(1)}, u32[]{:S(2)}, u32[]{:S(2)}) collective-permute-start(bf16[288,128]{1,0:T(8,128)(2,1)S(1)} %get-tuple-element.100), channel_id=1, source_target_pairs={{0,2},{1,3},{2,0},{3,1},{4,6},{5,7},{6,4},{7,5},{8,10},{9,11},{10,... | collective-permute-start | bytes 221192 | tf_op jit(solution)/shard_map/ppermute | solution.py:543
  38.2 5.9 %collective-permute-start.12 = (bf16[288,128]{1,0:T(8,128)(2,1)S(1)}, bf16[288,128]{1,0:T(8,128)(2,1)S(1)}, u32[]{:S(2)}, u32[]{:S(2)}) collective-permute-start(bf16[288,128]{1,0:T(8,128)(2,1)S(1)} %get-tuple-element.101), channel_id=1, source_target_pairs={{0,3},{1,0},{2,1},{3,2},{4,7},{5,4},{6,5},{7,6},{8,11},{9,8},{10,9... | collective-permute-start | bytes 221192 | tf_op jit(solution)/shard_map/ppermute | solution.py:543

commit v10 on v9

--- a/solution.py
+++ b/solution.py
@@ -172,7 +172,7 @@
 
 def inner_kernel(
     coarse, skip, cot, left, right, up_w, conv_w,
-    shifted, near, act, slope, partial, last_pre, conv_v, padded, pre, sem,
+    shifted, near, act, slope, partial, last_pre, conv_v, grad_act, padded, pre, sem,
 ):
     n_rows, n_cols, channels = coarse.shape
     rows, cols, _ = skip.shape
@@ -228,6 +228,12 @@
             source = shifted[2 - l, pl.ds(2 - k, rows)].reshape(-1, channels)
             partial[pl.ds((3 * k + l) * channels, channels), :] = dot(act_t, source)
     copy.wait()
+    total = jnp.zeros((rows * cols, channels), f32)
+    for k in range(3):
+        for l in range(3):
+            source = shifted[2 - l, pl.ds(2 - k, rows)].reshape(-1, channels)
+            total = total + dot_nt(source, conv_v[k, l])
+    grad_act[...] = total
 
 
 def act_kernel(
@@ -278,16 +284,21 @@
     other_core(partial, send)
 
 
-def grad_kernel(shifted, slope, conv_w, phases, fine):
+def grad_kernel(shifted, slope, grad_act, conv_w, phases, fine):
     rows, cols = shifted.shape[1] - 2, shifted.shape[2]
     channels = shifted.shape[3]
     n_rows, n_cols = rows // 2, cols // 2
-    total = jnp.zeros((rows * cols, channels), f32)
-    for k in range(3):
-        for l in range(3):
-            source = shifted[2 - l, pl.ds(2 - k, rows)].reshape(-1, channels)
-            total = total + dot_nt(source, conv_w[k, l])
-    put(fine, 0, (total * slope[...]).astype(bf16).astype(f32))
+    first = jnp.zeros((cols, channels), f32)
+    last = jnp.zeros((cols, channels), f32)
+    for l in range(3):
+        first = first + dot_nt(shifted[2 - l, 0], conv_w[2, l])
+        last = last + dot_nt(shifted[2 - l, rows + 1], conv_w[0, l])
+    cells = rows * cols
+    put(fine, 0, (grad_act[...] * slope[...]).astype(bf16).astype(f32))
+    total = (grad_act[:cols, :] + first) * slope[:cols, :]
+    put(fine, 0, total.astype(bf16).astype(f32))
+    total = (grad_act[cells - cols :, :] + last) * slope[cells - cols :, :]
+    put(fine, cells - cols, total.astype(bf16).astype(f32))
     whole = phases.shape[2]
     for row_phase in range(2):
         for col_phase in range(2):
@@ -591,9 +602,12 @@
         sds(shift_shape, bf16), sds((2, whole + 1, n_cols, channels), bf16),
         sds(skip.shape, bf16), sds((rows * cols, channels), f32), part,
     ]
-    *inner, last_pre, conv_weight = kernel_call(
+    *inner, last_pre, conv_weight, grad_act = kernel_call(
         inner_kernel,
-        [*blocks, sds((cols, channels), f32), sds(conv_weight.shape, bf16)],
+        [
+            *blocks, sds((cols, channels), f32), sds(conv_weight.shape, bf16),
+            sds((rows * cols, channels), f32),
+        ],
         [halves(rows * stride, channels), flat, pltpu.SemaphoreType.DMA],
         0, coarse, skip, cotangent, left, right, up_weight, conv_weight, far=(6,),
     )
@@ -606,7 +620,7 @@
     )
     phases = kernel_call(
         grad_kernel, [sds((2, 2, whole, n_cols, channels), bf16)], [flat],
-        0, shifted, slope, conv_weight,
+        0, shifted, slope, grad_act, conv_weight,
     )[0]
     part_up, send_up = kernel_call(up_kernel, [part, send], [], 0, near, phases)
     own_conv, to_conv = core_sum(after(part_conv, send_up), send_conv)

time: 45.1 us -> 45 us (level)
  starting transfers between devices: 20.5 us -> 20 us
    ppermute x3, starting transfers between devices: 4.88 us -> 4.19 us  [band_sum(): lax.ppermute(messages[k - 1], 'band', [(i, (i + k) % bands) for i in rang...]
    ppermute x4, waiting for transfers between devices: 2.26 us -> 1.78 us  [swap(): return (lax.ppermute(first, axis, one), lax.ppermute(second, axis, two))]
    ppermute x3, waiting for transfers between devices: 3.12 us -> 3.59 us  [band_sum(): lax.ppermute(messages[k - 1], 'band', [(i, (i + k) % bands) for i in rang...]
  transfers between devices with their start and end apart: 13 -> 13, of which waited for: 8 -> 8; matrix products, arithmetic and copies ran while one was open for 0% -> 0% of each run, Pallas kernels for 17% -> 18%
where the time goes in v10:
time: 45 us; the launch traced here: 44.8 us
  starting transfers between devices  20 us (44%)
  Pallas kernels  12 us (27%)
  waiting for transfers between devices  12 us (27%)
  between operations  0.74 us (2%)
    pallas_call x15, Pallas kernels, kernel_call(): pl.pallas_call(body, out_shape=tuple(outs), in_specs=[hbm if i in far els...  12 us
    ppermute x4, starting transfers between devices, swap(): return (lax.ppermute(first, axis, one), lax.ppermute(second, axis, two))  9.36 us
    ppermute x4, waiting for transfers between devices, plane_swap(): lax.ppermute(message, 'face', [(i, i ^ 2 << orders[i % 2][step]) for i in...  6.17 us
    ppermute x4, starting transfers between devices, plane_swap(): lax.ppermute(message, 'face', [(i, i ^ 2 << orders[i % 2][step]) for i in...  5.86 us
    ppermute x3, starting transfers between devices, band_sum(): lax.ppermute(messages[k - 1], 'band', [(i, (i + k) % bands) for i in rang...  4.19 us
    ppermute x3, waiting for transfers between devices, band_sum(): lax.ppermute(messages[k - 1], 'band', [(i, (i + k) % bands) for i in rang...  3.59 us
    ppermute x4, waiting for transfers between devices, swap(): return (lax.ppermute(first, axis, one), lax.ppermute(second, axis, two))  1.78 us
  transfers between devices with their start and end apart: 13, of which 8 were waited for; matrix products, arithmetic and copies ran while one was open for 0% of the time, Pallas kernels for 18%

profile of v10, /device:TPU:0, one launch (start us, length us, event | category | flops | bytes accessed | tf_op | source)
XLA Modules:
  0.0 44.8 jit_solution(12782540781038425522)
XLA Ops:
  0.6 1.3 %shard_map.84 = (bf16[96,256]{1,0:T(8,128)(2,1)S(1)}, bf16[96,256]{1,0:T(8,128)(2,1)S(1)}, bf16[24,32,256]{2,1,0:T(8,128)(2,1)S(1)}, bf16[24,32,256]{2,1,0:T(8,128)(2,1)S(1)}, bf16[12,16,256]{2,1,0:T(8,128)(2,1)S(1)}) custom-call(bf16[12,16,256]{2,1,0:T(8,128)(2,1)} %coarse.1, bf16[24,32,256]{2,1,0:T(8,128)(2,1)} %skip.1, bf16[24,32,256]{2,1,0:T(8,128)(2,1)} %cot.1), custom_call_target="tpu_custom_call" | custom-call | bytes 1867776 | tf_op jit(solution)/shard_map/pallas_call | solution.py:28
  2.5 3.6 %collective-permute-start.1 = (bf16[96,256]{1,0:T(8,128)(2,1)S(1)}, bf16[96,256]{1,0:T(8,128)(2,1)S(1)}, u32[]{:S(2)}, u32[]{:S(2)}) collective-permute-start(bf16[96,256]{1,0:T(8,128)(2,1)S(1)} %get-tuple-element.59), channel_id=1, source_target_pairs={{0,28},{4,8},{8,4},{12,16},{16,12},{20,24},{24,20},{28,0},{1,29},{... | collective-permute-start | bytes 147464 | tf_op jit(solution)/shard_map/ppermute | solution.py:566
  6.0 1.8 %collective-permute-done.1.got_second = bf16[96,256]{1,0:T(8,128)(2,1)S(1)} collective-permute-done((bf16[96,256]{1,0:T(8,128)(2,1)S(1)}, bf16[96,256]{1,0:T(8,128)(2,1)S(1)}, u32[]{:S(2)}, u32[]{:S(2)}) %collective-permute-start.1) | collective-permute-done | bytes 49184 | tf_op jit(solution)/shard_map/ppermute | solution.py:566
  7.9 0.7 %collective-permute-start.2 = (bf16[128,256]{1,0:T(8,128)(2,1)S(1)}, bf16[128,256]{1,0:T(8,128)(2,1)S(1)}, u32[]{:S(2)}, u32[]{:S(2)}) collective-permute-start(bf16[128,256]{1,0:T(8,128)(2,1)S(1)} %get-tuple-element.60), channel_id=1, source_target_pairs={{1,2},{2,1},{5,6},{6,5},{9,10},{10,9},{13,14},{14,13},{17,18},{18,... | collective-permute-start | bytes 196616 | tf_op jit(solution)/shard_map/ppermute | solution.py:566
  8.5 4.6 %collective-permute-start.3 = (bf16[128,256]{1,0:T(8,128)(2,1)S(1)}, bf16[128,256]{1,0:T(8,128)(2,1)S(1)}, u32[]{:S(2)}, u32[]{:S(2)}) collective-permute-start(bf16[128,256]{1,0:T(8,128)(2,1)S(1)} %get-tuple-element.61), channel_id=1, source_target_pairs={{0,1},{1,0},{2,3},{3,2},{4,5},{5,4},{6,7},{7,6},{8,9},{9,8},{10,11... | collective-permute-start | bytes 196616 | tf_op jit(solution)/shard_map/ppermute | solution.py:566
  13.2 2.9 %shard_map.86 = (bf16[3,26,32,256]{3,2,1,0:T(8,128)(2,1)S(1)}, bf16[2,17,16,256]{3,2,1,0:T(8,128)(2,1)S(1)}, bf16[24,32,256]{2,1,0:T(8,128)(2,1)S(1)}, f32[768,2...) custom-call(bf16[12,16,256]{2,1,0:T(8,128)(2,1)S(1)} %get-tuple-elem, ...), custom_call_target="tpu_custom_call" | custom-call | bytes 10534912 | tf_op jit(solution)/shard_map/pallas_call | solution.py:28
  16.1 1.3 %shard_map.87 = (bf16[3,26,32,256]{3,2,1,0:T(8,128)(2,1)S(1)}, bf16[2,17,16,256]{3,2,1,0:T(8,128)(2,1)S(1)}, bf16[24,32,256]{2,1,0:T(8,128)(2,1)S(1)}, f32[768,2...) custom-call(bf16[128,256]{1,0:T(8,128)(2,1)S(1)} %collective-permute, ...), custom_call_target="tpu_custom_call", output_to_operand_aliasing={{0}: (5, {}), {1}: (6, {}), {2}: (7, {}), {3}: (8, {}), {4}... | custom-call | bytes 12484608 | tf_op jit(solution)/shard_map/pallas_call | solution.py:28
  17.9 0.7 %shard_map.89 = (f32[2304,256]{1,0:T(8,128)S(1)}, bf16[4,288,256]{2,1,0:T(8,128)(2,1)S(1)}) custom-call(bf16[2,17,16,256]{3,2,1,0:T(8,128)(2,1)S(1)} %get-tuple-element.71.near, bf16[2,2,16,16,256]{4,3,2,1,0:T(8,128)(2,1)S(1)} %shard_map.88.phases), custom_call_target="tpu_custom_call" | custom-call | bytes 3751936 | tf_op jit(solution)/shard_map/pallas_call | solution.py:28
  19.6 1.0 %collective-permute-start.6 = (bf16[2,288,256]{2,1,0:T(8,128)(2,1)S(1)}, bf16[2,288,256]{2,1,0:T(8,128)(2,1)S(1)}, u32[]{:S(2)}, u32[]{:S(2)}) collective-permute-start(bf16[2,288,256]{2,1,0:T(8,128)(2,1)S(1)} %get-tuple-element.81), channel_id=1, source_target_pairs={{0,8},{4,20},{8,0},{12,28},{16,24},{20,4},{24,16},{28,12},{1,9},{5... | collective-permute-start | bytes 884744 | tf_op jit(solution)/shard_map/ppermute | solution.py:535
  21.0 1.3 %collective-permute-start.7 = (bf16[2,288,256]{2,1,0:T(8,128)(2,1)S(1)}, bf16[2,288,256]{2,1,0:T(8,128)(2,1)S(1)}, u32[]{:S(2)}, u32[]{:S(2)}) collective-permute-start(bf16[2,288,256]{2,1,0:T(8,128)(2,1)S(1)} %get-tuple-element.83), channel_id=1, source_target_pairs={{0,8},{4,20},{8,0},{12,28},{16,24},{20,4},{24,16},{28,12},{1,9},{5... | collective-permute-start | bytes 884744 | tf_op jit(solution)/shard_map/ppermute | solution.py:535
  22.3 0.8 %shard_map.92 = (f32[128,256]{1,0:T(8,128)S(1)}, f32[2,64,128]{2,1,0:T(8,128)S(1)}) custom-call(bf16[12,16,256]{2,1,0:T(8,128)(2,1)S(1)} %get-tuple-element.55.coarse, bf16[24,32,256]{2,1,0:T(8,128)(2,1)S(1)} %get-tuple-element.57.cot, f32[96,256]{1,0:T(8,128)S(1)} %get-tuple-element.84.left, f32[96,256]{1,0:T(8,128)S(1)} %get-tuple-element.62.right, ...), custom_call_target="tpu_custom_call" | custom-call | bytes 3506176 | tf_op jit(solution)/shard_map/pallas_call | solution.py:28
  23.0 3.3 %collective-permute-done.6.got = bf16[2,288,256]{2,1,0:T(8,128)(2,1)S(1)} collective-permute-done((bf16[2,288,256]{2,1,0:T(8,128)(2,1)S(1)}, bf16[2,288,256]{2,1,0:T(8,128)(2,1)S(1)}, u32[]{:S(2)}, u32[]{:S(2)}) %collective-permute-start.6) | collective-permute-done | bytes 294944 | tf_op jit(solution)/shard_map/ppermute | solution.py:535
  26.4 1.8 %collective-permute-start.8 = (bf16[1,288,256]{2,1,0:T(8,128)(2,1)S(1)}, bf16[1,288,256]{2,1,0:T(8,128)(2,1)S(1)}, u32[]{:S(2)}, u32[]{:S(2)}) collective-permute-start(bf16[1,288,256]{2,1,0:T(8,128)(2,1)S(1)} %get-tuple-element.90), channel_id=1, source_target_pairs={{0,16},{4,12},{8,24},{12,4},{16,0},{20,28},{24,8},{28,20},{1,17},{... | collective-permute-start | bytes 442376 | tf_op jit(solution)/shard_map/ppermute | solution.py:535
  28.2 1.8 %shard_map.94 = bf16[24,32,256]{2,1,0:T(8,128)(2,1)} custom-call(bf16[24,32,256]{2,1,0:T(8,128)(2,1)S(1)} %get-tuple-element.70.act, f32[128,256]{1,0:T(8,128)S(1)} %get-tuple-element.91.ring_act, bf16[3,3,256,256]{3,2,1,0:T(8,128)(2,1)S(1)} %get-tuple-element.75.conv_w), custom_call_target="tpu_custom_call" | custom-call | bytes 2097152 | tf_op jit(solution)/shard_map/pallas_call | solution.py:28
  30.0 0.6 %collective-permute-done.7.got = bf16[2,288,256]{2,1,0:T(8,128)(2,1)S(1)} collective-permute-done((bf16[2,288,256]{2,1,0:T(8,128)(2,1)S(1)}, bf16[2,288,256]{2,1,0:T(8,128)(2,1)S(1)}, u32[]{:S(2)}, u32[]{:S(2)}) %collective-permute-start.7) | collective-permute-done | bytes 294944 | tf_op jit(solution)/shard_map/ppermute | solution.py:535
  30.7 1.8 %collective-permute-start.9 = (bf16[1,288,256]{2,1,0:T(8,128)(2,1)S(1)}, bf16[1,288,256]{2,1,0:T(8,128)(2,1)S(1)}, u32[]{:S(2)}, u32[]{:S(2)}) collective-permute-start(bf16[1,288,256]{2,1,0:T(8,128)(2,1)S(1)} %get-tuple-element.95), channel_id=1, source_target_pairs={{0,16},{4,12},{8,24},{12,4},{16,0},{20,28},{24,8},{28,20},{1,17},{... | collective-permute-start | bytes 442376 | tf_op jit(solution)/shard_map/ppermute | solution.py:535
  32.5 1.2 %shard_map.96 = bf16[12,16,256]{2,1,0:T(8,128)(2,1)} custom-call(bf16[2,2,16,16,256]{4,3,2,1,0:T(8,128)(2,1)S(1)} %shard_map.88.phases, f32[2,64,128]{2,1,0:T(8,128)S(1)} %get-tuple-element.96.ring_grad, bf16[3,3,256,256]{3,2,1,0:T(8,128)(2,1)S(1)} %copy-done), custom_call_target="tpu_custom_call" | custom-call | bytes 1867776 | tf_op jit(solution)/shard_map/pallas_call | solution.py:28
  33.7 2.2 %collective-permute-done.9.got_up = bf16[1,288,256]{2,1,0:T(8,128)(2,1)S(1)} collective-permute-done((bf16[1,288,256]{2,1,0:T(8,128)(2,1)S(1)}, bf16[1,288,256]{2,1,0:T(8,128)(2,1)S(1)}, u32[]{:S(2)}, u32[]{:S(2)}) %collective-permute-start.9) | collective-permute-done | bytes 147488 | tf_op jit(solution)/shard_map/ppermute | solution.py:535
  36.2 1.4 %collective-permute-start.10 = (bf16[288,128]{1,0:T(8,128)(2,1)S(1)}, bf16[288,128]{1,0:T(8,128)(2,1)S(1)}, u32[]{:S(2)}, u32[]{:S(2)}) collective-permute-start(bf16[288,128]{1,0:T(8,128)(2,1)S(1)} %get-tuple-element.101), channel_id=1, source_target_pairs={{0,1},{1,2},{2,3},{3,0},{4,5},{5,6},{6,7},{7,4},{8,9},{9,10},{10,1... | collective-permute-start | bytes 221192 | tf_op jit(solution)/shard_map/ppermute | solution.py:554
  37.6 0.6 %collective-permute-start.11 = (bf16[288,128]{1,0:T(8,128)(2,1)S(1)}, bf16[288,128]{1,0:T(8,128)(2,1)S(1)}, u32[]{:S(2)}, u32[]{:S(2)}) collective-permute-start(bf16[288,128]{1,0:T(8,128)(2,1)S(1)} %get-tuple-element.102), channel_id=1, source_target_pairs={{0,2},{1,3},{2,0},{3,1},{4,6},{5,7},{6,4},{7,5},{8,10},{9,11},{10,... | collective-permute-start | bytes 221192 | tf_op jit(solution)/shard_map/ppermute | solution.py:554
  38.2 2.2 %collective-permute-start.12 = (bf16[288,128]{1,0:T(8,128)(2,1)S(1)}, bf16[288,128]{1,0:T(8,128)(2,1)S(1)}, u32[]{:S(2)}, u32[]{:S(2)}) collective-permute-start(bf16[288,128]{1,0:T(8,128)(2,1)S(1)} %get-tuple-element.103), channel_id=1, source_target_pairs={{0,3},{1,0},{2,1},{3,2},{4,7},{5,4},{6,5},{7,6},{8,11},{9,8},{10,9... | collective-permute-start | bytes 221192 | tf_op jit(solution)/shard_map/ppermute | solution.py:554
  40.4 2.1 %collective-permute-done.10.refs_0_ = bf16[288,128]{1,0:T(8,128)(2,1)S(1)} collective-permute-done((bf16[288,128]{1,0:T(8,128)(2,1)S(1)}, bf16[288,128]{1,0:T(8,128)(2,1)S(1)}, u32[]{:S(2)}, u32[]{:S(2)}) %collective-permute-start.10) | collective-permute-done | bytes 73760 | tf_op jit(solution)/shard_map/ppermute | solution.py:554
  42.5 1.5 %collective-permute-done.11.refs_1_ = bf16[288,128]{1,0:T(8,128)(2,1)S(1)} collective-permute-done((bf16[288,128]{1,0:T(8,128)(2,1)S(1)}, bf16[288,128]{1,0:T(8,128)(2,1)S(1)}, u32[]{:S(2)}, u32[]{:S(2)}) %collective-permute-start.11) | collective-permute-done | bytes 73760 | tf_op jit(solution)/shard_map/ppermute | solution.py:554
  44.0 0.8 %shard_map.98 = (f32[64,288]{1,0:T(8,128)}, f32[64,288]{1,0:T(8,128)}) custom-call(f32[288,128]{1,0:T(8,128)S(1)} %get-tuple-element.100.own, bf16[288,128]{1,0:T(8,128)(2,1)S(1)} %collective-permute-done.10.refs_0_, bf16[288,128]{1,0:T(8,128)(2,1)S(1)} %collective-permute-done.11.refs_1_, bf16[288,128]{1,0:T(8,128)(2,1)S(1)} %collective-permute-done.12.refs_2_), custom_call_target="tpu_custom_call" | custom-call | bytes 516096 | tf_op jit(solution)/shard_map/pallas_call | solution.py:28
  (19 shorter events, 2.8 us)
Async XLA Ops:
  0.6 12.5 %copy-start = (bf16[3,3,256,256]{3,2,1,0:T(8,128)(2,1)S(1)}, bf16[3,3,256,256]{3,2,1,0:T(8,128)(2,1)}, u32[]{:S(2)}) copy-start(bf16[3,3,256,256]{3,2,1,0:T(8,128)(2,1)} %up_w.7) | copy-start | bytes 3538948
  2.0 4.1 %collective-permute-start = (bf16[96,256]{1,0:T(8,128)(2,1)S(1)}, bf16[96,256]{1,0:T(8,128)(2,1)S(1)}, u32[]{:S(2)}, u32[]{:S(2)}) collective-permute-start(bf16[96,256]{1,0:T(8,128)(2,1)S(1)} %get-tuple-element.58), channel_id=1, source_target_pairs={{0,4},{4,0},{8,12},{12,8},{16,20},{20,16},{24,28},{28,24},{1,5},{5... | collective-permute-start | bytes 147464 | tf_op jit(solution)/shard_map/ppermute | solution.py:566
  2.5 5.3 %collective-permute-start.1 = (bf16[96,256]{1,0:T(8,128)(2,1)S(1)}, bf16[96,256]{1,0:T(8,128)(2,1)S(1)}, u32[]{:S(2)}, u32[]{:S(2)}) collective-permute-start(bf16[96,256]{1,0:T(8,128)(2,1)S(1)} %get-tuple-element.59), channel_id=1, source_target_pairs={{0,28},{4,8},{8,4},{12,16},{16,12},{20,24},{24,20},{28,0},{1,29},{... | collective-permute-start | bytes 147464 | tf_op jit(solution)/shard_map/ppermute | solution.py:566
  7.9 8.2 %collective-permute-start.2 = (bf16[128,256]{1,0:T(8,128)(2,1)S(1)}, bf16[128,256]{1,0:T(8,128)(2,1)S(1)}, u32[]{:S(2)}, u32[]{:S(2)}) collective-permute-start(bf16[128,256]{1,0:T(8,128)(2,1)S(1)} %get-tuple-element.60), channel_id=1, source_target_pairs={{1,2},{2,1},{5,6},{6,5},{9,10},{10,9},{13,14},{14,13},{17,18},{18,... | collective-permute-start | bytes 196616 | tf_op jit(solution)/shard_map/ppermute | solution.py:566
  8.5 7.5 %collective-permute-start.3 = (bf16[128,256]{1,0:T(8,128)(2,1)S(1)}, bf16[128,256]{1,0:T(8,128)(2,1)S(1)}, u32[]{:S(2)}, u32[]{:S(2)}) collective-permute-start(bf16[128,256]{1,0:T(8,128)(2,1)S(1)} %get-tuple-element.61), channel_id=1, source_target_pairs={{0,1},{1,0},{2,3},{3,2},{4,5},{5,4},{6,7},{7,6},{8,9},{9,8},{10,11... | collective-permute-start | bytes 196616 | tf_op jit(solution)/shard_map/ppermute | solution.py:566
  17.4 2.1 %collective-permute-start.4 = (bf16[4,288,256]{2,1,0:T(8,128)(2,1)S(1)}, bf16[4,288,256]{2,1,0:T(8,128)(2,1)S(1)}, u32[]{:S(2)}, u32[]{:S(2)}) collective-permute-start(bf16[4,288,256]{2,1,0:T(8,128)(2,1)S(1)} %get-tuple-element.80), channel_id=1, source_target_pairs={{0,4},{4,0},{8,12},{12,8},{16,20},{20,16},{24,28},{28,24},{1,5},{5... | collective-permute-start | bytes 1769480 | tf_op jit(solution)/shard_map/ppermute | solution.py:527
  18.7 2.2 %collective-permute-start.5 = (bf16[4,288,256]{2,1,0:T(8,128)(2,1)S(1)}, bf16[4,288,256]{2,1,0:T(8,128)(2,1)S(1)}, u32[]{:S(2)}, u32[]{:S(2)}) collective-permute-start(bf16[4,288,256]{2,1,0:T(8,128)(2,1)S(1)} %get-tuple-element.78), channel_id=1, source_target_pairs={{0,4},{4,0},{8,12},{12,8},{16,20},{20,16},{24,28},{28,24},{1,5},{5... | collective-permute-start | bytes 1769480 | tf_op jit(solution)/shard_map/ppermute | solution.py:527
  19.6 6.8 %collective-permute-start.6 = (bf16[2,288,256]{2,1,0:T(8,128)(2,1)S(1)}, bf16[2,288,256]{2,1,0:T(8,128)(2,1)S(1)}, u32[]{:S(2)}, u32[]{:S(2)}) collective-permute-start(bf16[2,288,256]{2,1,0:T(8,128)(2,1)S(1)} %get-tuple-element.81), channel_id=1, source_target_pairs={{0,8},{4,20},{8,0},{12,28},{16,24},{20,4},{24,16},{28,12},{1,9},{5... | collective-permute-start | bytes 884744 | tf_op jit(solution)/shard_map/ppermute | solution.py:535
  21.0 9.6 %collective-permute-start.7 = (bf16[2,288,256]{2,1,0:T(8,128)(2,1)S(1)}, bf16[2,288,256]{2,1,0:T(8,128)(2,1)S(1)}, u32[]{:S(2)}, u32[]{:S(2)}) collective-permute-start(bf16[2,288,256]{2,1,0:T(8,128)(2,1)S(1)} %get-tuple-element.83), channel_id=1, source_target_pairs={{0,8},{4,20},{8,0},{12,28},{16,24},{20,4},{24,16},{28,12},{1,9},{5... | collective-permute-start | bytes 884744 | tf_op jit(solution)/shard_map/ppermute | solution.py:535
  26.4 7.2 %collective-permute-start.8 = (bf16[1,288,256]{2,1,0:T(8,128)(2,1)S(1)}, bf16[1,288,256]{2,1,0:T(8,128)(2,1)S(1)}, u32[]{:S(2)}, u32[]{:S(2)}) collective-permute-start(bf16[1,288,256]{2,1,0:T(8,128)(2,1)S(1)} %get-tuple-element.90), channel_id=1, source_target_pairs={{0,16},{4,12},{8,24},{12,4},{16,0},{20,28},{24,8},{28,20},{1,17},{... | collective-permute-start | bytes 442376 | tf_op jit(solution)/shard_map/ppermute | solution.py:535
  30.7 5.2 %collective-permute-start.9 = (bf16[1,288,256]{2,1,0:T(8,128)(2,1)S(1)}, bf16[1,288,256]{2,1,0:T(8,128)(2,1)S(1)}, u32[]{:S(2)}, u32[]{:S(2)}) collective-permute-start(bf16[1,288,256]{2,1,0:T(8,128)(2,1)S(1)} %get-tuple-element.95), channel_id=1, source_target_pairs={{0,16},{4,12},{8,24},{12,4},{16,0},{20,28},{24,8},{28,20},{1,17},{... | collective-permute-start | bytes 442376 | tf_op jit(solution)/shard_map/ppermute | solution.py:535
  36.2 6.3 %collective-permute-start.10 = (bf16[288,128]{1,0:T(8,128)(2,1)S(1)}, bf16[288,128]{1,0:T(8,128)(2,1)S(1)}, u32[]{:S(2)}, u32[]{:S(2)}) collective-permute-start(bf16[288,128]{1,0:T(8,128)(2,1)S(1)} %get-tuple-element.101), channel_id=1, source_target_pairs={{0,1},{1,2},{2,3},{3,0},{4,5},{5,6},{6,7},{7,4},{8,9},{9,10},{10,1... | collective-permute-start | bytes 221192 | tf_op jit(solution)/shard_map/ppermute | solution.py:554
  37.6 6.4 %collective-permute-start.11 = (bf16[288,128]{1,0:T(8,128)(2,1)S(1)}, bf16[288,128]{1,0:T(8,128)(2,1)S(1)}, u32[]{:S(2)}, u32[]{:S(2)}) collective-permute-start(bf16[288,128]{1,0:T(8,128)(2,1)S(1)} %get-tuple-element.102), channel_id=1, source_target_pairs={{0,2},{1,3},{2,0},{3,1},{4,6},{5,7},{6,4},{7,5},{8,10},{9,11},{10,... | collective-permute-start | bytes 221192 | tf_op jit(solution)/shard_map/ppermute | solution.py:554
  38.2 5.8 %collective-permute-start.12 = (bf16[288,128]{1,0:T(8,128)(2,1)S(1)}, bf16[288,128]{1,0:T(8,128)(2,1)S(1)}, u32[]{:S(2)}, u32[]{:S(2)}) collective-permute-start(bf16[288,128]{1,0:T(8,128)(2,1)S(1)} %get-tuple-element.103), channel_id=1, source_target_pairs={{0,3},{1,0},{2,1},{3,2},{4,7},{5,4},{6,5},{7,6},{8,11},{9,8},{10,9... | collective-permute-start | bytes 221192 | tf_op jit(solution)/shard_map/ppermute | solution.py:554

commit v11 on v10

--- a/solution.py
+++ b/solution.py
@@ -494,28 +494,60 @@
             message[slot - half] = total.astype(bf16)
 
 
+def packing(rows, cols):
+    side = max(1, LANES // cols)
+    return side if rows % (16 * side) == 0 else 1
+
+
+def conv_band_kernel(conv, got, own, message, cut):
+    n_bands, _, cols = cut.shape
+    total = conv[0] + got[0].astype(f32)
+    for band in range(n_bands):
+        cut[band] = total[:, band * cols : (band + 1) * cols]
+    band = place_of()[2]
+    for slot in range(n_bands // 2):
+        lanes = slice(slot * cols, (slot + 1) * cols)
+        own[:, lanes] = cut[band ^ (2 * slot)]
+        message[:, lanes] = cut[band ^ (2 * slot + 1)].astype(bf16)
+
+
 def band_kernel(conv, got_conv, up, got_up, own, *refs):
-    n_bands, messages, cut = len(refs), refs[:-1], refs[-1]
-    conv_total = conv[0] + got_conv[0].astype(f32)
+    messages, cut = refs[:-1], refs[-1]
+    n_bands, rows, cols = cut.shape
+    conv_total = conv[...] + got_conv[...].astype(f32)
     up_total = up[0] + got_up[0].astype(f32)
-    cols = conv_total.shape[1] // n_bands
     for band in range(n_bands):
-        cut[band, :, :cols] = conv_total[:, band * cols : (band + 1) * cols]
-        cut[band, :, cols:] = up_total[:, band * cols : (band + 1) * cols]
+        cut[band] = up_total[:, band * cols : (band + 1) * cols]
     band = place_of()[2]
-    own[...] = cut[band]
-    for k, message in enumerate(messages):
-        message[...] = cut[lax.rem(band + k + 1, n_bands)].astype(bf16)
+    own[:, :cols] = conv_total[:, :cols]
+    own[:, cols:] = cut[band]
+    for k, message in enumerate(messages, 1):
+        piece = cut[band ^ k].astype(bf16)
+        if k % 2:
+            side = packing(rows, cols)
+            for part in range(side):
+                some = piece[part * rows // side : (part + 1) * rows // side]
+                message[:, part * cols : (part + 1) * cols] = some
+        else:
+            message[:, :cols] = conv_total[:, k // 2 * cols : (k // 2 + 1) * cols].astype(bf16)
+            message[:, cols:] = piece
 
 
 def last_kernel(own, *refs):
-    peers, (conv, up) = refs[:-2], refs[-2:]
-    total = own[...]
+    peers, (conv, up, total) = refs[:-3], refs[-3:]
+    rows, cols = own.shape[0], own.shape[1] // 2
+    total[...] = own[...]
     for peer in peers:
-        total = total + peer[...].astype(f32)
-    turned = total.T
-    conv[...] = turned[: conv.shape[0]]
-    up[...] = turned[conv.shape[0] :]
+        if peer.shape == own.shape:
+            total[...] += peer[...].astype(f32)
+            continue
+        side = peer.shape[1] // cols
+        for part in range(side):
+            some = slice(part * rows // side, (part + 1) * rows // side)
+            total[some, cols:] += peer[:, part * cols : (part + 1) * cols].astype(f32)
+    turned = total[...].T
+    conv[...] = turned[:cols]
+    up[...] = turned[cols:]
 
 
 def xor_pairs(count, bits):
@@ -541,20 +573,35 @@
     return kernel_call(plane_kernel, [sds(shape, f32), sds(shape, bf16)], [], 0, own, got)
 
 
+def conv_band_swap(conv, got):
+    bands = lax.axis_size("band")
+    _, block, channels = conv.shape
+    shape = (block, channels // 2)
+    own, message = kernel_call(
+        conv_band_kernel, [sds(shape, f32), sds(shape, bf16)],
+        [pltpu.VMEM((bands, block, channels // bands), f32)], 0, conv, got,
+    )
+    return own, lax.ppermute(message, "band", xor_pairs(bands, 1))
+
+
 def band_sum(conv, got_conv, up, got_up):
     bands = lax.axis_size("band")
-    _, block, channels = conv.shape
+    _, block, channels = up.shape
     cols = channels // bands
-    shape = (block, 2 * cols)
+    side = packing(block, cols)
+    shapes = [(block // side, cols * side) if k % 2 else (block, 2 * cols) for k in range(bands)]
     own, *messages = kernel_call(
-        band_kernel, [sds(shape, f32)] + [sds(shape, bf16)] * (bands - 1),
-        [pltpu.VMEM((bands,) + shape, f32)], 0, conv, got_conv, up, got_up,
+        band_kernel, [sds(shapes[0], f32)] + [sds(shape, bf16) for shape in shapes[1:]],
+        [pltpu.VMEM((bands, block, cols), f32)], 0, conv, got_conv, up, got_up,
     )
-    got = [
-        lax.ppermute(messages[k - 1], "band", [(i, (i + k) % bands) for i in range(bands)])
-        for k in range(1, bands)
+    order = sorted(range(1, bands), key=lambda k: (k % 2, -k))
+    got = [lax.ppermute(messages[k - 1], "band", xor_pairs(bands, k)) for k in order]
+    return [
+        a.T
+        for a in kernel_call(
+            last_kernel, [sds((cols, block), f32)] * 2, [pltpu.VMEM(shapes[0], f32)], 0, own, *got
+        )
     ]
-    return [a.T for a in kernel_call(last_kernel, [sds((cols, block), f32)] * 2, [], 0, own, *got)]
 
 
 def after(value, *others):
@@ -659,6 +706,7 @@
                 0, phases, after(ring_grad, to_up), up_weight,
             )[0]
             own_up = after(own_up, grad_coarse)
+    own_conv, got_conv = conv_band_swap(after(own_conv, to_up), got_conv)
     grad_conv, grad_up = band_sum(own_conv, got_conv, own_up, got_up)
     return (decoded, grad_coarse, grad_up, grad_conv)
 

time: 45 us -> 46.4 us (1.031)
  starting transfers between devices: 20 us -> 21 us
  Pallas kernels: 12 us -> 12.5 us
    ppermute x4, waiting for transfers between devices: 6.17 us -> 4.45 us  [plane_swap(): lax.ppermute(message, 'face', [(i, i ^ 2 << orders[i % 2][step]) for i in...]
    ppermute x3 -> x4, waiting for transfers between devices: 3.59 us -> 5.25 us  [the longest x3 3.96 us: band_sum(): lax.ppermute(messages[k - 1], 'band', xor_pairs(bands, k))]
    ppermute x3 -> x4, starting transfers between devices: 4.19 us -> 5.16 us  [the longest x3 3.76 us: band_sum(): lax.ppermute(messages[k - 1], 'band', xor_pairs(bands, k))]
    pallas_call x15 -> x16, Pallas kernels: 12 us -> 12.5 us  [kernel_call(): pl.pallas_call(body, out_shape=tuple(outs), in_specs=[hbm if i in far els...]
  transfers between devices with their start and end apart: 13 -> 14, of which waited for: 8 -> 9; matrix products, arithmetic and copies ran while one was open for 0% -> 0% of each run, Pallas kernels for 18% -> 18%
where the time goes in v11:
time: 46.4 us; the launch traced here: 46.2 us
  starting transfers between devices  21 us (45%)
  Pallas kernels  12.5 us (27%)
  waiting for transfers between devices  12 us (26%)
  between operations  0.74 us (2%)
    pallas_call x16, Pallas kernels, kernel_call(): pl.pallas_call(body, out_shape=tuple(outs), in_specs=[hbm if i in far els...  12.5 us
    ppermute x4, starting transfers between devices, swap(): return (lax.ppermute(first, axis, one), lax.ppermute(second, axis, two))  9.36 us
    ppermute x4, starting transfers between devices, plane_swap(): lax.ppermute(message, 'face', [(i, i ^ 2 << orders[i % 2][step]) for i in...  5.86 us
    ppermute x4, waiting for transfers between devices, plane_swap(): lax.ppermute(message, 'face', [(i, i ^ 2 << orders[i % 2][step]) for i in...  4.45 us
    ppermute x3, waiting for transfers between devices, band_sum(): lax.ppermute(messages[k - 1], 'band', xor_pairs(bands, k))  3.96 us
    ppermute x3, starting transfers between devices, band_sum(): lax.ppermute(messages[k - 1], 'band', xor_pairs(bands, k))  3.76 us
    ppermute x4, waiting for transfers between devices, swap(): return (lax.ppermute(first, axis, one), lax.ppermute(second, axis, two))  1.78 us
    ppermute x1, starting transfers between devices, conv_band_swap(): return (own, lax.ppermute(message, 'band', xor_pairs(bands, 1)))  1.4 us
  transfers between devices with their start and end apart: 14, of which 9 were waited for; matrix products, arithmetic and copies ran while one was open for 0% of the time, Pallas kernels for 18%

profile of v11, /device:TPU:0, one launch (start us, length us, event | category | flops | bytes accessed | tf_op | source)
XLA Modules:
  0.0 46.2 jit_solution(12288976933405893500)
XLA Ops:
  0.6 1.3 %shard_map.84 = (bf16[96,256]{1,0:T(8,128)(2,1)S(1)}, bf16[96,256]{1,0:T(8,128)(2,1)S(1)}, bf16[24,32,256]{2,1,0:T(8,128)(2,1)S(1)}, bf16[24,32,256]{2,1,0:T(8,128)(2,1)S(1)}, bf16[12,16,256]{2,1,0:T(8,128)(2,1)S(1)}) custom-call(bf16[12,16,256]{2,1,0:T(8,128)(2,1)} %coarse.1, bf16[24,32,256]{2,1,0:T(8,128)(2,1)} %skip.1, bf16[24,32,256]{2,1,0:T(8,128)(2,1)} %cot.1), custom_call_target="tpu_custom_call" | custom-call | bytes 1867776 | tf_op jit(solution)/shard_map/pallas_call | solution.py:28
  2.5 3.6 %collective-permute-start.1 = (bf16[96,256]{1,0:T(8,128)(2,1)S(1)}, bf16[96,256]{1,0:T(8,128)(2,1)S(1)}, u32[]{:S(2)}, u32[]{:S(2)}) collective-permute-start(bf16[96,256]{1,0:T(8,128)(2,1)S(1)} %get-tuple-element.62), channel_id=1, source_target_pairs={{0,28},{4,8},{8,4},{12,16},{16,12},{20,24},{24,20},{28,0},{1,29},{... | collective-permute-start | bytes 147464 | tf_op jit(solution)/shard_map/ppermute | solution.py:613
  6.0 1.8 %collective-permute-done.1.got_second = bf16[96,256]{1,0:T(8,128)(2,1)S(1)} collective-permute-done((bf16[96,256]{1,0:T(8,128)(2,1)S(1)}, bf16[96,256]{1,0:T(8,128)(2,1)S(1)}, u32[]{:S(2)}, u32[]{:S(2)}) %collective-permute-start.1) | collective-permute-done | bytes 49184 | tf_op jit(solution)/shard_map/ppermute | solution.py:613
  7.9 0.7 %collective-permute-start.2 = (bf16[128,256]{1,0:T(8,128)(2,1)S(1)}, bf16[128,256]{1,0:T(8,128)(2,1)S(1)}, u32[]{:S(2)}, u32[]{:S(2)}) collective-permute-start(bf16[128,256]{1,0:T(8,128)(2,1)S(1)} %get-tuple-element.63), channel_id=1, source_target_pairs={{1,2},{2,1},{5,6},{6,5},{9,10},{10,9},{13,14},{14,13},{17,18},{18,... | collective-permute-start | bytes 196616 | tf_op jit(solution)/shard_map/ppermute | solution.py:613
  8.5 4.6 %collective-permute-start.3 = (bf16[128,256]{1,0:T(8,128)(2,1)S(1)}, bf16[128,256]{1,0:T(8,128)(2,1)S(1)}, u32[]{:S(2)}, u32[]{:S(2)}) collective-permute-start(bf16[128,256]{1,0:T(8,128)(2,1)S(1)} %get-tuple-element.64), channel_id=1, source_target_pairs={{0,1},{1,0},{2,3},{3,2},{4,5},{5,4},{6,7},{7,6},{8,9},{9,8},{10,11... | collective-permute-start | bytes 196616 | tf_op jit(solution)/shard_map/ppermute | solution.py:613
  13.2 2.9 %shard_map.86 = (bf16[3,26,32,256]{3,2,1,0:T(8,128)(2,1)S(1)}, bf16[2,17,16,256]{3,2,1,0:T(8,128)(2,1)S(1)}, bf16[24,32,256]{2,1,0:T(8,128)(2,1)S(1)}, f32[768,2...) custom-call(bf16[12,16,256]{2,1,0:T(8,128)(2,1)S(1)} %get-tuple-elem, ...), custom_call_target="tpu_custom_call" | custom-call | bytes 10534912 | tf_op jit(solution)/shard_map/pallas_call | solution.py:28
  16.1 1.3 %shard_map.87 = (bf16[3,26,32,256]{3,2,1,0:T(8,128)(2,1)S(1)}, bf16[2,17,16,256]{3,2,1,0:T(8,128)(2,1)S(1)}, bf16[24,32,256]{2,1,0:T(8,128)(2,1)S(1)}, f32[768,2...) custom-call(bf16[128,256]{1,0:T(8,128)(2,1)S(1)} %collective-permute, ...), custom_call_target="tpu_custom_call", output_to_operand_aliasing={{0}: (5, {}), {1}: (6, {}), {2}: (7, {}), {3}: (8, {}), {4}... | custom-call | bytes 12484608 | tf_op jit(solution)/shard_map/pallas_call | solution.py:28
  17.9 0.7 %shard_map.89 = (f32[2304,256]{1,0:T(8,128)S(1)}, bf16[4,288,256]{2,1,0:T(8,128)(2,1)S(1)}) custom-call(bf16[2,17,16,256]{3,2,1,0:T(8,128)(2,1)S(1)} %get-tuple-element.74.near, bf16[2,2,16,16,256]{4,3,2,1,0:T(8,128)(2,1)S(1)} %shard_map.88.phases), custom_call_target="tpu_custom_call" | custom-call | bytes 3751936 | tf_op jit(solution)/shard_map/pallas_call | solution.py:28
  19.6 1.0 %collective-permute-start.6 = (bf16[2,288,256]{2,1,0:T(8,128)(2,1)S(1)}, bf16[2,288,256]{2,1,0:T(8,128)(2,1)S(1)}, u32[]{:S(2)}, u32[]{:S(2)}) collective-permute-start(bf16[2,288,256]{2,1,0:T(8,128)(2,1)S(1)} %get-tuple-element.84), channel_id=1, source_target_pairs={{0,8},{4,20},{8,0},{12,28},{16,24},{20,4},{24,16},{28,12},{1,9},{5... | collective-permute-start | bytes 884744 | tf_op jit(solution)/shard_map/ppermute | solution.py:567
  21.0 1.3 %collective-permute-start.7 = (bf16[2,288,256]{2,1,0:T(8,128)(2,1)S(1)}, bf16[2,288,256]{2,1,0:T(8,128)(2,1)S(1)}, u32[]{:S(2)}, u32[]{:S(2)}) collective-permute-start(bf16[2,288,256]{2,1,0:T(8,128)(2,1)S(1)} %get-tuple-element.86), channel_id=1, source_target_pairs={{0,8},{4,20},{8,0},{12,28},{16,24},{20,4},{24,16},{28,12},{1,9},{5... | collective-permute-start | bytes 884744 | tf_op jit(solution)/shard_map/ppermute | solution.py:567
  22.3 0.8 %shard_map.92 = (f32[128,256]{1,0:T(8,128)S(1)}, f32[2,64,128]{2,1,0:T(8,128)S(1)}) custom-call(bf16[12,16,256]{2,1,0:T(8,128)(2,1)S(1)} %get-tuple-element.58.coarse, bf16[24,32,256]{2,1,0:T(8,128)(2,1)S(1)} %get-tuple-element.60.cot, f32[96,256]{1,0:T(8,128)S(1)} %get-tuple-element.87.left, f32[96,256]{1,0:T(8,128)S(1)} %get-tuple-element.65.right, ...), custom_call_target="tpu_custom_call" | custom-call | bytes 3506176 | tf_op jit(solution)/shard_map/pallas_call | solution.py:28
  23.0 3.3 %collective-permute-done.6.got = bf16[2,288,256]{2,1,0:T(8,128)(2,1)S(1)} collective-permute-done((bf16[2,288,256]{2,1,0:T(8,128)(2,1)S(1)}, bf16[2,288,256]{2,1,0:T(8,128)(2,1)S(1)}, u32[]{:S(2)}, u32[]{:S(2)}) %collective-permute-start.6) | collective-permute-done | bytes 294944 | tf_op jit(solution)/shard_map/ppermute | solution.py:567
  26.4 1.8 %collective-permute-start.8 = (bf16[1,288,256]{2,1,0:T(8,128)(2,1)S(1)}, bf16[1,288,256]{2,1,0:T(8,128)(2,1)S(1)}, u32[]{:S(2)}, u32[]{:S(2)}) collective-permute-start(bf16[1,288,256]{2,1,0:T(8,128)(2,1)S(1)} %get-tuple-element.93), channel_id=1, source_target_pairs={{0,16},{4,12},{8,24},{12,4},{16,0},{20,28},{24,8},{28,20},{1,17},{... | collective-permute-start | bytes 442376 | tf_op jit(solution)/shard_map/ppermute | solution.py:567
  28.2 1.8 %shard_map.94 = bf16[24,32,256]{2,1,0:T(8,128)(2,1)} custom-call(bf16[24,32,256]{2,1,0:T(8,128)(2,1)S(1)} %get-tuple-element.73.act, f32[128,256]{1,0:T(8,128)S(1)} %get-tuple-element.94.ring_act, bf16[3,3,256,256]{3,2,1,0:T(8,128)(2,1)S(1)} %get-tuple-element.78.conv_w), custom_call_target="tpu_custom_call" | custom-call | bytes 2097152 | tf_op jit(solution)/shard_map/pallas_call | solution.py:28
  30.0 0.6 %collective-permute-done.7.got = bf16[2,288,256]{2,1,0:T(8,128)(2,1)S(1)} collective-permute-done((bf16[2,288,256]{2,1,0:T(8,128)(2,1)S(1)}, bf16[2,288,256]{2,1,0:T(8,128)(2,1)S(1)}, u32[]{:S(2)}, u32[]{:S(2)}) %collective-permute-start.7) | collective-permute-done | bytes 294944 | tf_op jit(solution)/shard_map/ppermute | solution.py:567
  30.7 1.8 %collective-permute-start.10 = (bf16[1,288,256]{2,1,0:T(8,128)(2,1)S(1)}, bf16[1,288,256]{2,1,0:T(8,128)(2,1)S(1)}, u32[]{:S(2)}, u32[]{:S(2)}) collective-permute-start(bf16[1,288,256]{2,1,0:T(8,128)(2,1)S(1)} %get-tuple-element.98), channel_id=1, source_target_pairs={{0,16},{4,12},{8,24},{12,4},{16,0},{20,28},{24,8},{28,20},{1,17},{... | collective-permute-start | bytes 442376 | tf_op jit(solution)/shard_map/ppermute | solution.py:567
  32.8 1.4 %collective-permute-start.9 = (bf16[288,128]{1,0:T(8,128)(2,1)S(1)}, bf16[288,128]{1,0:T(8,128)(2,1)S(1)}, u32[]{:S(2)}, u32[]{:S(2)}) collective-permute-start(bf16[288,128]{1,0:T(8,128)(2,1)S(1)} %get-tuple-element.103), channel_id=1, source_target_pairs={{0,1},{1,0},{2,3},{3,2},{4,5},{5,4},{6,7},{7,6},{8,9},{9,8},{10,11... | collective-permute-start | bytes 221192 | tf_op jit(solution)/shard_map/ppermute | solution.py:584
  34.2 1.2 %shard_map.96 = bf16[12,16,256]{2,1,0:T(8,128)(2,1)} custom-call(bf16[2,2,16,16,256]{4,3,2,1,0:T(8,128)(2,1)S(1)} %shard_map.88.phases, f32[2,64,128]{2,1,0:T(8,128)S(1)} %get-tuple-element.99.ring_grad, bf16[3,3,256,256]{3,2,1,0:T(8,128)(2,1)S(1)} %copy-done), custom_call_target="tpu_custom_call" | custom-call | bytes 1867776 | tf_op jit(solution)/shard_map/pallas_call | solution.py:28
  35.9 1.3 %collective-permute-done.9.got_conv = bf16[288,128]{1,0:T(8,128)(2,1)S(1)} collective-permute-done((bf16[288,128]{1,0:T(8,128)(2,1)S(1)}, bf16[288,128]{1,0:T(8,128)(2,1)S(1)}, u32[]{:S(2)}, u32[]{:S(2)}) %collective-permute-start.9) | collective-permute-done | bytes 73760 | tf_op jit(solution)/shard_map/ppermute | solution.py:584
  37.6 1.3 %collective-permute-start.11 = (bf16[288,128]{1,0:T(8,128)(2,1)S(1)}, bf16[288,128]{1,0:T(8,128)(2,1)S(1)}, u32[]{:S(2)}, u32[]{:S(2)}) collective-permute-start(bf16[288,128]{1,0:T(8,128)(2,1)S(1)} %get-tuple-element.107), channel_id=1, source_target_pairs={{0,2},{1,3},{2,0},{3,1},{4,6},{5,7},{6,4},{7,5},{8,10},{9,11},{10,... | collective-permute-start | bytes 221192 | tf_op jit(solution)/shard_map/ppermute | solution.py:598
  38.9 2.5 %collective-permute-start.12 = (bf16[144,128]{1,0:T(8,128)(2,1)S(1)}, bf16[144,128]{1,0:T(8,128)(2,1)S(1)}, u32[]{:S(2)}, u32[]{:S(2)}) collective-permute-start(bf16[144,128]{1,0:T(8,128)(2,1)S(1)} %get-tuple-element.108), channel_id=1, source_target_pairs={{0,3},{1,2},{2,1},{3,0},{4,7},{5,6},{6,5},{7,4},{8,11},{9,10},{10,... | collective-permute-start | bytes 110600 | tf_op jit(solution)/shard_map/ppermute | solution.py:598
  41.3 3.3 %collective-permute-done.12.refs_1_ = bf16[144,128]{1,0:T(8,128)(2,1)S(1)} collective-permute-done((bf16[144,128]{1,0:T(8,128)(2,1)S(1)}, bf16[144,128]{1,0:T(8,128)(2,1)S(1)}, u32[]{:S(2)}, u32[]{:S(2)}) %collective-permute-start.12) | collective-permute-done | bytes 36896 | tf_op jit(solution)/shard_map/ppermute | solution.py:598
  44.6 0.7 %collective-permute-done.13.refs_2_ = bf16[144,128]{1,0:T(8,128)(2,1)S(1)} collective-permute-done((bf16[144,128]{1,0:T(8,128)(2,1)S(1)}, bf16[144,128]{1,0:T(8,128)(2,1)S(1)}, u32[]{:S(2)}, u32[]{:S(2)}) %collective-permute-start.13) | collective-permute-done | bytes 36896 | tf_op jit(solution)/shard_map/ppermute | solution.py:598
  45.3 0.9 %shard_map.99 = (f32[64,288]{1,0:T(8,128)}, f32[64,288]{1,0:T(8,128)}) custom-call(f32[288,128]{1,0:T(8,128)S(1)} %get-tuple-element.106.own, bf16[288,128]{1,0:T(8,128)(2,1)S(1)} %collective-permute-done.11.refs_0_, bf16[144,128]{1,0:T(8,128)(2,1)S(1)} %collective-permute-done.12.refs_1_, bf16[144,128]{1,0:T(8,128)(2,1)S(1)} %collective-permute-done.13.refs_2_), custom_call_target="tpu_custom_call" | custom-call | bytes 442368 | tf_op jit(solution)/shard_map/pallas_call | solution.py:28
  (22 shorter events, 3.7 us)
Async XLA Ops:
  0.6 12.5 %copy-start = (bf16[3,3,256,256]{3,2,1,0:T(8,128)(2,1)S(1)}, bf16[3,3,256,256]{3,2,1,0:T(8,128)(2,1)}, u32[]{:S(2)}) copy-start(bf16[3,3,256,256]{3,2,1,0:T(8,128)(2,1)} %up_w.7) | copy-start | bytes 3538948
  2.0 4.1 %collective-permute-start = (bf16[96,256]{1,0:T(8,128)(2,1)S(1)}, bf16[96,256]{1,0:T(8,128)(2,1)S(1)}, u32[]{:S(2)}, u32[]{:S(2)}) collective-permute-start(bf16[96,256]{1,0:T(8,128)(2,1)S(1)} %get-tuple-element.61), channel_id=1, source_target_pairs={{0,4},{4,0},{8,12},{12,8},{16,20},{20,16},{24,28},{28,24},{1,5},{5... | collective-permute-start | bytes 147464 | tf_op jit(solution)/shard_map/ppermute | solution.py:613
  2.5 5.3 %collective-permute-start.1 = (bf16[96,256]{1,0:T(8,128)(2,1)S(1)}, bf16[96,256]{1,0:T(8,128)(2,1)S(1)}, u32[]{:S(2)}, u32[]{:S(2)}) collective-permute-start(bf16[96,256]{1,0:T(8,128)(2,1)S(1)} %get-tuple-element.62), channel_id=1, source_target_pairs={{0,28},{4,8},{8,4},{12,16},{16,12},{20,24},{24,20},{28,0},{1,29},{... | collective-permute-start | bytes 147464 | tf_op jit(solution)/shard_map/ppermute | solution.py:613
  7.9 8.2 %collective-permute-start.2 = (bf16[128,256]{1,0:T(8,128)(2,1)S(1)}, bf16[128,256]{1,0:T(8,128)(2,1)S(1)}, u32[]{:S(2)}, u32[]{:S(2)}) collective-permute-start(bf16[128,256]{1,0:T(8,128)(2,1)S(1)} %get-tuple-element.63), channel_id=1, source_target_pairs={{1,2},{2,1},{5,6},{6,5},{9,10},{10,9},{13,14},{14,13},{17,18},{18,... | collective-permute-start | bytes 196616 | tf_op jit(solution)/shard_map/ppermute | solution.py:613
  8.5 7.5 %collective-permute-start.3 = (bf16[128,256]{1,0:T(8,128)(2,1)S(1)}, bf16[128,256]{1,0:T(8,128)(2,1)S(1)}, u32[]{:S(2)}, u32[]{:S(2)}) collective-permute-start(bf16[128,256]{1,0:T(8,128)(2,1)S(1)} %get-tuple-element.64), channel_id=1, source_target_pairs={{0,1},{1,0},{2,3},{3,2},{4,5},{5,4},{6,7},{7,6},{8,9},{9,8},{10,11... | collective-permute-start | bytes 196616 | tf_op jit(solution)/shard_map/ppermute | solution.py:613
  17.4 2.1 %collective-permute-start.4 = (bf16[4,288,256]{2,1,0:T(8,128)(2,1)S(1)}, bf16[4,288,256]{2,1,0:T(8,128)(2,1)S(1)}, u32[]{:S(2)}, u32[]{:S(2)}) collective-permute-start(bf16[4,288,256]{2,1,0:T(8,128)(2,1)S(1)} %get-tuple-element.83), channel_id=1, source_target_pairs={{0,4},{4,0},{8,12},{12,8},{16,20},{20,16},{24,28},{28,24},{1,5},{5... | collective-permute-start | bytes 1769480 | tf_op jit(solution)/shard_map/ppermute | solution.py:559
  18.7 2.2 %collective-permute-start.5 = (bf16[4,288,256]{2,1,0:T(8,128)(2,1)S(1)}, bf16[4,288,256]{2,1,0:T(8,128)(2,1)S(1)}, u32[]{:S(2)}, u32[]{:S(2)}) collective-permute-start(bf16[4,288,256]{2,1,0:T(8,128)(2,1)S(1)} %get-tuple-element.81), channel_id=1, source_target_pairs={{0,4},{4,0},{8,12},{12,8},{16,20},{20,16},{24,28},{28,24},{1,5},{5... | collective-permute-start | bytes 1769480 | tf_op jit(solution)/shard_map/ppermute | solution.py:559
  19.6 6.8 %collective-permute-start.6 = (bf16[2,288,256]{2,1,0:T(8,128)(2,1)S(1)}, bf16[2,288,256]{2,1,0:T(8,128)(2,1)S(1)}, u32[]{:S(2)}, u32[]{:S(2)}) collective-permute-start(bf16[2,288,256]{2,1,0:T(8,128)(2,1)S(1)} %get-tuple-element.84), channel_id=1, source_target_pairs={{0,8},{4,20},{8,0},{12,28},{16,24},{20,4},{24,16},{28,12},{1,9},{5... | collective-permute-start | bytes 884744 | tf_op jit(solution)/shard_map/ppermute | solution.py:567
  21.0 9.6 %collective-permute-start.7 = (bf16[2,288,256]{2,1,0:T(8,128)(2,1)S(1)}, bf16[2,288,256]{2,1,0:T(8,128)(2,1)S(1)}, u32[]{:S(2)}, u32[]{:S(2)}) collective-permute-start(bf16[2,288,256]{2,1,0:T(8,128)(2,1)S(1)} %get-tuple-element.86), channel_id=1, source_target_pairs={{0,8},{4,20},{8,0},{12,28},{16,24},{20,4},{24,16},{28,12},{1,9},{5... | collective-permute-start | bytes 884744 | tf_op jit(solution)/shard_map/ppermute | solution.py:567
  26.4 6.0 %collective-permute-start.8 = (bf16[1,288,256]{2,1,0:T(8,128)(2,1)S(1)}, bf16[1,288,256]{2,1,0:T(8,128)(2,1)S(1)}, u32[]{:S(2)}, u32[]{:S(2)}) collective-permute-start(bf16[1,288,256]{2,1,0:T(8,128)(2,1)S(1)} %get-tuple-element.93), channel_id=1, source_target_pairs={{0,16},{4,12},{8,24},{12,4},{16,0},{20,28},{24,8},{28,20},{1,17},{... | collective-permute-start | bytes 442376 | tf_op jit(solution)/shard_map/ppermute | solution.py:567
  30.7 5.2 %collective-permute-start.10 = (bf16[1,288,256]{2,1,0:T(8,128)(2,1)S(1)}, bf16[1,288,256]{2,1,0:T(8,128)(2,1)S(1)}, u32[]{:S(2)}, u32[]{:S(2)}) collective-permute-start(bf16[1,288,256]{2,1,0:T(8,128)(2,1)S(1)} %get-tuple-element.98), channel_id=1, source_target_pairs={{0,16},{4,12},{8,24},{12,4},{16,0},{20,28},{24,8},{28,20},{1,17},{... | collective-permute-start | bytes 442376 | tf_op jit(solution)/shard_map/ppermute | solution.py:567
  32.8 4.4 %collective-permute-start.9 = (bf16[288,128]{1,0:T(8,128)(2,1)S(1)}, bf16[288,128]{1,0:T(8,128)(2,1)S(1)}, u32[]{:S(2)}, u32[]{:S(2)}) collective-permute-start(bf16[288,128]{1,0:T(8,128)(2,1)S(1)} %get-tuple-element.103), channel_id=1, source_target_pairs={{0,1},{1,0},{2,3},{3,2},{4,5},{5,4},{6,7},{7,6},{8,9},{9,8},{10,11... | collective-permute-start | bytes 221192 | tf_op jit(solution)/shard_map/ppermute | solution.py:584
  37.6 7.7 %collective-permute-start.11 = (bf16[288,128]{1,0:T(8,128)(2,1)S(1)}, bf16[288,128]{1,0:T(8,128)(2,1)S(1)}, u32[]{:S(2)}, u32[]{:S(2)}) collective-permute-start(bf16[288,128]{1,0:T(8,128)(2,1)S(1)} %get-tuple-element.107), channel_id=1, source_target_pairs={{0,2},{1,3},{2,0},{3,1},{4,6},{5,7},{6,4},{7,5},{8,10},{9,11},{10,... | collective-permute-start | bytes 221192 | tf_op jit(solution)/shard_map/ppermute | solution.py:598
  38.9 5.8 %collective-permute-start.12 = (bf16[144,128]{1,0:T(8,128)(2,1)S(1)}, bf16[144,128]{1,0:T(8,128)(2,1)S(1)}, u32[]{:S(2)}, u32[]{:S(2)}) collective-permute-start(bf16[144,128]{1,0:T(8,128)(2,1)S(1)} %get-tuple-element.108), channel_id=1, source_target_pairs={{0,3},{1,2},{2,1},{3,0},{4,7},{5,6},{6,5},{7,4},{8,11},{9,10},{10,... | collective-permute-start | bytes 110600 | tf_op jit(solution)/shard_map/ppermute | solution.py:598
  41.3 4.0 %collective-permute-start.13 = (bf16[144,128]{1,0:T(8,128)(2,1)S(1)}, bf16[144,128]{1,0:T(8,128)(2,1)S(1)}, u32[]{:S(2)}, u32[]{:S(2)}) collective-permute-start(bf16[144,128]{1,0:T(8,128)(2,1)S(1)} %get-tuple-element.109), channel_id=1, source_target_pairs={{0,1},{1,0},{2,3},{3,2},{4,5},{5,4},{6,7},{7,6},{8,9},{9,8},{10,11... | collective-permute-start | bytes 110600 | tf_op jit(solution)/shard_map/ppermute | solution.py:598

commit v12 on v10

--- a/solution.py
+++ b/solution.py
@@ -83,12 +83,12 @@
     ref[start : start + value.shape[0], :] = value
 
 
-def other_core(partial, send):
+def other_core(send, *terms):
     core = place_of()[0]
     groups, block, _ = send.shape
     for group in range(groups):
         theirs = pl.multiple_of((2 * group + 1 - core) * block, 16)
-        send[group] = partial[pl.ds(theirs, block), :].astype(bf16)
+        send[group] = sum(term[pl.ds(theirs, block), :] for term in terms).astype(bf16)
 
 
 class Layout:
@@ -170,16 +170,29 @@
     second[...] = jnp.where(even, before[...], after[...]).astype(bf16)
 
 
+def early_kernel(cot, conv_w, conv_v, grad_act, centre, sem):
+    rows, cols, channels = cot.shape
+    copy = pltpu.make_async_copy(conv_w, conv_v, sem)
+    copy.start()
+    for row in (0, rows + 1):
+        centre[row] = jnp.zeros((cols, channels), bf16)
+    centre[pl.ds(1, rows)] = cot[...]
+    copy.wait()
+    total = jnp.zeros((rows * cols, channels), f32)
+    for k in range(3):
+        source = centre[pl.ds(2 - k, rows)].reshape(-1, channels)
+        total = total + dot_nt(source, conv_v[k, 1])
+    grad_act[...] = total
+
+
 def inner_kernel(
-    coarse, skip, cot, left, right, up_w, conv_w,
-    shifted, near, act, slope, partial, last_pre, conv_v, grad_act, padded, pre, sem,
+    coarse, skip, cot, left, right, up_w, conv_w, grad_centre,
+    shifted, near, act, slope, partial, last_pre, grad_act, padded, pre,
 ):
     n_rows, n_cols, channels = coarse.shape
     rows, cols, _ = skip.shape
     at = Layout(n_rows, n_cols)
     stride = cols + 2 * MARGIN
-    copy = pltpu.make_async_copy(conv_w, conv_v, sem)
-    copy.start()
     for row in range(n_rows):
         near[0, row] = coarse[row]
         put(padded, row * stride, coarse[row].astype(f32))
@@ -227,18 +240,17 @@
         for l in range(3):
             source = shifted[2 - l, pl.ds(2 - k, rows)].reshape(-1, channels)
             partial[pl.ds((3 * k + l) * channels, channels), :] = dot(act_t, source)
-    copy.wait()
-    total = jnp.zeros((rows * cols, channels), f32)
-    for k in range(3):
-        for l in range(3):
+    total = grad_centre[...]
+    for k in range(3):
+        for l in (0, 2):
             source = shifted[2 - l, pl.ds(2 - k, rows)].reshape(-1, channels)
-            total = total + dot_nt(source, conv_v[k, l])
+            total = total + dot_nt(source, conv_w[k, l])
     grad_act[...] = total
 
 
 def act_kernel(
-    got_second, got_first, right, up_w, last_pre, shifted_in, near_in, act_in, slope_in, partial_in,
-    shifted, near, act, slope, partial, send, upper, lower, padded, pre,
+    got_first, got_second, right, up_w, last_pre, partial, shifted_in, near_in, act_in, slope_in,
+    shifted, near, act, slope, extra, send, upper, lower, padded, pre,
 ):
     rows, cols, channels = act.shape
     n_rows, n_cols = rows // 2, cols // 2
@@ -279,9 +291,8 @@
                 term = dot(both_t, jnp.concatenate([beside, shifted[2 - l, 0]], axis=0))
             else:
                 term = dot(last_t, beside)
-            tap = pl.ds((3 * k + l) * channels, channels)
-            partial[tap, :] = partial_in[tap, :] + term
-    other_core(partial, send)
+            extra[pl.ds((3 * k + l) * channels, channels), :] = term
+    other_core(send, partial, extra)
 
 
 def grad_kernel(shifted, slope, grad_act, conv_w, phases, fine):
@@ -324,7 +335,7 @@
             partial[pl.ds((3 * k + l) * channels, channels), :] = dot(
                 turned[row_off, col_off], source
             )
-    other_core(partial, send)
+    other_core(send, partial)
 
 
 def ring_kernel(
@@ -470,14 +481,15 @@
     return sum(1 << bit for step, bit in enumerate(order) if slot >> (last - step) & 1)
 
 
-def core_kernel(partial, got, own, message):
+def core_kernel(*refs):
+    *terms, got, own, message = refs
     slots, half, block = got.shape[0], own.shape[0], got.shape[1]
     core, chip, _, _ = place_of()
     even, odd = halving(2 * slots)
     for slot in range(slots):
         target = chip ^ jnp.where(core == 0, mask_of(slot, even), mask_of(slot, odd))
         mine = pl.multiple_of((2 * target + core) * block, 16)
-        total = partial[pl.ds(mine, block), :] + got[target].astype(f32)
+        total = sum(term[pl.ds(mine, block), :] for term in terms) + got[target].astype(f32)
         if slot < half:
             own[slot] = total
         else:
@@ -522,11 +534,11 @@
     return [(i, i ^ bits) for i in range(count)]
 
 
-def core_sum(partial, send):
+def core_sum(send, *terms):
     groups, block, channels = send.shape
     got = lax.ppermute(send, "face", xor_pairs(lax.axis_size("face"), 1))
     shape = (groups // 2, block, channels)
-    return kernel_call(core_kernel, [sds(shape, f32), sds(shape, bf16)], [], 0, partial, got)
+    return kernel_call(core_kernel, [sds(shape, f32), sds(shape, bf16)], [], 0, *terms, got)
 
 
 def plane_swap(message, step):
@@ -583,12 +595,18 @@
         0, coarse, skip, cotangent, far=(0, 1, 2),
     )
     first, second = swap(first, second, "face", True)
+    conv_weight, grad_centre = kernel_call(
+        early_kernel,
+        [sds(conv_weight.shape, bf16), sds((rows * cols, channels), f32)],
+        [pltpu.VMEM((rows + 2, cols, channels), bf16), pltpu.SemaphoreType.DMA],
+        0, cotangent, conv_weight, far=(1,),
+    )
     side = sds(message.shape, f32)
     message = sds((at.band_size, channels), bf16)
     edges = pltpu.VMEM(message.shape, f32)
     first, second, left, right = kernel_call(
         band_message, [message, message, side, side], [edges, edges],
-        0, coarse, skip, cotangent, first, second,
+        0, coarse, skip, after(cotangent, grad_centre), first, second,
     )
     first, second = swap(first, second, "band", False)
 
@@ -602,30 +620,30 @@
         sds(shift_shape, bf16), sds((2, whole + 1, n_cols, channels), bf16),
         sds(skip.shape, bf16), sds((rows * cols, channels), f32), part,
     ]
-    *inner, last_pre, conv_weight, grad_act = kernel_call(
+    *inner, part_conv, last_pre, grad_act = kernel_call(
         inner_kernel,
         [
-            *blocks, sds((cols, channels), f32), sds(conv_weight.shape, bf16),
-            sds((rows * cols, channels), f32),
+            *blocks, sds((cols, channels), f32), sds((rows * cols, channels), f32),
         ],
-        [halves(rows * stride, channels), flat, pltpu.SemaphoreType.DMA],
-        0, coarse, skip, cotangent, left, right, up_weight, conv_weight, far=(6,),
+        [halves(rows * stride, channels), flat],
+        0, coarse, skip, cotangent, left, right, up_weight, conv_weight, grad_centre,
     )
     send = sds((groups, block, channels), bf16)
     side = sds(message.shape, f32)
-    shifted, near, act, slope, part_conv, send_conv, upper, lower = kernel_call(
+    shifted, near, act, slope, extra_conv, send_conv, upper, lower = kernel_call(
         act_kernel, [*blocks, send, side, side],
         [halves(stride, channels), halves(cols, channels)],
-        0, second, first, right, up_weight, last_pre, *inner, changed={5 + i: i for i in range(5)},
+        0, first, second, right, up_weight, last_pre, part_conv, *inner,
+        changed={6 + i: i for i in range(4)},
     )
     phases = kernel_call(
         grad_kernel, [sds((2, 2, whole, n_cols, channels), bf16)], [flat],
         0, shifted, slope, grad_act, conv_weight,
     )[0]
     part_up, send_up = kernel_call(up_kernel, [part, send], [], 0, near, phases)
-    own_conv, to_conv = core_sum(after(part_conv, send_up), send_conv)
+    own_conv, to_conv = core_sum(send_conv, after(part_conv, send_up), extra_conv)
     got_conv = plane_swap(to_conv, 0)
-    own_up, to_up = core_sum(after(part_up, to_conv), send_up)
+    own_up, to_up = core_sum(send_up, after(part_up, to_conv))
     got_up = plane_swap(to_up, 0)
     ring_act, ring_grad = kernel_call(
         ring_kernel,

time: 45 us -> 44.2 us (0.982)
  waiting for transfers between devices: 12 us -> 8.14 us
  starting transfers between devices: 20 us -> 22 us
  Pallas kernels: 12 us -> 13.1 us
    ppermute x3, starting transfers between devices: 4.19 us -> 8.67 us  [band_sum(): lax.ppermute(messages[k - 1], 'band', [(i, (i + k) % bands) for i in rang...]
    ppermute x4, starting transfers between devices: 9.36 us -> 6.38 us  [swap(): return (lax.ppermute(first, axis, one), lax.ppermute(second, axis, two))]
    ppermute x4, waiting for transfers between devices: 1.78 us -> 0.01 us  [swap(): return (lax.ppermute(first, axis, one), lax.ppermute(second, axis, two))]
    ppermute x3, waiting for transfers between devices: 3.59 us -> 1.98 us  [band_sum(): lax.ppermute(messages[k - 1], 'band', [(i, (i + k) % bands) for i in rang...]
    pallas_call x15 -> x16, Pallas kernels: 12 us -> 13.1 us  [kernel_call(): pl.pallas_call(body, out_shape=tuple(outs), in_specs=[hbm if i in far els...]
    ppermute x4, starting transfers between devices: 5.86 us -> 6.35 us  [plane_swap(): lax.ppermute(message, 'face', [(i, i ^ 2 << orders[i % 2][step]) for i in...]
  transfers between devices with their start and end apart: 13 -> 13, of which waited for: 8 -> 6; matrix products, arithmetic and copies ran while one was open for 0% -> 0% of each run, Pallas kernels for 18% -> 22%
where the time goes in v12:
time: 44.2 us; the launch traced here: 44 us
  starting transfers between devices  22 us (50%)
  Pallas kernels  13.1 us (30%)
  waiting for transfers between devices  8.14 us (18%)
  between operations  0.76 us (2%)
    pallas_call x16, Pallas kernels, kernel_call(): pl.pallas_call(body, out_shape=tuple(outs), in_specs=[hbm if i in far els...  13.1 us
    ppermute x3, starting transfers between devices, band_sum(): lax.ppermute(messages[k - 1], 'band', [(i, (i + k) % bands) for i in rang...  8.67 us
    ppermute x4, starting transfers between devices, swap(): return (lax.ppermute(first, axis, one), lax.ppermute(second, axis, two))  6.38 us
    ppermute x4, starting transfers between devices, plane_swap(): lax.ppermute(message, 'face', [(i, i ^ 2 << orders[i % 2][step]) for i in...  6.35 us
    ppermute x4, waiting for transfers between devices, plane_swap(): lax.ppermute(message, 'face', [(i, i ^ 2 << orders[i % 2][step]) for i in...  5.92 us
    ppermute x3, waiting for transfers between devices, band_sum(): lax.ppermute(messages[k - 1], 'band', [(i, (i + k) % bands) for i in rang...  1.98 us
  transfers between devices with their start and end apart: 13, of which 6 were waited for; matrix products, arithmetic and copies ran while one was open for 0% of the time, Pallas kernels for 22%

profile of v12, /device:TPU:0, one launch (start us, length us, event | category | flops | bytes accessed | tf_op | source)
XLA Modules:
  0.0 44.0 jit_solution(227823899518251182)
XLA Ops:
  0.6 1.2 %shard_map.84 = (bf16[96,256]{1,0:T(8,128)(2,1)S(1)}, bf16[96,256]{1,0:T(8,128)(2,1)S(1)}, bf16[24,32,256]{2,1,0:T(8,128)(2,1)S(1)}, bf16[24,32,256]{2,1,0:T(8,128)(2,1)S(1)}, bf16[12,16,256]{2,1,0:T(8,128)(2,1)S(1)}) custom-call(bf16[12,16,256]{2,1,0:T(8,128)(2,1)} %coarse.1, bf16[24,32,256]{2,1,0:T(8,128)(2,1)} %skip.1, bf16[24,32,256]{2,1,0:T(8,128)(2,1)} %cot.1), custom_call_target="tpu_custom_call" | custom-call | bytes 1867776 | tf_op jit(solution)/shard_map/pallas_call | solution.py:28
  2.4 3.6 %collective-permute-start.1 = (bf16[96,256]{1,0:T(8,128)(2,1)S(1)}, bf16[96,256]{1,0:T(8,128)(2,1)S(1)}, u32[]{:S(2)}, u32[]{:S(2)}) collective-permute-start(bf16[96,256]{1,0:T(8,128)(2,1)S(1)} %get-tuple-element.63), channel_id=1, source_target_pairs={{0,28},{4,8},{8,4},{12,16},{16,12},{20,24},{24,20},{28,0},{1,29},{... | collective-permute-start | bytes 147464 | tf_op jit(solution)/shard_map/ppermute | solution.py:578
  5.9 1.9 %shard_map.85 = (bf16[3,3,256,256]{3,2,1,0:T(8,128)(2,1)S(1)}, f32[768,256]{1,0:T(8,128)S(1)}) custom-call(bf16[24,32,256]{2,1,0:T(8,128)(2,1)S(1)} %get-tuple-element.61.cot, bf16[3,3,256,256]{3,2,1,0:T(8,128)(2,1)} %conv_w.1), custom_call_target="tpu_custom_call" | custom-call | bytes 3538944 | tf_op jit(solution)/shard_map/pallas_call | solution.py:28
  7.9 1.7 %collective-permute-start.2 = (bf16[128,256]{1,0:T(8,128)(2,1)S(1)}, bf16[128,256]{1,0:T(8,128)(2,1)S(1)}, u32[]{:S(2)}, u32[]{:S(2)}) collective-permute-start(bf16[128,256]{1,0:T(8,128)(2,1)S(1)} %get-tuple-element.64), channel_id=1, source_target_pairs={{0,1},{1,0},{2,3},{3,2},{4,5},{5,4},{6,7},{7,6},{8,9},{9,8},{10,11... | collective-permute-start | bytes 196616 | tf_op jit(solution)/shard_map/ppermute | solution.py:578
  9.6 0.7 %collective-permute-start.3 = (bf16[128,256]{1,0:T(8,128)(2,1)S(1)}, bf16[128,256]{1,0:T(8,128)(2,1)S(1)}, u32[]{:S(2)}, u32[]{:S(2)}) collective-permute-start(bf16[128,256]{1,0:T(8,128)(2,1)S(1)} %get-tuple-element.65), channel_id=1, source_target_pairs={{1,2},{2,1},{5,6},{6,5},{9,10},{10,9},{13,14},{14,13},{17,18},{18,... | collective-permute-start | bytes 196616 | tf_op jit(solution)/shard_map/ppermute | solution.py:578
  10.2 2.3 %shard_map.87 = (bf16[3,26,32,256]{3,2,1,0:T(8,128)(2,1)S(1)}, bf16[2,17,16,256]{3,2,1,0:T(8,128)(2,1)S(1)}, bf16[24,32,256]{2,1,0:T(8,128)(2,1)S(1)}, f32[768,2...) custom-call(bf16[12,16,256]{2,1,0:T(8,128)(2,1)S(1)} %get-tuple-element.57.coarse, ...), custom_call_target="tpu_custom_call" | custom-call | bytes 10141696 | tf_op jit(solution)/shard_map/pallas_call | solution.py:28
  12.6 1.1 %shard_map.88 = (bf16[3,26,32,256]{3,2,1,0:T(8,128)(2,1)S(1)}, bf16[2,17,16,256]{3,2,1,0:T(8,128)(2,1)S(1)}, bf16[24,32,256]{2,1,0:T(8,128)(2,1)S(1)}, f32[768,2...) custom-call(bf16[128,256]{1,0:T(8,128)(2,1)S(1)} %collective-permute, ...), custom_call_target="tpu_custom_call", output_to_operand_aliasing={{0}: (6, {}), {1}: (7, {}), {2}: (8, {}), {3}: (9, {})} | custom-call | bytes 12484608 | tf_op jit(solution)/shard_map/pallas_call | solution.py:28
  14.3 0.8 %shard_map.90 = (f32[2304,256]{1,0:T(8,128)S(1)}, bf16[4,288,256]{2,1,0:T(8,128)(2,1)S(1)}) custom-call(bf16[2,17,16,256]{3,2,1,0:T(8,128)(2,1)S(1)} %get-tuple-element.76.near, bf16[2,2,16,16,256]{4,3,2,1,0:T(8,128)(2,1)S(1)} %shard_map.89.phases), custom_call_target="tpu_custom_call" | custom-call | bytes 3751936 | tf_op jit(solution)/shard_map/pallas_call | solution.py:28
  16.0 1.3 %collective-permute-start.6 = (bf16[2,288,256]{2,1,0:T(8,128)(2,1)S(1)}, bf16[2,288,256]{2,1,0:T(8,128)(2,1)S(1)}, u32[]{:S(2)}, u32[]{:S(2)}) collective-permute-start(bf16[2,288,256]{2,1,0:T(8,128)(2,1)S(1)} %get-tuple-element.85), channel_id=1, source_target_pairs={{0,8},{4,20},{8,0},{12,28},{16,24},{20,4},{24,16},{28,12},{1,9},{5... | collective-permute-start | bytes 884744 | tf_op jit(solution)/shard_map/ppermute | solution.py:547
  17.4 1.5 %collective-permute-start.7 = (bf16[2,288,256]{2,1,0:T(8,128)(2,1)S(1)}, bf16[2,288,256]{2,1,0:T(8,128)(2,1)S(1)}, u32[]{:S(2)}, u32[]{:S(2)}) collective-permute-start(bf16[2,288,256]{2,1,0:T(8,128)(2,1)S(1)} %get-tuple-element.87), channel_id=1, source_target_pairs={{0,8},{4,20},{8,0},{12,28},{16,24},{20,4},{24,16},{28,12},{1,9},{5... | collective-permute-start | bytes 884744 | tf_op jit(solution)/shard_map/ppermute | solution.py:547
  18.9 0.8 %shard_map.93 = (f32[128,256]{1,0:T(8,128)S(1)}, f32[2,64,128]{2,1,0:T(8,128)S(1)}) custom-call(bf16[12,16,256]{2,1,0:T(8,128)(2,1)S(1)} %get-tuple-element.57.coarse, bf16[24,32,256]{2,1,0:T(8,128)(2,1)S(1)} %get-tuple-element.61.cot, f32[96,256]{1,0:T(8,128)S(1)} %get-tuple-element.88.left, f32[96,256]{1,0:T(8,128)S(1)} %get-tuple-element.66.right, ...), custom_call_target="tpu_custom_call" | custom-call | bytes 3506176 | tf_op jit(solution)/shard_map/pallas_call | solution.py:28
  19.6 3.1 %collective-permute-done.6.got = bf16[2,288,256]{2,1,0:T(8,128)(2,1)S(1)} collective-permute-done((bf16[2,288,256]{2,1,0:T(8,128)(2,1)S(1)}, bf16[2,288,256]{2,1,0:T(8,128)(2,1)S(1)}, u32[]{:S(2)}, u32[]{:S(2)}) %collective-permute-start.6) | collective-permute-done | bytes 294944 | tf_op jit(solution)/shard_map/ppermute | solution.py:547
  22.8 1.8 %collective-permute-start.8 = (bf16[1,288,256]{2,1,0:T(8,128)(2,1)S(1)}, bf16[1,288,256]{2,1,0:T(8,128)(2,1)S(1)}, u32[]{:S(2)}, u32[]{:S(2)}) collective-permute-start(bf16[1,288,256]{2,1,0:T(8,128)(2,1)S(1)} %get-tuple-element.94), channel_id=1, source_target_pairs={{0,16},{4,12},{8,24},{12,4},{16,0},{20,28},{24,8},{28,20},{1,17},{... | collective-permute-start | bytes 442376 | tf_op jit(solution)/shard_map/ppermute | solution.py:547
  24.6 1.8 %shard_map.95 = bf16[24,32,256]{2,1,0:T(8,128)(2,1)} custom-call(bf16[24,32,256]{2,1,0:T(8,128)(2,1)S(1)} %get-tuple-element.75.act, f32[128,256]{1,0:T(8,128)S(1)} %get-tuple-element.95.ring_act, bf16[3,3,256,256]{3,2,1,0:T(8,128)(2,1)S(1)} %get-tuple-element.68.conv_w), custom_call_target="tpu_custom_call" | custom-call | bytes 2097152 | tf_op jit(solution)/shard_map/pallas_call | solution.py:28
  26.4 0.6 %collective-permute-done.7.got = bf16[2,288,256]{2,1,0:T(8,128)(2,1)S(1)} collective-permute-done((bf16[2,288,256]{2,1,0:T(8,128)(2,1)S(1)}, bf16[2,288,256]{2,1,0:T(8,128)(2,1)S(1)}, u32[]{:S(2)}, u32[]{:S(2)}) %collective-permute-start.7) | collective-permute-done | bytes 294944 | tf_op jit(solution)/shard_map/ppermute | solution.py:547
  27.1 1.8 %collective-permute-start.9 = (bf16[1,288,256]{2,1,0:T(8,128)(2,1)S(1)}, bf16[1,288,256]{2,1,0:T(8,128)(2,1)S(1)}, u32[]{:S(2)}, u32[]{:S(2)}) collective-permute-start(bf16[1,288,256]{2,1,0:T(8,128)(2,1)S(1)} %get-tuple-element.99), channel_id=1, source_target_pairs={{0,16},{4,12},{8,24},{12,4},{16,0},{20,28},{24,8},{28,20},{1,17},{... | collective-permute-start | bytes 442376 | tf_op jit(solution)/shard_map/ppermute | solution.py:547
  28.8 1.2 %shard_map.97 = bf16[12,16,256]{2,1,0:T(8,128)(2,1)} custom-call(bf16[2,2,16,16,256]{4,3,2,1,0:T(8,128)(2,1)S(1)} %shard_map.89.phases, f32[2,64,128]{2,1,0:T(8,128)S(1)} %get-tuple-element.100.ring_grad, bf16[3,3,256,256]{3,2,1,0:T(8,128)(2,1)S(1)} %copy-done), custom_call_target="tpu_custom_call" | custom-call | bytes 1867776 | tf_op jit(solution)/shard_map/pallas_call | solution.py:28
  30.0 2.2 %collective-permute-done.9.got_up = bf16[1,288,256]{2,1,0:T(8,128)(2,1)S(1)} collective-permute-done((bf16[1,288,256]{2,1,0:T(8,128)(2,1)S(1)}, bf16[1,288,256]{2,1,0:T(8,128)(2,1)S(1)}, u32[]{:S(2)}, u32[]{:S(2)}) %collective-permute-start.9) | collective-permute-done | bytes 147488 | tf_op jit(solution)/shard_map/ppermute | solution.py:547
  32.6 4.5 %collective-permute-start.10 = (bf16[288,128]{1,0:T(8,128)(2,1)S(1)}, bf16[288,128]{1,0:T(8,128)(2,1)S(1)}, u32[]{:S(2)}, u32[]{:S(2)}) collective-permute-start(bf16[288,128]{1,0:T(8,128)(2,1)S(1)} %get-tuple-element.105), channel_id=1, source_target_pairs={{0,1},{1,2},{2,3},{3,0},{4,5},{5,6},{6,7},{7,4},{8,9},{9,10},{10,1... | collective-permute-start | bytes 221192 | tf_op jit(solution)/shard_map/ppermute | solution.py:566
  37.0 1.4 %collective-permute-start.11 = (bf16[288,128]{1,0:T(8,128)(2,1)S(1)}, bf16[288,128]{1,0:T(8,128)(2,1)S(1)}, u32[]{:S(2)}, u32[]{:S(2)}) collective-permute-start(bf16[288,128]{1,0:T(8,128)(2,1)S(1)} %get-tuple-element.106), channel_id=1, source_target_pairs={{0,2},{1,3},{2,0},{3,1},{4,6},{5,7},{6,4},{7,5},{8,10},{9,11},{10,... | collective-permute-start | bytes 221192 | tf_op jit(solution)/shard_map/ppermute | solution.py:566
  38.4 2.8 %collective-permute-start.12 = (bf16[288,128]{1,0:T(8,128)(2,1)S(1)}, bf16[288,128]{1,0:T(8,128)(2,1)S(1)}, u32[]{:S(2)}, u32[]{:S(2)}) collective-permute-start(bf16[288,128]{1,0:T(8,128)(2,1)S(1)} %get-tuple-element.107), channel_id=1, source_target_pairs={{0,3},{1,0},{2,1},{3,2},{4,7},{5,4},{6,5},{7,6},{8,11},{9,8},{10,9... | collective-permute-start | bytes 221192 | tf_op jit(solution)/shard_map/ppermute | solution.py:566
  41.3 1.1 %collective-permute-done.11.refs_1_ = bf16[288,128]{1,0:T(8,128)(2,1)S(1)} collective-permute-done((bf16[288,128]{1,0:T(8,128)(2,1)S(1)}, bf16[288,128]{1,0:T(8,128)(2,1)S(1)}, u32[]{:S(2)}, u32[]{:S(2)}) %collective-permute-start.11) | collective-permute-done | bytes 73760 | tf_op jit(solution)/shard_map/ppermute | solution.py:566
  42.3 0.9 %collective-permute-done.12.refs_2_ = bf16[288,128]{1,0:T(8,128)(2,1)S(1)} collective-permute-done((bf16[288,128]{1,0:T(8,128)(2,1)S(1)}, bf16[288,128]{1,0:T(8,128)(2,1)S(1)}, u32[]{:S(2)}, u32[]{:S(2)}) %collective-permute-start.12) | collective-permute-done | bytes 73760 | tf_op jit(solution)/shard_map/ppermute | solution.py:566
  43.2 0.8 %shard_map.99 = (f32[64,288]{1,0:T(8,128)}, f32[64,288]{1,0:T(8,128)}) custom-call(f32[288,128]{1,0:T(8,128)S(1)} %get-tuple-element.104.own, bf16[288,128]{1,0:T(8,128)(2,1)S(1)} %collective-permute-done.10.refs_0_, bf16[288,128]{1,0:T(8,128)(2,1)S(1)} %collective-permute-done.11.refs_1_, bf16[288,128]{1,0:T(8,128)(2,1)S(1)} %collective-permute-done.12.refs_2_), custom_call_target="tpu_custom_call" | custom-call | bytes 516096 | tf_op jit(solution)/shard_map/pallas_call | solution.py:28
  (20 shorter events, 2.6 us)
Async XLA Ops:
  1.9 6.0 %collective-permute-start = (bf16[96,256]{1,0:T(8,128)(2,1)S(1)}, bf16[96,256]{1,0:T(8,128)(2,1)S(1)}, u32[]{:S(2)}, u32[]{:S(2)}) collective-permute-start(bf16[96,256]{1,0:T(8,128)(2,1)S(1)} %get-tuple-element.62), channel_id=1, source_target_pairs={{0,4},{4,0},{8,12},{12,8},{16,20},{20,16},{24,28},{28,24},{1,5},{5... | collective-permute-start | bytes 147464 | tf_op jit(solution)/shard_map/ppermute | solution.py:578
  2.4 5.5 %collective-permute-start.1 = (bf16[96,256]{1,0:T(8,128)(2,1)S(1)}, bf16[96,256]{1,0:T(8,128)(2,1)S(1)}, u32[]{:S(2)}, u32[]{:S(2)}) collective-permute-start(bf16[96,256]{1,0:T(8,128)(2,1)S(1)} %get-tuple-element.63), channel_id=1, source_target_pairs={{0,28},{4,8},{8,4},{12,16},{16,12},{20,24},{24,20},{28,0},{1,29},{... | collective-permute-start | bytes 147464 | tf_op jit(solution)/shard_map/ppermute | solution.py:578
  5.9 4.3 %copy-start = (bf16[3,3,256,256]{3,2,1,0:T(8,128)(2,1)S(1)}, bf16[3,3,256,256]{3,2,1,0:T(8,128)(2,1)}, u32[]{:S(2)}) copy-start(bf16[3,3,256,256]{3,2,1,0:T(8,128)(2,1)} %up_w.7) | copy-start | bytes 3538948
  7.9 4.7 %collective-permute-start.2 = (bf16[128,256]{1,0:T(8,128)(2,1)S(1)}, bf16[128,256]{1,0:T(8,128)(2,1)S(1)}, u32[]{:S(2)}, u32[]{:S(2)}) collective-permute-start(bf16[128,256]{1,0:T(8,128)(2,1)S(1)} %get-tuple-element.64), channel_id=1, source_target_pairs={{0,1},{1,0},{2,3},{3,2},{4,5},{5,4},{6,7},{7,6},{8,9},{9,8},{10,11... | collective-permute-start | bytes 196616 | tf_op jit(solution)/shard_map/ppermute | solution.py:578
  9.6 3.0 %collective-permute-start.3 = (bf16[128,256]{1,0:T(8,128)(2,1)S(1)}, bf16[128,256]{1,0:T(8,128)(2,1)S(1)}, u32[]{:S(2)}, u32[]{:S(2)}) collective-permute-start(bf16[128,256]{1,0:T(8,128)(2,1)S(1)} %get-tuple-element.65), channel_id=1, source_target_pairs={{1,2},{2,1},{5,6},{6,5},{9,10},{10,9},{13,14},{14,13},{17,18},{18,... | collective-permute-start | bytes 196616 | tf_op jit(solution)/shard_map/ppermute | solution.py:578
  13.7 2.1 %collective-permute-start.4 = (bf16[4,288,256]{2,1,0:T(8,128)(2,1)S(1)}, bf16[4,288,256]{2,1,0:T(8,128)(2,1)S(1)}, u32[]{:S(2)}, u32[]{:S(2)}) collective-permute-start(bf16[4,288,256]{2,1,0:T(8,128)(2,1)S(1)} %get-tuple-element.84), channel_id=1, source_target_pairs={{0,4},{4,0},{8,12},{12,8},{16,20},{20,16},{24,28},{28,24},{1,5},{5... | collective-permute-start | bytes 1769480 | tf_op jit(solution)/shard_map/ppermute | solution.py:539
  15.0 2.3 %collective-permute-start.5 = (bf16[4,288,256]{2,1,0:T(8,128)(2,1)S(1)}, bf16[4,288,256]{2,1,0:T(8,128)(2,1)S(1)}, u32[]{:S(2)}, u32[]{:S(2)}) collective-permute-start(bf16[4,288,256]{2,1,0:T(8,128)(2,1)S(1)} %get-tuple-element.81), channel_id=1, source_target_pairs={{0,4},{4,0},{8,12},{12,8},{16,20},{20,16},{24,28},{28,24},{1,5},{5... | collective-permute-start | bytes 1769480 | tf_op jit(solution)/shard_map/ppermute | solution.py:539
  16.0 6.8 %collective-permute-start.6 = (bf16[2,288,256]{2,1,0:T(8,128)(2,1)S(1)}, bf16[2,288,256]{2,1,0:T(8,128)(2,1)S(1)}, u32[]{:S(2)}, u32[]{:S(2)}) collective-permute-start(bf16[2,288,256]{2,1,0:T(8,128)(2,1)S(1)} %get-tuple-element.85), channel_id=1, source_target_pairs={{0,8},{4,20},{8,0},{12,28},{16,24},{20,4},{24,16},{28,12},{1,9},{5... | collective-permute-start | bytes 884744 | tf_op jit(solution)/shard_map/ppermute | solution.py:547
  17.4 9.6 %collective-permute-start.7 = (bf16[2,288,256]{2,1,0:T(8,128)(2,1)S(1)}, bf16[2,288,256]{2,1,0:T(8,128)(2,1)S(1)}, u32[]{:S(2)}, u32[]{:S(2)}) collective-permute-start(bf16[2,288,256]{2,1,0:T(8,128)(2,1)S(1)} %get-tuple-element.87), channel_id=1, source_target_pairs={{0,8},{4,20},{8,0},{12,28},{16,24},{20,4},{24,16},{28,12},{1,9},{5... | collective-permute-start | bytes 884744 | tf_op jit(solution)/shard_map/ppermute | solution.py:547
  22.8 7.2 %collective-permute-start.8 = (bf16[1,288,256]{2,1,0:T(8,128)(2,1)S(1)}, bf16[1,288,256]{2,1,0:T(8,128)(2,1)S(1)}, u32[]{:S(2)}, u32[]{:S(2)}) collective-permute-start(bf16[1,288,256]{2,1,0:T(8,128)(2,1)S(1)} %get-tuple-element.94), channel_id=1, source_target_pairs={{0,16},{4,12},{8,24},{12,4},{16,0},{20,28},{24,8},{28,20},{1,17},{... | collective-permute-start | bytes 442376 | tf_op jit(solution)/shard_map/ppermute | solution.py:547
  27.1 5.2 %collective-permute-start.9 = (bf16[1,288,256]{2,1,0:T(8,128)(2,1)S(1)}, bf16[1,288,256]{2,1,0:T(8,128)(2,1)S(1)}, u32[]{:S(2)}, u32[]{:S(2)}) collective-permute-start(bf16[1,288,256]{2,1,0:T(8,128)(2,1)S(1)} %get-tuple-element.99), channel_id=1, source_target_pairs={{0,16},{4,12},{8,24},{12,4},{16,0},{20,28},{24,8},{28,20},{1,17},{... | collective-permute-start | bytes 442376 | tf_op jit(solution)/shard_map/ppermute | solution.py:547
  32.6 8.7 %collective-permute-start.10 = (bf16[288,128]{1,0:T(8,128)(2,1)S(1)}, bf16[288,128]{1,0:T(8,128)(2,1)S(1)}, u32[]{:S(2)}, u32[]{:S(2)}) collective-permute-start(bf16[288,128]{1,0:T(8,128)(2,1)S(1)} %get-tuple-element.105), channel_id=1, source_target_pairs={{0,1},{1,2},{2,3},{3,0},{4,5},{5,6},{6,7},{7,4},{8,9},{9,10},{10,1... | collective-permute-start | bytes 221192 | tf_op jit(solution)/shard_map/ppermute | solution.py:566
  37.0 5.3 %collective-permute-start.11 = (bf16[288,128]{1,0:T(8,128)(2,1)S(1)}, bf16[288,128]{1,0:T(8,128)(2,1)S(1)}, u32[]{:S(2)}, u32[]{:S(2)}) collective-permute-start(bf16[288,128]{1,0:T(8,128)(2,1)S(1)} %get-tuple-element.106), channel_id=1, source_target_pairs={{0,2},{1,3},{2,0},{3,1},{4,6},{5,7},{6,4},{7,5},{8,10},{9,11},{10,... | collective-permute-start | bytes 221192 | tf_op jit(solution)/shard_map/ppermute | solution.py:566
  38.4 4.8 %collective-permute-start.12 = (bf16[288,128]{1,0:T(8,128)(2,1)S(1)}, bf16[288,128]{1,0:T(8,128)(2,1)S(1)}, u32[]{:S(2)}, u32[]{:S(2)}) collective-permute-start(bf16[288,128]{1,0:T(8,128)(2,1)S(1)} %get-tuple-element.107), channel_id=1, source_target_pairs={{0,3},{1,0},{2,1},{3,2},{4,7},{5,4},{6,5},{7,6},{8,11},{9,8},{10,9... | collective-permute-start | bytes 221192 | tf_op jit(solution)/shard_map/ppermute | solution.py:566

commit v13 on v12

--- a/solution.py
+++ b/solution.py
@@ -187,7 +187,7 @@
 
 def inner_kernel(
     coarse, skip, cot, left, right, up_w, conv_w, grad_centre,
-    shifted, near, act, slope, partial, last_pre, grad_act, padded, pre,
+    shifted, near, act, slope, partial, send, last_pre, grad_act, padded, pre,
 ):
     n_rows, n_cols, channels = coarse.shape
     rows, cols, _ = skip.shape
@@ -240,17 +240,17 @@
         for l in range(3):
             source = shifted[2 - l, pl.ds(2 - k, rows)].reshape(-1, channels)
             partial[pl.ds((3 * k + l) * channels, channels), :] = dot(act_t, source)
+    other_core(send, partial)
     total = grad_centre[...]
     for k in range(3):
-        for l in (0, 2):
-            source = shifted[2 - l, pl.ds(2 - k, rows)].reshape(-1, channels)
-            total = total + dot_nt(source, conv_w[k, l])
+        source = shifted[0, pl.ds(2 - k, rows)].reshape(-1, channels)
+        total = total + dot_nt(source, conv_w[k, 2])
     grad_act[...] = total
 
 
 def act_kernel(
-    got_first, got_second, right, up_w, last_pre, partial, shifted_in, near_in, act_in, slope_in,
-    shifted, near, act, slope, extra, send, upper, lower, padded, pre,
+    got_first, got_second, right, up_w, last_pre, shifted_in, near_in, act_in, slope_in,
+    shifted, near, act, slope, edge, upper, lower, padded, pre,
 ):
     rows, cols, channels = act.shape
     n_rows, n_cols = rows // 2, cols // 2
@@ -282,34 +282,31 @@
         shifted[0, row] = get(padded, MARGIN - 1, cols).astype(bf16)
         shifted[1, row] = centre.astype(bf16)
         shifted[2, row] = get(padded, MARGIN + 1, cols).astype(bf16)
-    last_t = last.T
-    both_t = jnp.concatenate([last, act_in[0]], axis=0).T
-    for k in range(3):
-        for l in range(3):
-            beside = shifted[2 - l, rows + 1 - k]
-            if k == 2:
-                term = dot(both_t, jnp.concatenate([beside, shifted[2 - l, 0]], axis=0))
-            else:
-                term = dot(last_t, beside)
-            extra[pl.ds((3 * k + l) * channels, channels), :] = term
-    other_core(send, partial, extra)
+    edge[0] = last
+    edge[1] = act_in[0]
+    for shift in range(3):
+        for place, row in enumerate((0, rows - 1, rows, rows + 1)):
+            edge[2 + 4 * shift + place] = shifted[shift, row]
 
 
 def grad_kernel(shifted, slope, grad_act, conv_w, phases, fine):
     rows, cols = shifted.shape[1] - 2, shifted.shape[2]
     channels = shifted.shape[3]
     n_rows, n_cols = rows // 2, cols // 2
+    cells = rows * cols
+    total = grad_act[...]
+    for k in range(3):
+        source = shifted[2, pl.ds(2 - k, rows)].reshape(cells, channels)
+        total = total + dot_nt(source, conv_w[k, 0])
     first = jnp.zeros((cols, channels), f32)
     last = jnp.zeros((cols, channels), f32)
-    for l in range(3):
+    for l in (1, 2):
         first = first + dot_nt(shifted[2 - l, 0], conv_w[2, l])
         last = last + dot_nt(shifted[2 - l, rows + 1], conv_w[0, l])
-    cells = rows * cols
-    put(fine, 0, (grad_act[...] * slope[...]).astype(bf16).astype(f32))
-    total = (grad_act[:cols, :] + first) * slope[:cols, :]
-    put(fine, 0, total.astype(bf16).astype(f32))
-    total = (grad_act[cells - cols :, :] + last) * slope[cells - cols :, :]
-    put(fine, cells - cols, total.astype(bf16).astype(f32))
+    put(fine, 0, (total * slope[...]).astype(bf16).astype(f32))
+    put(fine, 0, ((total[:cols] + first) * slope[:cols, :]).astype(bf16).astype(f32))
+    edge = (total[cells - cols :] + last) * slope[cells - cols :, :]
+    put(fine, cells - cols, edge.astype(bf16).astype(f32))
     whole = phases.shape[2]
     for row_phase in range(2):
         for col_phase in range(2):
@@ -481,6 +478,31 @@
     return sum(1 << bit for step, bit in enumerate(order) if slot >> (last - step) & 1)
 
 
+def edge_kernel(partial, got, edge, got_edge, own, message, extra):
+    channels, block = partial.shape[1], got.shape[1]
+    zero = jnp.zeros(edge.shape[1:], bf16)
+    sides = (edge, got_edge)
+    rows_t = jnp.concatenate([side[row] for side in sides for row in range(2)], axis=0).T
+
+    def add_blocks(core):
+        for tap in range(9):
+            first = 2 + 4 * (2 - tap % 3)
+            beside = []
+            for side in sides:
+                beside += [side[first + 3 - tap // 3], side[first] if tap >= 6 else zero]
+            beside = jnp.concatenate(beside, axis=0)
+            start = tap * channels
+            for mine in range(start // block, -(-(start + channels) // block)):
+                if mine % 2 == core:
+                    low = max(start, mine * block)
+                    high = min(start + channels, (mine + 1) * block)
+                    extra[low:high, :] = dot(rows_t[low - start : high - start], beside)
+
+    for core in range(2):
+        pl.when(place_of()[0] == core)(lambda core=core: add_blocks(core))
+    core_kernel(partial, extra, got, own, message)
+
+
 def core_kernel(*refs):
     *terms, got, own, message = refs
     slots, half, block = got.shape[0], own.shape[0], got.shape[1]
@@ -534,11 +556,15 @@
     return [(i, i ^ bits) for i in range(count)]
 
 
-def core_sum(send, *terms):
-    groups, block, channels = send.shape
-    got = lax.ppermute(send, "face", xor_pairs(lax.axis_size("face"), 1))
+def core_swap(send):
+    return lax.ppermute(send, "face", xor_pairs(lax.axis_size("face"), 1))
+
+
+def core_sum(body, scratch, partial, got, *rest):
+    groups, block, channels = got.shape
     shape = (groups // 2, block, channels)
-    return kernel_call(core_kernel, [sds(shape, f32), sds(shape, bf16)], [], 0, *terms, got)
+    outs = [sds(shape, f32), sds(shape, bf16)]
+    return kernel_call(body, outs, scratch, 0, partial, got, *rest)
 
 
 def plane_swap(message, step):
@@ -616,34 +642,37 @@
     shift_shape = (3, rows + 2, cols, channels)
     whole = -(-cells // 256) * 256 // n_cols
     part = sds((9 * channels, channels), f32)
+    send = sds((groups, block, channels), bf16)
     blocks = [
         sds(shift_shape, bf16), sds((2, whole + 1, n_cols, channels), bf16),
         sds(skip.shape, bf16), sds((rows * cols, channels), f32), part,
     ]
-    *inner, part_conv, last_pre, grad_act = kernel_call(
+    *inner, part_conv, send_conv, last_pre, grad_act = kernel_call(
         inner_kernel,
         [
-            *blocks, sds((cols, channels), f32), sds((rows * cols, channels), f32),
+            *blocks, send, sds((cols, channels), f32), sds((rows * cols, channels), f32),
         ],
         [halves(rows * stride, channels), flat],
         0, coarse, skip, cotangent, left, right, up_weight, conv_weight, grad_centre,
     )
-    send = sds((groups, block, channels), bf16)
     side = sds(message.shape, f32)
-    shifted, near, act, slope, extra_conv, send_conv, upper, lower = kernel_call(
-        act_kernel, [*blocks, send, side, side],
+    got_conv = core_swap(send_conv)
+    edge = sds((14, cols, channels), bf16)
+    shifted, near, act, slope, edge, upper, lower = kernel_call(
+        act_kernel, [*blocks[:-1], edge, side, side],
         [halves(stride, channels), halves(cols, channels)],
-        0, first, second, right, up_weight, last_pre, part_conv, *inner,
-        changed={6 + i: i for i in range(4)},
+        10**11, first, second, right, up_weight, last_pre, *inner, changed={5 + i: i for i in range(4)},
     )
     phases = kernel_call(
         grad_kernel, [sds((2, 2, whole, n_cols, channels), bf16)], [flat],
         0, shifted, slope, grad_act, conv_weight,
     )[0]
     part_up, send_up = kernel_call(up_kernel, [part, send], [], 0, near, phases)
-    own_conv, to_conv = core_sum(send_conv, after(part_conv, send_up), extra_conv)
+    own_conv, to_conv = core_sum(
+        edge_kernel, [pltpu.VMEM(part.shape, f32)], after(part_conv, send_up), got_conv, edge, core_swap(edge)
+    )
     got_conv = plane_swap(to_conv, 0)
-    own_up, to_up = core_sum(send_up, after(part_up, to_conv))
+    own_up, to_up = core_sum(core_kernel, [], part_up, core_swap(after(send_up, to_conv)))
     got_up = plane_swap(to_up, 0)
     ring_act, ring_grad = kernel_call(
         ring_kernel,

time: 44.2 us -> 43.7 us (0.989)
  waiting for transfers between devices: 8.14 us -> 7.69 us
    ppermute x4, waiting for transfers between devices: 5.92 us -> 5.26 us  [plane_swap(): lax.ppermute(message, 'face', [(i, i ^ 2 << orders[i % 2][step]) for i in...]
  transfers between devices with their start and end apart: 13 -> 14, of which waited for: 6 -> 7; matrix products, arithmetic and copies ran while one was open for 0% -> 0% of each run, Pallas kernels for 22% -> 23%
where the time goes in v13:
time: 43.7 us; the launch traced here: 43.5 us
  starting transfers between devices  22.2 us (51%)
  Pallas kernels  12.9 us (30%)
  waiting for transfers between devices  7.69 us (18%)
  between operations  0.77 us (2%)
    pallas_call x16, Pallas kernels, kernel_call(): pl.pallas_call(body, out_shape=tuple(outs), in_specs=[hbm if i in far els...  12.9 us
    ppermute x3, starting transfers between devices, band_sum(): lax.ppermute(messages[k - 1], 'band', [(i, (i + k) % bands) for i in rang...  8.62 us
    ppermute x4, starting transfers between devices, swap(): return (lax.ppermute(first, axis, one), lax.ppermute(second, axis, two))  6.38 us
    ppermute x4, starting transfers between devices, plane_swap(): lax.ppermute(message, 'face', [(i, i ^ 2 << orders[i % 2][step]) for i in...  6.35 us
    ppermute x4, waiting for transfers between devices, plane_swap(): lax.ppermute(message, 'face', [(i, i ^ 2 << orders[i % 2][step]) for i in...  5.26 us
    ppermute x3, waiting for transfers between devices, band_sum(): lax.ppermute(messages[k - 1], 'band', [(i, (i + k) % bands) for i in rang...  1.98 us
  transfers between devices with their start and end apart: 14, of which 7 were waited for; matrix products, arithmetic and copies ran while one was open for 0% of the time, Pallas kernels for 23%

profile of v13, /device:TPU:0, one launch (start us, length us, event | category | flops | bytes accessed | tf_op | source)
XLA Modules:
  0.0 43.5 jit_solution(9827928946791788648)
XLA Ops:
  0.6 1.2 %shard_map.84 = (bf16[96,256]{1,0:T(8,128)(2,1)S(1)}, bf16[96,256]{1,0:T(8,128)(2,1)S(1)}, bf16[24,32,256]{2,1,0:T(8,128)(2,1)S(1)}, bf16[24,32,256]{2,1,0:T(8,128)(2,1)S(1)}, bf16[12,16,256]{2,1,0:T(8,128)(2,1)S(1)}) custom-call(bf16[12,16,256]{2,1,0:T(8,128)(2,1)} %coarse.1, bf16[24,32,256]{2,1,0:T(8,128)(2,1)} %skip.1, bf16[24,32,256]{2,1,0:T(8,128)(2,1)} %cot.1), custom_call_target="tpu_custom_call" | custom-call | bytes 1867776 | tf_op jit(solution)/shard_map/pallas_call | solution.py:28
  2.4 3.6 %collective-permute-start.1 = (bf16[96,256]{1,0:T(8,128)(2,1)S(1)}, bf16[96,256]{1,0:T(8,128)(2,1)S(1)}, u32[]{:S(2)}, u32[]{:S(2)}) collective-permute-start(bf16[96,256]{1,0:T(8,128)(2,1)S(1)} %get-tuple-element.63), channel_id=1, source_target_pairs={{0,28},{4,8},{8,4},{12,16},{16,12},{20,24},{24,20},{28,0},{1,29},{... | collective-permute-start | bytes 147464 | tf_op jit(solution)/shard_map/ppermute | solution.py:604
  5.9 1.9 %shard_map.85 = (bf16[3,3,256,256]{3,2,1,0:T(8,128)(2,1)S(1)}, f32[768,256]{1,0:T(8,128)S(1)}) custom-call(bf16[24,32,256]{2,1,0:T(8,128)(2,1)S(1)} %get-tuple-element.61.cot, bf16[3,3,256,256]{3,2,1,0:T(8,128)(2,1)} %conv_w.1), custom_call_target="tpu_custom_call" | custom-call | bytes 3538944 | tf_op jit(solution)/shard_map/pallas_call | solution.py:28
  7.9 1.7 %collective-permute-start.2 = (bf16[128,256]{1,0:T(8,128)(2,1)S(1)}, bf16[128,256]{1,0:T(8,128)(2,1)S(1)}, u32[]{:S(2)}, u32[]{:S(2)}) collective-permute-start(bf16[128,256]{1,0:T(8,128)(2,1)S(1)} %get-tuple-element.64), channel_id=1, source_target_pairs={{0,1},{1,0},{2,3},{3,2},{4,5},{5,4},{6,7},{7,6},{8,9},{9,8},{10,11... | collective-permute-start | bytes 196616 | tf_op jit(solution)/shard_map/ppermute | solution.py:604
  9.6 0.7 %collective-permute-start.3 = (bf16[128,256]{1,0:T(8,128)(2,1)S(1)}, bf16[128,256]{1,0:T(8,128)(2,1)S(1)}, u32[]{:S(2)}, u32[]{:S(2)}) collective-permute-start(bf16[128,256]{1,0:T(8,128)(2,1)S(1)} %get-tuple-element.65), channel_id=1, source_target_pairs={{1,2},{2,1},{5,6},{6,5},{9,10},{10,9},{13,14},{14,13},{17,18},{18,... | collective-permute-start | bytes 196616 | tf_op jit(solution)/shard_map/ppermute | solution.py:604
  10.2 2.4 %shard_map.87 = (bf16[3,26,32,256]{3,2,1,0:T(8,128)(2,1)S(1)}, bf16[2,17,16,256]{3,2,1,0:T(8,128)(2,1)S(1)}, bf16[24,32,256]{2,1,0:T(8,128)(2,1)S(1)}, f32[768,2...) custom-call(bf16[12,16,256]{2,1,0:T(8,128)(2,1)S(1)} %get-tuple-elem, ...), custom_call_target="tpu_custom_call" | custom-call | bytes 10731520 | tf_op jit(solution)/shard_map/pallas_call | solution.py:28
  13.0 0.5 %collective-permute-start.5 = (bf16[14,32,256]{2,1,0:T(8,128)(2,1)S(1)}, bf16[14,32,256]{2,1,0:T(8,128)(2,1)S(1)}, u32[]{:S(2)}, u32[]{:S(2)}) collective-permute-start(bf16[14,32,256]{2,1,0:T(8,128)(2,1)S(1)} %get-tuple-element.84.edge), channel_id=1, source_target_pairs={{0,4},{4,0},{8,12},{12,8},{16,20},{20,16},{24,28},{28,24},{1,5},{5... | collective-permute-start | bytes 688136 | tf_op jit(solution)/shard_map/ppermute | solution.py:560
  13.6 0.7 %shard_map.89.phases = bf16[2,2,16,16,256]{4,3,2,1,0:T(8,128)(2,1)S(1)} custom-call(bf16[3,26,32,256]{3,2,1,0:T(8,128)(2,1)S(1)} %get-tuple-element.76.shifted, f32[768,256]{1,0:T(8,128)S(1)} %get-tuple-element.77.slope, f32[768,256]{1,0:T(8,128)S(1)} %get-tuple-element.78.grad_act, bf16[3,3,256,256]{3,2,1,0:T(8,128)(2,1)S(1)} %get-tuple-element.68.conv_w), custom_call_target="tpu_custom_call" | custom-call | bytes 4554752 | tf_op jit(solution)/shard_map/pallas_call | solution.py:28
  14.3 0.8 %shard_map.90 = (f32[2304,256]{1,0:T(8,128)S(1)}, bf16[4,288,256]{2,1,0:T(8,128)(2,1)S(1)}) custom-call(bf16[2,17,16,256]{3,2,1,0:T(8,128)(2,1)S(1)} %get-tuple-element.75.near, bf16[2,2,16,16,256]{4,3,2,1,0:T(8,128)(2,1)S(1)} %shard_map.89.phases), custom_call_target="tpu_custom_call" | custom-call | bytes 3751936 | tf_op jit(solution)/shard_map/pallas_call | solution.py:28
  15.8 1.5 %collective-permute-start.7 = (bf16[2,288,256]{2,1,0:T(8,128)(2,1)S(1)}, bf16[2,288,256]{2,1,0:T(8,128)(2,1)S(1)}, u32[]{:S(2)}, u32[]{:S(2)}) collective-permute-start(bf16[2,288,256]{2,1,0:T(8,128)(2,1)S(1)} %get-tuple-element.85), channel_id=1, source_target_pairs={{0,8},{4,20},{8,0},{12,28},{16,24},{20,4},{24,16},{28,12},{1,9},{5... | collective-permute-start | bytes 884744 | tf_op jit(solution)/shard_map/ppermute | solution.py:573
  17.8 1.3 %collective-permute-start.8 = (bf16[2,288,256]{2,1,0:T(8,128)(2,1)S(1)}, bf16[2,288,256]{2,1,0:T(8,128)(2,1)S(1)}, u32[]{:S(2)}, u32[]{:S(2)}) collective-permute-start(bf16[2,288,256]{2,1,0:T(8,128)(2,1)S(1)} %get-tuple-element.87), channel_id=1, source_target_pairs={{0,8},{4,20},{8,0},{12,28},{16,24},{20,4},{24,16},{28,12},{1,9},{5... | collective-permute-start | bytes 884744 | tf_op jit(solution)/shard_map/ppermute | solution.py:573
  19.1 0.8 %shard_map.93 = (f32[128,256]{1,0:T(8,128)S(1)}, f32[2,64,128]{2,1,0:T(8,128)S(1)}) custom-call(bf16[12,16,256]{2,1,0:T(8,128)(2,1)S(1)} %get-tuple-element.57.coarse, bf16[24,32,256]{2,1,0:T(8,128)(2,1)S(1)} %get-tuple-element.61.cot, f32[96,256]{1,0:T(8,128)S(1)} %get-tuple-element.88.left, f32[96,256]{1,0:T(8,128)S(1)} %get-tuple-element.66.right, ...), custom_call_target="tpu_custom_call" | custom-call | bytes 3506176 | tf_op jit(solution)/shard_map/pallas_call | solution.py:28
  19.9 2.7 %collective-permute-done.7.got = bf16[2,288,256]{2,1,0:T(8,128)(2,1)S(1)} collective-permute-done((bf16[2,288,256]{2,1,0:T(8,128)(2,1)S(1)}, bf16[2,288,256]{2,1,0:T(8,128)(2,1)S(1)}, u32[]{:S(2)}, u32[]{:S(2)}) %collective-permute-start.7) | collective-permute-done | bytes 294944 | tf_op jit(solution)/shard_map/ppermute | solution.py:573
  22.6 1.8 %collective-permute-start.9 = (bf16[1,288,256]{2,1,0:T(8,128)(2,1)S(1)}, bf16[1,288,256]{2,1,0:T(8,128)(2,1)S(1)}, u32[]{:S(2)}, u32[]{:S(2)}) collective-permute-start(bf16[1,288,256]{2,1,0:T(8,128)(2,1)S(1)} %get-tuple-element.94), channel_id=1, source_target_pairs={{0,16},{4,12},{8,24},{12,4},{16,0},{20,28},{24,8},{28,20},{1,17},{... | collective-permute-start | bytes 442376 | tf_op jit(solution)/shard_map/ppermute | solution.py:573
  24.4 1.8 %shard_map.95 = bf16[24,32,256]{2,1,0:T(8,128)(2,1)} custom-call(bf16[24,32,256]{2,1,0:T(8,128)(2,1)S(1)} %get-tuple-element.74.act, f32[128,256]{1,0:T(8,128)S(1)} %get-tuple-element.95.ring_act, bf16[3,3,256,256]{3,2,1,0:T(8,128)(2,1)S(1)} %get-tuple-element.68.conv_w), custom_call_target="tpu_custom_call" | custom-call | bytes 2097152 | tf_op jit(solution)/shard_map/pallas_call | solution.py:28
  26.6 1.8 %collective-permute-start.10 = (bf16[1,288,256]{2,1,0:T(8,128)(2,1)S(1)}, bf16[1,288,256]{2,1,0:T(8,128)(2,1)S(1)}, u32[]{:S(2)}, u32[]{:S(2)}) collective-permute-start(bf16[1,288,256]{2,1,0:T(8,128)(2,1)S(1)} %get-tuple-element.99), channel_id=1, source_target_pairs={{0,16},{4,12},{8,24},{12,4},{16,0},{20,28},{24,8},{28,20},{1,17},{... | collective-permute-start | bytes 442376 | tf_op jit(solution)/shard_map/ppermute | solution.py:573
  28.4 1.2 %shard_map.97 = bf16[12,16,256]{2,1,0:T(8,128)(2,1)} custom-call(bf16[2,2,16,16,256]{4,3,2,1,0:T(8,128)(2,1)S(1)} %shard_map.89.phases, f32[2,64,128]{2,1,0:T(8,128)S(1)} %get-tuple-element.100.ring_grad, bf16[3,3,256,256]{3,2,1,0:T(8,128)(2,1)S(1)} %copy-done), custom_call_target="tpu_custom_call" | custom-call | bytes 1867776 | tf_op jit(solution)/shard_map/pallas_call | solution.py:28
  29.6 2.2 %collective-permute-done.10.got_up = bf16[1,288,256]{2,1,0:T(8,128)(2,1)S(1)} collective-permute-done((bf16[1,288,256]{2,1,0:T(8,128)(2,1)S(1)}, bf16[1,288,256]{2,1,0:T(8,128)(2,1)S(1)}, u32[]{:S(2)}, u32[]{:S(2)}) %collective-permute-start.10) | collective-permute-done | bytes 147488 | tf_op jit(solution)/shard_map/ppermute | solution.py:573
  32.1 4.5 %collective-permute-start.11 = (bf16[288,128]{1,0:T(8,128)(2,1)S(1)}, bf16[288,128]{1,0:T(8,128)(2,1)S(1)}, u32[]{:S(2)}, u32[]{:S(2)}) collective-permute-start(bf16[288,128]{1,0:T(8,128)(2,1)S(1)} %get-tuple-element.105), channel_id=1, source_target_pairs={{0,1},{1,2},{2,3},{3,0},{4,5},{5,6},{6,7},{7,4},{8,9},{9,10},{10,1... | collective-permute-start | bytes 221192 | tf_op jit(solution)/shard_map/ppermute | solution.py:592
  36.6 1.3 %collective-permute-start.12 = (bf16[288,128]{1,0:T(8,128)(2,1)S(1)}, bf16[288,128]{1,0:T(8,128)(2,1)S(1)}, u32[]{:S(2)}, u32[]{:S(2)}) collective-permute-start(bf16[288,128]{1,0:T(8,128)(2,1)S(1)} %get-tuple-element.106), channel_id=1, source_target_pairs={{0,2},{1,3},{2,0},{3,1},{4,6},{5,7},{6,4},{7,5},{8,10},{9,11},{10,... | collective-permute-start | bytes 221192 | tf_op jit(solution)/shard_map/ppermute | solution.py:592
  37.9 2.8 %collective-permute-start.13 = (bf16[288,128]{1,0:T(8,128)(2,1)S(1)}, bf16[288,128]{1,0:T(8,128)(2,1)S(1)}, u32[]{:S(2)}, u32[]{:S(2)}) collective-permute-start(bf16[288,128]{1,0:T(8,128)(2,1)S(1)} %get-tuple-element.107), channel_id=1, source_target_pairs={{0,3},{1,0},{2,1},{3,2},{4,7},{5,4},{6,5},{7,6},{8,11},{9,8},{10,9... | collective-permute-start | bytes 221192 | tf_op jit(solution)/shard_map/ppermute | solution.py:592
  40.8 1.1 %collective-permute-done.12.refs_1_ = bf16[288,128]{1,0:T(8,128)(2,1)S(1)} collective-permute-done((bf16[288,128]{1,0:T(8,128)(2,1)S(1)}, bf16[288,128]{1,0:T(8,128)(2,1)S(1)}, u32[]{:S(2)}, u32[]{:S(2)}) %collective-permute-start.12) | collective-permute-done | bytes 73760 | tf_op jit(solution)/shard_map/ppermute | solution.py:592
  41.9 0.9 %collective-permute-done.13.refs_2_ = bf16[288,128]{1,0:T(8,128)(2,1)S(1)} collective-permute-done((bf16[288,128]{1,0:T(8,128)(2,1)S(1)}, bf16[288,128]{1,0:T(8,128)(2,1)S(1)}, u32[]{:S(2)}, u32[]{:S(2)}) %collective-permute-start.13) | collective-permute-done | bytes 73760 | tf_op jit(solution)/shard_map/ppermute | solution.py:592
  42.7 0.8 %shard_map.99 = (f32[64,288]{1,0:T(8,128)}, f32[64,288]{1,0:T(8,128)}) custom-call(f32[288,128]{1,0:T(8,128)S(1)} %get-tuple-element.104.own, bf16[288,128]{1,0:T(8,128)(2,1)S(1)} %collective-permute-done.11.refs_0_, bf16[288,128]{1,0:T(8,128)(2,1)S(1)} %collective-permute-done.12.refs_1_, bf16[288,128]{1,0:T(8,128)(2,1)S(1)} %collective-permute-done.13.refs_2_), custom_call_target="tpu_custom_call" | custom-call | bytes 516096 | tf_op jit(solution)/shard_map/pallas_call | solution.py:28
  (22 shorter events, 2.9 us)
Async XLA Ops:
  1.9 6.0 %collective-permute-start = (bf16[96,256]{1,0:T(8,128)(2,1)S(1)}, bf16[96,256]{1,0:T(8,128)(2,1)S(1)}, u32[]{:S(2)}, u32[]{:S(2)}) collective-permute-start(bf16[96,256]{1,0:T(8,128)(2,1)S(1)} %get-tuple-element.62), channel_id=1, source_target_pairs={{0,4},{4,0},{8,12},{12,8},{16,20},{20,16},{24,28},{28,24},{1,5},{5... | collective-permute-start | bytes 147464 | tf_op jit(solution)/shard_map/ppermute | solution.py:604
  2.4 5.5 %collective-permute-start.1 = (bf16[96,256]{1,0:T(8,128)(2,1)S(1)}, bf16[96,256]{1,0:T(8,128)(2,1)S(1)}, u32[]{:S(2)}, u32[]{:S(2)}) collective-permute-start(bf16[96,256]{1,0:T(8,128)(2,1)S(1)} %get-tuple-element.63), channel_id=1, source_target_pairs={{0,28},{4,8},{8,4},{12,16},{16,12},{20,24},{24,20},{28,0},{1,29},{... | collective-permute-start | bytes 147464 | tf_op jit(solution)/shard_map/ppermute | solution.py:604
  5.9 4.3 %copy-start = (bf16[3,3,256,256]{3,2,1,0:T(8,128)(2,1)S(1)}, bf16[3,3,256,256]{3,2,1,0:T(8,128)(2,1)}, u32[]{:S(2)}) copy-start(bf16[3,3,256,256]{3,2,1,0:T(8,128)(2,1)} %up_w.7) | copy-start | bytes 3538948
  7.9 4.9 %collective-permute-start.2 = (bf16[128,256]{1,0:T(8,128)(2,1)S(1)}, bf16[128,256]{1,0:T(8,128)(2,1)S(1)}, u32[]{:S(2)}, u32[]{:S(2)}) collective-permute-start(bf16[128,256]{1,0:T(8,128)(2,1)S(1)} %get-tuple-element.64), channel_id=1, source_target_pairs={{0,1},{1,0},{2,3},{3,2},{4,5},{5,4},{6,7},{7,6},{8,9},{9,8},{10,11... | collective-permute-start | bytes 196616 | tf_op jit(solution)/shard_map/ppermute | solution.py:604
  9.6 3.2 %collective-permute-start.3 = (bf16[128,256]{1,0:T(8,128)(2,1)S(1)}, bf16[128,256]{1,0:T(8,128)(2,1)S(1)}, u32[]{:S(2)}, u32[]{:S(2)}) collective-permute-start(bf16[128,256]{1,0:T(8,128)(2,1)S(1)} %get-tuple-element.65), channel_id=1, source_target_pairs={{1,2},{2,1},{5,6},{6,5},{9,10},{10,9},{13,14},{14,13},{17,18},{18,... | collective-permute-start | bytes 196616 | tf_op jit(solution)/shard_map/ppermute | solution.py:604
  12.7 2.4 %collective-permute-start.4 = (bf16[4,288,256]{2,1,0:T(8,128)(2,1)S(1)}, bf16[4,288,256]{2,1,0:T(8,128)(2,1)S(1)}, u32[]{:S(2)}, u32[]{:S(2)}) collective-permute-start(bf16[4,288,256]{2,1,0:T(8,128)(2,1)S(1)} %get-tuple-element.83), channel_id=1, source_target_pairs={{0,4},{4,0},{8,12},{12,8},{16,20},{20,16},{24,28},{28,24},{1,5},{5... | collective-permute-start | bytes 1769480 | tf_op jit(solution)/shard_map/ppermute | solution.py:560
  13.0 2.1 %collective-permute-start.5 = (bf16[14,32,256]{2,1,0:T(8,128)(2,1)S(1)}, bf16[14,32,256]{2,1,0:T(8,128)(2,1)S(1)}, u32[]{:S(2)}, u32[]{:S(2)}) collective-permute-start(bf16[14,32,256]{2,1,0:T(8,128)(2,1)S(1)} %get-tuple-element.84.edge), channel_id=1, source_target_pairs={{0,4},{4,0},{8,12},{12,8},{16,20},{20,16},{24,28},{28,24},{1,5},{5... | collective-permute-start | bytes 688136 | tf_op jit(solution)/shard_map/ppermute | solution.py:560
  15.6 2.1 %collective-permute-start.6 = (bf16[4,288,256]{2,1,0:T(8,128)(2,1)S(1)}, bf16[4,288,256]{2,1,0:T(8,128)(2,1)S(1)}, u32[]{:S(2)}, u32[]{:S(2)}) collective-permute-start(bf16[4,288,256]{2,1,0:T(8,128)(2,1)S(1)} %get-tuple-element.86), channel_id=1, source_target_pairs={{0,4},{4,0},{8,12},{12,8},{16,20},{20,16},{24,28},{28,24},{1,5},{5... | collective-permute-start | bytes 1769480 | tf_op jit(solution)/shard_map/ppermute | solution.py:560
  15.8 6.7 %collective-permute-start.7 = (bf16[2,288,256]{2,1,0:T(8,128)(2,1)S(1)}, bf16[2,288,256]{2,1,0:T(8,128)(2,1)S(1)}, u32[]{:S(2)}, u32[]{:S(2)}) collective-permute-start(bf16[2,288,256]{2,1,0:T(8,128)(2,1)S(1)} %get-tuple-element.85), channel_id=1, source_target_pairs={{0,8},{4,20},{8,0},{12,28},{16,24},{20,4},{24,16},{28,12},{1,9},{5... | collective-permute-start | bytes 884744 | tf_op jit(solution)/shard_map/ppermute | solution.py:573
  17.8 8.8 %collective-permute-start.8 = (bf16[2,288,256]{2,1,0:T(8,128)(2,1)S(1)}, bf16[2,288,256]{2,1,0:T(8,128)(2,1)S(1)}, u32[]{:S(2)}, u32[]{:S(2)}) collective-permute-start(bf16[2,288,256]{2,1,0:T(8,128)(2,1)S(1)} %get-tuple-element.87), channel_id=1, source_target_pairs={{0,8},{4,20},{8,0},{12,28},{16,24},{20,4},{24,16},{28,12},{1,9},{5... | collective-permute-start | bytes 884744 | tf_op jit(solution)/shard_map/ppermute | solution.py:573
  22.6 7.0 %collective-permute-start.9 = (bf16[1,288,256]{2,1,0:T(8,128)(2,1)S(1)}, bf16[1,288,256]{2,1,0:T(8,128)(2,1)S(1)}, u32[]{:S(2)}, u32[]{:S(2)}) collective-permute-start(bf16[1,288,256]{2,1,0:T(8,128)(2,1)S(1)} %get-tuple-element.94), channel_id=1, source_target_pairs={{0,16},{4,12},{8,24},{12,4},{16,0},{20,28},{24,8},{28,20},{1,17},{... | collective-permute-start | bytes 442376 | tf_op jit(solution)/shard_map/ppermute | solution.py:573
  26.6 5.2 %collective-permute-start.10 = (bf16[1,288,256]{2,1,0:T(8,128)(2,1)S(1)}, bf16[1,288,256]{2,1,0:T(8,128)(2,1)S(1)}, u32[]{:S(2)}, u32[]{:S(2)}) collective-permute-start(bf16[1,288,256]{2,1,0:T(8,128)(2,1)S(1)} %get-tuple-element.99), channel_id=1, source_target_pairs={{0,16},{4,12},{8,24},{12,4},{16,0},{20,28},{24,8},{28,20},{1,17},{... | collective-permute-start | bytes 442376 | tf_op jit(solution)/shard_map/ppermute | solution.py:573
  32.1 8.6 %collective-permute-start.11 = (bf16[288,128]{1,0:T(8,128)(2,1)S(1)}, bf16[288,128]{1,0:T(8,128)(2,1)S(1)}, u32[]{:S(2)}, u32[]{:S(2)}) collective-permute-start(bf16[288,128]{1,0:T(8,128)(2,1)S(1)} %get-tuple-element.105), channel_id=1, source_target_pairs={{0,1},{1,2},{2,3},{3,0},{4,5},{5,6},{6,7},{7,4},{8,9},{9,10},{10,1... | collective-permute-start | bytes 221192 | tf_op jit(solution)/shard_map/ppermute | solution.py:592
  36.6 5.3 %collective-permute-start.12 = (bf16[288,128]{1,0:T(8,128)(2,1)S(1)}, bf16[288,128]{1,0:T(8,128)(2,1)S(1)}, u32[]{:S(2)}, u32[]{:S(2)}) collective-permute-start(bf16[288,128]{1,0:T(8,128)(2,1)S(1)} %get-tuple-element.106), channel_id=1, source_target_pairs={{0,2},{1,3},{2,0},{3,1},{4,6},{5,7},{6,4},{7,5},{8,10},{9,11},{10,... | collective-permute-start | bytes 221192 | tf_op jit(solution)/shard_map/ppermute | solution.py:592
  37.9 4.8 %collective-permute-start.13 = (bf16[288,128]{1,0:T(8,128)(2,1)S(1)}, bf16[288,128]{1,0:T(8,128)(2,1)S(1)}, u32[]{:S(2)}, u32[]{:S(2)}) collective-permute-start(bf16[288,128]{1,0:T(8,128)(2,1)S(1)} %get-tuple-element.107), channel_id=1, source_target_pairs={{0,3},{1,0},{2,1},{3,2},{4,7},{5,4},{6,5},{7,6},{8,11},{9,8},{10,9... | collective-permute-start | bytes 221192 | tf_op jit(solution)/shard_map/ppermute | solution.py:592

commit v14 on v13

--- a/solution.py
+++ b/solution.py
@@ -539,7 +539,7 @@
     band = place_of()[2]
     own[...] = cut[band]
     for k, message in enumerate(messages):
-        message[...] = cut[lax.rem(band + k + 1, n_bands)].astype(bf16)
+        message[...] = cut[band ^ (k + 1)].astype(bf16)
 
 
 def last_kernel(own, *refs):
@@ -589,8 +589,8 @@
         [pltpu.VMEM((bands,) + shape, f32)], 0, conv, got_conv, up, got_up,
     )
     got = [
-        lax.ppermute(messages[k - 1], "band", [(i, (i + k) % bands) for i in range(bands)])
-        for k in range(1, bands)
+        lax.ppermute(messages[k - 1], "band", xor_pairs(bands, k))
+        for k in (3, 2, 1)
     ]
     return [a.T for a in kernel_call(last_kernel, [sds((cols, block), f32)] * 2, [], 0, own, *got)]
 

time: 43.7 us -> 43.4 us (level)
  starting transfers between devices: 22.2 us -> 19.8 us
  waiting for transfers between devices: 7.69 us -> 9.71 us
    ppermute x3, starting transfers between devices: 8.62 us -> 6.28 us  [band_sum(): lax.ppermute(messages[k - 1], 'band', xor_pairs(bands, k))]
    ppermute x3, waiting for transfers between devices: 1.98 us -> 4 us  [band_sum(): lax.ppermute(messages[k - 1], 'band', xor_pairs(bands, k))]
  transfers between devices with their start and end apart: 14 -> 14, of which waited for: 7 -> 8; matrix products, arithmetic and copies ran while one was open for 0% -> 0% of each run, Pallas kernels for 23% -> 23%
where the time goes in v14:
time: 43.4 us; the launch traced here: 43.2 us
  starting transfers between devices  19.8 us (46%)
  Pallas kernels  12.9 us (30%)
  waiting for transfers between devices  9.71 us (22%)
  between operations  0.78 us (2%)
    pallas_call x16, Pallas kernels, kernel_call(): pl.pallas_call(body, out_shape=tuple(outs), in_specs=[hbm if i in far els...  12.9 us
    ppermute x4, starting transfers between devices, swap(): return (lax.ppermute(first, axis, one), lax.ppermute(second, axis, two))  6.38 us
    ppermute x4, starting transfers between devices, plane_swap(): lax.ppermute(message, 'face', [(i, i ^ 2 << orders[i % 2][step]) for i in...  6.35 us
    ppermute x3, starting transfers between devices, band_sum(): lax.ppermute(messages[k - 1], 'band', xor_pairs(bands, k))  6.28 us
    ppermute x4, waiting for transfers between devices, plane_swap(): lax.ppermute(message, 'face', [(i, i ^ 2 << orders[i % 2][step]) for i in...  5.26 us
    ppermute x3, waiting for transfers between devices, band_sum(): lax.ppermute(messages[k - 1], 'band', xor_pairs(bands, k))  4 us
  transfers between devices with their start and end apart: 14, of which 8 were waited for; matrix products, arithmetic and copies ran while one was open for 0% of the time, Pallas kernels for 23%

profile of v14, /device:TPU:0, one launch (start us, length us, event | category | flops | bytes accessed | tf_op | source)
XLA Modules:
  0.0 43.2 jit_solution(2301086234238373489)
XLA Ops:
  0.6 1.2 %shard_map.84 = (bf16[96,256]{1,0:T(8,128)(2,1)S(1)}, bf16[96,256]{1,0:T(8,128)(2,1)S(1)}, bf16[24,32,256]{2,1,0:T(8,128)(2,1)S(1)}, bf16[24,32,256]{2,1,0:T(8,128)(2,1)S(1)}, bf16[12,16,256]{2,1,0:T(8,128)(2,1)S(1)}) custom-call(bf16[12,16,256]{2,1,0:T(8,128)(2,1)} %coarse.1, bf16[24,32,256]{2,1,0:T(8,128)(2,1)} %skip.1, bf16[24,32,256]{2,1,0:T(8,128)(2,1)} %cot.1), custom_call_target="tpu_custom_call" | custom-call | bytes 1867776 | tf_op jit(solution)/shard_map/pallas_call | solution.py:28
  1.9 0.5 %collective-permute-start = (bf16[96,256]{1,0:T(8,128)(2,1)S(1)}, bf16[96,256]{1,0:T(8,128)(2,1)S(1)}, u32[]{:S(2)}, u32[]{:S(2)}) collective-permute-start(bf16[96,256]{1,0:T(8,128)(2,1)S(1)} %get-tuple-element.62), channel_id=1, source_target_pairs={{0,4},{4,0},{8,12},{12,8},{16,20},{20,16},{24,28},{28,24},{1,5},{5... | collective-permute-start | bytes 147464 | tf_op jit(solution)/shard_map/ppermute | solution.py:604
  2.4 3.6 %collective-permute-start.1 = (bf16[96,256]{1,0:T(8,128)(2,1)S(1)}, bf16[96,256]{1,0:T(8,128)(2,1)S(1)}, u32[]{:S(2)}, u32[]{:S(2)}) collective-permute-start(bf16[96,256]{1,0:T(8,128)(2,1)S(1)} %get-tuple-element.63), channel_id=1, source_target_pairs={{0,28},{4,8},{8,4},{12,16},{16,12},{20,24},{24,20},{28,0},{1,29},{... | collective-permute-start | bytes 147464 | tf_op jit(solution)/shard_map/ppermute | solution.py:604
  5.9 1.9 %shard_map.85 = (bf16[3,3,256,256]{3,2,1,0:T(8,128)(2,1)S(1)}, f32[768,256]{1,0:T(8,128)S(1)}) custom-call(bf16[24,32,256]{2,1,0:T(8,128)(2,1)S(1)} %get-tuple-element.61.cot, bf16[3,3,256,256]{3,2,1,0:T(8,128)(2,1)} %conv_w.1), custom_call_target="tpu_custom_call" | custom-call | bytes 3538944 | tf_op jit(solution)/shard_map/pallas_call | solution.py:28
  7.9 1.7 %collective-permute-start.2 = (bf16[128,256]{1,0:T(8,128)(2,1)S(1)}, bf16[128,256]{1,0:T(8,128)(2,1)S(1)}, u32[]{:S(2)}, u32[]{:S(2)}) collective-permute-start(bf16[128,256]{1,0:T(8,128)(2,1)S(1)} %get-tuple-element.64), channel_id=1, source_target_pairs={{0,1},{1,0},{2,3},{3,2},{4,5},{5,4},{6,7},{7,6},{8,9},{9,8},{10,11... | collective-permute-start | bytes 196616 | tf_op jit(solution)/shard_map/ppermute | solution.py:604
  9.6 0.7 %collective-permute-start.3 = (bf16[128,256]{1,0:T(8,128)(2,1)S(1)}, bf16[128,256]{1,0:T(8,128)(2,1)S(1)}, u32[]{:S(2)}, u32[]{:S(2)}) collective-permute-start(bf16[128,256]{1,0:T(8,128)(2,1)S(1)} %get-tuple-element.65), channel_id=1, source_target_pairs={{1,2},{2,1},{5,6},{6,5},{9,10},{10,9},{13,14},{14,13},{17,18},{18,... | collective-permute-start | bytes 196616 | tf_op jit(solution)/shard_map/ppermute | solution.py:604
  10.2 2.4 %shard_map.87 = (bf16[3,26,32,256]{3,2,1,0:T(8,128)(2,1)S(1)}, bf16[2,17,16,256]{3,2,1,0:T(8,128)(2,1)S(1)}, bf16[24,32,256]{2,1,0:T(8,128)(2,1)S(1)}, f32[768,2...) custom-call(bf16[12,16,256]{2,1,0:T(8,128)(2,1)S(1)} %get-tuple-elem, ...), custom_call_target="tpu_custom_call" | custom-call | bytes 10731520 | tf_op jit(solution)/shard_map/pallas_call | solution.py:28
  13.0 0.5 %collective-permute-start.5 = (bf16[14,32,256]{2,1,0:T(8,128)(2,1)S(1)}, bf16[14,32,256]{2,1,0:T(8,128)(2,1)S(1)}, u32[]{:S(2)}, u32[]{:S(2)}) collective-permute-start(bf16[14,32,256]{2,1,0:T(8,128)(2,1)S(1)} %get-tuple-element.84.edge), channel_id=1, source_target_pairs={{0,4},{4,0},{8,12},{12,8},{16,20},{20,16},{24,28},{28,24},{1,5},{5... | collective-permute-start | bytes 688136 | tf_op jit(solution)/shard_map/ppermute | solution.py:560
  13.6 0.7 %shard_map.89.phases = bf16[2,2,16,16,256]{4,3,2,1,0:T(8,128)(2,1)S(1)} custom-call(bf16[3,26,32,256]{3,2,1,0:T(8,128)(2,1)S(1)} %get-tuple-element.76.shifted, f32[768,256]{1,0:T(8,128)S(1)} %get-tuple-element.77.slope, f32[768,256]{1,0:T(8,128)S(1)} %get-tuple-element.78.grad_act, bf16[3,3,256,256]{3,2,1,0:T(8,128)(2,1)S(1)} %get-tuple-element.68.conv_w), custom_call_target="tpu_custom_call" | custom-call | bytes 4554752 | tf_op jit(solution)/shard_map/pallas_call | solution.py:28
  14.3 0.8 %shard_map.90 = (f32[2304,256]{1,0:T(8,128)S(1)}, bf16[4,288,256]{2,1,0:T(8,128)(2,1)S(1)}) custom-call(bf16[2,17,16,256]{3,2,1,0:T(8,128)(2,1)S(1)} %get-tuple-element.75.near, bf16[2,2,16,16,256]{4,3,2,1,0:T(8,128)(2,1)S(1)} %shard_map.89.phases), custom_call_target="tpu_custom_call" | custom-call | bytes 3751936 | tf_op jit(solution)/shard_map/pallas_call | solution.py:28
  15.8 1.5 %collective-permute-start.7 = (bf16[2,288,256]{2,1,0:T(8,128)(2,1)S(1)}, bf16[2,288,256]{2,1,0:T(8,128)(2,1)S(1)}, u32[]{:S(2)}, u32[]{:S(2)}) collective-permute-start(bf16[2,288,256]{2,1,0:T(8,128)(2,1)S(1)} %get-tuple-element.85), channel_id=1, source_target_pairs={{0,8},{4,20},{8,0},{12,28},{16,24},{20,4},{24,16},{28,12},{1,9},{5... | collective-permute-start | bytes 884744 | tf_op jit(solution)/shard_map/ppermute | solution.py:573
  17.8 1.3 %collective-permute-start.8 = (bf16[2,288,256]{2,1,0:T(8,128)(2,1)S(1)}, bf16[2,288,256]{2,1,0:T(8,128)(2,1)S(1)}, u32[]{:S(2)}, u32[]{:S(2)}) collective-permute-start(bf16[2,288,256]{2,1,0:T(8,128)(2,1)S(1)} %get-tuple-element.87), channel_id=1, source_target_pairs={{0,8},{4,20},{8,0},{12,28},{16,24},{20,4},{24,16},{28,12},{1,9},{5... | collective-permute-start | bytes 884744 | tf_op jit(solution)/shard_map/ppermute | solution.py:573
  19.1 0.8 %shard_map.93 = (f32[128,256]{1,0:T(8,128)S(1)}, f32[2,64,128]{2,1,0:T(8,128)S(1)}) custom-call(bf16[12,16,256]{2,1,0:T(8,128)(2,1)S(1)} %get-tuple-element.57.coarse, bf16[24,32,256]{2,1,0:T(8,128)(2,1)S(1)} %get-tuple-element.61.cot, f32[96,256]{1,0:T(8,128)S(1)} %get-tuple-element.88.left, f32[96,256]{1,0:T(8,128)S(1)} %get-tuple-element.66.right, ...), custom_call_target="tpu_custom_call" | custom-call | bytes 3506176 | tf_op jit(solution)/shard_map/pallas_call | solution.py:28
  19.9 2.7 %collective-permute-done.7.got = bf16[2,288,256]{2,1,0:T(8,128)(2,1)S(1)} collective-permute-done((bf16[2,288,256]{2,1,0:T(8,128)(2,1)S(1)}, bf16[2,288,256]{2,1,0:T(8,128)(2,1)S(1)}, u32[]{:S(2)}, u32[]{:S(2)}) %collective-permute-start.7) | collective-permute-done | bytes 294944 | tf_op jit(solution)/shard_map/ppermute | solution.py:573
  22.6 1.8 %collective-permute-start.9 = (bf16[1,288,256]{2,1,0:T(8,128)(2,1)S(1)}, bf16[1,288,256]{2,1,0:T(8,128)(2,1)S(1)}, u32[]{:S(2)}, u32[]{:S(2)}) collective-permute-start(bf16[1,288,256]{2,1,0:T(8,128)(2,1)S(1)} %get-tuple-element.94), channel_id=1, source_target_pairs={{0,16},{4,12},{8,24},{12,4},{16,0},{20,28},{24,8},{28,20},{1,17},{... | collective-permute-start | bytes 442376 | tf_op jit(solution)/shard_map/ppermute | solution.py:573
  24.4 1.8 %shard_map.95 = bf16[24,32,256]{2,1,0:T(8,128)(2,1)} custom-call(bf16[24,32,256]{2,1,0:T(8,128)(2,1)S(1)} %get-tuple-element.74.act, f32[128,256]{1,0:T(8,128)S(1)} %get-tuple-element.95.ring_act, bf16[3,3,256,256]{3,2,1,0:T(8,128)(2,1)S(1)} %get-tuple-element.68.conv_w), custom_call_target="tpu_custom_call" | custom-call | bytes 2097152 | tf_op jit(solution)/shard_map/pallas_call | solution.py:28
  26.6 1.8 %collective-permute-start.10 = (bf16[1,288,256]{2,1,0:T(8,128)(2,1)S(1)}, bf16[1,288,256]{2,1,0:T(8,128)(2,1)S(1)}, u32[]{:S(2)}, u32[]{:S(2)}) collective-permute-start(bf16[1,288,256]{2,1,0:T(8,128)(2,1)S(1)} %get-tuple-element.99), channel_id=1, source_target_pairs={{0,16},{4,12},{8,24},{12,4},{16,0},{20,28},{24,8},{28,20},{1,17},{... | collective-permute-start | bytes 442376 | tf_op jit(solution)/shard_map/ppermute | solution.py:573
  28.4 1.2 %shard_map.97 = bf16[12,16,256]{2,1,0:T(8,128)(2,1)} custom-call(bf16[2,2,16,16,256]{4,3,2,1,0:T(8,128)(2,1)S(1)} %shard_map.89.phases, f32[2,64,128]{2,1,0:T(8,128)S(1)} %get-tuple-element.100.ring_grad, bf16[3,3,256,256]{3,2,1,0:T(8,128)(2,1)S(1)} %copy-done), custom_call_target="tpu_custom_call" | custom-call | bytes 1867776 | tf_op jit(solution)/shard_map/pallas_call | solution.py:28
  29.6 2.2 %collective-permute-done.10.got_up = bf16[1,288,256]{2,1,0:T(8,128)(2,1)S(1)} collective-permute-done((bf16[1,288,256]{2,1,0:T(8,128)(2,1)S(1)}, bf16[1,288,256]{2,1,0:T(8,128)(2,1)S(1)}, u32[]{:S(2)}, u32[]{:S(2)}) %collective-permute-start.10) | collective-permute-done | bytes 147488 | tf_op jit(solution)/shard_map/ppermute | solution.py:573
  32.1 3.3 %collective-permute-start.11 = (bf16[288,128]{1,0:T(8,128)(2,1)S(1)}, bf16[288,128]{1,0:T(8,128)(2,1)S(1)}, u32[]{:S(2)}, u32[]{:S(2)}) collective-permute-start(bf16[288,128]{1,0:T(8,128)(2,1)S(1)} %get-tuple-element.105), channel_id=1, source_target_pairs={{0,3},{1,2},{2,1},{3,0},{4,7},{5,6},{6,5},{7,4},{8,11},{9,10},{10,... | collective-permute-start | bytes 221192 | tf_op jit(solution)/shard_map/ppermute | solution.py:592
  35.4 2.6 %collective-permute-start.12 = (bf16[288,128]{1,0:T(8,128)(2,1)S(1)}, bf16[288,128]{1,0:T(8,128)(2,1)S(1)}, u32[]{:S(2)}, u32[]{:S(2)}) collective-permute-start(bf16[288,128]{1,0:T(8,128)(2,1)S(1)} %get-tuple-element.106), channel_id=1, source_target_pairs={{0,2},{1,3},{2,0},{3,1},{4,6},{5,7},{6,4},{7,5},{8,10},{9,11},{10,... | collective-permute-start | bytes 221192 | tf_op jit(solution)/shard_map/ppermute | solution.py:592
  38.9 2.3 %collective-permute-done.12.refs_1_ = bf16[288,128]{1,0:T(8,128)(2,1)S(1)} collective-permute-done((bf16[288,128]{1,0:T(8,128)(2,1)S(1)}, bf16[288,128]{1,0:T(8,128)(2,1)S(1)}, u32[]{:S(2)}, u32[]{:S(2)}) %collective-permute-start.12) | collective-permute-done | bytes 73760 | tf_op jit(solution)/shard_map/ppermute | solution.py:592
  41.2 1.2 %collective-permute-done.13.refs_2_ = bf16[288,128]{1,0:T(8,128)(2,1)S(1)} collective-permute-done((bf16[288,128]{1,0:T(8,128)(2,1)S(1)}, bf16[288,128]{1,0:T(8,128)(2,1)S(1)}, u32[]{:S(2)}, u32[]{:S(2)}) %collective-permute-start.13) | collective-permute-done | bytes 73760 | tf_op jit(solution)/shard_map/ppermute | solution.py:592
  42.4 0.8 %shard_map.99 = (f32[64,288]{1,0:T(8,128)}, f32[64,288]{1,0:T(8,128)}) custom-call(f32[288,128]{1,0:T(8,128)S(1)} %get-tuple-element.104.own, bf16[288,128]{1,0:T(8,128)(2,1)S(1)} %collective-permute-done.11.refs_0_, bf16[288,128]{1,0:T(8,128)(2,1)S(1)} %collective-permute-done.12.refs_1_, bf16[288,128]{1,0:T(8,128)(2,1)S(1)} %collective-permute-done.13.refs_2_), custom_call_target="tpu_custom_call" | custom-call | bytes 516096 | tf_op jit(solution)/shard_map/pallas_call | solution.py:28
  (22 shorter events, 3.2 us)
Async XLA Ops:
  1.9 6.0 %collective-permute-start = (bf16[96,256]{1,0:T(8,128)(2,1)S(1)}, bf16[96,256]{1,0:T(8,128)(2,1)S(1)}, u32[]{:S(2)}, u32[]{:S(2)}) collective-permute-start(bf16[96,256]{1,0:T(8,128)(2,1)S(1)} %get-tuple-element.62), channel_id=1, source_target_pairs={{0,4},{4,0},{8,12},{12,8},{16,20},{20,16},{24,28},{28,24},{1,5},{5... | collective-permute-start | bytes 147464 | tf_op jit(solution)/shard_map/ppermute | solution.py:604
  2.4 5.5 %collective-permute-start.1 = (bf16[96,256]{1,0:T(8,128)(2,1)S(1)}, bf16[96,256]{1,0:T(8,128)(2,1)S(1)}, u32[]{:S(2)}, u32[]{:S(2)}) collective-permute-start(bf16[96,256]{1,0:T(8,128)(2,1)S(1)} %get-tuple-element.63), channel_id=1, source_target_pairs={{0,28},{4,8},{8,4},{12,16},{16,12},{20,24},{24,20},{28,0},{1,29},{... | collective-permute-start | bytes 147464 | tf_op jit(solution)/shard_map/ppermute | solution.py:604
  5.9 4.3 %copy-start = (bf16[3,3,256,256]{3,2,1,0:T(8,128)(2,1)S(1)}, bf16[3,3,256,256]{3,2,1,0:T(8,128)(2,1)}, u32[]{:S(2)}) copy-start(bf16[3,3,256,256]{3,2,1,0:T(8,128)(2,1)} %up_w.7) | copy-start | bytes 3538948
  7.9 4.9 %collective-permute-start.2 = (bf16[128,256]{1,0:T(8,128)(2,1)S(1)}, bf16[128,256]{1,0:T(8,128)(2,1)S(1)}, u32[]{:S(2)}, u32[]{:S(2)}) collective-permute-start(bf16[128,256]{1,0:T(8,128)(2,1)S(1)} %get-tuple-element.64), channel_id=1, source_target_pairs={{0,1},{1,0},{2,3},{3,2},{4,5},{5,4},{6,7},{7,6},{8,9},{9,8},{10,11... | collective-permute-start | bytes 196616 | tf_op jit(solution)/shard_map/ppermute | solution.py:604
  9.6 3.2 %collective-permute-start.3 = (bf16[128,256]{1,0:T(8,128)(2,1)S(1)}, bf16[128,256]{1,0:T(8,128)(2,1)S(1)}, u32[]{:S(2)}, u32[]{:S(2)}) collective-permute-start(bf16[128,256]{1,0:T(8,128)(2,1)S(1)} %get-tuple-element.65), channel_id=1, source_target_pairs={{1,2},{2,1},{5,6},{6,5},{9,10},{10,9},{13,14},{14,13},{17,18},{18,... | collective-permute-start | bytes 196616 | tf_op jit(solution)/shard_map/ppermute | solution.py:604
  12.7 2.4 %collective-permute-start.4 = (bf16[4,288,256]{2,1,0:T(8,128)(2,1)S(1)}, bf16[4,288,256]{2,1,0:T(8,128)(2,1)S(1)}, u32[]{:S(2)}, u32[]{:S(2)}) collective-permute-start(bf16[4,288,256]{2,1,0:T(8,128)(2,1)S(1)} %get-tuple-element.83), channel_id=1, source_target_pairs={{0,4},{4,0},{8,12},{12,8},{16,20},{20,16},{24,28},{28,24},{1,5},{5... | collective-permute-start | bytes 1769480 | tf_op jit(solution)/shard_map/ppermute | solution.py:560
  13.0 2.1 %collective-permute-start.5 = (bf16[14,32,256]{2,1,0:T(8,128)(2,1)S(1)}, bf16[14,32,256]{2,1,0:T(8,128)(2,1)S(1)}, u32[]{:S(2)}, u32[]{:S(2)}) collective-permute-start(bf16[14,32,256]{2,1,0:T(8,128)(2,1)S(1)} %get-tuple-element.84.edge), channel_id=1, source_target_pairs={{0,4},{4,0},{8,12},{12,8},{16,20},{20,16},{24,28},{28,24},{1,5},{5... | collective-permute-start | bytes 688136 | tf_op jit(solution)/shard_map/ppermute | solution.py:560
  15.6 2.1 %collective-permute-start.6 = (bf16[4,288,256]{2,1,0:T(8,128)(2,1)S(1)}, bf16[4,288,256]{2,1,0:T(8,128)(2,1)S(1)}, u32[]{:S(2)}, u32[]{:S(2)}) collective-permute-start(bf16[4,288,256]{2,1,0:T(8,128)(2,1)S(1)} %get-tuple-element.86), channel_id=1, source_target_pairs={{0,4},{4,0},{8,12},{12,8},{16,20},{20,16},{24,28},{28,24},{1,5},{5... | collective-permute-start | bytes 1769480 | tf_op jit(solution)/shard_map/ppermute | solution.py:560
  15.8 6.7 %collective-permute-start.7 = (bf16[2,288,256]{2,1,0:T(8,128)(2,1)S(1)}, bf16[2,288,256]{2,1,0:T(8,128)(2,1)S(1)}, u32[]{:S(2)}, u32[]{:S(2)}) collective-permute-start(bf16[2,288,256]{2,1,0:T(8,128)(2,1)S(1)} %get-tuple-element.85), channel_id=1, source_target_pairs={{0,8},{4,20},{8,0},{12,28},{16,24},{20,4},{24,16},{28,12},{1,9},{5... | collective-permute-start | bytes 884744 | tf_op jit(solution)/shard_map/ppermute | solution.py:573
  17.8 8.8 %collective-permute-start.8 = (bf16[2,288,256]{2,1,0:T(8,128)(2,1)S(1)}, bf16[2,288,256]{2,1,0:T(8,128)(2,1)S(1)}, u32[]{:S(2)}, u32[]{:S(2)}) collective-permute-start(bf16[2,288,256]{2,1,0:T(8,128)(2,1)S(1)} %get-tuple-element.87), channel_id=1, source_target_pairs={{0,8},{4,20},{8,0},{12,28},{16,24},{20,4},{24,16},{28,12},{1,9},{5... | collective-permute-start | bytes 884744 | tf_op jit(solution)/shard_map/ppermute | solution.py:573
  22.6 7.0 %collective-permute-start.9 = (bf16[1,288,256]{2,1,0:T(8,128)(2,1)S(1)}, bf16[1,288,256]{2,1,0:T(8,128)(2,1)S(1)}, u32[]{:S(2)}, u32[]{:S(2)}) collective-permute-start(bf16[1,288,256]{2,1,0:T(8,128)(2,1)S(1)} %get-tuple-element.94), channel_id=1, source_target_pairs={{0,16},{4,12},{8,24},{12,4},{16,0},{20,28},{24,8},{28,20},{1,17},{... | collective-permute-start | bytes 442376 | tf_op jit(solution)/shard_map/ppermute | solution.py:573
  26.6 5.2 %collective-permute-start.10 = (bf16[1,288,256]{2,1,0:T(8,128)(2,1)S(1)}, bf16[1,288,256]{2,1,0:T(8,128)(2,1)S(1)}, u32[]{:S(2)}, u32[]{:S(2)}) collective-permute-start(bf16[1,288,256]{2,1,0:T(8,128)(2,1)S(1)} %get-tuple-element.99), channel_id=1, source_target_pairs={{0,16},{4,12},{8,24},{12,4},{16,0},{20,28},{24,8},{28,20},{1,17},{... | collective-permute-start | bytes 442376 | tf_op jit(solution)/shard_map/ppermute | solution.py:573
  32.1 6.8 %collective-permute-start.11 = (bf16[288,128]{1,0:T(8,128)(2,1)S(1)}, bf16[288,128]{1,0:T(8,128)(2,1)S(1)}, u32[]{:S(2)}, u32[]{:S(2)}) collective-permute-start(bf16[288,128]{1,0:T(8,128)(2,1)S(1)} %get-tuple-element.105), channel_id=1, source_target_pairs={{0,3},{1,2},{2,1},{3,0},{4,7},{5,6},{6,5},{7,4},{8,11},{9,10},{10,... | collective-permute-start | bytes 221192 | tf_op jit(solution)/shard_map/ppermute | solution.py:592
  35.4 5.8 %collective-permute-start.12 = (bf16[288,128]{1,0:T(8,128)(2,1)S(1)}, bf16[288,128]{1,0:T(8,128)(2,1)S(1)}, u32[]{:S(2)}, u32[]{:S(2)}) collective-permute-start(bf16[288,128]{1,0:T(8,128)(2,1)S(1)} %get-tuple-element.106), channel_id=1, source_target_pairs={{0,2},{1,3},{2,0},{3,1},{4,6},{5,7},{6,4},{7,5},{8,10},{9,11},{10,... | collective-permute-start | bytes 221192 | tf_op jit(solution)/shard_map/ppermute | solution.py:592
  38.0 4.4 %collective-permute-start.13 = (bf16[288,128]{1,0:T(8,128)(2,1)S(1)}, bf16[288,128]{1,0:T(8,128)(2,1)S(1)}, u32[]{:S(2)}, u32[]{:S(2)}) collective-permute-start(bf16[288,128]{1,0:T(8,128)(2,1)S(1)} %get-tuple-element.107), channel_id=1, source_target_pairs={{0,1},{1,0},{2,3},{3,2},{4,5},{5,4},{6,7},{7,6},{8,9},{9,8},{10,11... | collective-permute-start | bytes 221192 | tf_op jit(solution)/shard_map/ppermute | solution.py:592

commit v15 on v14

--- a/solution.py
+++ b/solution.py
@@ -564,7 +564,8 @@
     groups, block, channels = got.shape
     shape = (groups // 2, block, channels)
     outs = [sds(shape, f32), sds(shape, bf16)]
-    return kernel_call(body, outs, scratch, 0, partial, got, *rest)
+    cost = 10**11 if rest else 0
+    return kernel_call(body, outs, scratch, cost, partial, got, *rest)
 
 
 def plane_swap(message, step):
@@ -672,7 +673,7 @@
         edge_kernel, [pltpu.VMEM(part.shape, f32)], after(part_conv, send_up), got_conv, edge, core_swap(edge)
     )
     got_conv = plane_swap(to_conv, 0)
-    own_up, to_up = core_sum(core_kernel, [], part_up, core_swap(after(send_up, to_conv)))
+    own_up, to_up = core_sum(core_kernel, [], after(part_up, to_conv), core_swap(send_up))
     got_up = plane_swap(to_up, 0)
     ring_act, ring_grad = kernel_call(
         ring_kernel,
@@ -683,17 +684,15 @@
         [halves(at.ring_size, channels), halves((rows + 3) * stride, channels)],
         0, coarse, cotangent, after(left, to_up), right, upper, lower, conv_weight, up_weight,
     )
-    own_conv = after(own_conv, ring_act)
+    decoded = kernel_call(
+        decoded_kernel, [sds(skip.shape, bf16)], [padded, pltpu.VMEM(shift_shape, bf16)],
+        0, act, ring_act, conv_weight,
+    )[0]
+    own_conv = after(own_conv, decoded)
     steps = (faces // 2).bit_length() - 1
     for step in range(1, steps):
         own_conv, to_conv = plane_sum(own_conv, got_conv)
         got_conv = plane_swap(to_conv, step)
-        if step == 1:
-            decoded = kernel_call(
-                decoded_kernel, [sds(skip.shape, bf16)], [padded, pltpu.VMEM(shift_shape, bf16)],
-                0, act, after(ring_act, to_conv), conv_weight,
-            )[0]
-            own_up = after(own_up, decoded)
         own_up, to_up = plane_sum(own_up, got_up)
         got_up = plane_swap(to_up, step)
         if step == 1:

time: 43.4 us -> 43.3 us (level)
  transfers between devices with their start and end apart: 14 -> 14, of which waited for: 8 -> 5; matrix products, arithmetic and copies ran while one was open for 0% -> 0% of each run, Pallas kernels for 23% -> 24%
where the time goes in v15:
time: 43.3 us; the launch traced here: 43.2 us
  starting transfers between devices  19.9 us (46%)
  Pallas kernels  12.9 us (30%)
  waiting for transfers between devices  9.48 us (22%)
  between operations  0.83 us (2%)
    pallas_call x16, Pallas kernels, kernel_call(): pl.pallas_call(body, out_shape=tuple(outs), in_specs=[hbm if i in far els...  12.9 us
    ppermute x3, starting transfers between devices, band_sum(): lax.ppermute(messages[k - 1], 'band', xor_pairs(bands, k))  6.56 us
    ppermute x4, starting transfers between devices, swap(): return (lax.ppermute(first, axis, one), lax.ppermute(second, axis, two))  6.38 us
    ppermute x4, starting transfers between devices, plane_swap(): lax.ppermute(message, 'face', [(i, i ^ 2 << orders[i % 2][step]) for i in...  6.27 us
    ppermute x4, waiting for transfers between devices, plane_swap(): lax.ppermute(message, 'face', [(i, i ^ 2 << orders[i % 2][step]) for i in...  5.6 us
    ppermute x3, waiting for transfers between devices, band_sum(): lax.ppermute(messages[k - 1], 'band', xor_pairs(bands, k))  3.86 us
  transfers between devices with their start and end apart: 14, of which 5 were waited for; matrix products, arithmetic and copies ran while one was open for 0% of the time, Pallas kernels for 24%

profile of v15, /device:TPU:0, one launch (start us, length us, event | category | flops | bytes accessed | tf_op | source)
XLA Modules:
  0.0 43.2 jit_solution(8786886987122037383)
XLA Ops:
  0.6 1.2 %shard_map.84 = (bf16[96,256]{1,0:T(8,128)(2,1)S(1)}, bf16[96,256]{1,0:T(8,128)(2,1)S(1)}, bf16[24,32,256]{2,1,0:T(8,128)(2,1)S(1)}, bf16[24,32,256]{2,1,0:T(8,128)(2,1)S(1)}, bf16[12,16,256]{2,1,0:T(8,128)(2,1)S(1)}) custom-call(bf16[12,16,256]{2,1,0:T(8,128)(2,1)} %coarse.1, bf16[24,32,256]{2,1,0:T(8,128)(2,1)} %skip.1, bf16[24,32,256]{2,1,0:T(8,128)(2,1)} %cot.1), custom_call_target="tpu_custom_call" | custom-call | bytes 1867776 | tf_op jit(solution)/shard_map/pallas_call | solution.py:28
  2.4 3.6 %collective-permute-start.1 = (bf16[96,256]{1,0:T(8,128)(2,1)S(1)}, bf16[96,256]{1,0:T(8,128)(2,1)S(1)}, u32[]{:S(2)}, u32[]{:S(2)}) collective-permute-start(bf16[96,256]{1,0:T(8,128)(2,1)S(1)} %get-tuple-element.61), channel_id=1, source_target_pairs={{0,28},{4,8},{8,4},{12,16},{16,12},{20,24},{24,20},{28,0},{1,29},{... | collective-permute-start | bytes 147464 | tf_op jit(solution)/shard_map/ppermute | solution.py:605
  6.0 1.9 %shard_map.85 = (bf16[3,3,256,256]{3,2,1,0:T(8,128)(2,1)S(1)}, f32[768,256]{1,0:T(8,128)S(1)}) custom-call(bf16[24,32,256]{2,1,0:T(8,128)(2,1)S(1)} %get-tuple-element.59.cot, bf16[3,3,256,256]{3,2,1,0:T(8,128)(2,1)} %conv_w.1), custom_call_target="tpu_custom_call" | custom-call | bytes 3538944 | tf_op jit(solution)/shard_map/pallas_call | solution.py:28
  8.0 1.7 %collective-permute-start.2 = (bf16[128,256]{1,0:T(8,128)(2,1)S(1)}, bf16[128,256]{1,0:T(8,128)(2,1)S(1)}, u32[]{:S(2)}, u32[]{:S(2)}) collective-permute-start(bf16[128,256]{1,0:T(8,128)(2,1)S(1)} %get-tuple-element.62), channel_id=1, source_target_pairs={{0,1},{1,0},{2,3},{3,2},{4,5},{5,4},{6,7},{7,6},{8,9},{9,8},{10,11... | collective-permute-start | bytes 196616 | tf_op jit(solution)/shard_map/ppermute | solution.py:605
  9.6 0.7 %collective-permute-start.3 = (bf16[128,256]{1,0:T(8,128)(2,1)S(1)}, bf16[128,256]{1,0:T(8,128)(2,1)S(1)}, u32[]{:S(2)}, u32[]{:S(2)}) collective-permute-start(bf16[128,256]{1,0:T(8,128)(2,1)S(1)} %get-tuple-element.63), channel_id=1, source_target_pairs={{1,2},{2,1},{5,6},{6,5},{9,10},{10,9},{13,14},{14,13},{17,18},{18,... | collective-permute-start | bytes 196616 | tf_op jit(solution)/shard_map/ppermute | solution.py:605
  10.3 2.4 %shard_map.87 = (bf16[3,26,32,256]{3,2,1,0:T(8,128)(2,1)S(1)}, bf16[2,17,16,256]{3,2,1,0:T(8,128)(2,1)S(1)}, bf16[24,32,256]{2,1,0:T(8,128)(2,1)S(1)}, f32[768,2...) custom-call(bf16[12,16,256]{2,1,0:T(8,128)(2,1)S(1)} %get-tuple-elem, ...), custom_call_target="tpu_custom_call" | custom-call | bytes 10731520 | tf_op jit(solution)/shard_map/pallas_call | solution.py:28
  13.1 0.5 %collective-permute-start.5 = (bf16[14,32,256]{2,1,0:T(8,128)(2,1)S(1)}, bf16[14,32,256]{2,1,0:T(8,128)(2,1)S(1)}, u32[]{:S(2)}, u32[]{:S(2)}) collective-permute-start(bf16[14,32,256]{2,1,0:T(8,128)(2,1)S(1)} %get-tuple-element.82.edge), channel_id=1, source_target_pairs={{0,4},{4,0},{8,12},{12,8},{16,20},{20,16},{24,28},{28,24},{1,5},{5... | collective-permute-start | bytes 688136 | tf_op jit(solution)/shard_map/ppermute | solution.py:560
  13.6 0.7 %shard_map.89.phases = bf16[2,2,16,16,256]{4,3,2,1,0:T(8,128)(2,1)S(1)} custom-call(bf16[3,26,32,256]{3,2,1,0:T(8,128)(2,1)S(1)} %get-tuple-element.74.shifted, f32[768,256]{1,0:T(8,128)S(1)} %get-tuple-element.75.slope, f32[768,256]{1,0:T(8,128)S(1)} %get-tuple-element.76.grad_act, bf16[3,3,256,256]{3,2,1,0:T(8,128)(2,1)S(1)} %get-tuple-element.66.conv_w), custom_call_target="tpu_custom_call" | custom-call | bytes 4554752 | tf_op jit(solution)/shard_map/pallas_call | solution.py:28
  14.3 0.8 %shard_map.90 = (f32[2304,256]{1,0:T(8,128)S(1)}, bf16[4,288,256]{2,1,0:T(8,128)(2,1)S(1)}) custom-call(bf16[2,17,16,256]{3,2,1,0:T(8,128)(2,1)S(1)} %get-tuple-element.73.near, bf16[2,2,16,16,256]{4,3,2,1,0:T(8,128)(2,1)S(1)} %shard_map.89.phases), custom_call_target="tpu_custom_call" | custom-call | bytes 3751936 | tf_op jit(solution)/shard_map/pallas_call | solution.py:28
  15.7 1.7 %collective-permute-start.8 = (bf16[2,288,256]{2,1,0:T(8,128)(2,1)S(1)}, bf16[2,288,256]{2,1,0:T(8,128)(2,1)S(1)}, u32[]{:S(2)}, u32[]{:S(2)}) collective-permute-start(bf16[2,288,256]{2,1,0:T(8,128)(2,1)S(1)} %get-tuple-element.83), channel_id=1, source_target_pairs={{0,8},{4,20},{8,0},{12,28},{16,24},{20,4},{24,16},{28,12},{1,9},{5... | collective-permute-start | bytes 884744 | tf_op jit(solution)/shard_map/ppermute | solution.py:574
  17.5 1.1 %collective-permute-start.7 = (bf16[2,288,256]{2,1,0:T(8,128)(2,1)S(1)}, bf16[2,288,256]{2,1,0:T(8,128)(2,1)S(1)}, u32[]{:S(2)}, u32[]{:S(2)}) collective-permute-start(bf16[2,288,256]{2,1,0:T(8,128)(2,1)S(1)} %get-tuple-element.85), channel_id=1, source_target_pairs={{0,8},{4,20},{8,0},{12,28},{16,24},{20,4},{24,16},{28,12},{1,9},{5... | collective-permute-start | bytes 884744 | tf_op jit(solution)/shard_map/ppermute | solution.py:574
  18.6 0.8 %shard_map.93 = (f32[128,256]{1,0:T(8,128)S(1)}, f32[2,64,128]{2,1,0:T(8,128)S(1)}) custom-call(bf16[12,16,256]{2,1,0:T(8,128)(2,1)S(1)} %copy-done.4, bf16[24,32,256]{2,1,0:T(8,128)(2,1)S(1)} %copy-done.2, f32[96,256]{1,0:T(8,128)S(1)} %copy-done.6, f32[96,256]{1,0:T(8,128)S(1)} %get-tuple-element.64.right, f32[128,256]{1,0:T(8,128)S(1)} %get-tuple-element.87.upper, ...), custom_call_target="tpu_custom_call" | custom-call | bytes 3506176 | tf_op jit(solution)/shard_map/pallas_call | solution.py:28
  19.4 1.8 %shard_map.94 = bf16[24,32,256]{2,1,0:T(8,128)(2,1)} custom-call(bf16[24,32,256]{2,1,0:T(8,128)(2,1)S(1)} %get-tuple-element.72.act, f32[128,256]{1,0:T(8,128)S(1)} %get-tuple-element.89.ring_act, bf16[3,3,256,256]{3,2,1,0:T(8,128)(2,1)S(1)} %get-tuple-element.66.conv_w), custom_call_target="tpu_custom_call" | custom-call | bytes 2097152 | tf_op jit(solution)/shard_map/pallas_call | solution.py:28
  21.2 1.3 %collective-permute-done.8.got = bf16[2,288,256]{2,1,0:T(8,128)(2,1)S(1)} collective-permute-done((bf16[2,288,256]{2,1,0:T(8,128)(2,1)S(1)}, bf16[2,288,256]{2,1,0:T(8,128)(2,1)S(1)}, u32[]{:S(2)}, u32[]{:S(2)}) %collective-permute-start.8) | collective-permute-done | bytes 294944 | tf_op jit(solution)/shard_map/ppermute | solution.py:574
  22.5 1.8 %collective-permute-start.9 = (bf16[1,288,256]{2,1,0:T(8,128)(2,1)S(1)}, bf16[1,288,256]{2,1,0:T(8,128)(2,1)S(1)}, u32[]{:S(2)}, u32[]{:S(2)}) collective-permute-start(bf16[1,288,256]{2,1,0:T(8,128)(2,1)S(1)} %get-tuple-element.97), channel_id=1, source_target_pairs={{0,16},{4,12},{8,24},{12,4},{16,0},{20,28},{24,8},{28,20},{1,17},{... | collective-permute-start | bytes 442376 | tf_op jit(solution)/shard_map/ppermute | solution.py:574
  24.3 2.1 %collective-permute-done.7.got = bf16[2,288,256]{2,1,0:T(8,128)(2,1)S(1)} collective-permute-done((bf16[2,288,256]{2,1,0:T(8,128)(2,1)S(1)}, bf16[2,288,256]{2,1,0:T(8,128)(2,1)S(1)}, u32[]{:S(2)}, u32[]{:S(2)}) %collective-permute-start.7) | collective-permute-done | bytes 294944 | tf_op jit(solution)/shard_map/ppermute | solution.py:574
  26.4 1.8 %collective-permute-start.10 = (bf16[1,288,256]{2,1,0:T(8,128)(2,1)S(1)}, bf16[1,288,256]{2,1,0:T(8,128)(2,1)S(1)}, u32[]{:S(2)}, u32[]{:S(2)}) collective-permute-start(bf16[1,288,256]{2,1,0:T(8,128)(2,1)S(1)} %get-tuple-element.92), channel_id=1, source_target_pairs={{0,16},{4,12},{8,24},{12,4},{16,0},{20,28},{24,8},{28,20},{1,17},{... | collective-permute-start | bytes 442376 | tf_op jit(solution)/shard_map/ppermute | solution.py:574
  28.2 1.2 %shard_map.96 = bf16[12,16,256]{2,1,0:T(8,128)(2,1)} custom-call(bf16[2,2,16,16,256]{4,3,2,1,0:T(8,128)(2,1)S(1)} %shard_map.89.phases, f32[2,64,128]{2,1,0:T(8,128)S(1)} %get-tuple-element.93.ring_grad, bf16[3,3,256,256]{3,2,1,0:T(8,128)(2,1)S(1)} %copy-done), custom_call_target="tpu_custom_call" | custom-call | bytes 1867776 | tf_op jit(solution)/shard_map/pallas_call | solution.py:28
  29.4 2.2 %collective-permute-done.10.got_up = bf16[1,288,256]{2,1,0:T(8,128)(2,1)S(1)} collective-permute-done((bf16[1,288,256]{2,1,0:T(8,128)(2,1)S(1)}, bf16[1,288,256]{2,1,0:T(8,128)(2,1)S(1)}, u32[]{:S(2)}, u32[]{:S(2)}) %collective-permute-start.10) | collective-permute-done | bytes 147488 | tf_op jit(solution)/shard_map/ppermute | solution.py:574
  31.9 3.5 %collective-permute-start.11 = (bf16[288,128]{1,0:T(8,128)(2,1)S(1)}, bf16[288,128]{1,0:T(8,128)(2,1)S(1)}, u32[]{:S(2)}, u32[]{:S(2)}) collective-permute-start(bf16[288,128]{1,0:T(8,128)(2,1)S(1)} %get-tuple-element.101), channel_id=1, source_target_pairs={{0,3},{1,2},{2,1},{3,0},{4,7},{5,6},{6,5},{7,4},{8,11},{9,10},{10,... | collective-permute-start | bytes 221192 | tf_op jit(solution)/shard_map/ppermute | solution.py:593
  35.5 2.5 %collective-permute-start.12 = (bf16[288,128]{1,0:T(8,128)(2,1)S(1)}, bf16[288,128]{1,0:T(8,128)(2,1)S(1)}, u32[]{:S(2)}, u32[]{:S(2)}) collective-permute-start(bf16[288,128]{1,0:T(8,128)(2,1)S(1)} %get-tuple-element.102), channel_id=1, source_target_pairs={{0,2},{1,3},{2,0},{3,1},{4,6},{5,7},{6,4},{7,5},{8,10},{9,11},{10,... | collective-permute-start | bytes 221192 | tf_op jit(solution)/shard_map/ppermute | solution.py:593
  38.5 2.6 %collective-permute-done.12.refs_1_ = bf16[288,128]{1,0:T(8,128)(2,1)S(1)} collective-permute-done((bf16[288,128]{1,0:T(8,128)(2,1)S(1)}, bf16[288,128]{1,0:T(8,128)(2,1)S(1)}, u32[]{:S(2)}, u32[]{:S(2)}) %collective-permute-start.12) | collective-permute-done | bytes 73760 | tf_op jit(solution)/shard_map/ppermute | solution.py:593
  41.0 1.3 %collective-permute-done.13.refs_2_ = bf16[288,128]{1,0:T(8,128)(2,1)S(1)} collective-permute-done((bf16[288,128]{1,0:T(8,128)(2,1)S(1)}, bf16[288,128]{1,0:T(8,128)(2,1)S(1)}, u32[]{:S(2)}, u32[]{:S(2)}) %collective-permute-start.13) | collective-permute-done | bytes 73760 | tf_op jit(solution)/shard_map/ppermute | solution.py:593
  42.4 0.8 %shard_map.99 = (f32[64,288]{1,0:T(8,128)}, f32[64,288]{1,0:T(8,128)}) custom-call(f32[288,128]{1,0:T(8,128)S(1)} %get-tuple-element.100.own, bf16[288,128]{1,0:T(8,128)(2,1)S(1)} %collective-permute-done.11.refs_0_, bf16[288,128]{1,0:T(8,128)(2,1)S(1)} %collective-permute-done.12.refs_1_, bf16[288,128]{1,0:T(8,128)(2,1)S(1)} %collective-permute-done.13.refs_2_), custom_call_target="tpu_custom_call" | custom-call | bytes 516096 | tf_op jit(solution)/shard_map/pallas_call | solution.py:28
  (34 shorter events, 2.5 us)
Async XLA Ops:
  1.9 8.4 %copy-start.1 = (bf16[24,32,256]{2,1,0:T(8,128)(2,1)}, bf16[24,32,256]{2,1,0:T(8,128)(2,1)S(1)}, u32[]{:S(2)}) copy-start(bf16[24,32,256]{2,1,0:T(8,128)(2,1)S(1)} %get-tuple-element.59.cot) | copy-start | bytes 1179652
  1.9 8.4 %copy-start.3 = (bf16[12,16,256]{2,1,0:T(8,128)(2,1)}, bf16[12,16,256]{2,1,0:T(8,128)(2,1)S(1)}, u32[]{:S(2)}) copy-start(bf16[12,16,256]{2,1,0:T(8,128)(2,1)S(1)} %get-tuple-element.55.coarse) | copy-start | bytes 294916
  1.9 6.0 %collective-permute-start = (bf16[96,256]{1,0:T(8,128)(2,1)S(1)}, bf16[96,256]{1,0:T(8,128)(2,1)S(1)}, u32[]{:S(2)}, u32[]{:S(2)}) collective-permute-start(bf16[96,256]{1,0:T(8,128)(2,1)S(1)} %get-tuple-element.60), channel_id=1, source_target_pairs={{0,4},{4,0},{8,12},{12,8},{16,20},{20,16},{24,28},{28,24},{1,5},{5... | collective-permute-start | bytes 147464 | tf_op jit(solution)/shard_map/ppermute | solution.py:605
  2.4 5.5 %collective-permute-start.1 = (bf16[96,256]{1,0:T(8,128)(2,1)S(1)}, bf16[96,256]{1,0:T(8,128)(2,1)S(1)}, u32[]{:S(2)}, u32[]{:S(2)}) collective-permute-start(bf16[96,256]{1,0:T(8,128)(2,1)S(1)} %get-tuple-element.61), channel_id=1, source_target_pairs={{0,28},{4,8},{8,4},{12,16},{16,12},{20,24},{24,20},{28,0},{1,29},{... | collective-permute-start | bytes 147464 | tf_op jit(solution)/shard_map/ppermute | solution.py:605
  6.0 4.3 %copy-start = (bf16[3,3,256,256]{3,2,1,0:T(8,128)(2,1)S(1)}, bf16[3,3,256,256]{3,2,1,0:T(8,128)(2,1)}, u32[]{:S(2)}) copy-start(bf16[3,3,256,256]{3,2,1,0:T(8,128)(2,1)} %up_w.7) | copy-start | bytes 3538948
  7.9 4.8 %copy-start.5 = (f32[96,256]{1,0:T(8,128)}, f32[96,256]{1,0:T(8,128)S(1)}, u32[]{:S(2)}) copy-start(f32[96,256]{1,0:T(8,128)S(1)} %get-tuple-element.86.left) | copy-start | bytes 294916
  8.0 4.9 %collective-permute-start.2 = (bf16[128,256]{1,0:T(8,128)(2,1)S(1)}, bf16[128,256]{1,0:T(8,128)(2,1)S(1)}, u32[]{:S(2)}, u32[]{:S(2)}) collective-permute-start(bf16[128,256]{1,0:T(8,128)(2,1)S(1)} %get-tuple-element.62), channel_id=1, source_target_pairs={{0,1},{1,0},{2,3},{3,2},{4,5},{5,4},{6,7},{7,6},{8,9},{9,8},{10,11... | collective-permute-start | bytes 196616 | tf_op jit(solution)/shard_map/ppermute | solution.py:605
  9.6 3.2 %collective-permute-start.3 = (bf16[128,256]{1,0:T(8,128)(2,1)S(1)}, bf16[128,256]{1,0:T(8,128)(2,1)S(1)}, u32[]{:S(2)}, u32[]{:S(2)}) collective-permute-start(bf16[128,256]{1,0:T(8,128)(2,1)S(1)} %get-tuple-element.63), channel_id=1, source_target_pairs={{1,2},{2,1},{5,6},{6,5},{9,10},{10,9},{13,14},{14,13},{17,18},{18,... | collective-permute-start | bytes 196616 | tf_op jit(solution)/shard_map/ppermute | solution.py:605
  12.8 2.4 %collective-permute-start.4 = (bf16[4,288,256]{2,1,0:T(8,128)(2,1)S(1)}, bf16[4,288,256]{2,1,0:T(8,128)(2,1)S(1)}, u32[]{:S(2)}, u32[]{:S(2)}) collective-permute-start(bf16[4,288,256]{2,1,0:T(8,128)(2,1)S(1)} %get-tuple-element.81), channel_id=1, source_target_pairs={{0,4},{4,0},{8,12},{12,8},{16,20},{20,16},{24,28},{28,24},{1,5},{5... | collective-permute-start | bytes 1769480 | tf_op jit(solution)/shard_map/ppermute | solution.py:560
  13.1 2.1 %collective-permute-start.5 = (bf16[14,32,256]{2,1,0:T(8,128)(2,1)S(1)}, bf16[14,32,256]{2,1,0:T(8,128)(2,1)S(1)}, u32[]{:S(2)}, u32[]{:S(2)}) collective-permute-start(bf16[14,32,256]{2,1,0:T(8,128)(2,1)S(1)} %get-tuple-element.82.edge), channel_id=1, source_target_pairs={{0,4},{4,0},{8,12},{12,8},{16,20},{20,16},{24,28},{28,24},{1,5},{5... | collective-permute-start | bytes 688136 | tf_op jit(solution)/shard_map/ppermute | solution.py:560
  15.1 2.3 %collective-permute-start.6 = (bf16[4,288,256]{2,1,0:T(8,128)(2,1)S(1)}, bf16[4,288,256]{2,1,0:T(8,128)(2,1)S(1)}, u32[]{:S(2)}, u32[]{:S(2)}) collective-permute-start(bf16[4,288,256]{2,1,0:T(8,128)(2,1)S(1)} %get-tuple-element.79), channel_id=1, source_target_pairs={{0,4},{4,0},{8,12},{12,8},{16,20},{20,16},{24,28},{28,24},{1,5},{5... | collective-permute-start | bytes 1769480 | tf_op jit(solution)/shard_map/ppermute | solution.py:560
  15.7 6.8 %collective-permute-start.8 = (bf16[2,288,256]{2,1,0:T(8,128)(2,1)S(1)}, bf16[2,288,256]{2,1,0:T(8,128)(2,1)S(1)}, u32[]{:S(2)}, u32[]{:S(2)}) collective-permute-start(bf16[2,288,256]{2,1,0:T(8,128)(2,1)S(1)} %get-tuple-element.83), channel_id=1, source_target_pairs={{0,8},{4,20},{8,0},{12,28},{16,24},{20,4},{24,16},{28,12},{1,9},{5... | collective-permute-start | bytes 884744 | tf_op jit(solution)/shard_map/ppermute | solution.py:574
  17.3 1.2 %copy-start.2 = (bf16[24,32,256]{2,1,0:T(8,128)(2,1)S(1)}, bf16[24,32,256]{2,1,0:T(8,128)(2,1)}, u32[]{:S(2)}) copy-start(bf16[24,32,256]{2,1,0:T(8,128)(2,1)} %copy-done.1) | copy-start | bytes 1179652
  17.4 1.2 %copy-start.4 = (bf16[12,16,256]{2,1,0:T(8,128)(2,1)S(1)}, bf16[12,16,256]{2,1,0:T(8,128)(2,1)}, u32[]{:S(2)}) copy-start(bf16[12,16,256]{2,1,0:T(8,128)(2,1)} %copy-done.3) | copy-start | bytes 294916
  17.4 1.2 %copy-start.6 = (f32[96,256]{1,0:T(8,128)S(1)}, f32[96,256]{1,0:T(8,128)}, u32[]{:S(2)}) copy-start(f32[96,256]{1,0:T(8,128)} %copy-done.5) | copy-start | bytes 294916
  17.5 8.9 %collective-permute-start.7 = (bf16[2,288,256]{2,1,0:T(8,128)(2,1)S(1)}, bf16[2,288,256]{2,1,0:T(8,128)(2,1)S(1)}, u32[]{:S(2)}, u32[]{:S(2)}) collective-permute-start(bf16[2,288,256]{2,1,0:T(8,128)(2,1)S(1)} %get-tuple-element.85), channel_id=1, source_target_pairs={{0,8},{4,20},{8,0},{12,28},{16,24},{20,4},{24,16},{28,12},{1,9},{5... | collective-permute-start | bytes 884744 | tf_op jit(solution)/shard_map/ppermute | solution.py:574
  22.5 6.9 %collective-permute-start.9 = (bf16[1,288,256]{2,1,0:T(8,128)(2,1)S(1)}, bf16[1,288,256]{2,1,0:T(8,128)(2,1)S(1)}, u32[]{:S(2)}, u32[]{:S(2)}) collective-permute-start(bf16[1,288,256]{2,1,0:T(8,128)(2,1)S(1)} %get-tuple-element.97), channel_id=1, source_target_pairs={{0,16},{4,12},{8,24},{12,4},{16,0},{20,28},{24,8},{28,20},{1,17},{... | collective-permute-start | bytes 442376 | tf_op jit(solution)/shard_map/ppermute | solution.py:574
  26.4 5.2 %collective-permute-start.10 = (bf16[1,288,256]{2,1,0:T(8,128)(2,1)S(1)}, bf16[1,288,256]{2,1,0:T(8,128)(2,1)S(1)}, u32[]{:S(2)}, u32[]{:S(2)}) collective-permute-start(bf16[1,288,256]{2,1,0:T(8,128)(2,1)S(1)} %get-tuple-element.92), channel_id=1, source_target_pairs={{0,16},{4,12},{8,24},{12,4},{16,0},{20,28},{24,8},{28,20},{1,17},{... | collective-permute-start | bytes 442376 | tf_op jit(solution)/shard_map/ppermute | solution.py:574
  31.9 6.6 %collective-permute-start.11 = (bf16[288,128]{1,0:T(8,128)(2,1)S(1)}, bf16[288,128]{1,0:T(8,128)(2,1)S(1)}, u32[]{:S(2)}, u32[]{:S(2)}) collective-permute-start(bf16[288,128]{1,0:T(8,128)(2,1)S(1)} %get-tuple-element.101), channel_id=1, source_target_pairs={{0,3},{1,2},{2,1},{3,0},{4,7},{5,6},{6,5},{7,4},{8,11},{9,10},{10,... | collective-permute-start | bytes 221192 | tf_op jit(solution)/shard_map/ppermute | solution.py:593
  35.5 5.6 %collective-permute-start.12 = (bf16[288,128]{1,0:T(8,128)(2,1)S(1)}, bf16[288,128]{1,0:T(8,128)(2,1)S(1)}, u32[]{:S(2)}, u32[]{:S(2)}) collective-permute-start(bf16[288,128]{1,0:T(8,128)(2,1)S(1)} %get-tuple-element.102), channel_id=1, source_target_pairs={{0,2},{1,3},{2,0},{3,1},{4,6},{5,7},{6,4},{7,5},{8,10},{9,11},{10,... | collective-permute-start | bytes 221192 | tf_op jit(solution)/shard_map/ppermute | solution.py:593
  38.0 4.4 %collective-permute-start.13 = (bf16[288,128]{1,0:T(8,128)(2,1)S(1)}, bf16[288,128]{1,0:T(8,128)(2,1)S(1)}, u32[]{:S(2)}, u32[]{:S(2)}) collective-permute-start(bf16[288,128]{1,0:T(8,128)(2,1)S(1)} %get-tuple-element.103), channel_id=1, source_target_pairs={{0,1},{1,0},{2,3},{3,2},{4,5},{5,4},{6,7},{7,6},{8,9},{9,8},{10,11... | collective-permute-start | bytes 221192 | tf_op jit(solution)/shard_map/ppermute | solution.py:593

commit v16 on v15

--- a/solution.py
+++ b/solution.py
@@ -693,8 +693,6 @@
     for step in range(1, steps):
         own_conv, to_conv = plane_sum(own_conv, got_conv)
         got_conv = plane_swap(to_conv, step)
-        own_up, to_up = plane_sum(own_up, got_up)
-        got_up = plane_swap(to_up, step)
         if step == 1:
             grad_coarse = kernel_call(
                 coarse_kernel, [sds(coarse.shape, bf16)],
@@ -702,9 +700,11 @@
                     halves(n_rows * (n_cols + 2 * MARGIN), channels),
                     pltpu.VMEM((4, n_rows + 1, n_cols, channels), bf16),
                 ],
-                0, phases, after(ring_grad, to_up), up_weight,
+                0, phases, after(ring_grad, to_conv), up_weight,
             )[0]
             own_up = after(own_up, grad_coarse)
+        own_up, to_up = plane_sum(own_up, got_up)
+        got_up = plane_swap(to_up, step)
     grad_conv, grad_up = band_sum(own_conv, got_conv, own_up, got_up)
     return (decoded, grad_coarse, grad_up, grad_conv)
 

time: 43.3 us -> 43.3 us (level)
  no operation moved by 1% of the time
where the time goes in v16:
time: 43.3 us; the launch traced here: 43.2 us
  starting transfers between devices  19.9 us (46%)
  Pallas kernels  12.9 us (30%)
  waiting for transfers between devices  9.48 us (22%)
  between operations  0.83 us (2%)
    pallas_call x16, Pallas kernels, kernel_call(): pl.pallas_call(body, out_shape=tuple(outs), in_specs=[hbm if i in far els...  12.9 us
    ppermute x3, starting transfers between devices, band_sum(): lax.ppermute(messages[k - 1], 'band', xor_pairs(bands, k))  6.56 us
    ppermute x4, starting transfers between devices, swap(): return (lax.ppermute(first, axis, one), lax.ppermute(second, axis, two))  6.38 us
    ppermute x4, starting transfers between devices, plane_swap(): lax.ppermute(message, 'face', [(i, i ^ 2 << orders[i % 2][step]) for i in...  6.27 us
    ppermute x4, waiting for transfers between devices, plane_swap(): lax.ppermute(message, 'face', [(i, i ^ 2 << orders[i % 2][step]) for i in...  5.6 us
    ppermute x3, waiting for transfers between devices, band_sum(): lax.ppermute(messages[k - 1], 'band', xor_pairs(bands, k))  3.86 us
  transfers between devices with their start and end apart: 14, of which 5 were waited for; matrix products, arithmetic and copies ran while one was open for 0% of the time, Pallas kernels for 24%

profile of v16, /device:TPU:0, one launch (start us, length us, event | category | flops | bytes accessed | tf_op | source)
XLA Modules:
  0.0 43.2 jit_solution(10839212469471444128)
XLA Ops:
  0.6 1.2 %shard_map.84 = (bf16[96,256]{1,0:T(8,128)(2,1)S(1)}, bf16[96,256]{1,0:T(8,128)(2,1)S(1)}, bf16[24,32,256]{2,1,0:T(8,128)(2,1)S(1)}, bf16[24,32,256]{2,1,0:T(8,128)(2,1)S(1)}, bf16[12,16,256]{2,1,0:T(8,128)(2,1)S(1)}) custom-call(bf16[12,16,256]{2,1,0:T(8,128)(2,1)} %coarse.1, bf16[24,32,256]{2,1,0:T(8,128)(2,1)} %skip.1, bf16[24,32,256]{2,1,0:T(8,128)(2,1)} %cot.1), custom_call_target="tpu_custom_call" | custom-call | bytes 1867776 | tf_op jit(solution)/shard_map/pallas_call | solution.py:28
  2.4 3.6 %collective-permute-start.1 = (bf16[96,256]{1,0:T(8,128)(2,1)S(1)}, bf16[96,256]{1,0:T(8,128)(2,1)S(1)}, u32[]{:S(2)}, u32[]{:S(2)}) collective-permute-start(bf16[96,256]{1,0:T(8,128)(2,1)S(1)} %get-tuple-element.61), channel_id=1, source_target_pairs={{0,28},{4,8},{8,4},{12,16},{16,12},{20,24},{24,20},{28,0},{1,29},{... | collective-permute-start | bytes 147464 | tf_op jit(solution)/shard_map/ppermute | solution.py:605
  6.0 1.9 %shard_map.85 = (bf16[3,3,256,256]{3,2,1,0:T(8,128)(2,1)S(1)}, f32[768,256]{1,0:T(8,128)S(1)}) custom-call(bf16[24,32,256]{2,1,0:T(8,128)(2,1)S(1)} %get-tuple-element.59.cot, bf16[3,3,256,256]{3,2,1,0:T(8,128)(2,1)} %conv_w.1), custom_call_target="tpu_custom_call" | custom-call | bytes 3538944 | tf_op jit(solution)/shard_map/pallas_call | solution.py:28
  8.0 1.7 %collective-permute-start.2 = (bf16[128,256]{1,0:T(8,128)(2,1)S(1)}, bf16[128,256]{1,0:T(8,128)(2,1)S(1)}, u32[]{:S(2)}, u32[]{:S(2)}) collective-permute-start(bf16[128,256]{1,0:T(8,128)(2,1)S(1)} %get-tuple-element.62), channel_id=1, source_target_pairs={{0,1},{1,0},{2,3},{3,2},{4,5},{5,4},{6,7},{7,6},{8,9},{9,8},{10,11... | collective-permute-start | bytes 196616 | tf_op jit(solution)/shard_map/ppermute | solution.py:605
  9.6 0.7 %collective-permute-start.3 = (bf16[128,256]{1,0:T(8,128)(2,1)S(1)}, bf16[128,256]{1,0:T(8,128)(2,1)S(1)}, u32[]{:S(2)}, u32[]{:S(2)}) collective-permute-start(bf16[128,256]{1,0:T(8,128)(2,1)S(1)} %get-tuple-element.63), channel_id=1, source_target_pairs={{1,2},{2,1},{5,6},{6,5},{9,10},{10,9},{13,14},{14,13},{17,18},{18,... | collective-permute-start | bytes 196616 | tf_op jit(solution)/shard_map/ppermute | solution.py:605
  10.3 2.4 %shard_map.87 = (bf16[3,26,32,256]{3,2,1,0:T(8,128)(2,1)S(1)}, bf16[2,17,16,256]{3,2,1,0:T(8,128)(2,1)S(1)}, bf16[24,32,256]{2,1,0:T(8,128)(2,1)S(1)}, f32[768,2...) custom-call(bf16[12,16,256]{2,1,0:T(8,128)(2,1)S(1)} %get-tuple-elem, ...), custom_call_target="tpu_custom_call" | custom-call | bytes 10731520 | tf_op jit(solution)/shard_map/pallas_call | solution.py:28
  13.1 0.5 %collective-permute-start.5 = (bf16[14,32,256]{2,1,0:T(8,128)(2,1)S(1)}, bf16[14,32,256]{2,1,0:T(8,128)(2,1)S(1)}, u32[]{:S(2)}, u32[]{:S(2)}) collective-permute-start(bf16[14,32,256]{2,1,0:T(8,128)(2,1)S(1)} %get-tuple-element.82.edge), channel_id=1, source_target_pairs={{0,4},{4,0},{8,12},{12,8},{16,20},{20,16},{24,28},{28,24},{1,5},{5... | collective-permute-start | bytes 688136 | tf_op jit(solution)/shard_map/ppermute | solution.py:560
  13.6 0.7 %shard_map.89.phases = bf16[2,2,16,16,256]{4,3,2,1,0:T(8,128)(2,1)S(1)} custom-call(bf16[3,26,32,256]{3,2,1,0:T(8,128)(2,1)S(1)} %get-tuple-element.74.shifted, f32[768,256]{1,0:T(8,128)S(1)} %get-tuple-element.75.slope, f32[768,256]{1,0:T(8,128)S(1)} %get-tuple-element.76.grad_act, bf16[3,3,256,256]{3,2,1,0:T(8,128)(2,1)S(1)} %get-tuple-element.66.conv_w), custom_call_target="tpu_custom_call" | custom-call | bytes 4554752 | tf_op jit(solution)/shard_map/pallas_call | solution.py:28
  14.3 0.8 %shard_map.90 = (f32[2304,256]{1,0:T(8,128)S(1)}, bf16[4,288,256]{2,1,0:T(8,128)(2,1)S(1)}) custom-call(bf16[2,17,16,256]{3,2,1,0:T(8,128)(2,1)S(1)} %get-tuple-element.73.near, bf16[2,2,16,16,256]{4,3,2,1,0:T(8,128)(2,1)S(1)} %shard_map.89.phases), custom_call_target="tpu_custom_call" | custom-call | bytes 3751936 | tf_op jit(solution)/shard_map/pallas_call | solution.py:28
  15.7 1.7 %collective-permute-start.7 = (bf16[2,288,256]{2,1,0:T(8,128)(2,1)S(1)}, bf16[2,288,256]{2,1,0:T(8,128)(2,1)S(1)}, u32[]{:S(2)}, u32[]{:S(2)}) collective-permute-start(bf16[2,288,256]{2,1,0:T(8,128)(2,1)S(1)} %get-tuple-element.83), channel_id=1, source_target_pairs={{0,8},{4,20},{8,0},{12,28},{16,24},{20,4},{24,16},{28,12},{1,9},{5... | collective-permute-start | bytes 884744 | tf_op jit(solution)/shard_map/ppermute | solution.py:574
  17.5 1.1 %collective-permute-start.9 = (bf16[2,288,256]{2,1,0:T(8,128)(2,1)S(1)}, bf16[2,288,256]{2,1,0:T(8,128)(2,1)S(1)}, u32[]{:S(2)}, u32[]{:S(2)}) collective-permute-start(bf16[2,288,256]{2,1,0:T(8,128)(2,1)S(1)} %get-tuple-element.85), channel_id=1, source_target_pairs={{0,8},{4,20},{8,0},{12,28},{16,24},{20,4},{24,16},{28,12},{1,9},{5... | collective-permute-start | bytes 884744 | tf_op jit(solution)/shard_map/ppermute | solution.py:574
  18.6 0.8 %shard_map.93 = (f32[128,256]{1,0:T(8,128)S(1)}, f32[2,64,128]{2,1,0:T(8,128)S(1)}) custom-call(bf16[12,16,256]{2,1,0:T(8,128)(2,1)S(1)} %copy-done.4, bf16[24,32,256]{2,1,0:T(8,128)(2,1)S(1)} %copy-done.2, f32[96,256]{1,0:T(8,128)S(1)} %copy-done.6, f32[96,256]{1,0:T(8,128)S(1)} %get-tuple-element.64.right, f32[128,256]{1,0:T(8,128)S(1)} %get-tuple-element.87.upper, ...), custom_call_target="tpu_custom_call" | custom-call | bytes 3506176 | tf_op jit(solution)/shard_map/pallas_call | solution.py:28
  19.4 1.8 %shard_map.94 = bf16[24,32,256]{2,1,0:T(8,128)(2,1)} custom-call(bf16[24,32,256]{2,1,0:T(8,128)(2,1)S(1)} %get-tuple-element.72.act, f32[128,256]{1,0:T(8,128)S(1)} %get-tuple-element.89.ring_act, bf16[3,3,256,256]{3,2,1,0:T(8,128)(2,1)S(1)} %get-tuple-element.66.conv_w), custom_call_target="tpu_custom_call" | custom-call | bytes 2097152 | tf_op jit(solution)/shard_map/pallas_call | solution.py:28
  21.2 1.3 %collective-permute-done.7.got = bf16[2,288,256]{2,1,0:T(8,128)(2,1)S(1)} collective-permute-done((bf16[2,288,256]{2,1,0:T(8,128)(2,1)S(1)}, bf16[2,288,256]{2,1,0:T(8,128)(2,1)S(1)}, u32[]{:S(2)}, u32[]{:S(2)}) %collective-permute-start.7) | collective-permute-done | bytes 294944 | tf_op jit(solution)/shard_map/ppermute | solution.py:574
  22.5 1.8 %collective-permute-start.8 = (bf16[1,288,256]{2,1,0:T(8,128)(2,1)S(1)}, bf16[1,288,256]{2,1,0:T(8,128)(2,1)S(1)}, u32[]{:S(2)}, u32[]{:S(2)}) collective-permute-start(bf16[1,288,256]{2,1,0:T(8,128)(2,1)S(1)} %get-tuple-element.93), channel_id=1, source_target_pairs={{0,16},{4,12},{8,24},{12,4},{16,0},{20,28},{24,8},{28,20},{1,17},{... | collective-permute-start | bytes 442376 | tf_op jit(solution)/shard_map/ppermute | solution.py:574
  24.3 1.2 %shard_map.96 = bf16[12,16,256]{2,1,0:T(8,128)(2,1)} custom-call(bf16[2,2,16,16,256]{4,3,2,1,0:T(8,128)(2,1)S(1)} %shard_map.89.phases, f32[2,64,128]{2,1,0:T(8,128)S(1)} %get-tuple-element.94.ring_grad, bf16[3,3,256,256]{3,2,1,0:T(8,128)(2,1)S(1)} %copy-done), custom_call_target="tpu_custom_call" | custom-call | bytes 1867776 | tf_op jit(solution)/shard_map/pallas_call | solution.py:28
  25.5 0.9 %collective-permute-done.9.got = bf16[2,288,256]{2,1,0:T(8,128)(2,1)S(1)} collective-permute-done((bf16[2,288,256]{2,1,0:T(8,128)(2,1)S(1)}, bf16[2,288,256]{2,1,0:T(8,128)(2,1)S(1)}, u32[]{:S(2)}, u32[]{:S(2)}) %collective-permute-start.9) | collective-permute-done | bytes 294944 | tf_op jit(solution)/shard_map/ppermute | solution.py:574
  26.4 1.8 %collective-permute-start.10 = (bf16[1,288,256]{2,1,0:T(8,128)(2,1)S(1)}, bf16[1,288,256]{2,1,0:T(8,128)(2,1)S(1)}, u32[]{:S(2)}, u32[]{:S(2)}) collective-permute-start(bf16[1,288,256]{2,1,0:T(8,128)(2,1)S(1)} %get-tuple-element.99), channel_id=1, source_target_pairs={{0,16},{4,12},{8,24},{12,4},{16,0},{20,28},{24,8},{28,20},{1,17},{... | collective-permute-start | bytes 442376 | tf_op jit(solution)/shard_map/ppermute | solution.py:574
  28.2 3.4 %collective-permute-done.10.got_up = bf16[1,288,256]{2,1,0:T(8,128)(2,1)S(1)} collective-permute-done((bf16[1,288,256]{2,1,0:T(8,128)(2,1)S(1)}, bf16[1,288,256]{2,1,0:T(8,128)(2,1)S(1)}, u32[]{:S(2)}, u32[]{:S(2)}) %collective-permute-start.10) | collective-permute-done | bytes 147488 | tf_op jit(solution)/shard_map/ppermute | solution.py:574
  31.9 3.5 %collective-permute-start.11 = (bf16[288,128]{1,0:T(8,128)(2,1)S(1)}, bf16[288,128]{1,0:T(8,128)(2,1)S(1)}, u32[]{:S(2)}, u32[]{:S(2)}) collective-permute-start(bf16[288,128]{1,0:T(8,128)(2,1)S(1)} %get-tuple-element.101), channel_id=1, source_target_pairs={{0,3},{1,2},{2,1},{3,0},{4,7},{5,6},{6,5},{7,4},{8,11},{9,10},{10,... | collective-permute-start | bytes 221192 | tf_op jit(solution)/shard_map/ppermute | solution.py:593
  35.5 2.5 %collective-permute-start.12 = (bf16[288,128]{1,0:T(8,128)(2,1)S(1)}, bf16[288,128]{1,0:T(8,128)(2,1)S(1)}, u32[]{:S(2)}, u32[]{:S(2)}) collective-permute-start(bf16[288,128]{1,0:T(8,128)(2,1)S(1)} %get-tuple-element.102), channel_id=1, source_target_pairs={{0,2},{1,3},{2,0},{3,1},{4,6},{5,7},{6,4},{7,5},{8,10},{9,11},{10,... | collective-permute-start | bytes 221192 | tf_op jit(solution)/shard_map/ppermute | solution.py:593
  38.5 2.6 %collective-permute-done.12.refs_1_ = bf16[288,128]{1,0:T(8,128)(2,1)S(1)} collective-permute-done((bf16[288,128]{1,0:T(8,128)(2,1)S(1)}, bf16[288,128]{1,0:T(8,128)(2,1)S(1)}, u32[]{:S(2)}, u32[]{:S(2)}) %collective-permute-start.12) | collective-permute-done | bytes 73760 | tf_op jit(solution)/shard_map/ppermute | solution.py:593
  41.0 1.3 %collective-permute-done.13.refs_2_ = bf16[288,128]{1,0:T(8,128)(2,1)S(1)} collective-permute-done((bf16[288,128]{1,0:T(8,128)(2,1)S(1)}, bf16[288,128]{1,0:T(8,128)(2,1)S(1)}, u32[]{:S(2)}, u32[]{:S(2)}) %collective-permute-start.13) | collective-permute-done | bytes 73760 | tf_op jit(solution)/shard_map/ppermute | solution.py:593
  42.4 0.8 %shard_map.99 = (f32[64,288]{1,0:T(8,128)}, f32[64,288]{1,0:T(8,128)}) custom-call(f32[288,128]{1,0:T(8,128)S(1)} %get-tuple-element.100.own, bf16[288,128]{1,0:T(8,128)(2,1)S(1)} %collective-permute-done.11.refs_0_, bf16[288,128]{1,0:T(8,128)(2,1)S(1)} %collective-permute-done.12.refs_1_, bf16[288,128]{1,0:T(8,128)(2,1)S(1)} %collective-permute-done.13.refs_2_), custom_call_target="tpu_custom_call" | custom-call | bytes 516096 | tf_op jit(solution)/shard_map/pallas_call | solution.py:28
  (34 shorter events, 2.5 us)
Async XLA Ops:
  1.9 8.4 %copy-start.1 = (bf16[24,32,256]{2,1,0:T(8,128)(2,1)}, bf16[24,32,256]{2,1,0:T(8,128)(2,1)S(1)}, u32[]{:S(2)}) copy-start(bf16[24,32,256]{2,1,0:T(8,128)(2,1)S(1)} %get-tuple-element.59.cot) | copy-start | bytes 1179652
  1.9 8.4 %copy-start.3 = (bf16[12,16,256]{2,1,0:T(8,128)(2,1)}, bf16[12,16,256]{2,1,0:T(8,128)(2,1)S(1)}, u32[]{:S(2)}) copy-start(bf16[12,16,256]{2,1,0:T(8,128)(2,1)S(1)} %get-tuple-element.55.coarse) | copy-start | bytes 294916
  1.9 6.0 %collective-permute-start = (bf16[96,256]{1,0:T(8,128)(2,1)S(1)}, bf16[96,256]{1,0:T(8,128)(2,1)S(1)}, u32[]{:S(2)}, u32[]{:S(2)}) collective-permute-start(bf16[96,256]{1,0:T(8,128)(2,1)S(1)} %get-tuple-element.60), channel_id=1, source_target_pairs={{0,4},{4,0},{8,12},{12,8},{16,20},{20,16},{24,28},{28,24},{1,5},{5... | collective-permute-start | bytes 147464 | tf_op jit(solution)/shard_map/ppermute | solution.py:605
  2.4 5.5 %collective-permute-start.1 = (bf16[96,256]{1,0:T(8,128)(2,1)S(1)}, bf16[96,256]{1,0:T(8,128)(2,1)S(1)}, u32[]{:S(2)}, u32[]{:S(2)}) collective-permute-start(bf16[96,256]{1,0:T(8,128)(2,1)S(1)} %get-tuple-element.61), channel_id=1, source_target_pairs={{0,28},{4,8},{8,4},{12,16},{16,12},{20,24},{24,20},{28,0},{1,29},{... | collective-permute-start | bytes 147464 | tf_op jit(solution)/shard_map/ppermute | solution.py:605
  6.0 4.3 %copy-start = (bf16[3,3,256,256]{3,2,1,0:T(8,128)(2,1)S(1)}, bf16[3,3,256,256]{3,2,1,0:T(8,128)(2,1)}, u32[]{:S(2)}) copy-start(bf16[3,3,256,256]{3,2,1,0:T(8,128)(2,1)} %up_w.7) | copy-start | bytes 3538948
  7.9 4.8 %copy-start.5 = (f32[96,256]{1,0:T(8,128)}, f32[96,256]{1,0:T(8,128)S(1)}, u32[]{:S(2)}) copy-start(f32[96,256]{1,0:T(8,128)S(1)} %get-tuple-element.86.left) | copy-start | bytes 294916
  8.0 4.9 %collective-permute-start.2 = (bf16[128,256]{1,0:T(8,128)(2,1)S(1)}, bf16[128,256]{1,0:T(8,128)(2,1)S(1)}, u32[]{:S(2)}, u32[]{:S(2)}) collective-permute-start(bf16[128,256]{1,0:T(8,128)(2,1)S(1)} %get-tuple-element.62), channel_id=1, source_target_pairs={{0,1},{1,0},{2,3},{3,2},{4,5},{5,4},{6,7},{7,6},{8,9},{9,8},{10,11... | collective-permute-start | bytes 196616 | tf_op jit(solution)/shard_map/ppermute | solution.py:605
  9.6 3.2 %collective-permute-start.3 = (bf16[128,256]{1,0:T(8,128)(2,1)S(1)}, bf16[128,256]{1,0:T(8,128)(2,1)S(1)}, u32[]{:S(2)}, u32[]{:S(2)}) collective-permute-start(bf16[128,256]{1,0:T(8,128)(2,1)S(1)} %get-tuple-element.63), channel_id=1, source_target_pairs={{1,2},{2,1},{5,6},{6,5},{9,10},{10,9},{13,14},{14,13},{17,18},{18,... | collective-permute-start | bytes 196616 | tf_op jit(solution)/shard_map/ppermute | solution.py:605
  12.8 2.4 %collective-permute-start.4 = (bf16[4,288,256]{2,1,0:T(8,128)(2,1)S(1)}, bf16[4,288,256]{2,1,0:T(8,128)(2,1)S(1)}, u32[]{:S(2)}, u32[]{:S(2)}) collective-permute-start(bf16[4,288,256]{2,1,0:T(8,128)(2,1)S(1)} %get-tuple-element.81), channel_id=1, source_target_pairs={{0,4},{4,0},{8,12},{12,8},{16,20},{20,16},{24,28},{28,24},{1,5},{5... | collective-permute-start | bytes 1769480 | tf_op jit(solution)/shard_map/ppermute | solution.py:560
  13.1 2.1 %collective-permute-start.5 = (bf16[14,32,256]{2,1,0:T(8,128)(2,1)S(1)}, bf16[14,32,256]{2,1,0:T(8,128)(2,1)S(1)}, u32[]{:S(2)}, u32[]{:S(2)}) collective-permute-start(bf16[14,32,256]{2,1,0:T(8,128)(2,1)S(1)} %get-tuple-element.82.edge), channel_id=1, source_target_pairs={{0,4},{4,0},{8,12},{12,8},{16,20},{20,16},{24,28},{28,24},{1,5},{5... | collective-permute-start | bytes 688136 | tf_op jit(solution)/shard_map/ppermute | solution.py:560
  15.1 2.3 %collective-permute-start.6 = (bf16[4,288,256]{2,1,0:T(8,128)(2,1)S(1)}, bf16[4,288,256]{2,1,0:T(8,128)(2,1)S(1)}, u32[]{:S(2)}, u32[]{:S(2)}) collective-permute-start(bf16[4,288,256]{2,1,0:T(8,128)(2,1)S(1)} %get-tuple-element.79), channel_id=1, source_target_pairs={{0,4},{4,0},{8,12},{12,8},{16,20},{20,16},{24,28},{28,24},{1,5},{5... | collective-permute-start | bytes 1769480 | tf_op jit(solution)/shard_map/ppermute | solution.py:560
  15.7 6.8 %collective-permute-start.7 = (bf16[2,288,256]{2,1,0:T(8,128)(2,1)S(1)}, bf16[2,288,256]{2,1,0:T(8,128)(2,1)S(1)}, u32[]{:S(2)}, u32[]{:S(2)}) collective-permute-start(bf16[2,288,256]{2,1,0:T(8,128)(2,1)S(1)} %get-tuple-element.83), channel_id=1, source_target_pairs={{0,8},{4,20},{8,0},{12,28},{16,24},{20,4},{24,16},{28,12},{1,9},{5... | collective-permute-start | bytes 884744 | tf_op jit(solution)/shard_map/ppermute | solution.py:574
  17.3 1.2 %copy-start.2 = (bf16[24,32,256]{2,1,0:T(8,128)(2,1)S(1)}, bf16[24,32,256]{2,1,0:T(8,128)(2,1)}, u32[]{:S(2)}) copy-start(bf16[24,32,256]{2,1,0:T(8,128)(2,1)} %copy-done.1) | copy-start | bytes 1179652
  17.4 1.2 %copy-start.4 = (bf16[12,16,256]{2,1,0:T(8,128)(2,1)S(1)}, bf16[12,16,256]{2,1,0:T(8,128)(2,1)}, u32[]{:S(2)}) copy-start(bf16[12,16,256]{2,1,0:T(8,128)(2,1)} %copy-done.3) | copy-start | bytes 294916
  17.4 1.2 %copy-start.6 = (f32[96,256]{1,0:T(8,128)S(1)}, f32[96,256]{1,0:T(8,128)}, u32[]{:S(2)}) copy-start(f32[96,256]{1,0:T(8,128)} %copy-done.5) | copy-start | bytes 294916
  17.5 8.9 %collective-permute-start.9 = (bf16[2,288,256]{2,1,0:T(8,128)(2,1)S(1)}, bf16[2,288,256]{2,1,0:T(8,128)(2,1)S(1)}, u32[]{:S(2)}, u32[]{:S(2)}) collective-permute-start(bf16[2,288,256]{2,1,0:T(8,128)(2,1)S(1)} %get-tuple-element.85), channel_id=1, source_target_pairs={{0,8},{4,20},{8,0},{12,28},{16,24},{20,4},{24,16},{28,12},{1,9},{5... | collective-permute-start | bytes 884744 | tf_op jit(solution)/shard_map/ppermute | solution.py:574
  22.5 5.7 %collective-permute-start.8 = (bf16[1,288,256]{2,1,0:T(8,128)(2,1)S(1)}, bf16[1,288,256]{2,1,0:T(8,128)(2,1)S(1)}, u32[]{:S(2)}, u32[]{:S(2)}) collective-permute-start(bf16[1,288,256]{2,1,0:T(8,128)(2,1)S(1)} %get-tuple-element.93), channel_id=1, source_target_pairs={{0,16},{4,12},{8,24},{12,4},{16,0},{20,28},{24,8},{28,20},{1,17},{... | collective-permute-start | bytes 442376 | tf_op jit(solution)/shard_map/ppermute | solution.py:574
  26.4 5.2 %collective-permute-start.10 = (bf16[1,288,256]{2,1,0:T(8,128)(2,1)S(1)}, bf16[1,288,256]{2,1,0:T(8,128)(2,1)S(1)}, u32[]{:S(2)}, u32[]{:S(2)}) collective-permute-start(bf16[1,288,256]{2,1,0:T(8,128)(2,1)S(1)} %get-tuple-element.99), channel_id=1, source_target_pairs={{0,16},{4,12},{8,24},{12,4},{16,0},{20,28},{24,8},{28,20},{1,17},{... | collective-permute-start | bytes 442376 | tf_op jit(solution)/shard_map/ppermute | solution.py:574
  31.9 6.6 %collective-permute-start.11 = (bf16[288,128]{1,0:T(8,128)(2,1)S(1)}, bf16[288,128]{1,0:T(8,128)(2,1)S(1)}, u32[]{:S(2)}, u32[]{:S(2)}) collective-permute-start(bf16[288,128]{1,0:T(8,128)(2,1)S(1)} %get-tuple-element.101), channel_id=1, source_target_pairs={{0,3},{1,2},{2,1},{3,0},{4,7},{5,6},{6,5},{7,4},{8,11},{9,10},{10,... | collective-permute-start | bytes 221192 | tf_op jit(solution)/shard_map/ppermute | solution.py:593
  35.5 5.6 %collective-permute-start.12 = (bf16[288,128]{1,0:T(8,128)(2,1)S(1)}, bf16[288,128]{1,0:T(8,128)(2,1)S(1)}, u32[]{:S(2)}, u32[]{:S(2)}) collective-permute-start(bf16[288,128]{1,0:T(8,128)(2,1)S(1)} %get-tuple-element.102), channel_id=1, source_target_pairs={{0,2},{1,3},{2,0},{3,1},{4,6},{5,7},{6,4},{7,5},{8,10},{9,11},{10,... | collective-permute-start | bytes 221192 | tf_op jit(solution)/shard_map/ppermute | solution.py:593
  38.0 4.4 %collective-permute-start.13 = (bf16[288,128]{1,0:T(8,128)(2,1)S(1)}, bf16[288,128]{1,0:T(8,128)(2,1)S(1)}, u32[]{:S(2)}, u32[]{:S(2)}) collective-permute-start(bf16[288,128]{1,0:T(8,128)(2,1)S(1)} %get-tuple-element.103), channel_id=1, source_target_pairs={{0,1},{1,0},{2,3},{3,2},{4,5},{5,4},{6,7},{7,6},{8,9},{9,8},{10,11... | collective-permute-start | bytes 221192 | tf_op jit(solution)/shard_map/ppermute | solution.py:593

commit v17 on v15

--- a/solution.py
+++ b/solution.py
@@ -704,7 +704,6 @@
                 ],
                 0, phases, after(ring_grad, to_up), up_weight,
             )[0]
-            own_up = after(own_up, grad_coarse)
     grad_conv, grad_up = band_sum(own_conv, got_conv, own_up, got_up)
     return (decoded, grad_coarse, grad_up, grad_conv)
 

time: 43.3 us -> 43.3 us (level)
    ppermute x3, waiting for transfers between devices: 3.86 us -> 2.65 us  [band_sum(): lax.ppermute(messages[k - 1], 'band', xor_pairs(bands, k))]
    ppermute x4, waiting for transfers between devices: 5.6 us -> 6.81 us  [plane_swap(): lax.ppermute(message, 'face', [(i, i ^ 2 << orders[i % 2][step]) for i in...]
where the time goes in v17:
time: 43.3 us; the launch traced here: 43.2 us
  starting transfers between devices  19.9 us (46%)
  Pallas kernels  12.9 us (30%)
  waiting for transfers between devices  9.48 us (22%)
  between operations  0.83 us (2%)
    pallas_call x16, Pallas kernels, kernel_call(): pl.pallas_call(body, out_shape=tuple(outs), in_specs=[hbm if i in far els...  12.9 us
    ppermute x4, waiting for transfers between devices, plane_swap(): lax.ppermute(message, 'face', [(i, i ^ 2 << orders[i % 2][step]) for i in...  6.81 us
    ppermute x3, starting transfers between devices, band_sum(): lax.ppermute(messages[k - 1], 'band', xor_pairs(bands, k))  6.56 us
    ppermute x4, starting transfers between devices, swap(): return (lax.ppermute(first, axis, one), lax.ppermute(second, axis, two))  6.38 us
    ppermute x4, starting transfers between devices, plane_swap(): lax.ppermute(message, 'face', [(i, i ^ 2 << orders[i % 2][step]) for i in...  6.27 us
    ppermute x3, waiting for transfers between devices, band_sum(): lax.ppermute(messages[k - 1], 'band', xor_pairs(bands, k))  2.65 us
  transfers between devices with their start and end apart: 14, of which 5 were waited for; matrix products, arithmetic and copies ran while one was open for 0% of the time, Pallas kernels for 24%

profile of v17, /device:TPU:0, one launch (start us, length us, event | category | flops | bytes accessed | tf_op | source)
XLA Modules:
  0.0 43.2 jit_solution(16749282489622833843)
XLA Ops:
  0.6 1.2 %shard_map.84 = (bf16[96,256]{1,0:T(8,128)(2,1)S(1)}, bf16[96,256]{1,0:T(8,128)(2,1)S(1)}, bf16[24,32,256]{2,1,0:T(8,128)(2,1)S(1)}, bf16[24,32,256]{2,1,0:T(8,128)(2,1)S(1)}, bf16[12,16,256]{2,1,0:T(8,128)(2,1)S(1)}) custom-call(bf16[12,16,256]{2,1,0:T(8,128)(2,1)} %coarse.1, bf16[24,32,256]{2,1,0:T(8,128)(2,1)} %skip.1, bf16[24,32,256]{2,1,0:T(8,128)(2,1)} %cot.1), custom_call_target="tpu_custom_call" | custom-call | bytes 1867776 | tf_op jit(solution)/shard_map/pallas_call | solution.py:28
  2.4 3.6 %collective-permute-start.1 = (bf16[96,256]{1,0:T(8,128)(2,1)S(1)}, bf16[96,256]{1,0:T(8,128)(2,1)S(1)}, u32[]{:S(2)}, u32[]{:S(2)}) collective-permute-start(bf16[96,256]{1,0:T(8,128)(2,1)S(1)} %get-tuple-element.60), channel_id=1, source_target_pairs={{0,28},{4,8},{8,4},{12,16},{16,12},{20,24},{24,20},{28,0},{1,29},{... | collective-permute-start | bytes 147464 | tf_op jit(solution)/shard_map/ppermute | solution.py:605
  6.0 1.9 %shard_map.85 = (bf16[3,3,256,256]{3,2,1,0:T(8,128)(2,1)S(1)}, f32[768,256]{1,0:T(8,128)S(1)}) custom-call(bf16[24,32,256]{2,1,0:T(8,128)(2,1)S(1)} %get-tuple-element.58.cot, bf16[3,3,256,256]{3,2,1,0:T(8,128)(2,1)} %conv_w.1), custom_call_target="tpu_custom_call" | custom-call | bytes 3538944 | tf_op jit(solution)/shard_map/pallas_call | solution.py:28
  8.0 1.7 %collective-permute-start.2 = (bf16[128,256]{1,0:T(8,128)(2,1)S(1)}, bf16[128,256]{1,0:T(8,128)(2,1)S(1)}, u32[]{:S(2)}, u32[]{:S(2)}) collective-permute-start(bf16[128,256]{1,0:T(8,128)(2,1)S(1)} %get-tuple-element.61), channel_id=1, source_target_pairs={{0,1},{1,0},{2,3},{3,2},{4,5},{5,4},{6,7},{7,6},{8,9},{9,8},{10,11... | collective-permute-start | bytes 196616 | tf_op jit(solution)/shard_map/ppermute | solution.py:605
  9.6 0.7 %collective-permute-start.3 = (bf16[128,256]{1,0:T(8,128)(2,1)S(1)}, bf16[128,256]{1,0:T(8,128)(2,1)S(1)}, u32[]{:S(2)}, u32[]{:S(2)}) collective-permute-start(bf16[128,256]{1,0:T(8,128)(2,1)S(1)} %get-tuple-element.62), channel_id=1, source_target_pairs={{1,2},{2,1},{5,6},{6,5},{9,10},{10,9},{13,14},{14,13},{17,18},{18,... | collective-permute-start | bytes 196616 | tf_op jit(solution)/shard_map/ppermute | solution.py:605
  10.3 2.4 %shard_map.87 = (bf16[3,26,32,256]{3,2,1,0:T(8,128)(2,1)S(1)}, bf16[2,17,16,256]{3,2,1,0:T(8,128)(2,1)S(1)}, bf16[24,32,256]{2,1,0:T(8,128)(2,1)S(1)}, f32[768,2...) custom-call(bf16[12,16,256]{2,1,0:T(8,128)(2,1)S(1)} %get-tuple-elem, ...), custom_call_target="tpu_custom_call" | custom-call | bytes 10731520 | tf_op jit(solution)/shard_map/pallas_call | solution.py:28
  13.1 0.5 %collective-permute-start.5 = (bf16[14,32,256]{2,1,0:T(8,128)(2,1)S(1)}, bf16[14,32,256]{2,1,0:T(8,128)(2,1)S(1)}, u32[]{:S(2)}, u32[]{:S(2)}) collective-permute-start(bf16[14,32,256]{2,1,0:T(8,128)(2,1)S(1)} %get-tuple-element.81.edge), channel_id=1, source_target_pairs={{0,4},{4,0},{8,12},{12,8},{16,20},{20,16},{24,28},{28,24},{1,5},{5... | collective-permute-start | bytes 688136 | tf_op jit(solution)/shard_map/ppermute | solution.py:560
  13.6 0.7 %shard_map.89.phases = bf16[2,2,16,16,256]{4,3,2,1,0:T(8,128)(2,1)S(1)} custom-call(bf16[3,26,32,256]{3,2,1,0:T(8,128)(2,1)S(1)} %get-tuple-element.73.shifted, f32[768,256]{1,0:T(8,128)S(1)} %get-tuple-element.74.slope, f32[768,256]{1,0:T(8,128)S(1)} %get-tuple-element.75.grad_act, bf16[3,3,256,256]{3,2,1,0:T(8,128)(2,1)S(1)} %get-tuple-element.65.conv_w), custom_call_target="tpu_custom_call" | custom-call | bytes 4554752 | tf_op jit(solution)/shard_map/pallas_call | solution.py:28
  14.3 0.8 %shard_map.90 = (f32[2304,256]{1,0:T(8,128)S(1)}, bf16[4,288,256]{2,1,0:T(8,128)(2,1)S(1)}) custom-call(bf16[2,17,16,256]{3,2,1,0:T(8,128)(2,1)S(1)} %get-tuple-element.72.near, bf16[2,2,16,16,256]{4,3,2,1,0:T(8,128)(2,1)S(1)} %shard_map.89.phases), custom_call_target="tpu_custom_call" | custom-call | bytes 3751936 | tf_op jit(solution)/shard_map/pallas_call | solution.py:28
  15.7 1.7 %collective-permute-start.8 = (bf16[2,288,256]{2,1,0:T(8,128)(2,1)S(1)}, bf16[2,288,256]{2,1,0:T(8,128)(2,1)S(1)}, u32[]{:S(2)}, u32[]{:S(2)}) collective-permute-start(bf16[2,288,256]{2,1,0:T(8,128)(2,1)S(1)} %get-tuple-element.82), channel_id=1, source_target_pairs={{0,8},{4,20},{8,0},{12,28},{16,24},{20,4},{24,16},{28,12},{1,9},{5... | collective-permute-start | bytes 884744 | tf_op jit(solution)/shard_map/ppermute | solution.py:574
  17.5 1.1 %collective-permute-start.7 = (bf16[2,288,256]{2,1,0:T(8,128)(2,1)S(1)}, bf16[2,288,256]{2,1,0:T(8,128)(2,1)S(1)}, u32[]{:S(2)}, u32[]{:S(2)}) collective-permute-start(bf16[2,288,256]{2,1,0:T(8,128)(2,1)S(1)} %get-tuple-element.84), channel_id=1, source_target_pairs={{0,8},{4,20},{8,0},{12,28},{16,24},{20,4},{24,16},{28,12},{1,9},{5... | collective-permute-start | bytes 884744 | tf_op jit(solution)/shard_map/ppermute | solution.py:574
  18.6 0.8 %shard_map.93 = (f32[128,256]{1,0:T(8,128)S(1)}, f32[2,64,128]{2,1,0:T(8,128)S(1)}) custom-call(bf16[12,16,256]{2,1,0:T(8,128)(2,1)S(1)} %copy-done.4, bf16[24,32,256]{2,1,0:T(8,128)(2,1)S(1)} %copy-done.2, f32[96,256]{1,0:T(8,128)S(1)} %copy-done.6, f32[96,256]{1,0:T(8,128)S(1)} %get-tuple-element.63.right, f32[128,256]{1,0:T(8,128)S(1)} %get-tuple-element.86.upper, ...), custom_call_target="tpu_custom_call" | custom-call | bytes 3506176 | tf_op jit(solution)/shard_map/pallas_call | solution.py:28
  19.4 1.8 %shard_map.94 = bf16[24,32,256]{2,1,0:T(8,128)(2,1)} custom-call(bf16[24,32,256]{2,1,0:T(8,128)(2,1)S(1)} %get-tuple-element.71.act, f32[128,256]{1,0:T(8,128)S(1)} %get-tuple-element.88.ring_act, bf16[3,3,256,256]{3,2,1,0:T(8,128)(2,1)S(1)} %get-tuple-element.65.conv_w), custom_call_target="tpu_custom_call" | custom-call | bytes 2097152 | tf_op jit(solution)/shard_map/pallas_call | solution.py:28
  21.2 1.3 %collective-permute-done.8.got = bf16[2,288,256]{2,1,0:T(8,128)(2,1)S(1)} collective-permute-done((bf16[2,288,256]{2,1,0:T(8,128)(2,1)S(1)}, bf16[2,288,256]{2,1,0:T(8,128)(2,1)S(1)}, u32[]{:S(2)}, u32[]{:S(2)}) %collective-permute-start.8) | collective-permute-done | bytes 294944 | tf_op jit(solution)/shard_map/ppermute | solution.py:574
  22.5 1.8 %collective-permute-start.9 = (bf16[1,288,256]{2,1,0:T(8,128)(2,1)S(1)}, bf16[1,288,256]{2,1,0:T(8,128)(2,1)S(1)}, u32[]{:S(2)}, u32[]{:S(2)}) collective-permute-start(bf16[1,288,256]{2,1,0:T(8,128)(2,1)S(1)} %get-tuple-element.96), channel_id=1, source_target_pairs={{0,16},{4,12},{8,24},{12,4},{16,0},{20,28},{24,8},{28,20},{1,17},{... | collective-permute-start | bytes 442376 | tf_op jit(solution)/shard_map/ppermute | solution.py:574
  24.3 2.1 %collective-permute-done.7.got = bf16[2,288,256]{2,1,0:T(8,128)(2,1)S(1)} collective-permute-done((bf16[2,288,256]{2,1,0:T(8,128)(2,1)S(1)}, bf16[2,288,256]{2,1,0:T(8,128)(2,1)S(1)}, u32[]{:S(2)}, u32[]{:S(2)}) %collective-permute-start.7) | collective-permute-done | bytes 294944 | tf_op jit(solution)/shard_map/ppermute | solution.py:574
  26.4 1.8 %collective-permute-start.10 = (bf16[1,288,256]{2,1,0:T(8,128)(2,1)S(1)}, bf16[1,288,256]{2,1,0:T(8,128)(2,1)S(1)}, u32[]{:S(2)}, u32[]{:S(2)}) collective-permute-start(bf16[1,288,256]{2,1,0:T(8,128)(2,1)S(1)} %get-tuple-element.91), channel_id=1, source_target_pairs={{0,16},{4,12},{8,24},{12,4},{16,0},{20,28},{24,8},{28,20},{1,17},{... | collective-permute-start | bytes 442376 | tf_op jit(solution)/shard_map/ppermute | solution.py:574
  28.2 3.4 %collective-permute-done.10.got_up = bf16[1,288,256]{2,1,0:T(8,128)(2,1)S(1)} collective-permute-done((bf16[1,288,256]{2,1,0:T(8,128)(2,1)S(1)}, bf16[1,288,256]{2,1,0:T(8,128)(2,1)S(1)}, u32[]{:S(2)}, u32[]{:S(2)}) %collective-permute-start.10) | collective-permute-done | bytes 147488 | tf_op jit(solution)/shard_map/ppermute | solution.py:574
  31.9 3.5 %collective-permute-start.11 = (bf16[288,128]{1,0:T(8,128)(2,1)S(1)}, bf16[288,128]{1,0:T(8,128)(2,1)S(1)}, u32[]{:S(2)}, u32[]{:S(2)}) collective-permute-start(bf16[288,128]{1,0:T(8,128)(2,1)S(1)} %get-tuple-element.99), channel_id=1, source_target_pairs={{0,3},{1,2},{2,1},{3,0},{4,7},{5,6},{6,5},{7,4},{8,11},{9,10},{10,... | collective-permute-start | bytes 221192 | tf_op jit(solution)/shard_map/ppermute | solution.py:593
  35.5 2.5 %collective-permute-start.12 = (bf16[288,128]{1,0:T(8,128)(2,1)S(1)}, bf16[288,128]{1,0:T(8,128)(2,1)S(1)}, u32[]{:S(2)}, u32[]{:S(2)}) collective-permute-start(bf16[288,128]{1,0:T(8,128)(2,1)S(1)} %get-tuple-element.100), channel_id=1, source_target_pairs={{0,2},{1,3},{2,0},{3,1},{4,6},{5,7},{6,4},{7,5},{8,10},{9,11},{10,... | collective-permute-start | bytes 221192 | tf_op jit(solution)/shard_map/ppermute | solution.py:593
  38.5 1.2 %shard_map.96 = bf16[12,16,256]{2,1,0:T(8,128)(2,1)} custom-call(bf16[2,2,16,16,256]{4,3,2,1,0:T(8,128)(2,1)S(1)} %shard_map.89.phases, f32[2,64,128]{2,1,0:T(8,128)S(1)} %get-tuple-element.92.ring_grad, bf16[3,3,256,256]{3,2,1,0:T(8,128)(2,1)S(1)} %copy-done), custom_call_target="tpu_custom_call" | custom-call | bytes 1867776 | tf_op jit(solution)/shard_map/pallas_call | solution.py:28
  39.7 1.3 %collective-permute-done.12.refs_1_ = bf16[288,128]{1,0:T(8,128)(2,1)S(1)} collective-permute-done((bf16[288,128]{1,0:T(8,128)(2,1)S(1)}, bf16[288,128]{1,0:T(8,128)(2,1)S(1)}, u32[]{:S(2)}, u32[]{:S(2)}) %collective-permute-start.12) | collective-permute-done | bytes 73760 | tf_op jit(solution)/shard_map/ppermute | solution.py:593
  41.0 1.3 %collective-permute-done.13.refs_2_ = bf16[288,128]{1,0:T(8,128)(2,1)S(1)} collective-permute-done((bf16[288,128]{1,0:T(8,128)(2,1)S(1)}, bf16[288,128]{1,0:T(8,128)(2,1)S(1)}, u32[]{:S(2)}, u32[]{:S(2)}) %collective-permute-start.13) | collective-permute-done | bytes 73760 | tf_op jit(solution)/shard_map/ppermute | solution.py:593
  42.4 0.8 %shard_map.99 = (f32[64,288]{1,0:T(8,128)}, f32[64,288]{1,0:T(8,128)}) custom-call(f32[288,128]{1,0:T(8,128)S(1)} %get-tuple-element.98.own, bf16[288,128]{1,0:T(8,128)(2,1)S(1)} %collective-permute-done.11.refs_0_, bf16[288,128]{1,0:T(8,128)(2,1)S(1)} %collective-permute-done.12.refs_1_, bf16[288,128]{1,0:T(8,128)(2,1)S(1)} %collective-permute-done.13.refs_2_), custom_call_target="tpu_custom_call" | custom-call | bytes 516096 | tf_op jit(solution)/shard_map/pallas_call | solution.py:28
  (34 shorter events, 2.5 us)
Async XLA Ops:
  1.9 8.4 %copy-start.1 = (bf16[24,32,256]{2,1,0:T(8,128)(2,1)}, bf16[24,32,256]{2,1,0:T(8,128)(2,1)S(1)}, u32[]{:S(2)}) copy-start(bf16[24,32,256]{2,1,0:T(8,128)(2,1)S(1)} %get-tuple-element.58.cot) | copy-start | bytes 1179652
  1.9 8.4 %copy-start.3 = (bf16[12,16,256]{2,1,0:T(8,128)(2,1)}, bf16[12,16,256]{2,1,0:T(8,128)(2,1)S(1)}, u32[]{:S(2)}) copy-start(bf16[12,16,256]{2,1,0:T(8,128)(2,1)S(1)} %get-tuple-element.54.coarse) | copy-start | bytes 294916
  1.9 6.0 %collective-permute-start = (bf16[96,256]{1,0:T(8,128)(2,1)S(1)}, bf16[96,256]{1,0:T(8,128)(2,1)S(1)}, u32[]{:S(2)}, u32[]{:S(2)}) collective-permute-start(bf16[96,256]{1,0:T(8,128)(2,1)S(1)} %get-tuple-element.59), channel_id=1, source_target_pairs={{0,4},{4,0},{8,12},{12,8},{16,20},{20,16},{24,28},{28,24},{1,5},{5... | collective-permute-start | bytes 147464 | tf_op jit(solution)/shard_map/ppermute | solution.py:605
  2.4 5.5 %collective-permute-start.1 = (bf16[96,256]{1,0:T(8,128)(2,1)S(1)}, bf16[96,256]{1,0:T(8,128)(2,1)S(1)}, u32[]{:S(2)}, u32[]{:S(2)}) collective-permute-start(bf16[96,256]{1,0:T(8,128)(2,1)S(1)} %get-tuple-element.60), channel_id=1, source_target_pairs={{0,28},{4,8},{8,4},{12,16},{16,12},{20,24},{24,20},{28,0},{1,29},{... | collective-permute-start | bytes 147464 | tf_op jit(solution)/shard_map/ppermute | solution.py:605
  6.0 4.3 %copy-start = (bf16[3,3,256,256]{3,2,1,0:T(8,128)(2,1)S(1)}, bf16[3,3,256,256]{3,2,1,0:T(8,128)(2,1)}, u32[]{:S(2)}) copy-start(bf16[3,3,256,256]{3,2,1,0:T(8,128)(2,1)} %up_w.7) | copy-start | bytes 3538948
  7.9 4.8 %copy-start.5 = (f32[96,256]{1,0:T(8,128)}, f32[96,256]{1,0:T(8,128)S(1)}, u32[]{:S(2)}) copy-start(f32[96,256]{1,0:T(8,128)S(1)} %get-tuple-element.85.left) | copy-start | bytes 294916
  8.0 4.9 %collective-permute-start.2 = (bf16[128,256]{1,0:T(8,128)(2,1)S(1)}, bf16[128,256]{1,0:T(8,128)(2,1)S(1)}, u32[]{:S(2)}, u32[]{:S(2)}) collective-permute-start(bf16[128,256]{1,0:T(8,128)(2,1)S(1)} %get-tuple-element.61), channel_id=1, source_target_pairs={{0,1},{1,0},{2,3},{3,2},{4,5},{5,4},{6,7},{7,6},{8,9},{9,8},{10,11... | collective-permute-start | bytes 196616 | tf_op jit(solution)/shard_map/ppermute | solution.py:605
  9.6 3.2 %collective-permute-start.3 = (bf16[128,256]{1,0:T(8,128)(2,1)S(1)}, bf16[128,256]{1,0:T(8,128)(2,1)S(1)}, u32[]{:S(2)}, u32[]{:S(2)}) collective-permute-start(bf16[128,256]{1,0:T(8,128)(2,1)S(1)} %get-tuple-element.62), channel_id=1, source_target_pairs={{1,2},{2,1},{5,6},{6,5},{9,10},{10,9},{13,14},{14,13},{17,18},{18,... | collective-permute-start | bytes 196616 | tf_op jit(solution)/shard_map/ppermute | solution.py:605
  12.8 2.4 %collective-permute-start.4 = (bf16[4,288,256]{2,1,0:T(8,128)(2,1)S(1)}, bf16[4,288,256]{2,1,0:T(8,128)(2,1)S(1)}, u32[]{:S(2)}, u32[]{:S(2)}) collective-permute-start(bf16[4,288,256]{2,1,0:T(8,128)(2,1)S(1)} %get-tuple-element.80), channel_id=1, source_target_pairs={{0,4},{4,0},{8,12},{12,8},{16,20},{20,16},{24,28},{28,24},{1,5},{5... | collective-permute-start | bytes 1769480 | tf_op jit(solution)/shard_map/ppermute | solution.py:560
  13.1 2.1 %collective-permute-start.5 = (bf16[14,32,256]{2,1,0:T(8,128)(2,1)S(1)}, bf16[14,32,256]{2,1,0:T(8,128)(2,1)S(1)}, u32[]{:S(2)}, u32[]{:S(2)}) collective-permute-start(bf16[14,32,256]{2,1,0:T(8,128)(2,1)S(1)} %get-tuple-element.81.edge), channel_id=1, source_target_pairs={{0,4},{4,0},{8,12},{12,8},{16,20},{20,16},{24,28},{28,24},{1,5},{5... | collective-permute-start | bytes 688136 | tf_op jit(solution)/shard_map/ppermute | solution.py:560
  15.1 2.3 %collective-permute-start.6 = (bf16[4,288,256]{2,1,0:T(8,128)(2,1)S(1)}, bf16[4,288,256]{2,1,0:T(8,128)(2,1)S(1)}, u32[]{:S(2)}, u32[]{:S(2)}) collective-permute-start(bf16[4,288,256]{2,1,0:T(8,128)(2,1)S(1)} %get-tuple-element.78), channel_id=1, source_target_pairs={{0,4},{4,0},{8,12},{12,8},{16,20},{20,16},{24,28},{28,24},{1,5},{5... | collective-permute-start | bytes 1769480 | tf_op jit(solution)/shard_map/ppermute | solution.py:560
  15.7 6.8 %collective-permute-start.8 = (bf16[2,288,256]{2,1,0:T(8,128)(2,1)S(1)}, bf16[2,288,256]{2,1,0:T(8,128)(2,1)S(1)}, u32[]{:S(2)}, u32[]{:S(2)}) collective-permute-start(bf16[2,288,256]{2,1,0:T(8,128)(2,1)S(1)} %get-tuple-element.82), channel_id=1, source_target_pairs={{0,8},{4,20},{8,0},{12,28},{16,24},{20,4},{24,16},{28,12},{1,9},{5... | collective-permute-start | bytes 884744 | tf_op jit(solution)/shard_map/ppermute | solution.py:574
  17.3 1.2 %copy-start.2 = (bf16[24,32,256]{2,1,0:T(8,128)(2,1)S(1)}, bf16[24,32,256]{2,1,0:T(8,128)(2,1)}, u32[]{:S(2)}) copy-start(bf16[24,32,256]{2,1,0:T(8,128)(2,1)} %copy-done.1) | copy-start | bytes 1179652
  17.4 1.2 %copy-start.4 = (bf16[12,16,256]{2,1,0:T(8,128)(2,1)S(1)}, bf16[12,16,256]{2,1,0:T(8,128)(2,1)}, u32[]{:S(2)}) copy-start(bf16[12,16,256]{2,1,0:T(8,128)(2,1)} %copy-done.3) | copy-start | bytes 294916
  17.4 1.2 %copy-start.6 = (f32[96,256]{1,0:T(8,128)S(1)}, f32[96,256]{1,0:T(8,128)}, u32[]{:S(2)}) copy-start(f32[96,256]{1,0:T(8,128)} %copy-done.5) | copy-start | bytes 294916
  17.5 8.9 %collective-permute-start.7 = (bf16[2,288,256]{2,1,0:T(8,128)(2,1)S(1)}, bf16[2,288,256]{2,1,0:T(8,128)(2,1)S(1)}, u32[]{:S(2)}, u32[]{:S(2)}) collective-permute-start(bf16[2,288,256]{2,1,0:T(8,128)(2,1)S(1)} %get-tuple-element.84), channel_id=1, source_target_pairs={{0,8},{4,20},{8,0},{12,28},{16,24},{20,4},{24,16},{28,12},{1,9},{5... | collective-permute-start | bytes 884744 | tf_op jit(solution)/shard_map/ppermute | solution.py:574
  22.5 5.7 %collective-permute-start.9 = (bf16[1,288,256]{2,1,0:T(8,128)(2,1)S(1)}, bf16[1,288,256]{2,1,0:T(8,128)(2,1)S(1)}, u32[]{:S(2)}, u32[]{:S(2)}) collective-permute-start(bf16[1,288,256]{2,1,0:T(8,128)(2,1)S(1)} %get-tuple-element.96), channel_id=1, source_target_pairs={{0,16},{4,12},{8,24},{12,4},{16,0},{20,28},{24,8},{28,20},{1,17},{... | collective-permute-start | bytes 442376 | tf_op jit(solution)/shard_map/ppermute | solution.py:574
  26.4 5.2 %collective-permute-start.10 = (bf16[1,288,256]{2,1,0:T(8,128)(2,1)S(1)}, bf16[1,288,256]{2,1,0:T(8,128)(2,1)S(1)}, u32[]{:S(2)}, u32[]{:S(2)}) collective-permute-start(bf16[1,288,256]{2,1,0:T(8,128)(2,1)S(1)} %get-tuple-element.91), channel_id=1, source_target_pairs={{0,16},{4,12},{8,24},{12,4},{16,0},{20,28},{24,8},{28,20},{1,17},{... | collective-permute-start | bytes 442376 | tf_op jit(solution)/shard_map/ppermute | solution.py:574
  31.9 7.8 %collective-permute-start.11 = (bf16[288,128]{1,0:T(8,128)(2,1)S(1)}, bf16[288,128]{1,0:T(8,128)(2,1)S(1)}, u32[]{:S(2)}, u32[]{:S(2)}) collective-permute-start(bf16[288,128]{1,0:T(8,128)(2,1)S(1)} %get-tuple-element.99), channel_id=1, source_target_pairs={{0,3},{1,2},{2,1},{3,0},{4,7},{5,6},{6,5},{7,4},{8,11},{9,10},{10,... | collective-permute-start | bytes 221192 | tf_op jit(solution)/shard_map/ppermute | solution.py:593
  35.5 5.6 %collective-permute-start.12 = (bf16[288,128]{1,0:T(8,128)(2,1)S(1)}, bf16[288,128]{1,0:T(8,128)(2,1)S(1)}, u32[]{:S(2)}, u32[]{:S(2)}) collective-permute-start(bf16[288,128]{1,0:T(8,128)(2,1)S(1)} %get-tuple-element.100), channel_id=1, source_target_pairs={{0,2},{1,3},{2,0},{3,1},{4,6},{5,7},{6,4},{7,5},{8,10},{9,11},{10,... | collective-permute-start | bytes 221192 | tf_op jit(solution)/shard_map/ppermute | solution.py:593
  38.0 4.4 %collective-permute-start.13 = (bf16[288,128]{1,0:T(8,128)(2,1)S(1)}, bf16[288,128]{1,0:T(8,128)(2,1)S(1)}, u32[]{:S(2)}, u32[]{:S(2)}) collective-permute-start(bf16[288,128]{1,0:T(8,128)(2,1)S(1)} %get-tuple-element.101), channel_id=1, source_target_pairs={{0,1},{1,0},{2,3},{3,2},{4,5},{5,4},{6,7},{7,6},{8,9},{9,8},{10,11... | collective-permute-start | bytes 221192 | tf_op jit(solution)/shard_map/ppermute | solution.py:593
